TPU v7x, 32 devices: a whole 2x2x4 slice. The times are simulated.
32 devices in a mesh: rows: 2 (over x), cols: 16 (over z, y, core).
Axes of the slice: x: 2, y: 2, z: 4, core: 2. Of those that a mesh axis runs over, the one named last changes fastest.
Arguments:
- plan: bfloat16 [4096, 8192], P('rows', 'cols'), may hold values from 0.049804688 to 20
- source: bfloat16 [4096, 512], P('rows', 'cols'), may hold values from -6 to 6
- target: bfloat16 [8192, 512], P('cols', 'rows'), may hold values from -6 to 6
- source_mass: float32 [4096], P('rows'), may hold values from 0.5 to 2
- target_mass: float32 [8192], P('cols'), may hold values from 0.5 to 2
Outputs:
- row_scaling: float32 [4096], P('rows')
- col_scaling: float32 [8192], P('cols')
All inputs are finite; a program needn't handle non-finite values.
Results may differ from a plain program's by a relative error of at most 0.00089.
Values may be sent and summed in bfloat16 or wider, within the bound.
No kernel may reach another device: no remote copies, remote signals or barrier semaphores. Data moves between devices by JAX's collectives and lax.ppermute only.
A program may use at most 64 MiB of HBM per device.

v0:
```python
import jax
import jax.numpy as jnp
from jax import lax
from jax.sharding import PartitionSpec as P

sharpness = 1.5


def unit_rows(matrix):
    values = matrix.astype(jnp.float32)
    return (values * lax.rsqrt(jnp.sum(values * values, axis=1, keepdims=True) + 1e-06)).astype(
        jnp.bfloat16
    )


def body(plan, source, target, source_mass, target_mass):
    sources_unit = unit_rows(lax.all_gather(source, "cols", axis=1, tiled=True))
    targets_unit = unit_rows(lax.all_gather(target, "rows", axis=1, tiled=True))
    projected = jnp.dot(plan, targets_unit, preferred_element_type=jnp.float32).astype(jnp.bfloat16)
    partial_coupling = lax.dot_general(
        sources_unit, projected, (((0,), (0,)), ((), ())), preferred_element_type=jnp.float32
    )
    coupling = lax.psum(partial_coupling, ("rows", "cols"))
    normalized = (coupling * lax.rsqrt(jnp.sum(coupling * coupling) / 2048.0 + 1e-06)).astype(
        jnp.bfloat16
    )
    lifted = jnp.dot(sources_unit, normalized, preferred_element_type=jnp.float32).astype(
        jnp.bfloat16
    )
    scores = lax.dot_general(
        lifted, targets_unit, (((1,), (1,)), ((), ())), preferred_element_type=jnp.float32
    )
    kernel = jnp.exp(sharpness * scores)
    source_count = plan.shape[0] * lax.axis_size("rows")
    target_count = plan.shape[1] * lax.axis_size("cols")
    col_scaling = jnp.ones((plan.shape[1],), jnp.float32)
    row_scaling = source_mass
    for repeat in range(2):
        row_totals = lax.psum(jnp.dot(kernel, col_scaling, precision=lax.Precision.HIGHEST), "cols")
        row_scaling = source_mass / (row_totals / target_count)
        col_totals = lax.psum(jnp.dot(row_scaling, kernel, precision=lax.Precision.HIGHEST), "rows")
        col_scaling = target_mass / (col_totals / source_count)
    return (row_scaling, col_scaling)


def solution(mesh):
    return jax.shard_map(
        body,
        mesh=mesh,
        in_specs=(P("rows", "cols"), P("rows", "cols"), P("cols", "rows"), P("rows"), P("cols")),
        out_specs=(P("rows"), P("cols")),
        check_vma=False,
    )
```

profile of v0, /device:TPU:0, one launch (start us, length us, event | category | flops | bytes accessed | tf_op | source)
XLA Modules:
  0.0 297.7 jit_solution(6843977840057809733)
XLA Ops:
  7.2 0.0 copy-start
  7.2 0.0 all-gather.2.cloned.1.call-start
  7.2 0.7 all-gather.2.cloned.1.call-update
  7.9 0.0 all-reduce.2.cloned.1.call-start
  8.0 10.2 %all_gather.7 = bf16[512,512]{1,0:T(8,128)(2,1)S(1)} all-gather(bf16[512,256]{1,0:T(8,128)(2,1)} %param.7), channel_id=1, replica_groups=mesh['rows'=2,'cols'=16] {'rows'}, dimensions={1}, use_global_device_ids=true | all-gather | bytes 786432 | tf_op jit(solution)/shard_map/all_gather | solution.py:18
  18.1 0.2 fusion.7
  18.3 36.0 %all-gather.2.cloned.1.call-done = bf16[2048,512]{0,1:T(8,128)(2,1)} async-done(((bf16[2048,32]{0,1:T(8,128)(2,1)}), bf16[2048,512]{0,1:T(8,128)(2,1)}) %all-gather.2.cloned.1.call-update) | async-done | bytes 2097168 | tf_op jit(solution)/shard_map/all_gather | solution.py:17
  54.3 2.0 fusion
  56.4 0.0 copy-done
  56.4 5.1 %fusion.3 = f32[512,512]{1,0:T(8,128)} fusion(bf16[2048,512]{0,1:T(8,128)(2,1)} %all-gather.2.cloned.1.call-done, f32[2048]{0:T(1024)S(1)} %add_rsqrt_fusion, bf16[2048,512]{1,0:T(8,128)(2,1)S(1)} %copy-done, bf16[512,512]{1,0:T(8,128)(2,1)S(1)} %all_gather.7, f32[512]{0:T(512)S(1)} %add_rsqrt_fusion.1), kind=kOutput, calls=%fused_computation.7 | convolution fusion | flops 2152464384 | bytes 5777408 | tf_op jit(solution)/shard_map/dot_general | solution.py:20
  61.5 0.0 all-reduce.2.cloned.1.call-update
  61.5 128.7 %all-reduce.2.cloned.1.call-done = f32[512,512]{1,0:T(8,128)} async-done(((f32[512,512]{1,0:T(8,128)}), f32[512,512]{1,0:T(8,128)}) %all-reduce.2.cloned.1.call-update) | async-done | bytes 1048592 | tf_op jit(solution)/shard_map/psum | solution.py:23
  190.2 2.1 multiply_reduce_fusion
  193.0 6.2 %multiply_exponential_fusion = f32[2048,512]{1,0:T(8,128)} fusion(bf16[2048,512]{0,1:T(8,128)(2,1)} %all-gather.2.cloned.1.call-done, f32[2048]{0:T(1024)S(1)} %add_rsqrt_fusion, f32[512,512]{1,0:T(8,128)} %all-reduce.2.cloned.1.call-done, f32[]{:T(128)S(6)} %rsqrt.21, bf16[512,512]{1,0:T(8,128)(2,1)S(1)} %all_gather.7, f32[512]{0:T(512)S(1)} %add_rsqrt_fusion.1), kind=kOutput, calls=%fused_computation.4 | convolution fusion | flops 2154037248 | bytes 7874564 | tf_op jit(solution)/shard_map/dot_general | solution.py:30
  199.2 0.0 copy-start.2
  199.2 0.0 copy-start.3
  199.2 5.8 %fusion.14 = f32[1,2048]{1,0:T(1,128)S(1)} fusion(f32[2048,512]{1,0:T(8,128)} %multiply_exponential_fusion), kind=kOutput, calls=%fused_computation.21 | convolution fusion | flops 12582912 | bytes 4202496 | tf_op jit(solution)/shard_map/dot_general | solution.py:39
  205.0 30.9 %psum.36 = f32[2048]{0:T(1024)S(1)} all-reduce(f32[2048]{0:T(1024)S(1)} %bitcast.18), channel_id=1, replica_groups=mesh['rows'=2,'cols'=16] {'cols'}, use_global_device_ids=true, to_apply=%region_4.0 | all-reduce | flops 2048 | bytes 16384 | tf_op jit(solution)/shard_map/psum | solution.py:39
  235.9 0.0 copy-done.2
  235.9 4.3 %fusion.17 = f32[1,512]{1,0:T(1,128)S(1)} fusion(f32[2048,1]{0,1:T(1,128)S(1)} %bitcast.16, f32[2048,512]{1,0:T(8,128)} %multiply_exponential_fusion), kind=kOutput, calls=%fused_computation.24 | convolution fusion | flops 12582912 | bytes 4204544 | tf_op jit(solution)/shard_map/dot_general | solution.py:41
  240.2 5.1 %psum.37 = f32[512]{0:T(512)S(1)} all-reduce(f32[512]{0:T(512)S(1)} %bitcast.20), channel_id=1, replica_groups=mesh['rows'=2,'cols'=16] {'rows'}, use_global_device_ids=true, to_apply=%region_5.0 | all-reduce | flops 512 | bytes 4096 | tf_op jit(solution)/shard_map/psum | solution.py:41
  245.3 0.0 copy-done.3
  245.3 5.8 %fusion.18 = f32[1,2048]{1,0:T(1,128)S(1)} fusion(f32[2048,512]{1,0:T(8,128)} %multiply_exponential_fusion, f32[512,1]{0,1:T(1,128)S(1)} %bitcast.19), kind=kOutput, calls=%fused_computation.25 | convolution fusion | flops 12582912 | bytes 4204544 | tf_op jit(solution)/shard_map/dot_general | solution.py:39
  251.0 30.0 %psum.38 = f32[2048]{0:T(1024)S(1)} all-reduce(f32[2048]{0:T(1024)S(1)} %bitcast.17), channel_id=1, replica_groups=mesh['rows'=2,'cols'=16] {'cols'}, use_global_device_ids=true, to_apply=%region_6.0 | all-reduce | flops 2048 | bytes 16384 | tf_op jit(solution)/shard_map/psum | solution.py:39
  281.1 0.0 copy-start.1
  281.1 4.3 %fusion.19 = f32[1,512]{1,0:T(1,128)S(1)} fusion(f32[2048,1]{0,1:T(1,128)S(1)} %bitcast.15, f32[2048,512]{1,0:T(8,128)} %multiply_exponential_fusion), kind=kOutput, calls=%fused_computation.26 | convolution fusion | flops 12582912 | bytes 4204544 | tf_op jit(solution)/shard_map/dot_general | solution.py:41
  285.3 4.9 %psum.39 = f32[512]{0:T(512)S(1)} all-reduce(f32[512]{0:T(512)S(1)} %bitcast.21), channel_id=1, replica_groups=mesh['rows'=2,'cols'=16] {'rows'}, use_global_device_ids=true, to_apply=%region_7.0 | all-reduce | flops 512 | bytes 4096 | tf_op jit(solution)/shard_map/psum | solution.py:41
  290.3 0.6 multiply_divide_fusion.2
  290.9 0.0 copy-done.1
  (5 shorter events, 0.0 us)
Async XLA Ops:
  7.2 49.2 %copy-start = (bf16[2048,512]{1,0:T(8,128)(2,1)S(1)}, bf16[2048,512]{1,0:T(8,128)(2,1)}, u32[]{:S(2)}) copy-start(bf16[2048,512]{1,0:T(8,128)(2,1)} %param.5) | copy-start | bytes 6291460
  7.2 47.1 %all-gather.2.cloned.1.call-start = ((), (), s32[]{:S(2)}) async-start(), calls=%async_computation | async-start | bytes 2228224 | tf_op jit(solution)/shard_map/all_gather | solution.py:17
  7.9 182.3 %all-reduce.2.cloned.1.call-start = ((), (), s32[]{:S(2)}) async-start(), calls=%async_computation.1 | async-start | bytes 2097152 | tf_op jit(solution)/shard_map/psum | solution.py:23
  199.2 36.7 %copy-start.2 = (f32[2048]{0:T(1024)S(1)}, f32[2048]{0:T(1024)}, u32[]{:S(2)}) copy-start(f32[2048]{0:T(1024)} %param.8) | copy-start | bytes 24580
  199.2 46.1 %copy-start.3 = (f32[512]{0:T(512)S(1)}, f32[512]{0:T(512)}, u32[]{:S(2)}) copy-start(f32[512]{0:T(512)} %param.9) | copy-start | bytes 6148
  281.1 9.8 %copy-start.1 = (f32[2048]{0:T(1024)}, f32[2048]{0:T(1024)S(1)}, u32[]{:S(2)}) copy-start(f32[2048]{0:T(1024)S(1)} %multiply_divide_fusion) | copy-start | bytes 24580
Sparse Core Ops, SparseCore 0:
  10.2 44.0 all-gather.1
  61.6 128.5 all-reduce.1
where the time goes:
time: 298 us
  waiting for transfers between devices  165 us (55%)
  blocking collectives  81.1 us (27%)
  matrix products  31.4 us (11%)
  between operations  14.8 us (5%)
  other arithmetic  4.94 us (2%)
    psum x1, waiting for transfers between devices, body(): coupling = lax.psum(partial_coupling, ('rows', 'cols'))  129 us
    psum x2, blocking collectives, body(): lax.psum(jnp.dot(kernel, col_scaling, precision=lax.Precision.HIGHEST), '...  60.9 us
    all_gather x1, waiting for transfers between devices, body(): sources_unit = unit_rows(lax.all_gather(source, 'cols', axis=1, tiled=True))  36 us
    dot_general x2, matrix products, body(): jnp.dot(kernel, col_scaling, precision=lax.Precision.HIGHEST)  11.6 us
    all_gather x1, blocking collectives, body(): targets_unit = unit_rows(lax.all_gather(target, 'rows', axis=1, tiled=True))  10.2 us
    psum x2, blocking collectives, body(): lax.psum(jnp.dot(row_scaling, kernel, precision=lax.Precision.HIGHEST), '...  10 us
    dot_general x2, matrix products, body(): jnp.dot(row_scaling, kernel, precision=lax.Precision.HIGHEST)  8.53 us
    dot_general x1, matrix products, body(): lax.dot_general(lifted, targets_unit, (((1,), (1,)), ((), ())), preferred...  6.2 us
  transfers between devices with their start and end apart: 2, of which 2 were waited for; matrix products, arithmetic and copies ran while one was open for 0% of the time, Pallas kernels for 0%

commit v1 on v0

v1 whole, which is shorter than its diff:
```python
import functools

import jax
import jax.numpy as jnp
from jax import lax
from jax.experimental import pallas as pl
from jax.experimental.pallas import tpu as pltpu
from jax.sharding import PartitionSpec as P

sharpness = 1.5
LANES = 128
F32 = jnp.float32
BF16 = jnp.bfloat16
VMEM = pl.BlockSpec(memory_space=pltpu.VMEM)
PARAMS = pltpu.CompilerParams(vmem_limit_bytes=40 * 1024 * 1024)


def unit_rows(matrix):
    values = matrix.astype(F32)
    return (values * lax.rsqrt(jnp.sum(values * values, axis=1, keepdims=True) + 1e-06)).astype(
        BF16
    )


def plain_body(plan, source, target, source_mass, target_mass):
    sources_unit = unit_rows(lax.all_gather(source, "cols", axis=1, tiled=True))
    targets_unit = unit_rows(lax.all_gather(target, "rows", axis=1, tiled=True))
    projected = jnp.dot(plan, targets_unit, preferred_element_type=F32).astype(BF16)
    partial_coupling = lax.dot_general(
        sources_unit, projected, (((0,), (0,)), ((), ())), preferred_element_type=F32
    )
    coupling = lax.psum(partial_coupling, ("rows", "cols"))
    normalized = (coupling * lax.rsqrt(jnp.sum(coupling * coupling) / 2048.0 + 1e-06)).astype(BF16)
    lifted = jnp.dot(sources_unit, normalized, preferred_element_type=F32).astype(BF16)
    scores = lax.dot_general(
        lifted, targets_unit, (((1,), (1,)), ((), ())), preferred_element_type=F32
    )
    kernel = jnp.exp(sharpness * scores)
    source_count = plan.shape[0] * lax.axis_size("rows")
    target_count = plan.shape[1] * lax.axis_size("cols")
    col_scaling = jnp.ones((plan.shape[1],), F32)
    row_scaling = source_mass
    for repeat in range(2):
        row_totals = lax.psum(jnp.dot(kernel, col_scaling, precision=lax.Precision.HIGHEST), "cols")
        row_scaling = source_mass / (row_totals / target_count)
        col_totals = lax.psum(jnp.dot(row_scaling, kernel, precision=lax.Precision.HIGHEST), "rows")
        col_scaling = target_mass / (col_totals / source_count)
    return (row_scaling, col_scaling)


def kernel_block(targets, near, far, xs_nn, xs_fn, xs_nf, xs_ff, out, sums):
    a, b = near[...], far[...]
    squares = jnp.sum(a.astype(F32) ** 2) + jnp.sum(b.astype(F32) ** 2)
    scale = lax.rsqrt(squares / 2048.0 + 1e-06)
    nt = (((1,), (1,)), ((), ()))
    left_a = (lax.dot_general(targets[...], a, nt, preferred_element_type=F32) * scale).astype(BF16)
    left_b = (lax.dot_general(targets[...], b, nt, preferred_element_type=F32) * scale).astype(BF16)
    width = min(512, xs_nn.shape[1])
    for side, (first, second) in enumerate(((xs_nn, xs_fn), (xs_nf, xs_ff))):

        def step(i, _):
            here = pl.multiple_of(i * width, width)
            scores = jnp.dot(left_a, first[:, pl.ds(here, width)], preferred_element_type=F32)
            scores += jnp.dot(left_b, second[:, pl.ds(here, width)], preferred_element_type=F32)
            block = jnp.exp(sharpness * scores)
            at = pl.multiple_of(side * first.shape[1] + i * width, width)
            out[:, pl.ds(at, width)] = block
            total = jnp.sum(block, axis=0, keepdims=True)
            row = side * (first.shape[1] // LANES) + i * (width // LANES)
            for j in range(width // LANES):
                sums[pl.ds(row + j, 1), :] = total[:, j * LANES : (j + 1) * LANES]
            return 0

        lax.fori_loop(0, xs_nn.shape[1] // width, step, 0)


def weighted(block, base, height, rows):
    total = jnp.zeros((height, LANES), F32)
    for j in range(rows.shape[0]):
        total += block[pl.ds(base, height), j * LANES : (j + 1) * LANES] * rows[j : j + 1, :]
    return total


def sweep(target_count, block, totals, mass, target_mass, sums, acc, rows_ref):
    count, height = block.shape[1], 64
    rows_ref[...] = mass[...] / (totals[...] / target_count)
    acc[...] = jnp.zeros_like(acc)

    def step(i, _):
        base = pl.multiple_of(i * height, height)
        total = jnp.sum(weighted(block, base, height, rows_ref), axis=1, keepdims=True)
        col = target_mass[pl.ds(base, height), :] / (total / count)
        spread = jnp.broadcast_to(col, (height, LANES))
        for j in range(count // LANES):
            part = block[pl.ds(base, height), j * LANES : (j + 1) * LANES] * spread
            acc[j] += jnp.sum(part.reshape(height // 8, 8, LANES), axis=0)
        return 0

    lax.fori_loop(0, block.shape[0] // height, step, 0)
    sums[...] = jnp.sum(acc[...], axis=1)


def last_sweep(target_count, block, totals, mass, target_mass, rows_out, cols_out, rows_ref, acc):
    count, height = block.shape[1], 64
    rows_ref[...] = mass[...] / (totals[...] / target_count)
    rows_out[...] = rows_ref[: rows_out.shape[0], :]

    def step(i, _):
        base = pl.multiple_of(i * height, height)
        acc[pl.ds(base, height), :] = weighted(block, base, height, rows_ref)
        return 0

    lax.fori_loop(0, block.shape[0] // height, step, 0)
    total = jnp.sum(acc[...].T, axis=0, keepdims=True)
    cols_out[...] = target_mass[...] / (total / count)


def body(plan, source, target, source_mass, target_mass):
    n = lax.axis_size("cols")
    outer = n // 4

    def swap(value, bits):
        return lax.ppermute(value, "cols", [(i, i ^ bits) for i in range(n)])

    def cross(value):
        return lax.ppermute(value, "rows", [(0, 1), (1, 0)])

    sources, targets = plan.shape
    target_count = targets * n
    mine = source.T
    pieces = [mine] + [swap(mine, 4 * j) for j in range(1, outer)]
    near = jnp.concatenate(pieces, axis=0)
    near = jnp.concatenate([near, swap(near, 2)], axis=0)

    targets_unit = unit_rows(jnp.concatenate([target, cross(target)], axis=1))
    projected = jnp.dot(plan, targets_unit, preferred_element_type=F32).astype(BF16)
    projected = (projected.astype(F32) + swap(projected, 1).astype(F32)).astype(BF16)

    squares = jnp.sum(near.astype(F32) ** 2, axis=0, keepdims=True)
    inverse = lax.rsqrt(squares + swap(squares, 1) + 1e-06)
    xs_nn = (near.astype(F32) * inverse).astype(BF16)
    xs_nf = cross(xs_nn)
    xs_fn = swap(xs_nn, 1)

    coupling = jnp.dot(xs_nn, projected, preferred_element_type=F32)
    half = coupling.shape[0] // 2
    coupling = coupling[:half] + swap(coupling[half:].astype(BF16), 2).astype(F32)
    step = 1
    while step < outer:
        other = swap(coupling.astype(BF16), 4 * step).astype(F32)
        other = other.reshape(outer // step, step, -1, coupling.shape[1])
        other = jnp.stack([other[i ^ 1] for i in range(outer // step)])
        coupling = coupling + other.reshape(coupling.shape)
        step *= 2
    other = cross(coupling.astype(BF16)).astype(F32)
    split = coupling.shape[1] // 2
    coupling = coupling + jnp.concatenate([other[:, split:], other[:, :split]], axis=1)
    coupling = coupling.astype(BF16)
    coupling = jnp.concatenate([coupling, swap(coupling, 2)], axis=0)
    coupling_far = swap(coupling, 1)
    xs_ff = swap(xs_nf, 1)

    count = 2 * sources
    block, sums = pl.pallas_call(
        kernel_block,
        out_shape=(
            jax.ShapeDtypeStruct((targets, count), F32),
            jax.ShapeDtypeStruct((count // LANES, LANES), F32),
        ),
        in_specs=[VMEM] * 7,
        out_specs=(VMEM, VMEM),
        compiler_params=PARAMS,
    )(targets_unit, coupling, coupling_far, xs_nn, xs_fn, xs_nf, xs_ff)

    def summed(value):
        bits = 1
        while bits < n:
            value = value + swap(value, bits)
            bits *= 2
        return value

    mass = source_mass.reshape(-1, LANES)
    mass = jnp.concatenate([mass, cross(mass)], axis=0)
    rows_scratch = pltpu.VMEM((count // LANES, LANES), F32)
    sums = pl.pallas_call(
        functools.partial(sweep, target_count),
        out_shape=jax.ShapeDtypeStruct((count // LANES, LANES), F32),
        in_specs=[VMEM] * 4,
        out_specs=VMEM,
        scratch_shapes=[pltpu.VMEM((count // LANES, 8, LANES), F32), rows_scratch],
        compiler_params=PARAMS,
    )(block, summed(sums), mass, target_mass.reshape(-1, 1))
    row_scaling, col_scaling = pl.pallas_call(
        functools.partial(last_sweep, target_count),
        out_shape=(
            jax.ShapeDtypeStruct((sources // LANES, LANES), F32),
            jax.ShapeDtypeStruct((1, targets), F32),
        ),
        in_specs=[VMEM] * 4,
        out_specs=(VMEM, VMEM),
        scratch_shapes=[rows_scratch, pltpu.VMEM((targets, LANES), F32)],
        compiler_params=PARAMS,
    )(block, summed(sums), mass, target_mass.reshape(1, -1))
    return (row_scaling.reshape(-1), col_scaling.reshape(-1))


def pick(mesh, plan, source):
    rows, n = mesh.shape["rows"], mesh.shape["cols"]
    features = source[1] // n
    fits = plan[0] * (plan[1] // n) * 4 <= 16 * 1024 * 1024
    even = n >= 8 and n & (n - 1) == 0 and features % 16 == 0
    whole = plan[0] % (rows * 512) == 0 and plan[1] % (n * 128) == 0
    return body if rows == 2 and fits and even and whole else plain_body


def solution(mesh):
    def run(plan, source, target, source_mass, target_mass):
        chosen = pick(mesh, plan.shape, source.shape)
        return jax.shard_map(
            chosen,
            mesh=mesh,
            in_specs=(P("rows", "cols"), P("rows", "cols"), P("cols", "rows"), P("rows"), P("cols")),
            out_specs=(P("rows"), P("cols")),
            check_vma=False,
        )(plan, source, target, source_mass, target_mass)

    return run
```

time: 298 us -> 117 us (0.39)
  waiting for transfers between devices: 165 us -> 63.1 us
  blocking collectives: 81.1 us -> 0 us
  starting transfers between devices: 0.08 us -> 31.7 us
  matrix products: 31.4 us -> 2.05 us
  between operations: 14.8 us -> 0.98 us
  Pallas kernels: 0 us -> 8.05 us
  local copies, waits for them, and re-layouts: 0.02 us -> 7.88 us
    psum x1 -> x0, waiting for transfers between devices: 129 us -> none  [body(): coupling = lax.psum(partial_coupling, ('rows', 'cols'))]
    psum x4 -> x0, blocking collectives: 70.9 us -> none  [the longest x2 60.9 us: body(): lax.psum(jnp.dot(kernel, col_scaling, precision=lax.Precision.HIGHEST), '...]
    ppermute x0 -> x25, waiting for transfers between devices: none -> 63.1 us  [the longest x21 44.6 us: swap(): return lax.ppermute(value, 'cols', [(i, i ^ bits) for i in range(n)])]
    all_gather x1 -> x0, waiting for transfers between devices: 36 us -> none  [body(): sources_unit = unit_rows(lax.all_gather(source, 'cols', axis=1, tiled=True))]
    ppermute x0 -> x25, starting transfers between devices: none -> 31.7 us  [the longest x21 25.4 us: swap(): return lax.ppermute(value, 'cols', [(i, i ^ bits) for i in range(n)])]
    dot_general x6 -> x2, matrix products: 31.4 us -> 2.05 us  [the longest x1 1.31 us: body(): jnp.dot(plan, targets_unit, preferred_element_type=F32).astype(BF16)]
    all_gather x1 -> x0, blocking collectives: 10.2 us -> none  [body(): targets_unit = unit_rows(lax.all_gather(target, 'rows', axis=1, tiled=True))]
    pallas_call x0 -> x3, Pallas kernels: none -> 8.05 us  [the longest x1 4.13 us: body(): pl.pallas_call(kernel_block, out_shape=(jax.ShapeDtypeStruct((targets, co...]
  transfers between devices with their start and end apart: 2 -> 25, of which waited for: 2 -> 18; matrix products, arithmetic and copies ran while one was open for 0% -> 5% of each run, Pallas kernels for 0% -> 0%
where the time goes in v1:
time: 117 us
  waiting for transfers between devices  63.1 us (54%)
  starting transfers between devices  31.7 us (27%)
  Pallas kernels  8.05 us (7%)
  local copies, waits for them, and re-layouts  7.88 us (7%)
  other arithmetic  3.04 us (3%)
  matrix products  2.05 us (2%)
    ppermute x21, waiting for transfers between devices, swap(): return lax.ppermute(value, 'cols', [(i, i ^ bits) for i in range(n)])  44.6 us
    ppermute x21, starting transfers between devices, swap(): return lax.ppermute(value, 'cols', [(i, i ^ bits) for i in range(n)])  25.4 us
    ppermute x4, waiting for transfers between devices, cross(): return lax.ppermute(value, 'rows', [(0, 1), (1, 0)])  18.4 us
    unnamed x16, local copies, waits for them, and re-layouts  7.62 us
    ppermute x4, starting transfers between devices, cross(): return lax.ppermute(value, 'rows', [(0, 1), (1, 0)])  6.27 us
    pallas_call x1, Pallas kernels, body(): pl.pallas_call(kernel_block, out_shape=(jax.ShapeDtypeStruct((targets, co...  4.13 us
    pallas_call x1, Pallas kernels, body(): pl.pallas_call(functools.partial(sweep, target_count), out_shape=jax.Shap...  2.41 us
  transfers between devices with their start and end apart: 25, of which 18 were waited for; matrix products, arithmetic and copies ran while one was open for 5% of the time, Pallas kernels for 0%

profile of v1, /device:TPU:0, one launch (start us, length us, event | category | flops | bytes accessed | tf_op | source)
XLA Modules:
  0.0 116.8 jit_solution(16815776840342869063)
XLA Ops:
  0.6 3.1 %collective-permute-start.1 = (bf16[32,2048]{1,0:T(8,128)(2,1)}, bf16[32,2048]{1,0:T(8,128)(2,1)S(1)}, u32[]{:S(2)}, u32[]{:S(2)}) collective-permute-start(bf16[32,2048]{1,0:T(8,128)(2,1)} %bitcast.37), channel_id=1, source_target_pairs={{0,4},{1,5},{2,6},{3,7},{4,0},{5,1},{6,2},{7,3},{8,12},{9,13},{10,... | collective-permute-start | bytes 393224 | tf_op jit(solution)/shard_map/ppermute | solution.py:123
  3.7 2.6 %collective-permute-start.2 = (bf16[32,2048]{1,0:T(8,128)(2,1)}, bf16[32,2048]{1,0:T(8,128)(2,1)S(1)}, u32[]{:S(2)}, u32[]{:S(2)}) collective-permute-start(bf16[32,2048]{1,0:T(8,128)(2,1)} %bitcast.38), channel_id=1, source_target_pairs={{0,8},{1,9},{2,10},{3,11},{4,12},{5,13},{6,14},{7,15},{8,0},{9,1},... | collective-permute-start | bytes 393224 | tf_op jit(solution)/shard_map/ppermute | solution.py:123
  6.3 1.7 %collective-permute-start = (bf16[512,256]{1,0:T(8,128)(2,1)}, bf16[512,256]{1,0:T(8,128)(2,1)S(1)}, u32[]{:S(2)}, u32[]{:S(2)}) collective-permute-start(bf16[512,256]{1,0:T(8,128)(2,1)} %param.7), channel_id=1, source_target_pairs={{0,16},{16,0},{1,17},{17,1},{2,18},{18,2},{3,19},{19,3},{4,20},{20... | collective-permute-start | bytes 786440 | tf_op jit(solution)/shard_map/ppermute | solution.py:126
  9.0 5.1 %collective-permute-done = bf16[512,256]{1,0:T(8,128)(2,1)S(1)} collective-permute-done((bf16[512,256]{1,0:T(8,128)(2,1)}, bf16[512,256]{1,0:T(8,128)(2,1)S(1)}, u32[]{:S(2)}, u32[]{:S(2)}) %collective-permute-start) | collective-permute-done | bytes 262176 | tf_op jit(solution)/shard_map/ppermute | solution.py:126
  17.8 1.6 %collective-permute-start.4 = (bf16[128,2048]{1,0:T(8,128)(2,1)S(1)}, bf16[128,2048]{1,0:T(8,128)(2,1)S(1)}, u32[]{:S(2)}, u32[]{:S(2)}) collective-permute-start(bf16[128,2048]{1,0:T(8,128)(2,1)S(1)} %pad_maximum_fusion.1), channel_id=1, source_target_pairs={{0,2},{1,3},{2,0},{3,1},{4,6},{5,7},{6,4},{7,5},{8,10},{9,11},{10,... | collective-permute-start | bytes 1572872 | tf_op jit(solution)/shard_map/ppermute | solution.py:123
  19.4 12.7 %collective-permute-done.4 = bf16[128,2048]{1,0:T(8,128)(2,1)S(1)} collective-permute-done((bf16[128,2048]{1,0:T(8,128)(2,1)S(1)}, bf16[128,2048]{1,0:T(8,128)(2,1)S(1)}, u32[]{:S(2)}, u32[]{:S(2)}) %collective-permute-start.4) | collective-permute-done | bytes 524320 | tf_op jit(solution)/shard_map/ppermute | solution.py:123
  34.7 1.6 %collective-permute-start.7 = (bf16[128,512]{1,0:T(8,128)(2,1)S(1)}, bf16[128,512]{1,0:T(8,128)(2,1)S(1)}, u32[]{:S(2)}, u32[]{:S(2)}) collective-permute-start(bf16[128,512]{1,0:T(8,128)(2,1)S(1)} %slice.85), channel_id=1, source_target_pairs={{0,2},{1,3},{2,0},{3,1},{4,6},{5,7},{6,4},{7,5},{8,10},{9,11},{10,... | collective-permute-start | bytes 393224 | tf_op jit(solution)/shard_map/ppermute | solution.py:123
  36.3 4.1 %collective-permute-done.7 = bf16[128,512]{1,0:T(8,128)(2,1)S(1)} collective-permute-done((bf16[128,512]{1,0:T(8,128)(2,1)S(1)}, bf16[128,512]{1,0:T(8,128)(2,1)S(1)}, u32[]{:S(2)}, u32[]{:S(2)}) %collective-permute-start.7) | collective-permute-done | bytes 131104 | tf_op jit(solution)/shard_map/ppermute | solution.py:123
  41.1 1.5 %collective-permute-start.14 = (bf16[256,2048]{1,0:T(8,128)(2,1)S(1)}, bf16[256,2048]{1,0:T(8,128)(2,1)S(1)}, u32[]{:S(2)}, u32[]{:S(2)}) collective-permute-start(bf16[256,2048]{1,0:T(8,128)(2,1)S(1)} %fusion.2.xs_nn), channel_id=1, source_target_pairs={{0,16},{16,0},{1,17},{17,1},{2,18},{18,2},{3,19},{19,3},{4,20},{20... | collective-permute-start | bytes 3145736 | tf_op jit(solution)/shard_map/ppermute | solution.py:126
  42.6 2.9 %collective-permute-done.8 = bf16[128,512]{1,0:T(8,128)(2,1)S(1)} collective-permute-done((bf16[128,512]{1,0:T(8,128)(2,1)S(1)}, bf16[128,512]{1,0:T(8,128)(2,1)S(1)}, u32[]{:S(2)}, u32[]{:S(2)}) %collective-permute-start.8) | collective-permute-done | bytes 131104 | tf_op jit(solution)/shard_map/ppermute | solution.py:123
  45.6 2.2 %collective-permute-start.9 = (bf16[128,512]{1,0:T(8,128)(2,1)S(1)}, bf16[128,512]{1,0:T(8,128)(2,1)S(1)}, u32[]{:S(2)}, u32[]{:S(2)}) collective-permute-start(bf16[128,512]{1,0:T(8,128)(2,1)S(1)} %get-tuple-element.10), channel_id=1, source_target_pairs={{0,8},{1,9},{2,10},{3,11},{4,12},{5,13},{6,14},{7,15},{8,0},{9,1},... | collective-permute-start | bytes 393224 | tf_op jit(solution)/shard_map/ppermute | solution.py:123
  47.8 5.2 %collective-permute-done.9 = bf16[128,512]{1,0:T(8,128)(2,1)S(1)} collective-permute-done((bf16[128,512]{1,0:T(8,128)(2,1)S(1)}, bf16[128,512]{1,0:T(8,128)(2,1)S(1)}, u32[]{:S(2)}, u32[]{:S(2)}) %collective-permute-start.9) | collective-permute-done | bytes 131104 | tf_op jit(solution)/shard_map/ppermute | solution.py:123
  53.0 1.6 %collective-permute-start.10 = (bf16[128,512]{1,0:T(8,128)(2,1)S(1)}, bf16[128,512]{1,0:T(8,128)(2,1)S(1)}, u32[]{:S(2)}, u32[]{:S(2)}) collective-permute-start(bf16[128,512]{1,0:T(8,128)(2,1)S(1)} %fusion.8), channel_id=1, source_target_pairs={{0,16},{16,0},{1,17},{17,1},{2,18},{18,2},{3,19},{19,3},{4,20},{20... | collective-permute-start | bytes 393224 | tf_op jit(solution)/shard_map/ppermute | solution.py:126
  54.6 12.0 %collective-permute-done.14.xs_nf = bf16[256,2048]{1,0:T(8,128)(2,1)S(1)} collective-permute-done((bf16[256,2048]{1,0:T(8,128)(2,1)S(1)}, bf16[256,2048]{1,0:T(8,128)(2,1)S(1)}, u32[]{:S(2)}, u32[]{:S(2)}) %collective-permute-start.14) | collective-permute-done | bytes 1048608 | tf_op jit(solution)/shard_map/ppermute | solution.py:126
  68.1 1.6 %collective-permute-start.11 = (bf16[128,512]{1,0:T(8,128)(2,1)S(1)}, bf16[128,512]{1,0:T(8,128)(2,1)S(1)}, u32[]{:S(2)}, u32[]{:S(2)}) collective-permute-start(bf16[128,512]{1,0:T(8,128)(2,1)S(1)} %fusion.6), channel_id=1, source_target_pairs={{0,2},{1,3},{2,0},{3,1},{4,6},{5,7},{6,4},{7,5},{8,10},{9,11},{10,... | collective-permute-start | bytes 393224 | tf_op jit(solution)/shard_map/ppermute | solution.py:123
  69.7 3.4 %collective-permute-done.11 = bf16[128,512]{1,0:T(8,128)(2,1)S(1)} collective-permute-done((bf16[128,512]{1,0:T(8,128)(2,1)S(1)}, bf16[128,512]{1,0:T(8,128)(2,1)S(1)}, u32[]{:S(2)}, u32[]{:S(2)}) %collective-permute-start.11) | collective-permute-done | bytes 131104 | tf_op jit(solution)/shard_map/ppermute | solution.py:123
  73.3 1.5 %collective-permute-done.12.far = bf16[256,512]{1,0:T(8,128)(2,1)S(1)} collective-permute-done((bf16[256,512]{1,0:T(8,128)(2,1)S(1)}, bf16[256,512]{1,0:T(8,128)(2,1)S(1)}, u32[]{:S(2)}, u32[]{:S(2)}) %collective-permute-start.12) | collective-permute-done | bytes 262176 | tf_op jit(solution)/shard_map/ppermute | solution.py:123
  74.8 4.1 %shard_map.68 = (f32[512,4096]{1,0:T(8,128)S(1)}, f32[32,128]{1,0:T(8,128)S(1)}) custom-call(bf16[512,512]{1,0:T(8,128)(2,1)S(1)} %fusion.5.targets, bf16[256,512]{1,0:T(8,128)(2,1)S(1)} %pad_maximum_fusion.4.near, bf16[256,512]{1,0:T(8,128)(2,1)S(1)} %collective-permute-done.12.far, bf16[256,2048]{1,0:T(8,128)(2,1)S(1)} %fusion.2.xs_nn, ...), custom_call_target="tpu_custom_call" | custom-call | tf_op jit(solution)/shard_map/pallas_call | solution.py:164
  78.9 3.3 %copy-done.1 = f32[512,4096]{1,0:T(8,128)} copy-done((f32[512,4096]{1,0:T(8,128)}, f32[512,4096]{1,0:T(8,128)S(1)}, u32[]{:S(2)}) %copy-start.1) | copy-done | bytes 8388632
  83.4 1.5 %collective-permute-start.17 = (f32[32,128]{1,0:T(8,128)S(1)}, f32[32,128]{1,0:T(8,128)S(1)}, u32[]{:S(2)}, u32[]{:S(2)}) collective-permute-start(f32[32,128]{1,0:T(8,128)S(1)} %add.69), channel_id=1, source_target_pairs={{0,2},{1,3},{2,0},{3,1},{4,6},{5,7},{6,4},{7,5},{8,10},{9,11},{10,... | collective-permute-start | bytes 49160 | tf_op jit(solution)/shard_map/ppermute | solution.py:123
  84.9 2.2 %collective-permute-done.17 = f32[32,128]{1,0:T(8,128)S(1)} collective-permute-done((f32[32,128]{1,0:T(8,128)S(1)}, f32[32,128]{1,0:T(8,128)S(1)}, u32[]{:S(2)}, u32[]{:S(2)}) %collective-permute-start.17) | collective-permute-done | bytes 16416 | tf_op jit(solution)/shard_map/ppermute | solution.py:123
  88.5 1.5 %collective-permute-start.20 = (f32[16,128]{1,0:T(8,128)S(1)}, f32[16,128]{1,0:T(8,128)S(1)}, u32[]{:S(2)}, u32[]{:S(2)}) collective-permute-start(f32[16,128]{1,0:T(8,128)S(1)} %bitcast.44), channel_id=1, source_target_pairs={{0,16},{16,0},{1,17},{17,1},{2,18},{18,2},{3,19},{19,3},{4,20},{20... | collective-permute-start | bytes 24584 | tf_op jit(solution)/shard_map/ppermute | solution.py:126
  90.9 3.5 %collective-permute-start.19 = (f32[32,128]{1,0:T(8,128)S(1)}, f32[32,128]{1,0:T(8,128)S(1)}, u32[]{:S(2)}, u32[]{:S(2)}) collective-permute-start(f32[32,128]{1,0:T(8,128)S(1)} %add.71), channel_id=1, source_target_pairs={{0,8},{1,9},{2,10},{3,11},{4,12},{5,13},{6,14},{7,15},{8,0},{9,1},... | collective-permute-start | bytes 49160 | tf_op jit(solution)/shard_map/ppermute | solution.py:123
  94.4 1.7 %collective-permute-done.19 = f32[32,128]{1,0:T(8,128)S(1)} collective-permute-done((f32[32,128]{1,0:T(8,128)S(1)}, f32[32,128]{1,0:T(8,128)S(1)}, u32[]{:S(2)}, u32[]{:S(2)}) %collective-permute-start.19) | collective-permute-done | bytes 16416 | tf_op jit(solution)/shard_map/ppermute | solution.py:123
  96.1 3.4 %copy-done.2 = f32[512,4096]{1,0:T(8,128)S(1)} copy-done((f32[512,4096]{1,0:T(8,128)S(1)}, f32[512,4096]{1,0:T(8,128)}, u32[]{:S(2)}) %copy-start.2) | copy-done | bytes 8388632
  99.5 2.4 %shard_map.69 = f32[32,128]{1,0:T(8,128)S(1)} custom-call(f32[512,4096]{1,0:T(8,128)S(1)} %copy-done.2, f32[32,128]{1,0:T(8,128)S(1)} %add.72.totals, f32[32,128]{1,0:T(8,128)S(1)} %pad_maximum_fusion.5.mass, f32[512,1]{1,0:T(8,128)S(1)} %copy.7.target_mass), custom_call_target="tpu_custom_call" | custom-call | tf_op jit(solution)/shard_map/pallas_call | solution.py:185
  103.1 1.5 %collective-permute-start.22 = (f32[32,128]{1,0:T(8,128)S(1)}, f32[32,128]{1,0:T(8,128)S(1)}, u32[]{:S(2)}, u32[]{:S(2)}) collective-permute-start(f32[32,128]{1,0:T(8,128)S(1)} %add.73), channel_id=1, source_target_pairs={{0,2},{1,3},{2,0},{3,1},{4,6},{5,7},{6,4},{7,5},{8,10},{9,11},{10,... | collective-permute-start | bytes 49160 | tf_op jit(solution)/shard_map/ppermute | solution.py:123
  104.6 2.2 %collective-permute-done.22 = f32[32,128]{1,0:T(8,128)S(1)} collective-permute-done((f32[32,128]{1,0:T(8,128)S(1)}, f32[32,128]{1,0:T(8,128)S(1)}, u32[]{:S(2)}, u32[]{:S(2)}) %collective-permute-start.22) | collective-permute-done | bytes 16416 | tf_op jit(solution)/shard_map/ppermute | solution.py:123
  107.7 2.9 %collective-permute-done.23 = f32[32,128]{1,0:T(8,128)S(1)} collective-permute-done((f32[32,128]{1,0:T(8,128)S(1)}, f32[32,128]{1,0:T(8,128)S(1)}, u32[]{:S(2)}, u32[]{:S(2)}) %collective-permute-start.23) | collective-permute-done | bytes 16416 | tf_op jit(solution)/shard_map/ppermute | solution.py:123
  110.6 2.9 %collective-permute-start.24 = (f32[32,128]{1,0:T(8,128)S(1)}, f32[32,128]{1,0:T(8,128)S(1)}, u32[]{:S(2)}, u32[]{:S(2)}) collective-permute-start(f32[32,128]{1,0:T(8,128)S(1)} %add.75), channel_id=1, source_target_pairs={{0,8},{1,9},{2,10},{3,11},{4,12},{5,13},{6,14},{7,15},{8,0},{9,1},... | collective-permute-start | bytes 49160 | tf_op jit(solution)/shard_map/ppermute | solution.py:123
  113.5 1.7 %collective-permute-done.24 = f32[32,128]{1,0:T(8,128)S(1)} collective-permute-done((f32[32,128]{1,0:T(8,128)S(1)}, f32[32,128]{1,0:T(8,128)S(1)}, u32[]{:S(2)}, u32[]{:S(2)}) %collective-permute-start.24) | collective-permute-done | bytes 16416 | tf_op jit(solution)/shard_map/ppermute | solution.py:123
  115.3 1.5 %shard_map.70 = (f32[16,128]{1,0:T(8,128)}, f32[1,512]{1,0:T(1,128)}) custom-call(f32[512,4096]{1,0:T(8,128)S(1)} %copy-done.2, f32[32,128]{1,0:T(8,128)S(1)} %add.76.totals, f32[32,128]{1,0:T(8,128)S(1)} %pad_maximum_fusion.5.mass, f32[1,512]{1,0:T(1,128)S(1)} %bitcast.34), custom_call_target="tpu_custom_call" | custom-call | tf_op jit(solution)/shard_map/pallas_call | solution.py:193
  (69 shorter events, 15.2 us)
Async XLA Ops:
  0.6 15.7 %copy-start = (bf16[2048,512]{1,0:T(8,128)(2,1)S(1)}, bf16[2048,512]{1,0:T(8,128)(2,1)}, u32[]{:S(2)}) copy-start(bf16[2048,512]{1,0:T(8,128)(2,1)} %param.5) | copy-start | bytes 6291460
  0.6 17.1 %collective-permute-start.1 = (bf16[32,2048]{1,0:T(8,128)(2,1)}, bf16[32,2048]{1,0:T(8,128)(2,1)S(1)}, u32[]{:S(2)}, u32[]{:S(2)}) collective-permute-start(bf16[32,2048]{1,0:T(8,128)(2,1)} %bitcast.37), channel_id=1, source_target_pairs={{0,4},{1,5},{2,6},{3,7},{4,0},{5,1},{6,2},{7,3},{8,12},{9,13},{10,... | collective-permute-start | bytes 393224 | tf_op jit(solution)/shard_map/ppermute | solution.py:123
  3.7 14.0 %collective-permute-start.2 = (bf16[32,2048]{1,0:T(8,128)(2,1)}, bf16[32,2048]{1,0:T(8,128)(2,1)S(1)}, u32[]{:S(2)}, u32[]{:S(2)}) collective-permute-start(bf16[32,2048]{1,0:T(8,128)(2,1)} %bitcast.38), channel_id=1, source_target_pairs={{0,8},{1,9},{2,10},{3,11},{4,12},{5,13},{6,14},{7,15},{8,0},{9,1},... | collective-permute-start | bytes 393224 | tf_op jit(solution)/shard_map/ppermute | solution.py:123
  6.3 11.4 %collective-permute-start.3 = (bf16[32,2048]{1,0:T(8,128)(2,1)}, bf16[32,2048]{1,0:T(8,128)(2,1)S(1)}, u32[]{:S(2)}, u32[]{:S(2)}) collective-permute-start(bf16[32,2048]{1,0:T(8,128)(2,1)} %bitcast.39), channel_id=1, source_target_pairs={{0,12},{1,13},{2,14},{3,15},{4,8},{5,9},{6,10},{7,11},{8,4},{9,5},... | collective-permute-start | bytes 393224 | tf_op jit(solution)/shard_map/ppermute | solution.py:123
  6.3 7.7 %collective-permute-start = (bf16[512,256]{1,0:T(8,128)(2,1)}, bf16[512,256]{1,0:T(8,128)(2,1)S(1)}, u32[]{:S(2)}, u32[]{:S(2)}) collective-permute-start(bf16[512,256]{1,0:T(8,128)(2,1)} %param.7), channel_id=1, source_target_pairs={{0,16},{16,0},{1,17},{17,1},{2,18},{18,2},{3,19},{19,3},{4,20},{20... | collective-permute-start | bytes 786440 | tf_op jit(solution)/shard_map/ppermute | solution.py:126
  16.3 1.4 %copy-start.4 = (bf16[2048,32]{0,1:T(8,128)(2,1)S(1)}, bf16[2048,32]{0,1:T(8,128)(2,1)}, u32[]{:S(2)}) copy-start(bf16[2048,32]{0,1:T(8,128)(2,1)} %param.6) | copy-start | bytes 393220
  17.6 16.3 %collective-permute-start.6 = (bf16[2048,512]{0,1:T(8,128)(2,1)S(1)}, bf16[2048,512]{0,1:T(8,128)(2,1)S(1)}, u32[]{:S(2)}, u32[]{:S(2)}) collective-permute-start(bf16[2048,512]{0,1:T(8,128)(2,1)S(1)} %fusion), channel_id=1, source_target_pairs={{0,1},{1,0},{2,3},{3,2},{4,5},{5,4},{6,7},{7,6},{8,9},{9,8},{10,11... | collective-permute-start | bytes 6291464 | tf_op jit(solution)/shard_map/ppermute | solution.py:123
  17.8 14.4 %collective-permute-start.4 = (bf16[128,2048]{1,0:T(8,128)(2,1)S(1)}, bf16[128,2048]{1,0:T(8,128)(2,1)S(1)}, u32[]{:S(2)}, u32[]{:S(2)}) collective-permute-start(bf16[128,2048]{1,0:T(8,128)(2,1)S(1)} %pad_maximum_fusion.1), channel_id=1, source_target_pairs={{0,2},{1,3},{2,0},{3,1},{4,6},{5,7},{6,4},{7,5},{8,10},{9,11},{10,... | collective-permute-start | bytes 1572872 | tf_op jit(solution)/shard_map/ppermute | solution.py:123
  32.4 1.2 %collective-permute-start.5 = (f32[1,2048]{1,0:T(1,128)S(1)}, f32[1,2048]{1,0:T(1,128)S(1)}, u32[]{:S(2)}, u32[]{:S(2)}) collective-permute-start(f32[1,2048]{1,0:T(1,128)S(1)} %bitcast.41), channel_id=1, source_target_pairs={{0,1},{1,0},{2,3},{3,2},{4,5},{5,4},{6,7},{7,6},{8,9},{9,8},{10,11... | collective-permute-start | bytes 24584 | tf_op jit(solution)/shard_map/ppermute | solution.py:123
  34.7 5.6 %collective-permute-start.7 = (bf16[128,512]{1,0:T(8,128)(2,1)S(1)}, bf16[128,512]{1,0:T(8,128)(2,1)S(1)}, u32[]{:S(2)}, u32[]{:S(2)}) collective-permute-start(bf16[128,512]{1,0:T(8,128)(2,1)S(1)} %slice.85), channel_id=1, source_target_pairs={{0,2},{1,3},{2,0},{3,1},{4,6},{5,7},{6,4},{7,5},{8,10},{9,11},{10,... | collective-permute-start | bytes 393224 | tf_op jit(solution)/shard_map/ppermute | solution.py:123
  40.4 5.0 %collective-permute-start.8 = (bf16[128,512]{1,0:T(8,128)(2,1)S(1)}, bf16[128,512]{1,0:T(8,128)(2,1)S(1)}, u32[]{:S(2)}, u32[]{:S(2)}) collective-permute-start(bf16[128,512]{1,0:T(8,128)(2,1)S(1)} %fusion.7), channel_id=1, source_target_pairs={{0,4},{1,5},{2,6},{3,7},{4,0},{5,1},{6,2},{7,3},{8,12},{9,13},{10,... | collective-permute-start | bytes 393224 | tf_op jit(solution)/shard_map/ppermute | solution.py:123
  41.1 25.5 %collective-permute-start.14 = (bf16[256,2048]{1,0:T(8,128)(2,1)S(1)}, bf16[256,2048]{1,0:T(8,128)(2,1)S(1)}, u32[]{:S(2)}, u32[]{:S(2)}) collective-permute-start(bf16[256,2048]{1,0:T(8,128)(2,1)S(1)} %fusion.2.xs_nn), channel_id=1, source_target_pairs={{0,16},{16,0},{1,17},{17,1},{2,18},{18,2},{3,19},{19,3},{4,20},{20... | collective-permute-start | bytes 3145736 | tf_op jit(solution)/shard_map/ppermute | solution.py:126
  45.6 7.4 %collective-permute-start.9 = (bf16[128,512]{1,0:T(8,128)(2,1)S(1)}, bf16[128,512]{1,0:T(8,128)(2,1)S(1)}, u32[]{:S(2)}, u32[]{:S(2)}) collective-permute-start(bf16[128,512]{1,0:T(8,128)(2,1)S(1)} %get-tuple-element.10), channel_id=1, source_target_pairs={{0,8},{1,9},{2,10},{3,11},{4,12},{5,13},{6,14},{7,15},{8,0},{9,1},... | collective-permute-start | bytes 393224 | tf_op jit(solution)/shard_map/ppermute | solution.py:123
  53.0 15.0 %collective-permute-start.10 = (bf16[128,512]{1,0:T(8,128)(2,1)S(1)}, bf16[128,512]{1,0:T(8,128)(2,1)S(1)}, u32[]{:S(2)}, u32[]{:S(2)}) collective-permute-start(bf16[128,512]{1,0:T(8,128)(2,1)S(1)} %fusion.8), channel_id=1, source_target_pairs={{0,16},{16,0},{1,17},{17,1},{2,18},{18,2},{3,19},{19,3},{4,20},{20... | collective-permute-start | bytes 393224 | tf_op jit(solution)/shard_map/ppermute | solution.py:126
  54.6 18.6 %collective-permute-start.13 = (bf16[256,2048]{1,0:T(8,128)(2,1)S(1)}, bf16[256,2048]{1,0:T(8,128)(2,1)S(1)}, u32[]{:S(2)}, u32[]{:S(2)}) collective-permute-start(bf16[256,2048]{1,0:T(8,128)(2,1)S(1)} %fusion.2.xs_nn), channel_id=1, source_target_pairs={{0,1},{1,0},{2,3},{3,2},{4,5},{5,4},{6,7},{7,6},{8,9},{9,8},{10,11... | collective-permute-start | bytes 3145736 | tf_op jit(solution)/shard_map/ppermute | solution.py:123
  66.6 6.7 %collective-permute-start.15 = (bf16[256,2048]{1,0:T(8,128)(2,1)S(1)}, bf16[256,2048]{1,0:T(8,128)(2,1)S(1)}, u32[]{:S(2)}, u32[]{:S(2)}) collective-permute-start(bf16[256,2048]{1,0:T(8,128)(2,1)S(1)} %collective-permute-done.14.xs_nf), channel_id=1, source_target_pairs={{0,1},{1,0},{2,3},{3,2},{4,5},{5,4},{6,7},{7,6},{8,9},{9,8},{10,11... | collective-permute-start | bytes 3145736 | tf_op jit(solution)/shard_map/ppermute | solution.py:123
  68.1 5.0 %collective-permute-start.11 = (bf16[128,512]{1,0:T(8,128)(2,1)S(1)}, bf16[128,512]{1,0:T(8,128)(2,1)S(1)}, u32[]{:S(2)}, u32[]{:S(2)}) collective-permute-start(bf16[128,512]{1,0:T(8,128)(2,1)S(1)} %fusion.6), channel_id=1, source_target_pairs={{0,2},{1,3},{2,0},{3,1},{4,6},{5,7},{6,4},{7,5},{8,10},{9,11},{10,... | collective-permute-start | bytes 393224 | tf_op jit(solution)/shard_map/ppermute | solution.py:123
  73.2 15.4 %copy-start.5 = (f32[2048]{0:T(1024)S(1)}, f32[2048]{0:T(1024)}, u32[]{:S(2)}) copy-start(f32[2048]{0:T(1024)} %param.8) | copy-start | bytes 24580
  73.2 16.9 %copy-start.3 = (f32[512]{0:T(512)S(1)}, f32[512]{0:T(512)}, u32[]{:S(2)}) copy-start(f32[512]{0:T(512)} %param.9) | copy-start | bytes 6148
  73.2 1.6 %collective-permute-start.12 = (bf16[256,512]{1,0:T(8,128)(2,1)S(1)}, bf16[256,512]{1,0:T(8,128)(2,1)S(1)}, u32[]{:S(2)}, u32[]{:S(2)}) collective-permute-start(bf16[256,512]{1,0:T(8,128)(2,1)S(1)} %pad_maximum_fusion.4.near), channel_id=1, source_target_pairs={{0,1},{1,0},{2,3},{3,2},{4,5},{5,4},{6,7},{7,6},{8,9},{9,8},{10,11... | collective-permute-start | bytes 786440 | tf_op jit(solution)/shard_map/ppermute | solution.py:123
  78.9 3.3 %copy-start.1 = (f32[512,4096]{1,0:T(8,128)}, f32[512,4096]{1,0:T(8,128)S(1)}, u32[]{:S(2)}) copy-start(f32[512,4096]{1,0:T(8,128)S(1)} %get-tuple-element.6.block) | copy-start | bytes 25165828
  82.2 1.2 %collective-permute-start.16 = (f32[32,128]{1,0:T(8,128)S(1)}, f32[32,128]{1,0:T(8,128)S(1)}, u32[]{:S(2)}, u32[]{:S(2)}) collective-permute-start(f32[32,128]{1,0:T(8,128)S(1)} %get-tuple-element.7), channel_id=1, source_target_pairs={{0,1},{1,0},{2,3},{3,2},{4,5},{5,4},{6,7},{7,6},{8,9},{9,8},{10,11... | collective-permute-start | bytes 49160 | tf_op jit(solution)/shard_map/ppermute | solution.py:123
  83.4 3.7 %collective-permute-start.17 = (f32[32,128]{1,0:T(8,128)S(1)}, f32[32,128]{1,0:T(8,128)S(1)}, u32[]{:S(2)}, u32[]{:S(2)}) collective-permute-start(f32[32,128]{1,0:T(8,128)S(1)} %add.69), channel_id=1, source_target_pairs={{0,2},{1,3},{2,0},{3,1},{4,6},{5,7},{6,4},{7,5},{8,10},{9,11},{10,... | collective-permute-start | bytes 49160 | tf_op jit(solution)/shard_map/ppermute | solution.py:123
  87.1 3.7 %collective-permute-start.18 = (f32[32,128]{1,0:T(8,128)S(1)}, f32[32,128]{1,0:T(8,128)S(1)}, u32[]{:S(2)}, u32[]{:S(2)}) collective-permute-start(f32[32,128]{1,0:T(8,128)S(1)} %add.70), channel_id=1, source_target_pairs={{0,4},{1,5},{2,6},{3,7},{4,0},{5,1},{6,2},{7,3},{8,12},{9,13},{10,... | collective-permute-start | bytes 49160 | tf_op jit(solution)/shard_map/ppermute | solution.py:123
  88.5 5.8 %collective-permute-start.20 = (f32[16,128]{1,0:T(8,128)S(1)}, f32[16,128]{1,0:T(8,128)S(1)}, u32[]{:S(2)}, u32[]{:S(2)}) collective-permute-start(f32[16,128]{1,0:T(8,128)S(1)} %bitcast.44), channel_id=1, source_target_pairs={{0,16},{16,0},{1,17},{17,1},{2,18},{18,2},{3,19},{19,3},{4,20},{20... | collective-permute-start | bytes 24584 | tf_op jit(solution)/shard_map/ppermute | solution.py:126
  90.9 5.2 %collective-permute-start.19 = (f32[32,128]{1,0:T(8,128)S(1)}, f32[32,128]{1,0:T(8,128)S(1)}, u32[]{:S(2)}, u32[]{:S(2)}) collective-permute-start(f32[32,128]{1,0:T(8,128)S(1)} %add.71), channel_id=1, source_target_pairs={{0,8},{1,9},{2,10},{3,11},{4,12},{5,13},{6,14},{7,15},{8,0},{9,1},... | collective-permute-start | bytes 49160 | tf_op jit(solution)/shard_map/ppermute | solution.py:123
  96.1 3.4 %copy-start.2 = (f32[512,4096]{1,0:T(8,128)S(1)}, f32[512,4096]{1,0:T(8,128)}, u32[]{:S(2)}) copy-start(f32[512,4096]{1,0:T(8,128)} %copy-done.1) | copy-start | bytes 25165828
  101.9 1.2 %collective-permute-start.21 = (f32[32,128]{1,0:T(8,128)S(1)}, f32[32,128]{1,0:T(8,128)S(1)}, u32[]{:S(2)}, u32[]{:S(2)}) collective-permute-start(f32[32,128]{1,0:T(8,128)S(1)} %shard_map.69), channel_id=1, source_target_pairs={{0,1},{1,0},{2,3},{3,2},{4,5},{5,4},{6,7},{7,6},{8,9},{9,8},{10,11... | collective-permute-start | bytes 49160 | tf_op jit(solution)/shard_map/ppermute | solution.py:123
  103.1 3.7 %collective-permute-start.22 = (f32[32,128]{1,0:T(8,128)S(1)}, f32[32,128]{1,0:T(8,128)S(1)}, u32[]{:S(2)}, u32[]{:S(2)}) collective-permute-start(f32[32,128]{1,0:T(8,128)S(1)} %add.73), channel_id=1, source_target_pairs={{0,2},{1,3},{2,0},{3,1},{4,6},{5,7},{6,4},{7,5},{8,10},{9,11},{10,... | collective-permute-start | bytes 49160 | tf_op jit(solution)/shard_map/ppermute | solution.py:123
  106.9 3.7 %collective-permute-start.23 = (f32[32,128]{1,0:T(8,128)S(1)}, f32[32,128]{1,0:T(8,128)S(1)}, u32[]{:S(2)}, u32[]{:S(2)}) collective-permute-start(f32[32,128]{1,0:T(8,128)S(1)} %add.74), channel_id=1, source_target_pairs={{0,4},{1,5},{2,6},{3,7},{4,0},{5,1},{6,2},{7,3},{8,12},{9,13},{10,... | collective-permute-start | bytes 49160 | tf_op jit(solution)/shard_map/ppermute | solution.py:123
  110.6 4.6 %collective-permute-start.24 = (f32[32,128]{1,0:T(8,128)S(1)}, f32[32,128]{1,0:T(8,128)S(1)}, u32[]{:S(2)}, u32[]{:S(2)}) collective-permute-start(f32[32,128]{1,0:T(8,128)S(1)} %add.75), channel_id=1, source_target_pairs={{0,8},{1,9},{2,10},{3,11},{4,12},{5,13},{6,14},{7,15},{8,0},{9,1},... | collective-permute-start | bytes 49160 | tf_op jit(solution)/shard_map/ppermute | solution.py:123

commit v2 on v0

v2 whole, which is shorter than its diff:
```python
import functools

import jax
import jax.numpy as jnp
from jax import lax
from jax.experimental import pallas as pl
from jax.experimental.pallas import tpu as pltpu
from jax.sharding import PartitionSpec as P

sharpness = 1.5
LANES = 128
F32 = jnp.float32
BF16 = jnp.bfloat16
VMEM = pl.BlockSpec(memory_space=pltpu.VMEM)
ANY = pl.BlockSpec(memory_space=pl.ANY)
MIB = 1024 * 1024
LOG2E = 1.4426950408889634


def unit_rows(matrix):
    values = matrix.astype(F32)
    return (values * lax.rsqrt(jnp.sum(values * values, axis=1, keepdims=True) + 1e-06)).astype(
        BF16
    )


def plain_body(plan, source, target, source_mass, target_mass):
    sources_unit = unit_rows(lax.all_gather(source, "cols", axis=1, tiled=True))
    targets_unit = unit_rows(lax.all_gather(target, "rows", axis=1, tiled=True))
    projected = jnp.dot(plan, targets_unit, preferred_element_type=F32).astype(BF16)
    partial_coupling = lax.dot_general(
        sources_unit, projected, (((0,), (0,)), ((), ())), preferred_element_type=F32
    )
    coupling = lax.psum(partial_coupling, ("rows", "cols"))
    normalized = (coupling * lax.rsqrt(jnp.sum(coupling * coupling) / 2048.0 + 1e-06)).astype(BF16)
    lifted = jnp.dot(sources_unit, normalized, preferred_element_type=F32).astype(BF16)
    scores = lax.dot_general(
        lifted, targets_unit, (((1,), (1,)), ((), ())), preferred_element_type=F32
    )
    kernel = jnp.exp(sharpness * scores)
    source_count = plan.shape[0] * lax.axis_size("rows")
    target_count = plan.shape[1] * lax.axis_size("cols")
    col_scaling = jnp.ones((plan.shape[1],), F32)
    row_scaling = source_mass
    for repeat in range(2):
        row_totals = lax.psum(jnp.dot(kernel, col_scaling, precision=lax.Precision.HIGHEST), "cols")
        row_scaling = source_mass / (row_totals / target_count)
        col_totals = lax.psum(jnp.dot(row_scaling, kernel, precision=lax.Precision.HIGHEST), "rows")
        col_scaling = target_mass / (col_totals / source_count)
    return (row_scaling, col_scaling)


def unit_targets(plan, near, near_x, units):
    a, b = near[...].astype(F32), near_x[...].astype(F32)
    squares = jnp.sum(a * a, axis=1, keepdims=True) + jnp.sum(b * b, axis=1, keepdims=True)
    inverse = lax.rsqrt(squares + 1e-06)
    units[:, : a.shape[1]] = (a * inverse).astype(BF16)
    units[:, a.shape[1] :] = (b * inverse).astype(BF16)


def project(start, plan, plan_far, units, units_far, out):
    height = min(512, out.shape[0])

    def step(i, _):
        at = pl.multiple_of(i * height, height)
        here = pl.ds(pl.multiple_of(start + i * height, height), height)
        total = jnp.dot(plan[here, :], units[...], preferred_element_type=F32)
        total += jnp.dot(plan_far[here, :], units_far[...], preferred_element_type=F32)
        out[pl.ds(at, height), :] = total.astype(BF16)
        return 0

    lax.fori_loop(0, out.shape[0] // height, step, 0)


def sum_squares(*refs):
    total = 0.0
    for piece in refs[:-1]:
        total += jnp.sum(piece[...].astype(F32) ** 2, axis=0, keepdims=True)
    refs[-1][...] = total


def couple(p0, p1, p2, p3, p4, p5, p6, p7, squares, squares_y, upper, lower, keep, to_x, to_y, to_xy, units):
    inverse = lax.rsqrt(squares[...] + squares_y[...] + 1e-06)
    rows = p0.shape[0]
    for i, piece in enumerate((p0, p1, p2, p3, p4, p5, p6, p7)):
        units[i * rows : (i + 1) * rows, :] = (piece[...].astype(F32) * inverse).astype(BF16)
    half, split = keep.shape
    part = upper.shape[0]
    product = jnp.dot(units[:, :part], upper[...], preferred_element_type=F32)
    product += jnp.dot(units[:, part:], lower[...], preferred_element_type=F32)
    keep[...] = product[:half, :split]
    to_x[...] = product[:half, split:].astype(BF16)
    to_y[...] = product[half:, :split].astype(BF16)
    to_xy[...] = product[half:, split:].astype(BF16)


def kernel_block(targets, c0, x0, c1, x1, c2, x2, c3, x3, near, far, out, sums, left):
    pieces = ((c0, x0), (c1, x1), (c2, x2), (c3, x3))
    rows, split = c0.shape
    squares = 0.0
    for piece in pieces:
        squares += jnp.sum(piece[0][...].astype(F32) ** 2 + piece[1][...].astype(F32) ** 2)
    scale = lax.rsqrt(squares / 2048.0 + 1e-06) * (sharpness * LOG2E)
    nt = (((1,), (1,)), ((), ()))
    for i, piece in enumerate(pieces):
        product = lax.dot_general(targets[:, :split], piece[0][...], nt, preferred_element_type=F32)
        product += lax.dot_general(targets[:, split:], piece[1][...], nt, preferred_element_type=F32)
        left[:, i * rows : (i + 1) * rows] = (product * scale).astype(BF16)
    half = 2 * rows
    width = min(512, near.shape[1])

    def step(i, _):
        here = pl.ds(pl.multiple_of(i * width, width), width)
        scores = jnp.dot(left[:, :half], near[:, here], preferred_element_type=F32)
        scores += jnp.dot(left[:, half:], far[:, here], preferred_element_type=F32)
        block = jnp.exp2(scores)
        out[:, here] = block
        total = jnp.sum(block, axis=0, keepdims=True)
        for j in range(width // LANES):
            row = i * (width // LANES) + j
            sums[pl.ds(row, 1), :] = total[:, j * LANES : (j + 1) * LANES]
        return 0

    lax.fori_loop(0, near.shape[1] // width, step, 0)


def sweep_rows(target_count, block, totals, mass, rows, sums, acc):
    height = 64
    rows[...] = mass[...] / (totals[...] / target_count)

    def step(i, _):
        here = pl.ds(pl.multiple_of(i * height, height), height)
        total = jnp.zeros((height, LANES), F32)
        for j in range(rows.shape[0]):
            total += block[here, j * LANES : (j + 1) * LANES] * rows[j : j + 1, :]
        acc[here, :] = total
        return 0

    lax.fori_loop(0, block.shape[0] // height, step, 0)
    sums[...] = jnp.sum(acc[...].T, axis=0, keepdims=True)


def sweep_cols(source_count, block, totals, totals_x, mass, sums, acc, spread):
    height = 64
    cols = mass[...] / ((totals[...] + totals_x[...]) / source_count)
    spread[...] = jnp.broadcast_to(cols, (LANES, block.shape[0])).T
    acc[...] = jnp.zeros_like(acc)

    def step(i, _):
        here = pl.ds(pl.multiple_of(i * height, height), height)
        for j in range(acc.shape[0]):
            part = block[here, j * LANES : (j + 1) * LANES] * spread[here, :]
            acc[j] += jnp.sum(part.reshape(height // 8, 8, LANES), axis=0)
        return 0

    lax.fori_loop(0, block.shape[0] // height, step, 0)
    sums[...] = jnp.sum(acc[...], axis=1)


def turned(value, order):
    blocks = value.astype(F32).reshape(len(order), -1, value.shape[1])
    return jnp.concatenate([blocks[i] for i in order], axis=0)


def body(plan, source, target, source_mass, target_mass):
    n = lax.axis_size("cols")

    def swap(value, bits):
        return lax.ppermute(value, "cols", [(i, i ^ bits) for i in range(n)])

    def cross(value):
        return lax.ppermute(value, "rows", [(0, 1), (1, 0)])

    def both(value):
        pairs = [(r * n + i, (1 - r) * n + (i ^ 2)) for r in range(2) for i in range(n)]
        return lax.ppermute(value, ("rows", "cols"), pairs)

    def call(function, shapes, *values, scratch=(), mib=16, flops=0, loose=()):
        outs = tuple(jax.ShapeDtypeStruct(shape, kind) for shape, kind in shapes)
        moved = sum(value.size * value.dtype.itemsize for value in values + outs)
        return pl.pallas_call(
            function,
            out_shape=outs,
            in_specs=[ANY if i in loose else VMEM for i in range(len(values))],
            out_specs=(VMEM,) * len(shapes),
            scratch_shapes=[pltpu.VMEM(shape, kind) for shape, kind in scratch],
            compiler_params=pltpu.CompilerParams(vmem_limit_bytes=mib * MIB),
            cost_estimate=pl.CostEstimate(flops=flops, bytes_accessed=moved, transcendentals=0),
        )(*values)

    hold = lax.optimization_barrier
    sources, targets = plan.shape
    target_count = targets * n
    source_count = sources * lax.axis_size("rows")
    features = source.shape[1] * n
    half = features // 4
    split = features // 2

    own = source.T
    z2, z1, y0 = swap(own, 8), swap(own, 4), swap(own, 2)
    wide, part = (targets, features), sources // 2
    target_x = cross(target)
    plan_far = swap(plan, 1)
    (units,) = call(unit_targets, ((wide, BF16),), plan, target, target_x, loose=(0,))
    units, y0, z1, z2 = hold((units, y0, z1, z2))
    units_far = swap(units, 1)
    z3, yz2, yz1 = swap(z2, 4), swap(z2, 2), swap(z1, 2)
    (upper,) = call(
        functools.partial(project, 0),
        (((part, features), BF16),),
        plan,
        plan_far,
        units,
        units_far,
        flops=4 * part * targets * features,
    )
    upper, z3 = hold((upper, z3))
    yz3 = swap(z3, 2)
    (lower,) = call(
        functools.partial(project, part),
        (((part, features), BF16),),
        plan,
        plan_far,
        units,
        units_far,
        flops=4 * part * targets * features,
    )
    (squares,) = call(sum_squares, (((1, sources), F32),), own, z2, z1, z3)
    yz1, yz2, squares, lower = hold((yz1, yz2, squares, lower))
    squares += swap(squares, 1)
    squares_y = swap(squares, 2)
    yz3, squares_y = hold((yz3, squares_y))
    pieces = [own, z2, z1, z3, y0, yz2, yz1, yz3]
    quarter = ((half, split), BF16)
    coupling, to_x, to_y, to_xy, xs = call(
        couple,
        (((half, split), F32), quarter, quarter, quarter, ((split, sources), BF16)),
        *pieces,
        squares,
        squares_y,
        upper,
        lower,
        flops=2 * sources * split * features,
    )
    xs_far = swap(xs, 1)

    for other in (cross(to_x), swap(to_y, 2), both(to_xy)):
        coupling += other.astype(F32)
    coupling += turned(swap(coupling.astype(BF16), 4), (2, 3, 0, 1))
    coupling += turned(swap(coupling.astype(BF16), 8), (1, 0, 3, 2))
    coupling = coupling.astype(BF16)
    blocks = [coupling, cross(coupling), swap(coupling, 2), both(coupling)]
    blocks += [swap(block, 1) for block in blocks]

    tall, wide = (sources // LANES, LANES), (1, targets)
    block, sums = call(
        kernel_block,
        (((targets, sources), F32), (tall, F32)),
        units,
        *blocks,
        xs,
        xs_far,
        scratch=(((targets, features), BF16),),
        flops=2 * targets * features * (sources + features),
    )

    mass, target_mass = source_mass.reshape(tall), target_mass.reshape(wide)
    for repeat in range(2):
        sums = sums + swap(sums, 1)
        sums = sums + swap(sums, 2) + swap(sums, 4) + swap(sums, 6)
        sums = sums + swap(sums, 8)
        rows, totals = call(
            functools.partial(sweep_rows, target_count),
            ((tall, F32), (wide, F32)),
            block,
            sums,
            mass,
            scratch=(((targets, LANES), F32),),
        )
        totals_x = cross(totals)
        if repeat == 0:
            (sums,) = call(
                functools.partial(sweep_cols, source_count),
                ((tall, F32),),
                block,
                totals,
                totals_x,
                target_mass,
                scratch=(((tall[0], 8, LANES), F32), ((targets, LANES), F32)),
            )
    cols = target_mass / ((totals + totals_x) / source_count)
    return (rows.reshape(-1), cols.reshape(-1))


def pick(mesh, plan, source):
    rows, n = mesh.shape["rows"], mesh.shape["cols"]
    features = source[1] // n
    fits = (plan[0] // rows) * (plan[1] // n) * 4 <= 4 * MIB
    even = n == 16 and features % 16 == 0
    whole = plan[0] % (rows * 512) == 0 and plan[1] % (n * 128) == 0
    return body if rows == 2 and fits and even and whole else plain_body


def solution(mesh):
    def run(plan, source, target, source_mass, target_mass):
        chosen = pick(mesh, plan.shape, source.shape)
        return jax.shard_map(
            chosen,
            mesh=mesh,
            in_specs=(P("rows", "cols"), P("rows", "cols"), P("cols", "rows"), P("rows"), P("cols")),
            out_specs=(P("rows"), P("cols")),
            check_vma=False,
        )(plan, source, target, source_mass, target_mass)

    return run
```

time: 298 us -> 93.3 us (0.31)
  waiting for transfers between devices: 165 us -> 36.6 us
  blocking collectives: 81.1 us -> 0 us
  starting transfers between devices: 0.08 us -> 43.5 us
  matrix products: 31.4 us -> 0 us
  between operations: 14.8 us -> 0.82 us
  Pallas kernels: 0 us -> 8.91 us
  other arithmetic: 4.94 us -> 0.7 us
    psum x1 -> x0, waiting for transfers between devices: 129 us -> none  [body(): coupling = lax.psum(partial_coupling, ('rows', 'cols'))]
    psum x4 -> x0, blocking collectives: 70.9 us -> none  [the longest x2 60.9 us: body(): lax.psum(jnp.dot(kernel, col_scaling, precision=lax.Precision.HIGHEST), '...]
    ppermute x0 -> x37, starting transfers between devices: none -> 43.5 us  [the longest x30 33.9 us: swap(): return lax.ppermute(value, 'cols', [(i, i ^ bits) for i in range(n)])]
    ppermute x0 -> x37, waiting for transfers between devices: none -> 36.6 us  [the longest x30 25.9 us: swap(): return lax.ppermute(value, 'cols', [(i, i ^ bits) for i in range(n)])]
    all_gather x1 -> x0, waiting for transfers between devices: 36 us -> none  [body(): sources_unit = unit_rows(lax.all_gather(source, 'cols', axis=1, tiled=True))]
    dot_general x6 -> x0, matrix products: 31.4 us -> none  [the longest x2 11.6 us: body(): jnp.dot(kernel, col_scaling, precision=lax.Precision.HIGHEST)]
    all_gather x1 -> x0, blocking collectives: 10.2 us -> none  [body(): targets_unit = unit_rows(lax.all_gather(target, 'rows', axis=1, tiled=True))]
    pallas_call x0 -> x9, Pallas kernels: none -> 8.91 us  [call(): pl.pallas_call(function, out_shape=outs, in_specs=[ANY if i in loose else...]
  transfers between devices with their start and end apart: 2 -> 37, of which waited for: 2 -> 27; matrix products, arithmetic and copies ran while one was open for 0% -> 0% of each run, Pallas kernels for 0% -> 3%
where the time goes in v2:
time: 93.3 us; the launch traced here: 93.1 us
  starting transfers between devices  43.5 us (47%)
  waiting for transfers between devices  36.6 us (39%)
  Pallas kernels  8.91 us (10%)
  local copies, waits for them, and re-layouts  2.58 us (3%)
    ppermute x30, starting transfers between devices, swap(): return lax.ppermute(value, 'cols', [(i, i ^ bits) for i in range(n)])  33.9 us
    ppermute x30, waiting for transfers between devices, swap(): return lax.ppermute(value, 'cols', [(i, i ^ bits) for i in range(n)])  25.9 us
    pallas_call x9, Pallas kernels, call(): pl.pallas_call(function, out_shape=outs, in_specs=[ANY if i in loose else...  8.91 us
    ppermute x5, starting transfers between devices, cross(): return lax.ppermute(value, 'rows', [(0, 1), (1, 0)])  8.71 us
    ppermute x5, waiting for transfers between devices, cross(): return lax.ppermute(value, 'rows', [(0, 1), (1, 0)])  7.1 us
    ppermute x2, waiting for transfers between devices, both(): return lax.ppermute(value, ('rows', 'cols'), pairs)  3.59 us
    unnamed x12, local copies, waits for them, and re-layouts  2.56 us
  transfers between devices with their start and end apart: 37, of which 27 were waited for; matrix products, arithmetic and copies ran while one was open for 0% of the time, Pallas kernels for 3%

profile of v2, /device:TPU:0, one launch (start us, length us, event | category | flops | bytes accessed | tf_op | source)
XLA Modules:
  0.0 93.1 jit_solution(17649204505956699817)
XLA Ops:
  1.1 2.6 %collective-permute-start = (bf16[512,256]{1,0:T(8,128)(2,1)}, bf16[512,256]{1,0:T(8,128)(2,1)S(1)}, u32[]{:S(2)}, u32[]{:S(2)}) collective-permute-start(bf16[512,256]{1,0:T(8,128)(2,1)} %near.1), channel_id=1, source_target_pairs={{0,16},{16,0},{1,17},{17,1},{2,18},{18,2},{3,19},{19,3},{4,20},{20... | collective-permute-start | bytes 786440 | tf_op jit(solution)/shard_map/ppermute | solution.py:172
  3.7 2.6 %collective-permute-start.3 = (bf16[32,2048]{1,0:T(8,128)(2,1)}, bf16[32,2048]{1,0:T(8,128)(2,1)S(1)}, u32[]{:S(2)}, u32[]{:S(2)}) collective-permute-start(bf16[32,2048]{1,0:T(8,128)(2,1)} %bitcast.5), channel_id=1, source_target_pairs={{0,8},{1,9},{2,10},{3,11},{4,12},{5,13},{6,14},{7,15},{8,0},{9,1},... | collective-permute-start | bytes 393224 | tf_op jit(solution)/shard_map/ppermute | solution.py:169
  6.3 1.6 %collective-permute-start.2 = (bf16[32,2048]{1,0:T(8,128)(2,1)}, bf16[32,2048]{1,0:T(8,128)(2,1)S(1)}, u32[]{:S(2)}, u32[]{:S(2)}) collective-permute-start(bf16[32,2048]{1,0:T(8,128)(2,1)} %bitcast.6), channel_id=1, source_target_pairs={{0,4},{1,5},{2,6},{3,7},{4,0},{5,1},{6,2},{7,3},{8,12},{9,13},{10,... | collective-permute-start | bytes 393224 | tf_op jit(solution)/shard_map/ppermute | solution.py:169
  7.9 1.5 %collective-permute-start.1 = (bf16[32,2048]{1,0:T(8,128)(2,1)}, bf16[32,2048]{1,0:T(8,128)(2,1)S(1)}, u32[]{:S(2)}, u32[]{:S(2)}) collective-permute-start(bf16[32,2048]{1,0:T(8,128)(2,1)} %bitcast.7), channel_id=1, source_target_pairs={{0,2},{1,3},{2,0},{3,1},{4,6},{5,7},{6,4},{7,5},{8,10},{9,11},{10,... | collective-permute-start | bytes 393224 | tf_op jit(solution)/shard_map/ppermute | solution.py:169
  10.8 1.6 %copy-done = bf16[2048,512]{1,0:T(8,128)(2,1)S(1)} copy-done((bf16[2048,512]{1,0:T(8,128)(2,1)S(1)}, bf16[2048,512]{1,0:T(8,128)(2,1)}, u32[]{:S(2)}) %copy-start) | copy-done | bytes 2097176
  13.7 1.9 %collective-permute-start.6 = (bf16[32,2048]{1,0:T(8,128)(2,1)S(1)}, bf16[32,2048]{1,0:T(8,128)(2,1)S(1)}, u32[]{:S(2)}, u32[]{:S(2)}) collective-permute-start(bf16[32,2048]{1,0:T(8,128)(2,1)S(1)} %collective-permute-done.3.refs_1_.p1), channel_id=1, source_target_pairs={{0,4},{1,5},{2,6},{3,7},{4,0},{5,1},{6,2},{7,3},{8,12},{9,13},{10,... | collective-permute-start | bytes 393224 | tf_op jit(solution)/shard_map/ppermute | solution.py:169
  15.6 1.6 %collective-permute-start.8 = (bf16[32,2048]{1,0:T(8,128)(2,1)S(1)}, bf16[32,2048]{1,0:T(8,128)(2,1)S(1)}, u32[]{:S(2)}, u32[]{:S(2)}) collective-permute-start(bf16[32,2048]{1,0:T(8,128)(2,1)S(1)} %collective-permute-done.3.refs_1_.p1), channel_id=1, source_target_pairs={{0,2},{1,3},{2,0},{3,1},{4,6},{5,7},{6,4},{7,5},{8,10},{9,11},{10,... | collective-permute-start | bytes 393224 | tf_op jit(solution)/shard_map/ppermute | solution.py:169
  19.7 1.7 %collective-permute-start.9 = (bf16[32,2048]{1,0:T(8,128)(2,1)S(1)}, bf16[32,2048]{1,0:T(8,128)(2,1)S(1)}, u32[]{:S(2)}, u32[]{:S(2)}) collective-permute-start(bf16[32,2048]{1,0:T(8,128)(2,1)S(1)} %collective-permute-done.6.refs_3_.p3), channel_id=1, source_target_pairs={{0,2},{1,3},{2,0},{3,1},{4,6},{5,7},{6,4},{7,5},{8,10},{9,11},{10,... | collective-permute-start | bytes 393224 | tf_op jit(solution)/shard_map/ppermute | solution.py:169
  23.0 1.8 %collective-permute-done.7.p6 = bf16[32,2048]{1,0:T(8,128)(2,1)S(1)} collective-permute-done((bf16[32,2048]{1,0:T(8,128)(2,1)S(1)}, bf16[32,2048]{1,0:T(8,128)(2,1)S(1)}, u32[]{:S(2)}, u32[]{:S(2)}) %collective-permute-start.7) | collective-permute-done | bytes 131104 | tf_op jit(solution)/shard_map/ppermute | solution.py:169
  26.0 1.6 %collective-permute-start.11 = (f32[1,2048]{1,0:T(1,128)S(1)}, f32[1,2048]{1,0:T(1,128)S(1)}, u32[]{:S(2)}, u32[]{:S(2)}) collective-permute-start(f32[1,2048]{1,0:T(1,128)S(1)} %add.51.squares), channel_id=1, source_target_pairs={{0,2},{1,3},{2,0},{3,1},{4,6},{5,7},{6,4},{7,5},{8,10},{9,11},{10,... | collective-permute-start | bytes 24584 | tf_op jit(solution)/shard_map/ppermute | solution.py:169
  27.6 2.1 %collective-permute-done.11.squares_y = f32[1,2048]{1,0:T(1,128)S(1)} collective-permute-done((f32[1,2048]{1,0:T(1,128)S(1)}, f32[1,2048]{1,0:T(1,128)S(1)}, u32[]{:S(2)}, u32[]{:S(2)}) %collective-permute-start.11) | collective-permute-done | bytes 8224 | tf_op jit(solution)/shard_map/ppermute | solution.py:169
  30.4 1.6 %collective-permute-start.12 = (bf16[128,256]{1,0:T(8,128)(2,1)S(1)}, bf16[128,256]{1,0:T(8,128)(2,1)S(1)}, u32[]{:S(2)}, u32[]{:S(2)}) collective-permute-start(bf16[128,256]{1,0:T(8,128)(2,1)S(1)} %get-tuple-element.37), channel_id=1, source_target_pairs={{0,16},{16,0},{1,17},{17,1},{2,18},{18,2},{3,19},{19,3},{4,20},{20... | collective-permute-start | bytes 196616 | tf_op jit(solution)/shard_map/ppermute | solution.py:172
  32.0 1.6 %collective-permute-start.13 = (bf16[128,256]{1,0:T(8,128)(2,1)S(1)}, bf16[128,256]{1,0:T(8,128)(2,1)S(1)}, u32[]{:S(2)}, u32[]{:S(2)}) collective-permute-start(bf16[128,256]{1,0:T(8,128)(2,1)S(1)} %get-tuple-element.38), channel_id=1, source_target_pairs={{0,2},{1,3},{2,0},{3,1},{4,6},{5,7},{6,4},{7,5},{8,10},{9,11},{10,... | collective-permute-start | bytes 196616 | tf_op jit(solution)/shard_map/ppermute | solution.py:169
  35.1 1.8 %collective-permute-done.13 = bf16[128,256]{1,0:T(8,128)(2,1)S(1)} collective-permute-done((bf16[128,256]{1,0:T(8,128)(2,1)S(1)}, bf16[128,256]{1,0:T(8,128)(2,1)S(1)}, u32[]{:S(2)}, u32[]{:S(2)}) %collective-permute-start.13) | collective-permute-done | bytes 65568 | tf_op jit(solution)/shard_map/ppermute | solution.py:169
  36.9 1.8 %collective-permute-done.14 = bf16[128,256]{1,0:T(8,128)(2,1)S(1)} collective-permute-done((bf16[128,256]{1,0:T(8,128)(2,1)S(1)}, bf16[128,256]{1,0:T(8,128)(2,1)S(1)}, u32[]{:S(2)}, u32[]{:S(2)}) %collective-permute-start.14) | collective-permute-done | bytes 65568 | tf_op jit(solution)/shard_map/ppermute | solution.py:176
  39.1 4.0 %collective-permute-done.15 = bf16[128,256]{1,0:T(8,128)(2,1)S(1)} collective-permute-done((bf16[128,256]{1,0:T(8,128)(2,1)S(1)}, bf16[128,256]{1,0:T(8,128)(2,1)S(1)}, u32[]{:S(2)}, u32[]{:S(2)}) %collective-permute-start.15) | collective-permute-done | bytes 65568 | tf_op jit(solution)/shard_map/ppermute | solution.py:169
  43.1 3.3 %collective-permute-start.16 = (bf16[128,256]{1,0:T(8,128)(2,1)S(1)}, bf16[128,256]{1,0:T(8,128)(2,1)S(1)}, u32[]{:S(2)}, u32[]{:S(2)}) collective-permute-start(bf16[128,256]{1,0:T(8,128)(2,1)S(1)} %fusion.1), channel_id=1, source_target_pairs={{0,8},{1,9},{2,10},{3,11},{4,12},{5,13},{6,14},{7,15},{8,0},{9,1},... | collective-permute-start | bytes 196616 | tf_op jit(solution)/shard_map/ppermute | solution.py:169
  46.4 2.3 %collective-permute-done.16 = bf16[128,256]{1,0:T(8,128)(2,1)S(1)} collective-permute-done((bf16[128,256]{1,0:T(8,128)(2,1)S(1)}, bf16[128,256]{1,0:T(8,128)(2,1)S(1)}, u32[]{:S(2)}, u32[]{:S(2)}) %collective-permute-start.16) | collective-permute-done | bytes 65568 | tf_op jit(solution)/shard_map/ppermute | solution.py:169
  49.3 1.6 %collective-permute-start.18 = (bf16[128,256]{1,0:T(8,128)(2,1)S(1)}, bf16[128,256]{1,0:T(8,128)(2,1)S(1)}, u32[]{:S(2)}, u32[]{:S(2)}) collective-permute-start(bf16[128,256]{1,0:T(8,128)(2,1)S(1)} %fusion.c0), channel_id=1, source_target_pairs={{0,2},{1,3},{2,0},{3,1},{4,6},{5,7},{6,4},{7,5},{8,10},{9,11},{10,... | collective-permute-start | bytes 196616 | tf_op jit(solution)/shard_map/ppermute | solution.py:169
  52.4 1.8 %collective-permute-done.19.x1 = bf16[128,256]{1,0:T(8,128)(2,1)S(1)} collective-permute-done((bf16[128,256]{1,0:T(8,128)(2,1)S(1)}, bf16[128,256]{1,0:T(8,128)(2,1)S(1)}, u32[]{:S(2)}, u32[]{:S(2)}) %collective-permute-start.19) | collective-permute-done | bytes 65568 | tf_op jit(solution)/shard_map/ppermute | solution.py:176
  56.4 2.6 %shard_map.73 = (f32[512,2048]{1,0:T(8,128)S(1)}, f32[16,128]{1,0:T(8,128)S(1)}) custom-call(bf16[512,512]{1,0:T(8,128)(2,1)S(1)} %shard_map.68.units.targets, bf16[128,256]{1,0:T(8,128)(2,1)S(1)} %fusion.c0, bf16[128,256]{1,0:T(8,128)(2,1)S(1)} %collective-permute-done.17.x0, bf16[128,256]{1,0:T(8,128)(2,1)S(1)} %collective-permute-done.18.c1, ...), custom_call_target="tpu_custom_call" | custom-call | flops 1342177280 | bytes 7348224 | tf_op jit(solution)/shard_map/pallas_call | solution.py:181
  60.2 1.8 %collective-permute-start.27 = (f32[16,128]{1,0:T(8,128)S(1)}, f32[16,128]{1,0:T(8,128)S(1)}, u32[]{:S(2)}, u32[]{:S(2)}) collective-permute-start(f32[16,128]{1,0:T(8,128)S(1)} %add.57), channel_id=1, source_target_pairs={{0,4},{1,5},{2,6},{3,7},{4,0},{5,1},{6,2},{7,3},{8,12},{9,13},{10,... | collective-permute-start | bytes 24584 | tf_op jit(solution)/shard_map/ppermute | solution.py:169
  62.1 1.6 %collective-permute-start.26 = (f32[16,128]{1,0:T(8,128)S(1)}, f32[16,128]{1,0:T(8,128)S(1)}, u32[]{:S(2)}, u32[]{:S(2)}) collective-permute-start(f32[16,128]{1,0:T(8,128)S(1)} %add.57), channel_id=1, source_target_pairs={{0,2},{1,3},{2,0},{3,1},{4,6},{5,7},{6,4},{7,5},{8,10},{9,11},{10,... | collective-permute-start | bytes 24584 | tf_op jit(solution)/shard_map/ppermute | solution.py:169
  65.8 2.9 %collective-permute-start.29 = (f32[16,128]{1,0:T(8,128)S(1)}, f32[16,128]{1,0:T(8,128)S(1)}, u32[]{:S(2)}, u32[]{:S(2)}) collective-permute-start(f32[16,128]{1,0:T(8,128)S(1)} %add_add_fusion.1), channel_id=1, source_target_pairs={{0,8},{1,9},{2,10},{3,11},{4,12},{5,13},{6,14},{7,15},{8,0},{9,1},... | collective-permute-start | bytes 24584 | tf_op jit(solution)/shard_map/ppermute | solution.py:169
  68.7 1.6 %collective-permute-done.29 = f32[16,128]{1,0:T(8,128)S(1)} collective-permute-done((f32[16,128]{1,0:T(8,128)S(1)}, f32[16,128]{1,0:T(8,128)S(1)}, u32[]{:S(2)}, u32[]{:S(2)}) %collective-permute-start.29) | collective-permute-done | bytes 8224 | tf_op jit(solution)/shard_map/ppermute | solution.py:169
  71.3 1.6 %collective-permute-start.30 = (f32[1,512]{1,0:T(1,128)S(1)}, f32[1,512]{1,0:T(1,128)S(1)}, u32[]{:S(2)}, u32[]{:S(2)}) collective-permute-start(f32[1,512]{1,0:T(1,128)S(1)} %get-tuple-element.43.totals), channel_id=1, source_target_pairs={{0,16},{16,0},{1,17},{17,1},{2,18},{18,2},{3,19},{19,3},{4,20},{20... | collective-permute-start | bytes 6152 | tf_op jit(solution)/shard_map/ppermute | solution.py:172
  72.9 2.0 %collective-permute-done.30.totals_x = f32[1,512]{1,0:T(1,128)S(1)} collective-permute-done((f32[1,512]{1,0:T(1,128)S(1)}, f32[1,512]{1,0:T(1,128)S(1)}, u32[]{:S(2)}, u32[]{:S(2)}) %collective-permute-start.30) | collective-permute-done | bytes 2080 | tf_op jit(solution)/shard_map/ppermute | solution.py:172
  77.8 2.0 %collective-permute-start.33 = (f32[16,128]{1,0:T(8,128)S(1)}, f32[16,128]{1,0:T(8,128)S(1)}, u32[]{:S(2)}, u32[]{:S(2)}) collective-permute-start(f32[16,128]{1,0:T(8,128)S(1)} %add.62), channel_id=1, source_target_pairs={{0,4},{1,5},{2,6},{3,7},{4,0},{5,1},{6,2},{7,3},{8,12},{9,13},{10,... | collective-permute-start | bytes 24584 | tf_op jit(solution)/shard_map/ppermute | solution.py:169
  81.5 1.9 %collective-permute-done.32 = f32[16,128]{1,0:T(8,128)S(1)} collective-permute-done((f32[16,128]{1,0:T(8,128)S(1)}, f32[16,128]{1,0:T(8,128)S(1)}, u32[]{:S(2)}, u32[]{:S(2)}) %collective-permute-start.32) | collective-permute-done | bytes 8224 | tf_op jit(solution)/shard_map/ppermute | solution.py:169
  83.4 2.8 %collective-permute-start.35 = (f32[16,128]{1,0:T(8,128)S(1)}, f32[16,128]{1,0:T(8,128)S(1)}, u32[]{:S(2)}, u32[]{:S(2)}) collective-permute-start(f32[16,128]{1,0:T(8,128)S(1)} %add_add_fusion), channel_id=1, source_target_pairs={{0,8},{1,9},{2,10},{3,11},{4,12},{5,13},{6,14},{7,15},{8,0},{9,1},... | collective-permute-start | bytes 24584 | tf_op jit(solution)/shard_map/ppermute | solution.py:169
  86.2 1.7 %collective-permute-done.35 = f32[16,128]{1,0:T(8,128)S(1)} collective-permute-done((f32[16,128]{1,0:T(8,128)S(1)}, f32[16,128]{1,0:T(8,128)S(1)}, u32[]{:S(2)}, u32[]{:S(2)}) %collective-permute-start.35) | collective-permute-done | bytes 8224 | tf_op jit(solution)/shard_map/ppermute | solution.py:169
  90.4 2.1 %collective-permute-done.36 = f32[1,512]{1,0:T(1,128)S(1)} collective-permute-done((f32[1,512]{1,0:T(1,128)S(1)}, f32[1,512]{1,0:T(1,128)S(1)}, u32[]{:S(2)}, u32[]{:S(2)}) %collective-permute-start.36) | collective-permute-done | bytes 2080 | tf_op jit(solution)/shard_map/ppermute | solution.py:172
  (76 shorter events, 27.3 us)
Async XLA Ops:
  0.6 17.0 %collective-permute-start.4 = (bf16[2048,512]{1,0:T(8,128)(2,1)}, bf16[2048,512]{1,0:T(8,128)(2,1)S(1)}, u32[]{:S(2)}, u32[]{:S(2)}) collective-permute-start(bf16[2048,512]{1,0:T(8,128)(2,1)} %plan.5), channel_id=1, source_target_pairs={{0,1},{1,0},{2,3},{3,2},{4,5},{5,4},{6,7},{7,6},{8,9},{9,8},{10,11... | collective-permute-start | bytes 6291464 | tf_op jit(solution)/shard_map/ppermute | solution.py:169
  1.1 9.7 %collective-permute-start = (bf16[512,256]{1,0:T(8,128)(2,1)}, bf16[512,256]{1,0:T(8,128)(2,1)S(1)}, u32[]{:S(2)}, u32[]{:S(2)}) collective-permute-start(bf16[512,256]{1,0:T(8,128)(2,1)} %near.1), channel_id=1, source_target_pairs={{0,16},{16,0},{1,17},{17,1},{2,18},{18,2},{3,19},{19,3},{4,20},{20... | collective-permute-start | bytes 786440 | tf_op jit(solution)/shard_map/ppermute | solution.py:172
  3.7 9.9 %collective-permute-start.3 = (bf16[32,2048]{1,0:T(8,128)(2,1)}, bf16[32,2048]{1,0:T(8,128)(2,1)S(1)}, u32[]{:S(2)}, u32[]{:S(2)}) collective-permute-start(bf16[32,2048]{1,0:T(8,128)(2,1)} %bitcast.5), channel_id=1, source_target_pairs={{0,8},{1,9},{2,10},{3,11},{4,12},{5,13},{6,14},{7,15},{8,0},{9,1},... | collective-permute-start | bytes 393224 | tf_op jit(solution)/shard_map/ppermute | solution.py:169
  6.3 7.3 %collective-permute-start.2 = (bf16[32,2048]{1,0:T(8,128)(2,1)}, bf16[32,2048]{1,0:T(8,128)(2,1)S(1)}, u32[]{:S(2)}, u32[]{:S(2)}) collective-permute-start(bf16[32,2048]{1,0:T(8,128)(2,1)} %bitcast.6), channel_id=1, source_target_pairs={{0,4},{1,5},{2,6},{3,7},{4,0},{5,1},{6,2},{7,3},{8,12},{9,13},{10,... | collective-permute-start | bytes 393224 | tf_op jit(solution)/shard_map/ppermute | solution.py:169
  7.9 5.8 %collective-permute-start.1 = (bf16[32,2048]{1,0:T(8,128)(2,1)}, bf16[32,2048]{1,0:T(8,128)(2,1)S(1)}, u32[]{:S(2)}, u32[]{:S(2)}) collective-permute-start(bf16[32,2048]{1,0:T(8,128)(2,1)} %bitcast.7), channel_id=1, source_target_pairs={{0,2},{1,3},{2,0},{3,1},{4,6},{5,7},{6,4},{7,5},{8,10},{9,11},{10,... | collective-permute-start | bytes 393224 | tf_op jit(solution)/shard_map/ppermute | solution.py:169
  13.7 4.0 %collective-permute-start.5 = (bf16[512,512]{1,0:T(8,128)(2,1)S(1)}, bf16[512,512]{1,0:T(8,128)(2,1)S(1)}, u32[]{:S(2)}, u32[]{:S(2)}) collective-permute-start(bf16[512,512]{1,0:T(8,128)(2,1)S(1)} %shard_map.68.units.targets), channel_id=1, source_target_pairs={{0,1},{1,0},{2,3},{3,2},{4,5},{5,4},{6,7},{7,6},{8,9},{9,8},{10,11... | collective-permute-start | bytes 1572872 | tf_op jit(solution)/shard_map/ppermute | solution.py:169
  13.7 6.0 %collective-permute-start.6 = (bf16[32,2048]{1,0:T(8,128)(2,1)S(1)}, bf16[32,2048]{1,0:T(8,128)(2,1)S(1)}, u32[]{:S(2)}, u32[]{:S(2)}) collective-permute-start(bf16[32,2048]{1,0:T(8,128)(2,1)S(1)} %collective-permute-done.3.refs_1_.p1), channel_id=1, source_target_pairs={{0,4},{1,5},{2,6},{3,7},{4,0},{5,1},{6,2},{7,3},{8,12},{9,13},{10,... | collective-permute-start | bytes 393224 | tf_op jit(solution)/shard_map/ppermute | solution.py:169
  15.6 9.2 %collective-permute-start.8 = (bf16[32,2048]{1,0:T(8,128)(2,1)S(1)}, bf16[32,2048]{1,0:T(8,128)(2,1)S(1)}, u32[]{:S(2)}, u32[]{:S(2)}) collective-permute-start(bf16[32,2048]{1,0:T(8,128)(2,1)S(1)} %collective-permute-done.3.refs_1_.p1), channel_id=1, source_target_pairs={{0,2},{1,3},{2,0},{3,1},{4,6},{5,7},{6,4},{7,5},{8,10},{9,11},{10,... | collective-permute-start | bytes 393224 | tf_op jit(solution)/shard_map/ppermute | solution.py:169
  17.2 7.6 %collective-permute-start.7 = (bf16[32,2048]{1,0:T(8,128)(2,1)S(1)}, bf16[32,2048]{1,0:T(8,128)(2,1)S(1)}, u32[]{:S(2)}, u32[]{:S(2)}) collective-permute-start(bf16[32,2048]{1,0:T(8,128)(2,1)S(1)} %collective-permute-done.2.refs_2_.p2), channel_id=1, source_target_pairs={{0,2},{1,3},{2,0},{3,1},{4,6},{5,7},{6,4},{7,5},{8,10},{9,11},{10,... | collective-permute-start | bytes 393224 | tf_op jit(solution)/shard_map/ppermute | solution.py:169
  19.7 10.0 %collective-permute-start.9 = (bf16[32,2048]{1,0:T(8,128)(2,1)S(1)}, bf16[32,2048]{1,0:T(8,128)(2,1)S(1)}, u32[]{:S(2)}, u32[]{:S(2)}) collective-permute-start(bf16[32,2048]{1,0:T(8,128)(2,1)S(1)} %collective-permute-done.6.refs_3_.p3), channel_id=1, source_target_pairs={{0,2},{1,3},{2,0},{3,1},{4,6},{5,7},{6,4},{7,5},{8,10},{9,11},{10,... | collective-permute-start | bytes 393224 | tf_op jit(solution)/shard_map/ppermute | solution.py:169
  26.0 3.7 %collective-permute-start.11 = (f32[1,2048]{1,0:T(1,128)S(1)}, f32[1,2048]{1,0:T(1,128)S(1)}, u32[]{:S(2)}, u32[]{:S(2)}) collective-permute-start(f32[1,2048]{1,0:T(1,128)S(1)} %add.51.squares), channel_id=1, source_target_pairs={{0,2},{1,3},{2,0},{3,1},{4,6},{5,7},{6,4},{7,5},{8,10},{9,11},{10,... | collective-permute-start | bytes 24584 | tf_op jit(solution)/shard_map/ppermute | solution.py:169
  30.4 4.7 %collective-permute-start.12 = (bf16[128,256]{1,0:T(8,128)(2,1)S(1)}, bf16[128,256]{1,0:T(8,128)(2,1)S(1)}, u32[]{:S(2)}, u32[]{:S(2)}) collective-permute-start(bf16[128,256]{1,0:T(8,128)(2,1)S(1)} %get-tuple-element.37), channel_id=1, source_target_pairs={{0,16},{16,0},{1,17},{17,1},{2,18},{18,2},{3,19},{19,3},{4,20},{20... | collective-permute-start | bytes 196616 | tf_op jit(solution)/shard_map/ppermute | solution.py:172
  32.0 4.9 %collective-permute-start.13 = (bf16[128,256]{1,0:T(8,128)(2,1)S(1)}, bf16[128,256]{1,0:T(8,128)(2,1)S(1)}, u32[]{:S(2)}, u32[]{:S(2)}) collective-permute-start(bf16[128,256]{1,0:T(8,128)(2,1)S(1)} %get-tuple-element.38), channel_id=1, source_target_pairs={{0,2},{1,3},{2,0},{3,1},{4,6},{5,7},{6,4},{7,5},{8,10},{9,11},{10,... | collective-permute-start | bytes 196616 | tf_op jit(solution)/shard_map/ppermute | solution.py:169
  33.5 5.2 %collective-permute-start.14 = (bf16[128,256]{1,0:T(8,128)(2,1)S(1)}, bf16[128,256]{1,0:T(8,128)(2,1)S(1)}, u32[]{:S(2)}, u32[]{:S(2)}) collective-permute-start(bf16[128,256]{1,0:T(8,128)(2,1)S(1)} %get-tuple-element.39), channel_id=1, source_target_pairs={{0,18},{1,19},{2,16},{3,17},{4,22},{5,23},{6,20},{7,21},{8,26},{9,... | collective-permute-start | bytes 196616 | tf_op jit(solution)/shard_map/ppermute | solution.py:176
  38.7 4.3 %collective-permute-start.15 = (bf16[128,256]{1,0:T(8,128)(2,1)S(1)}, bf16[128,256]{1,0:T(8,128)(2,1)S(1)}, u32[]{:S(2)}, u32[]{:S(2)}) collective-permute-start(bf16[128,256]{1,0:T(8,128)(2,1)S(1)} %get-tuple-element.46), channel_id=1, source_target_pairs={{0,4},{1,5},{2,6},{3,7},{4,0},{5,1},{6,2},{7,3},{8,12},{9,13},{10,... | collective-permute-start | bytes 196616 | tf_op jit(solution)/shard_map/ppermute | solution.py:169
  39.1 17.3 %collective-permute-start.24 = (bf16[256,2048]{1,0:T(8,128)(2,1)S(1)}, bf16[256,2048]{1,0:T(8,128)(2,1)S(1)}, u32[]{:S(2)}, u32[]{:S(2)}) collective-permute-start(bf16[256,2048]{1,0:T(8,128)(2,1)S(1)} %get-tuple-element.40.near), channel_id=1, source_target_pairs={{0,1},{1,0},{2,3},{3,2},{4,5},{5,4},{6,7},{7,6},{8,9},{9,8},{10,11... | collective-permute-start | bytes 3145736 | tf_op jit(solution)/shard_map/ppermute | solution.py:169
  43.1 5.7 %collective-permute-start.16 = (bf16[128,256]{1,0:T(8,128)(2,1)S(1)}, bf16[128,256]{1,0:T(8,128)(2,1)S(1)}, u32[]{:S(2)}, u32[]{:S(2)}) collective-permute-start(bf16[128,256]{1,0:T(8,128)(2,1)S(1)} %fusion.1), channel_id=1, source_target_pairs={{0,8},{1,9},{2,10},{3,11},{4,12},{5,13},{6,14},{7,15},{8,0},{9,1},... | collective-permute-start | bytes 196616 | tf_op jit(solution)/shard_map/ppermute | solution.py:169
  48.8 5.3 %collective-permute-start.19 = (bf16[128,256]{1,0:T(8,128)(2,1)S(1)}, bf16[128,256]{1,0:T(8,128)(2,1)S(1)}, u32[]{:S(2)}, u32[]{:S(2)}) collective-permute-start(bf16[128,256]{1,0:T(8,128)(2,1)S(1)} %fusion.c0), channel_id=1, source_target_pairs={{0,18},{1,19},{2,16},{3,17},{4,22},{5,23},{6,20},{7,21},{8,26},{9,... | collective-permute-start | bytes 196616 | tf_op jit(solution)/shard_map/ppermute | solution.py:176
  49.3 5.0 %collective-permute-start.18 = (bf16[128,256]{1,0:T(8,128)(2,1)S(1)}, bf16[128,256]{1,0:T(8,128)(2,1)S(1)}, u32[]{:S(2)}, u32[]{:S(2)}) collective-permute-start(bf16[128,256]{1,0:T(8,128)(2,1)S(1)} %fusion.c0), channel_id=1, source_target_pairs={{0,2},{1,3},{2,0},{3,1},{4,6},{5,7},{6,4},{7,5},{8,10},{9,11},{10,... | collective-permute-start | bytes 196616 | tf_op jit(solution)/shard_map/ppermute | solution.py:169
  50.9 4.3 %collective-permute-start.17 = (bf16[128,256]{1,0:T(8,128)(2,1)S(1)}, bf16[128,256]{1,0:T(8,128)(2,1)S(1)}, u32[]{:S(2)}, u32[]{:S(2)}) collective-permute-start(bf16[128,256]{1,0:T(8,128)(2,1)S(1)} %fusion.c0), channel_id=1, source_target_pairs={{0,16},{16,0},{1,17},{17,1},{2,18},{18,2},{3,19},{19,3},{4,20},{20... | collective-permute-start | bytes 196616 | tf_op jit(solution)/shard_map/ppermute | solution.py:172
  52.4 2.8 %collective-permute-start.20 = (bf16[128,256]{1,0:T(8,128)(2,1)S(1)}, bf16[128,256]{1,0:T(8,128)(2,1)S(1)}, u32[]{:S(2)}, u32[]{:S(2)}) collective-permute-start(bf16[128,256]{1,0:T(8,128)(2,1)S(1)} %fusion.c0), channel_id=1, source_target_pairs={{0,1},{1,0},{2,3},{3,2},{4,5},{5,4},{6,7},{7,6},{8,9},{9,8},{10,11... | collective-permute-start | bytes 196616 | tf_op jit(solution)/shard_map/ppermute | solution.py:169
  54.2 1.4 %collective-permute-start.22 = (bf16[128,256]{1,0:T(8,128)(2,1)S(1)}, bf16[128,256]{1,0:T(8,128)(2,1)S(1)}, u32[]{:S(2)}, u32[]{:S(2)}) collective-permute-start(bf16[128,256]{1,0:T(8,128)(2,1)S(1)} %collective-permute-done.18.c1), channel_id=1, source_target_pairs={{0,1},{1,0},{2,3},{3,2},{4,5},{5,4},{6,7},{7,6},{8,9},{9,8},{10,11... | collective-permute-start | bytes 196616 | tf_op jit(solution)/shard_map/ppermute | solution.py:169
  60.2 4.5 %collective-permute-start.28 = (f32[16,128]{1,0:T(8,128)S(1)}, f32[16,128]{1,0:T(8,128)S(1)}, u32[]{:S(2)}, u32[]{:S(2)}) collective-permute-start(f32[16,128]{1,0:T(8,128)S(1)} %add.57), channel_id=1, source_target_pairs={{0,6},{1,7},{2,4},{3,5},{4,2},{5,3},{6,0},{7,1},{8,14},{9,15},{10,... | collective-permute-start | bytes 24584 | tf_op jit(solution)/shard_map/ppermute | solution.py:169
  60.2 4.5 %collective-permute-start.27 = (f32[16,128]{1,0:T(8,128)S(1)}, f32[16,128]{1,0:T(8,128)S(1)}, u32[]{:S(2)}, u32[]{:S(2)}) collective-permute-start(f32[16,128]{1,0:T(8,128)S(1)} %add.57), channel_id=1, source_target_pairs={{0,4},{1,5},{2,6},{3,7},{4,0},{5,1},{6,2},{7,3},{8,12},{9,13},{10,... | collective-permute-start | bytes 24584 | tf_op jit(solution)/shard_map/ppermute | solution.py:169
  62.1 3.7 %collective-permute-start.26 = (f32[16,128]{1,0:T(8,128)S(1)}, f32[16,128]{1,0:T(8,128)S(1)}, u32[]{:S(2)}, u32[]{:S(2)}) collective-permute-start(f32[16,128]{1,0:T(8,128)S(1)} %add.57), channel_id=1, source_target_pairs={{0,2},{1,3},{2,0},{3,1},{4,6},{5,7},{6,4},{7,5},{8,10},{9,11},{10,... | collective-permute-start | bytes 24584 | tf_op jit(solution)/shard_map/ppermute | solution.py:169
  65.8 4.5 %collective-permute-start.29 = (f32[16,128]{1,0:T(8,128)S(1)}, f32[16,128]{1,0:T(8,128)S(1)}, u32[]{:S(2)}, u32[]{:S(2)}) collective-permute-start(f32[16,128]{1,0:T(8,128)S(1)} %add_add_fusion.1), channel_id=1, source_target_pairs={{0,8},{1,9},{2,10},{3,11},{4,12},{5,13},{6,14},{7,15},{8,0},{9,1},... | collective-permute-start | bytes 24584 | tf_op jit(solution)/shard_map/ppermute | solution.py:169
  71.3 3.6 %collective-permute-start.30 = (f32[1,512]{1,0:T(1,128)S(1)}, f32[1,512]{1,0:T(1,128)S(1)}, u32[]{:S(2)}, u32[]{:S(2)}) collective-permute-start(f32[1,512]{1,0:T(1,128)S(1)} %get-tuple-element.43.totals), channel_id=1, source_target_pairs={{0,16},{16,0},{1,17},{17,1},{2,18},{18,2},{3,19},{19,3},{4,20},{20... | collective-permute-start | bytes 6152 | tf_op jit(solution)/shard_map/ppermute | solution.py:172
  76.7 4.5 %collective-permute-start.34 = (f32[16,128]{1,0:T(8,128)S(1)}, f32[16,128]{1,0:T(8,128)S(1)}, u32[]{:S(2)}, u32[]{:S(2)}) collective-permute-start(f32[16,128]{1,0:T(8,128)S(1)} %add.62), channel_id=1, source_target_pairs={{0,6},{1,7},{2,4},{3,5},{4,2},{5,3},{6,0},{7,1},{8,14},{9,15},{10,... | collective-permute-start | bytes 24584 | tf_op jit(solution)/shard_map/ppermute | solution.py:169
  77.8 3.7 %collective-permute-start.33 = (f32[16,128]{1,0:T(8,128)S(1)}, f32[16,128]{1,0:T(8,128)S(1)}, u32[]{:S(2)}, u32[]{:S(2)}) collective-permute-start(f32[16,128]{1,0:T(8,128)S(1)} %add.62), channel_id=1, source_target_pairs={{0,4},{1,5},{2,6},{3,7},{4,0},{5,1},{6,2},{7,3},{8,12},{9,13},{10,... | collective-permute-start | bytes 24584 | tf_op jit(solution)/shard_map/ppermute | solution.py:169
  79.8 3.7 %collective-permute-start.32 = (f32[16,128]{1,0:T(8,128)S(1)}, f32[16,128]{1,0:T(8,128)S(1)}, u32[]{:S(2)}, u32[]{:S(2)}) collective-permute-start(f32[16,128]{1,0:T(8,128)S(1)} %add.62), channel_id=1, source_target_pairs={{0,2},{1,3},{2,0},{3,1},{4,6},{5,7},{6,4},{7,5},{8,10},{9,11},{10,... | collective-permute-start | bytes 24584 | tf_op jit(solution)/shard_map/ppermute | solution.py:169
  83.4 4.5 %collective-permute-start.35 = (f32[16,128]{1,0:T(8,128)S(1)}, f32[16,128]{1,0:T(8,128)S(1)}, u32[]{:S(2)}, u32[]{:S(2)}) collective-permute-start(f32[16,128]{1,0:T(8,128)S(1)} %add_add_fusion), channel_id=1, source_target_pairs={{0,8},{1,9},{2,10},{3,11},{4,12},{5,13},{6,14},{7,15},{8,0},{9,1},... | collective-permute-start | bytes 24584 | tf_op jit(solution)/shard_map/ppermute | solution.py:169
  88.9 3.6 %collective-permute-start.36 = (f32[1,512]{1,0:T(1,128)S(1)}, f32[1,512]{1,0:T(1,128)S(1)}, u32[]{:S(2)}, u32[]{:S(2)}) collective-permute-start(f32[1,512]{1,0:T(1,128)S(1)} %get-tuple-element.45), channel_id=1, source_target_pairs={{0,16},{16,0},{1,17},{17,1},{2,18},{18,2},{3,19},{19,3},{4,20},{20... | collective-permute-start | bytes 6152 | tf_op jit(solution)/shard_map/ppermute | solution.py:172
  (11 other events, 50.5 us)

commit v3 on v2

--- a/solution.py
+++ b/solution.py
@@ -50,10 +50,17 @@
     return (row_scaling, col_scaling)
 
 
-def unit_targets(plan, near, near_x, units):
+def square_targets(plan, near, mass, target_mass, squares, mass_out, target_mass_out):
+    mass_out[...] = mass[...]
+    target_mass_out[...] = target_mass[...]
+    values = near[...].astype(F32)
+    total = jnp.sum(values * values, axis=1, keepdims=True)
+    squares[...] = jnp.broadcast_to(total, squares.shape)
+
+
+def unit_targets(near, near_x, squares, units):
     a, b = near[...].astype(F32), near_x[...].astype(F32)
-    squares = jnp.sum(a * a, axis=1, keepdims=True) + jnp.sum(b * b, axis=1, keepdims=True)
-    inverse = lax.rsqrt(squares + 1e-06)
+    inverse = lax.rsqrt(squares[:, :1] + jnp.sum(b * b, axis=1, keepdims=True) + 1e-06)
     units[:, : a.shape[1]] = (a * inverse).astype(BF16)
     units[:, a.shape[1] :] = (b * inverse).astype(BF16)
 
@@ -94,67 +101,56 @@
     to_xy[...] = product[half:, split:].astype(BF16)
 
 
-def kernel_block(targets, c0, x0, c1, x1, c2, x2, c3, x3, near, far, out, sums, left):
-    pieces = ((c0, x0), (c1, x1), (c2, x2), (c3, x3))
+def kernel_block(targets, c0, x0, c1, x1, c2, x2, c3, x3, near, far, out, sums, left, whole):
     rows, split = c0.shape
-    squares = 0.0
-    for piece in pieces:
-        squares += jnp.sum(piece[0][...].astype(F32) ** 2 + piece[1][...].astype(F32) ** 2)
+    for i, pair in enumerate(((c0, x0), (c1, x1), (c2, x2), (c3, x3))):
+        for j, piece in enumerate(pair):
+            whole[i * rows : (i + 1) * rows, j * split : (j + 1) * split] = piece[...]
+    nt = (((1,), (1,)), ((), ()))
+    product = lax.dot_general(targets[...], whole[...], nt, preferred_element_type=F32)
+    squares = jnp.sum(whole[...].astype(F32) ** 2)
     scale = lax.rsqrt(squares / 2048.0 + 1e-06) * (sharpness * LOG2E)
-    nt = (((1,), (1,)), ((), ()))
-    for i, piece in enumerate(pieces):
-        product = lax.dot_general(targets[:, :split], piece[0][...], nt, preferred_element_type=F32)
-        product += lax.dot_general(targets[:, split:], piece[1][...], nt, preferred_element_type=F32)
-        left[:, i * rows : (i + 1) * rows] = (product * scale).astype(BF16)
+    left[...] = (product * scale).astype(BF16)
     half = 2 * rows
     width = min(512, near.shape[1])
-
-    def step(i, _):
-        here = pl.ds(pl.multiple_of(i * width, width), width)
+    for start in range(0, near.shape[1], width):
+        here = slice(start, start + width)
         scores = jnp.dot(left[:, :half], near[:, here], preferred_element_type=F32)
         scores += jnp.dot(left[:, half:], far[:, here], preferred_element_type=F32)
         block = jnp.exp2(scores)
         out[:, here] = block
         total = jnp.sum(block, axis=0, keepdims=True)
         for j in range(width // LANES):
-            row = i * (width // LANES) + j
-            sums[pl.ds(row, 1), :] = total[:, j * LANES : (j + 1) * LANES]
-        return 0
-
-    lax.fori_loop(0, near.shape[1] // width, step, 0)
-
-
-def sweep_rows(target_count, block, totals, mass, rows, sums, acc):
-    height = 64
+            row = start // LANES + j
+            sums[row : row + 1, :] = total[:, j * LANES : (j + 1) * LANES]
+
+
+def sweep_rows(target_count, block, totals, mass, sums, rows, acc):
     rows[...] = mass[...] / (totals[...] / target_count)
-
-    def step(i, _):
-        here = pl.ds(pl.multiple_of(i * height, height), height)
-        total = jnp.zeros((height, LANES), F32)
+    for start in range(0, block.shape[0], 64):
+        here = slice(start, start + 64)
+        total = jnp.zeros((64, LANES), F32)
         for j in range(rows.shape[0]):
             total += block[here, j * LANES : (j + 1) * LANES] * rows[j : j + 1, :]
         acc[here, :] = total
-        return 0
-
-    lax.fori_loop(0, block.shape[0] // height, step, 0)
     sums[...] = jnp.sum(acc[...].T, axis=0, keepdims=True)
 
 
 def sweep_cols(source_count, block, totals, totals_x, mass, sums, acc, spread):
-    height = 64
     cols = mass[...] / ((totals[...] + totals_x[...]) / source_count)
     spread[...] = jnp.broadcast_to(cols, (LANES, block.shape[0])).T
     acc[...] = jnp.zeros_like(acc)
-
-    def step(i, _):
-        here = pl.ds(pl.multiple_of(i * height, height), height)
+    for start in range(0, block.shape[0], 64):
+        here = slice(start, start + 64)
         for j in range(acc.shape[0]):
             part = block[here, j * LANES : (j + 1) * LANES] * spread[here, :]
-            acc[j] += jnp.sum(part.reshape(height // 8, 8, LANES), axis=0)
-        return 0
-
-    lax.fori_loop(0, block.shape[0] // height, step, 0)
+            acc[j] += jnp.sum(part.reshape(8, 8, LANES), axis=0)
     sums[...] = jnp.sum(acc[...], axis=1)
+
+
+def finish(source_count, rows_in, totals, totals_x, mass, rows, cols):
+    rows[...] = rows_in[...]
+    cols[...] = mass[...] / ((totals[...] + totals_x[...]) / source_count)
 
 
 def turned(value, order):
@@ -172,7 +168,7 @@
         return lax.ppermute(value, "rows", [(0, 1), (1, 0)])
 
     def both(value):
-        pairs = [(r * n + i, (1 - r) * n + (i ^ 2)) for r in range(2) for i in range(n)]
+        pairs = [(r * n + i, (1 - r) * n + (i ^ 3)) for r in range(2) for i in range(n)]
         return lax.ppermute(value, ("rows", "cols"), pairs)
 
     def call(function, shapes, *values, scratch=(), mib=16, flops=0, loose=()):
@@ -197,14 +193,25 @@
     split = features // 2
 
     own = source.T
-    z2, z1, y0 = swap(own, 8), swap(own, 4), swap(own, 2)
+    z2, z1, y0 = swap(own, 9), swap(own, 5), swap(own, 3)
     wide, part = (targets, features), sources // 2
     target_x = cross(target)
     plan_far = swap(plan, 1)
-    (units,) = call(unit_targets, ((wide, BF16),), plan, target, target_x, loose=(0,))
-    units, y0, z1, z2 = hold((units, y0, z1, z2))
+    tall, flat = (sources // LANES, LANES), (1, targets)
+    weights, mass, target_mass = call(
+        square_targets,
+        (((targets, LANES), F32), (tall, F32), (flat, F32)),
+        plan,
+        target,
+        source_mass.reshape(tall),
+        target_mass.reshape(flat),
+        loose=(0,),
+    )
+    weights, y0, z1, z2 = hold((weights, y0, z1, z2))
+    z3, yz2, yz1 = swap(z2, 5), swap(z2, 3), swap(z1, 3)
+    target_x, z1 = hold((target_x, z1))
+    (units,) = call(unit_targets, ((wide, BF16),), target, target_x, weights)
     units_far = swap(units, 1)
-    z3, yz2, yz1 = swap(z2, 4), swap(z2, 2), swap(z1, 2)
     (upper,) = call(
         functools.partial(project, 0),
         (((part, features), BF16),),
@@ -214,8 +221,8 @@
         units_far,
         flops=4 * part * targets * features,
     )
-    upper, z3 = hold((upper, z3))
-    yz3 = swap(z3, 2)
+    upper, yz1, z3 = hold((upper, yz1, z3))
+    yz3 = swap(z3, 3)
     (lower,) = call(
         functools.partial(project, part),
         (((part, features), BF16),),
@@ -226,10 +233,11 @@
         flops=4 * part * targets * features,
     )
     (squares,) = call(sum_squares, (((1, sources), F32),), own, z2, z1, z3)
-    yz1, yz2, squares, lower = hold((yz1, yz2, squares, lower))
+
     squares += swap(squares, 1)
-    squares_y = swap(squares, 2)
-    yz3, squares_y = hold((yz3, squares_y))
+    yz2, squares = hold((yz2, squares))
+    squares_y = swap(squares, 3)
+    yz3, squares_y, lower = hold((yz3, squares_y, lower))
     pieces = [own, z2, z1, z3, y0, yz2, yz1, yz3]
     quarter = ((half, split), BF16)
     coupling, to_x, to_y, to_xy, xs = call(
@@ -244,15 +252,14 @@
     )
     xs_far = swap(xs, 1)
 
-    for other in (cross(to_x), swap(to_y, 2), both(to_xy)):
+    for other in (cross(to_x), swap(to_y, 3), both(to_xy)):
         coupling += other.astype(F32)
-    coupling += turned(swap(coupling.astype(BF16), 4), (2, 3, 0, 1))
-    coupling += turned(swap(coupling.astype(BF16), 8), (1, 0, 3, 2))
+    coupling += turned(swap(coupling.astype(BF16), 5), (2, 3, 0, 1))
+    coupling += turned(swap(coupling.astype(BF16), 9), (1, 0, 3, 2))
     coupling = coupling.astype(BF16)
-    blocks = [coupling, cross(coupling), swap(coupling, 2), both(coupling)]
+    blocks = [coupling, cross(coupling), swap(coupling, 3), both(coupling)]
     blocks += [swap(block, 1) for block in blocks]
 
-    tall, wide = (sources // LANES, LANES), (1, targets)
     block, sums = call(
         kernel_block,
         (((targets, sources), F32), (tall, F32)),
@@ -260,22 +267,22 @@
         *blocks,
         xs,
         xs_far,
-        scratch=(((targets, features), BF16),),
+        scratch=(((targets, features), BF16), ((features, features), BF16)),
         flops=2 * targets * features * (sources + features),
     )
 
-    mass, target_mass = source_mass.reshape(tall), target_mass.reshape(wide)
     for repeat in range(2):
         sums = sums + swap(sums, 1)
-        sums = sums + swap(sums, 2) + swap(sums, 4) + swap(sums, 6)
-        sums = sums + swap(sums, 8)
-        rows, totals = call(
+        sums = sums + swap(sums, 3) + swap(sums, 5) + swap(sums, 7)
+        sums = sums + swap(sums, 9)
+        shapes, scratch = ((flat, F32), (tall, F32)), (((targets, LANES), F32),)
+        totals, *rows = call(
             functools.partial(sweep_rows, target_count),
-            ((tall, F32), (wide, F32)),
+            shapes[: 1 + repeat],
             block,
             sums,
             mass,
-            scratch=(((targets, LANES), F32),),
+            scratch=scratch if repeat else shapes[1:] + scratch,
         )
         totals_x = cross(totals)
         if repeat == 0:
@@ -288,7 +295,14 @@
                 target_mass,
                 scratch=(((tall[0], 8, LANES), F32), ((targets, LANES), F32)),
             )
-    cols = target_mass / ((totals + totals_x) / source_count)
+    rows, cols = call(
+        functools.partial(finish, source_count),
+        ((tall, F32), (flat, F32)),
+        rows[0],
+        totals,
+        totals_x,
+        target_mass,
+    )
     return (rows.reshape(-1), cols.reshape(-1))
 
 

time: 93.3 us -> 83.5 us (0.89)
  waiting for transfers between devices: 36.6 us -> 30.9 us
  starting transfers between devices: 43.5 us -> 39.9 us
  local copies, waits for them, and re-layouts: 2.58 us -> 3.95 us
  Pallas kernels: 8.91 us -> 7.56 us
    ppermute x30, starting transfers between devices: 33.9 us -> 28.1 us  [swap(): return lax.ppermute(value, 'cols', [(i, i ^ bits) for i in range(n)])]
    ppermute x2, starting transfers between devices: 0.87 us -> 5.76 us  [both(): return lax.ppermute(value, ('rows', 'cols'), pairs)]
    ppermute x30, waiting for transfers between devices: 25.9 us -> 21.6 us  [swap(): return lax.ppermute(value, 'cols', [(i, i ^ bits) for i in range(n)])]
    ppermute x5, starting transfers between devices: 8.71 us -> 6.03 us  [cross(): return lax.ppermute(value, 'rows', [(0, 1), (1, 0)])]
    unnamed x12, local copies, waits for them, and re-layouts: 2.56 us -> 3.93 us
    pallas_call x9 -> x11, Pallas kernels: 8.91 us -> 7.56 us  [call(): pl.pallas_call(function, out_shape=outs, in_specs=[ANY if i in loose else...]
  transfers between devices with their start and end apart: 37 -> 37, of which waited for: 27 -> 27; matrix products, arithmetic and copies ran while one was open for 0% -> 0% of each run, Pallas kernels for 3% -> 4%
where the time goes in v3:
time: 83.5 us; the launch traced here: 83.2 us
  starting transfers between devices  39.9 us (48%)
  waiting for transfers between devices  30.9 us (37%)
  Pallas kernels  7.56 us (9%)
  local copies, waits for them, and re-layouts  3.95 us (5%)
    ppermute x30, starting transfers between devices, swap(): return lax.ppermute(value, 'cols', [(i, i ^ bits) for i in range(n)])  28.1 us
    ppermute x30, waiting for transfers between devices, swap(): return lax.ppermute(value, 'cols', [(i, i ^ bits) for i in range(n)])  21.6 us
    pallas_call x11, Pallas kernels, call(): pl.pallas_call(function, out_shape=outs, in_specs=[ANY if i in loose else...  7.56 us
    ppermute x5, waiting for transfers between devices, cross(): return lax.ppermute(value, 'rows', [(0, 1), (1, 0)])  6.39 us
    ppermute x5, starting transfers between devices, cross(): return lax.ppermute(value, 'rows', [(0, 1), (1, 0)])  6.03 us
    ppermute x2, starting transfers between devices, both(): return lax.ppermute(value, ('rows', 'cols'), pairs)  5.76 us
    unnamed x12, local copies, waits for them, and re-layouts  3.93 us
    ppermute x2, waiting for transfers between devices, both(): return lax.ppermute(value, ('rows', 'cols'), pairs)  2.93 us
  transfers between devices with their start and end apart: 37, of which 27 were waited for; matrix products, arithmetic and copies ran while one was open for 0% of the time, Pallas kernels for 4%

profile of v3, /device:TPU:0, one launch (start us, length us, event | category | flops | bytes accessed | tf_op | source)
XLA Modules:
  0.0 83.2 jit_solution(9468907085736402575)
XLA Ops:
  1.1 2.6 %collective-permute-start = (bf16[512,256]{1,0:T(8,128)(2,1)}, bf16[512,256]{1,0:T(8,128)(2,1)S(1)}, u32[]{:S(2)}, u32[]{:S(2)}) collective-permute-start(bf16[512,256]{1,0:T(8,128)(2,1)} %near.3), channel_id=1, source_target_pairs={{0,16},{16,0},{1,17},{17,1},{2,18},{18,2},{3,19},{19,3},{4,20},{20... | collective-permute-start | bytes 786440 | tf_op jit(solution)/shard_map/ppermute | solution.py:168
  3.7 2.4 %collective-permute-start.3 = (bf16[32,2048]{1,0:T(8,128)(2,1)}, bf16[32,2048]{1,0:T(8,128)(2,1)S(1)}, u32[]{:S(2)}, u32[]{:S(2)}) collective-permute-start(bf16[32,2048]{1,0:T(8,128)(2,1)} %bitcast.5), channel_id=1, source_target_pairs={{0,9},{1,8},{2,11},{3,10},{4,13},{5,12},{6,15},{7,14},{8,1},{9,0},... | collective-permute-start | bytes 393224 | tf_op jit(solution)/shard_map/ppermute | solution.py:165
  6.1 1.5 %collective-permute-start.2 = (bf16[32,2048]{1,0:T(8,128)(2,1)}, bf16[32,2048]{1,0:T(8,128)(2,1)S(1)}, u32[]{:S(2)}, u32[]{:S(2)}) collective-permute-start(bf16[32,2048]{1,0:T(8,128)(2,1)} %bitcast.6), channel_id=1, source_target_pairs={{0,5},{1,4},{2,7},{3,6},{4,1},{5,0},{6,3},{7,2},{8,13},{9,12},{10,... | collective-permute-start | bytes 393224 | tf_op jit(solution)/shard_map/ppermute | solution.py:165
  7.6 1.3 %collective-permute-start.1 = (bf16[32,2048]{1,0:T(8,128)(2,1)}, bf16[32,2048]{1,0:T(8,128)(2,1)S(1)}, u32[]{:S(2)}, u32[]{:S(2)}) collective-permute-start(bf16[32,2048]{1,0:T(8,128)(2,1)} %bitcast.7), channel_id=1, source_target_pairs={{0,3},{1,2},{2,1},{3,0},{4,7},{5,6},{6,5},{7,4},{8,11},{9,10},{10,... | collective-permute-start | bytes 393224 | tf_op jit(solution)/shard_map/ppermute | solution.py:165
  8.9 1.6 %copy-done = bf16[2048,512]{1,0:T(8,128)(2,1)S(1)} copy-done((bf16[2048,512]{1,0:T(8,128)(2,1)S(1)}, bf16[2048,512]{1,0:T(8,128)(2,1)}, u32[]{:S(2)}) %copy-start) | copy-done | bytes 2097176
  13.9 1.4 %collective-permute-start.6 = (bf16[32,2048]{1,0:T(8,128)(2,1)S(1)}, bf16[32,2048]{1,0:T(8,128)(2,1)S(1)}, u32[]{:S(2)}, u32[]{:S(2)}) collective-permute-start(bf16[32,2048]{1,0:T(8,128)(2,1)S(1)} %collective-permute-done.2.refs_2_.p2), channel_id=1, source_target_pairs={{0,3},{1,2},{2,1},{3,0},{4,7},{5,6},{6,5},{7,4},{8,11},{9,10},{10,... | collective-permute-start | bytes 393224 | tf_op jit(solution)/shard_map/ppermute | solution.py:165
  15.3 1.3 %collective-permute-start.7 = (bf16[32,2048]{1,0:T(8,128)(2,1)S(1)}, bf16[32,2048]{1,0:T(8,128)(2,1)S(1)}, u32[]{:S(2)}, u32[]{:S(2)}) collective-permute-start(bf16[32,2048]{1,0:T(8,128)(2,1)S(1)} %collective-permute-done.3.refs_1_.p1), channel_id=1, source_target_pairs={{0,5},{1,4},{2,7},{3,6},{4,1},{5,0},{6,3},{7,2},{8,13},{9,12},{10,... | collective-permute-start | bytes 393224 | tf_op jit(solution)/shard_map/ppermute | solution.py:165
  17.1 1.4 %shard_map.70.upper = bf16[1024,512]{1,0:T(8,128)(2,1)S(1)} custom-call(bf16[2048,512]{1,0:T(8,128)(2,1)S(1)} %copy-done.1, bf16[2048,512]{1,0:T(8,128)(2,1)S(1)} %collective-permute-done.4.plan_far, bf16[512,512]{1,0:T(8,128)(2,1)S(1)} %shard_map.69.units.targets, bf16[512,512]{1,0:T(8,128)(2,1)S(1)} %collective-permute-done.5.units_far), custom_call_target="tpu_custom_call" | custom-call | flops 1073741824 | bytes 6291456 | tf_op jit(solution)/shard_map/pallas_call | solution.py:177
  19.4 1.4 %collective-permute-done.7.refs_3_.p3 = bf16[32,2048]{1,0:T(8,128)(2,1)S(1)} collective-permute-done((bf16[32,2048]{1,0:T(8,128)(2,1)S(1)}, bf16[32,2048]{1,0:T(8,128)(2,1)S(1)}, u32[]{:S(2)}, u32[]{:S(2)}) %collective-permute-start.7) | collective-permute-done | bytes 131104 | tf_op jit(solution)/shard_map/ppermute | solution.py:165
  22.7 1.4 %collective-permute-start.11 = (f32[1,2048]{1,0:T(1,128)S(1)}, f32[1,2048]{1,0:T(1,128)S(1)}, u32[]{:S(2)}, u32[]{:S(2)}) collective-permute-start(f32[1,2048]{1,0:T(1,128)S(1)} %add.48.squares), channel_id=1, source_target_pairs={{0,3},{1,2},{2,1},{3,0},{4,7},{5,6},{6,5},{7,4},{8,11},{9,10},{10,... | collective-permute-start | bytes 24584 | tf_op jit(solution)/shard_map/ppermute | solution.py:165
  24.1 1.4 %shard_map.72.lower = bf16[1024,512]{1,0:T(8,128)(2,1)S(1)} custom-call(bf16[2048,512]{1,0:T(8,128)(2,1)S(1)} %copy-done.1, bf16[2048,512]{1,0:T(8,128)(2,1)S(1)} %collective-permute-done.4.plan_far, bf16[512,512]{1,0:T(8,128)(2,1)S(1)} %shard_map.69.units.targets, bf16[512,512]{1,0:T(8,128)(2,1)S(1)} %collective-permute-done.5.units_far), custom_call_target="tpu_custom_call" | custom-call | flops 1073741824 | bytes 6291456 | tf_op jit(solution)/shard_map/pallas_call | solution.py:177
  28.2 1.9 %collective-permute-start.14 = (bf16[128,256]{1,0:T(8,128)(2,1)S(1)}, bf16[128,256]{1,0:T(8,128)(2,1)S(1)}, u32[]{:S(2)}, u32[]{:S(2)}) collective-permute-start(bf16[128,256]{1,0:T(8,128)(2,1)S(1)} %get-tuple-element.48), channel_id=1, source_target_pairs={{0,19},{1,18},{2,17},{3,16},{4,23},{5,22},{6,21},{7,20},{8,27},{9,... | collective-permute-start | bytes 196616 | tf_op jit(solution)/shard_map/ppermute | solution.py:172
  31.5 1.3 %collective-permute-done.14 = bf16[128,256]{1,0:T(8,128)(2,1)S(1)} collective-permute-done((bf16[128,256]{1,0:T(8,128)(2,1)S(1)}, bf16[128,256]{1,0:T(8,128)(2,1)S(1)}, u32[]{:S(2)}, u32[]{:S(2)}) %collective-permute-start.14) | collective-permute-done | bytes 65568 | tf_op jit(solution)/shard_map/ppermute | solution.py:172
  32.8 1.9 %collective-permute-start.15 = (bf16[128,256]{1,0:T(8,128)(2,1)S(1)}, bf16[128,256]{1,0:T(8,128)(2,1)S(1)}, u32[]{:S(2)}, u32[]{:S(2)}) collective-permute-start(bf16[128,256]{1,0:T(8,128)(2,1)S(1)} %get-tuple-element.58), channel_id=1, source_target_pairs={{0,5},{1,4},{2,7},{3,6},{4,1},{5,0},{6,3},{7,2},{8,13},{9,12},{10,... | collective-permute-start | bytes 196616 | tf_op jit(solution)/shard_map/ppermute | solution.py:165
  34.7 1.9 %collective-permute-done.15 = bf16[128,256]{1,0:T(8,128)(2,1)S(1)} collective-permute-done((bf16[128,256]{1,0:T(8,128)(2,1)S(1)}, bf16[128,256]{1,0:T(8,128)(2,1)S(1)}, u32[]{:S(2)}, u32[]{:S(2)}) %collective-permute-start.15) | collective-permute-done | bytes 65568 | tf_op jit(solution)/shard_map/ppermute | solution.py:165
  36.7 2.7 %collective-permute-start.16 = (bf16[128,256]{1,0:T(8,128)(2,1)S(1)}, bf16[128,256]{1,0:T(8,128)(2,1)S(1)}, u32[]{:S(2)}, u32[]{:S(2)}) collective-permute-start(bf16[128,256]{1,0:T(8,128)(2,1)S(1)} %fusion.1), channel_id=1, source_target_pairs={{0,9},{1,8},{2,11},{3,10},{4,13},{5,12},{6,15},{7,14},{8,1},{9,0},... | collective-permute-start | bytes 196616 | tf_op jit(solution)/shard_map/ppermute | solution.py:165
  39.4 2.2 %collective-permute-done.16 = bf16[128,256]{1,0:T(8,128)(2,1)S(1)} collective-permute-done((bf16[128,256]{1,0:T(8,128)(2,1)S(1)}, bf16[128,256]{1,0:T(8,128)(2,1)S(1)}, u32[]{:S(2)}, u32[]{:S(2)}) %collective-permute-start.16) | collective-permute-done | bytes 65568 | tf_op jit(solution)/shard_map/ppermute | solution.py:165
  41.7 3.8 %collective-permute-start.19 = (bf16[128,256]{1,0:T(8,128)(2,1)S(1)}, bf16[128,256]{1,0:T(8,128)(2,1)S(1)}, u32[]{:S(2)}, u32[]{:S(2)}) collective-permute-start(bf16[128,256]{1,0:T(8,128)(2,1)S(1)} %fusion.c0), channel_id=1, source_target_pairs={{0,19},{1,18},{2,17},{3,16},{4,23},{5,22},{6,21},{7,20},{8,27},{9,... | collective-permute-start | bytes 196616 | tf_op jit(solution)/shard_map/ppermute | solution.py:172
  46.4 1.7 %collective-permute-done.19.x1 = bf16[128,256]{1,0:T(8,128)(2,1)S(1)} collective-permute-done((bf16[128,256]{1,0:T(8,128)(2,1)S(1)}, bf16[128,256]{1,0:T(8,128)(2,1)S(1)}, u32[]{:S(2)}, u32[]{:S(2)}) %collective-permute-start.19) | collective-permute-done | bytes 65568 | tf_op jit(solution)/shard_map/ppermute | solution.py:172
  48.0 1.3 %collective-permute-done.18.c1 = bf16[128,256]{1,0:T(8,128)(2,1)S(1)} collective-permute-done((bf16[128,256]{1,0:T(8,128)(2,1)S(1)}, bf16[128,256]{1,0:T(8,128)(2,1)S(1)}, u32[]{:S(2)}, u32[]{:S(2)}) %collective-permute-start.18) | collective-permute-done | bytes 65568 | tf_op jit(solution)/shard_map/ppermute | solution.py:165
  51.4 1.8 %shard_map.74 = (f32[512,2048]{1,0:T(8,128)S(1)}, f32[16,128]{1,0:T(8,128)S(1)}) custom-call(bf16[512,512]{1,0:T(8,128)(2,1)S(1)} %shard_map.69.units.targets, bf16[128,256]{1,0:T(8,128)(2,1)S(1)} %fusion.c0, bf16[128,256]{1,0:T(8,128)(2,1)S(1)} %collective-permute-done.17.x0, bf16[128,256]{1,0:T(8,128)(2,1)S(1)} %collective-permute-done.18.c1, ...), custom_call_target="tpu_custom_call" | custom-call | flops 1342177280 | bytes 7348224 | tf_op jit(solution)/shard_map/pallas_call | solution.py:177
  54.4 1.6 %collective-permute-start.28 = (f32[16,128]{1,0:T(8,128)S(1)}, f32[16,128]{1,0:T(8,128)S(1)}, u32[]{:S(2)}, u32[]{:S(2)}) collective-permute-start(f32[16,128]{1,0:T(8,128)S(1)} %add.54), channel_id=1, source_target_pairs={{0,7},{1,6},{2,5},{3,4},{4,3},{5,2},{6,1},{7,0},{8,15},{9,14},{10,... | collective-permute-start | bytes 24584 | tf_op jit(solution)/shard_map/ppermute | solution.py:165
  56.0 1.3 %collective-permute-start.27 = (f32[16,128]{1,0:T(8,128)S(1)}, f32[16,128]{1,0:T(8,128)S(1)}, u32[]{:S(2)}, u32[]{:S(2)}) collective-permute-start(f32[16,128]{1,0:T(8,128)S(1)} %add.54), channel_id=1, source_target_pairs={{0,5},{1,4},{2,7},{3,6},{4,1},{5,0},{6,3},{7,2},{8,13},{9,12},{10,... | collective-permute-start | bytes 24584 | tf_op jit(solution)/shard_map/ppermute | solution.py:165
  59.1 1.3 %collective-permute-done.26 = f32[16,128]{1,0:T(8,128)S(1)} collective-permute-done((f32[16,128]{1,0:T(8,128)S(1)}, f32[16,128]{1,0:T(8,128)S(1)}, u32[]{:S(2)}, u32[]{:S(2)}) %collective-permute-start.26) | collective-permute-done | bytes 8224 | tf_op jit(solution)/shard_map/ppermute | solution.py:165
  60.4 2.1 %collective-permute-start.29 = (f32[16,128]{1,0:T(8,128)S(1)}, f32[16,128]{1,0:T(8,128)S(1)}, u32[]{:S(2)}, u32[]{:S(2)}) collective-permute-start(f32[16,128]{1,0:T(8,128)S(1)} %add_add_fusion.1), channel_id=1, source_target_pairs={{0,9},{1,8},{2,11},{3,10},{4,13},{5,12},{6,15},{7,14},{8,1},{9,0},... | collective-permute-start | bytes 24584 | tf_op jit(solution)/shard_map/ppermute | solution.py:165
  62.4 1.9 %collective-permute-done.29 = f32[16,128]{1,0:T(8,128)S(1)} collective-permute-done((f32[16,128]{1,0:T(8,128)S(1)}, f32[16,128]{1,0:T(8,128)S(1)}, u32[]{:S(2)}, u32[]{:S(2)}) %collective-permute-start.29) | collective-permute-done | bytes 8224 | tf_op jit(solution)/shard_map/ppermute | solution.py:165
  65.4 3.0 %collective-permute-done.30.totals_x = f32[1,512]{1,0:T(1,128)S(1)} collective-permute-done((f32[1,512]{1,0:T(1,128)S(1)}, f32[1,512]{1,0:T(1,128)S(1)}, u32[]{:S(2)}, u32[]{:S(2)}) %collective-permute-start.30) | collective-permute-done | bytes 2080 | tf_op jit(solution)/shard_map/ppermute | solution.py:168
  71.5 1.5 %collective-permute-start.32 = (f32[16,128]{1,0:T(8,128)S(1)}, f32[16,128]{1,0:T(8,128)S(1)}, u32[]{:S(2)}, u32[]{:S(2)}) collective-permute-start(f32[16,128]{1,0:T(8,128)S(1)} %add.59), channel_id=1, source_target_pairs={{0,3},{1,2},{2,1},{3,0},{4,7},{5,6},{6,5},{7,4},{8,11},{9,10},{10,... | collective-permute-start | bytes 24584 | tf_op jit(solution)/shard_map/ppermute | solution.py:165
  74.6 2.3 %collective-permute-start.35 = (f32[16,128]{1,0:T(8,128)S(1)}, f32[16,128]{1,0:T(8,128)S(1)}, u32[]{:S(2)}, u32[]{:S(2)}) collective-permute-start(f32[16,128]{1,0:T(8,128)S(1)} %add_add_fusion), channel_id=1, source_target_pairs={{0,9},{1,8},{2,11},{3,10},{4,13},{5,12},{6,15},{7,14},{8,1},{9,0},... | collective-permute-start | bytes 24584 | tf_op jit(solution)/shard_map/ppermute | solution.py:165
  76.9 1.7 %collective-permute-done.35 = f32[16,128]{1,0:T(8,128)S(1)} collective-permute-done((f32[16,128]{1,0:T(8,128)S(1)}, f32[16,128]{1,0:T(8,128)S(1)}, u32[]{:S(2)}, u32[]{:S(2)}) %collective-permute-start.35) | collective-permute-done | bytes 8224 | tf_op jit(solution)/shard_map/ppermute | solution.py:165
  79.0 1.6 %collective-permute-start.36 = (f32[1,512]{1,0:T(1,128)S(1)}, f32[1,512]{1,0:T(1,128)S(1)}, u32[]{:S(2)}, u32[]{:S(2)}) collective-permute-start(f32[1,512]{1,0:T(1,128)S(1)} %get-tuple-element.55.totals), channel_id=1, source_target_pairs={{0,16},{16,0},{1,17},{17,1},{2,18},{18,2},{3,19},{19,3},{4,20},{20... | collective-permute-start | bytes 6152 | tf_op jit(solution)/shard_map/ppermute | solution.py:168
  80.5 2.1 %collective-permute-done.36.totals_x = f32[1,512]{1,0:T(1,128)S(1)} collective-permute-done((f32[1,512]{1,0:T(1,128)S(1)}, f32[1,512]{1,0:T(1,128)S(1)}, u32[]{:S(2)}, u32[]{:S(2)}) %collective-permute-start.36) | collective-permute-done | bytes 2080 | tf_op jit(solution)/shard_map/ppermute | solution.py:168
  (77 shorter events, 24.0 us)
Async XLA Ops:
  0.6 16.5 %collective-permute-start.4 = (bf16[2048,512]{1,0:T(8,128)(2,1)}, bf16[2048,512]{1,0:T(8,128)(2,1)S(1)}, u32[]{:S(2)}, u32[]{:S(2)}) collective-permute-start(bf16[2048,512]{1,0:T(8,128)(2,1)} %plan.5), channel_id=1, source_target_pairs={{0,1},{1,0},{2,3},{3,2},{4,5},{5,4},{6,7},{7,6},{8,9},{9,8},{10,11... | collective-permute-start | bytes 6291464 | tf_op jit(solution)/shard_map/ppermute | solution.py:165
  1.1 12.2 %collective-permute-start = (bf16[512,256]{1,0:T(8,128)(2,1)}, bf16[512,256]{1,0:T(8,128)(2,1)S(1)}, u32[]{:S(2)}, u32[]{:S(2)}) collective-permute-start(bf16[512,256]{1,0:T(8,128)(2,1)} %near.3), channel_id=1, source_target_pairs={{0,16},{16,0},{1,17},{17,1},{2,18},{18,2},{3,19},{19,3},{4,20},{20... | collective-permute-start | bytes 786440 | tf_op jit(solution)/shard_map/ppermute | solution.py:168
  3.7 9.6 %collective-permute-start.3 = (bf16[32,2048]{1,0:T(8,128)(2,1)}, bf16[32,2048]{1,0:T(8,128)(2,1)S(1)}, u32[]{:S(2)}, u32[]{:S(2)}) collective-permute-start(bf16[32,2048]{1,0:T(8,128)(2,1)} %bitcast.5), channel_id=1, source_target_pairs={{0,9},{1,8},{2,11},{3,10},{4,13},{5,12},{6,15},{7,14},{8,1},{9,0},... | collective-permute-start | bytes 393224 | tf_op jit(solution)/shard_map/ppermute | solution.py:165
  6.1 7.2 %collective-permute-start.2 = (bf16[32,2048]{1,0:T(8,128)(2,1)}, bf16[32,2048]{1,0:T(8,128)(2,1)S(1)}, u32[]{:S(2)}, u32[]{:S(2)}) collective-permute-start(bf16[32,2048]{1,0:T(8,128)(2,1)} %bitcast.6), channel_id=1, source_target_pairs={{0,5},{1,4},{2,7},{3,6},{4,1},{5,0},{6,3},{7,2},{8,13},{9,12},{10,... | collective-permute-start | bytes 393224 | tf_op jit(solution)/shard_map/ppermute | solution.py:165
  7.6 5.8 %collective-permute-start.1 = (bf16[32,2048]{1,0:T(8,128)(2,1)}, bf16[32,2048]{1,0:T(8,128)(2,1)S(1)}, u32[]{:S(2)}, u32[]{:S(2)}) collective-permute-start(bf16[32,2048]{1,0:T(8,128)(2,1)} %bitcast.7), channel_id=1, source_target_pairs={{0,3},{1,2},{2,1},{3,0},{4,7},{5,6},{6,5},{7,4},{8,11},{9,10},{10,... | collective-permute-start | bytes 393224 | tf_op jit(solution)/shard_map/ppermute | solution.py:165
  13.6 3.5 %collective-permute-start.5 = (bf16[512,512]{1,0:T(8,128)(2,1)S(1)}, bf16[512,512]{1,0:T(8,128)(2,1)S(1)}, u32[]{:S(2)}, u32[]{:S(2)}) collective-permute-start(bf16[512,512]{1,0:T(8,128)(2,1)S(1)} %shard_map.69.units.targets), channel_id=1, source_target_pairs={{0,1},{1,0},{2,3},{3,2},{4,5},{5,4},{6,7},{7,6},{8,9},{9,8},{10,11... | collective-permute-start | bytes 1572872 | tf_op jit(solution)/shard_map/ppermute | solution.py:165
  13.9 5.4 %collective-permute-start.6 = (bf16[32,2048]{1,0:T(8,128)(2,1)S(1)}, bf16[32,2048]{1,0:T(8,128)(2,1)S(1)}, u32[]{:S(2)}, u32[]{:S(2)}) collective-permute-start(bf16[32,2048]{1,0:T(8,128)(2,1)S(1)} %collective-permute-done.2.refs_2_.p2), channel_id=1, source_target_pairs={{0,3},{1,2},{2,1},{3,0},{4,7},{5,6},{6,5},{7,4},{8,11},{9,10},{10,... | collective-permute-start | bytes 393224 | tf_op jit(solution)/shard_map/ppermute | solution.py:165
  15.3 5.4 %collective-permute-start.7 = (bf16[32,2048]{1,0:T(8,128)(2,1)S(1)}, bf16[32,2048]{1,0:T(8,128)(2,1)S(1)}, u32[]{:S(2)}, u32[]{:S(2)}) collective-permute-start(bf16[32,2048]{1,0:T(8,128)(2,1)S(1)} %collective-permute-done.3.refs_1_.p1), channel_id=1, source_target_pairs={{0,5},{1,4},{2,7},{3,6},{4,1},{5,0},{6,3},{7,2},{8,13},{9,12},{10,... | collective-permute-start | bytes 393224 | tf_op jit(solution)/shard_map/ppermute | solution.py:165
  16.6 6.1 %collective-permute-start.8 = (bf16[32,2048]{1,0:T(8,128)(2,1)S(1)}, bf16[32,2048]{1,0:T(8,128)(2,1)S(1)}, u32[]{:S(2)}, u32[]{:S(2)}) collective-permute-start(bf16[32,2048]{1,0:T(8,128)(2,1)S(1)} %collective-permute-done.3.refs_1_.p1), channel_id=1, source_target_pairs={{0,3},{1,2},{2,1},{3,0},{4,7},{5,6},{6,5},{7,4},{8,11},{9,10},{10,... | collective-permute-start | bytes 393224 | tf_op jit(solution)/shard_map/ppermute | solution.py:165
  20.8 5.4 %collective-permute-start.10 = (bf16[32,2048]{1,0:T(8,128)(2,1)S(1)}, bf16[32,2048]{1,0:T(8,128)(2,1)S(1)}, u32[]{:S(2)}, u32[]{:S(2)}) collective-permute-start(bf16[32,2048]{1,0:T(8,128)(2,1)S(1)} %collective-permute-done.7.refs_3_.p3), channel_id=1, source_target_pairs={{0,3},{1,2},{2,1},{3,0},{4,7},{5,6},{6,5},{7,4},{8,11},{9,10},{10,... | collective-permute-start | bytes 393224 | tf_op jit(solution)/shard_map/ppermute | solution.py:165
  22.7 3.4 %collective-permute-start.11 = (f32[1,2048]{1,0:T(1,128)S(1)}, f32[1,2048]{1,0:T(1,128)S(1)}, u32[]{:S(2)}, u32[]{:S(2)}) collective-permute-start(f32[1,2048]{1,0:T(1,128)S(1)} %add.48.squares), channel_id=1, source_target_pairs={{0,3},{1,2},{2,1},{3,0},{4,7},{5,6},{6,5},{7,4},{8,11},{9,10},{10,... | collective-permute-start | bytes 24584 | tf_op jit(solution)/shard_map/ppermute | solution.py:165
  26.9 4.5 %collective-permute-start.12 = (bf16[128,256]{1,0:T(8,128)(2,1)S(1)}, bf16[128,256]{1,0:T(8,128)(2,1)S(1)}, u32[]{:S(2)}, u32[]{:S(2)}) collective-permute-start(bf16[128,256]{1,0:T(8,128)(2,1)S(1)} %get-tuple-element.46), channel_id=1, source_target_pairs={{0,16},{16,0},{1,17},{17,1},{2,18},{18,2},{3,19},{19,3},{4,20},{20... | collective-permute-start | bytes 196616 | tf_op jit(solution)/shard_map/ppermute | solution.py:168
  27.5 4.1 %collective-permute-start.13 = (bf16[128,256]{1,0:T(8,128)(2,1)S(1)}, bf16[128,256]{1,0:T(8,128)(2,1)S(1)}, u32[]{:S(2)}, u32[]{:S(2)}) collective-permute-start(bf16[128,256]{1,0:T(8,128)(2,1)S(1)} %get-tuple-element.47), channel_id=1, source_target_pairs={{0,3},{1,2},{2,1},{3,0},{4,7},{5,6},{6,5},{7,4},{8,11},{9,10},{10,... | collective-permute-start | bytes 196616 | tf_op jit(solution)/shard_map/ppermute | solution.py:165
  28.2 4.6 %collective-permute-start.14 = (bf16[128,256]{1,0:T(8,128)(2,1)S(1)}, bf16[128,256]{1,0:T(8,128)(2,1)S(1)}, u32[]{:S(2)}, u32[]{:S(2)}) collective-permute-start(bf16[128,256]{1,0:T(8,128)(2,1)S(1)} %get-tuple-element.48), channel_id=1, source_target_pairs={{0,19},{1,18},{2,17},{3,16},{4,23},{5,22},{6,21},{7,20},{8,27},{9,... | collective-permute-start | bytes 196616 | tf_op jit(solution)/shard_map/ppermute | solution.py:172
  32.8 3.8 %collective-permute-start.15 = (bf16[128,256]{1,0:T(8,128)(2,1)S(1)}, bf16[128,256]{1,0:T(8,128)(2,1)S(1)}, u32[]{:S(2)}, u32[]{:S(2)}) collective-permute-start(bf16[128,256]{1,0:T(8,128)(2,1)S(1)} %get-tuple-element.58), channel_id=1, source_target_pairs={{0,5},{1,4},{2,7},{3,6},{4,1},{5,0},{6,3},{7,2},{8,13},{9,12},{10,... | collective-permute-start | bytes 196616 | tf_op jit(solution)/shard_map/ppermute | solution.py:165
  34.7 16.7 %collective-permute-start.24 = (bf16[256,2048]{1,0:T(8,128)(2,1)S(1)}, bf16[256,2048]{1,0:T(8,128)(2,1)S(1)}, u32[]{:S(2)}, u32[]{:S(2)}) collective-permute-start(bf16[256,2048]{1,0:T(8,128)(2,1)S(1)} %get-tuple-element.49.near), channel_id=1, source_target_pairs={{0,1},{1,0},{2,3},{3,2},{4,5},{5,4},{6,7},{7,6},{8,9},{9,8},{10,11... | collective-permute-start | bytes 3145736 | tf_op jit(solution)/shard_map/ppermute | solution.py:165
  36.7 4.9 %collective-permute-start.16 = (bf16[128,256]{1,0:T(8,128)(2,1)S(1)}, bf16[128,256]{1,0:T(8,128)(2,1)S(1)}, u32[]{:S(2)}, u32[]{:S(2)}) collective-permute-start(bf16[128,256]{1,0:T(8,128)(2,1)S(1)} %fusion.1), channel_id=1, source_target_pairs={{0,9},{1,8},{2,11},{3,10},{4,13},{5,12},{6,15},{7,14},{8,1},{9,0},... | collective-permute-start | bytes 196616 | tf_op jit(solution)/shard_map/ppermute | solution.py:165
  41.7 6.4 %collective-permute-start.19 = (bf16[128,256]{1,0:T(8,128)(2,1)S(1)}, bf16[128,256]{1,0:T(8,128)(2,1)S(1)}, u32[]{:S(2)}, u32[]{:S(2)}) collective-permute-start(bf16[128,256]{1,0:T(8,128)(2,1)S(1)} %fusion.c0), channel_id=1, source_target_pairs={{0,19},{1,18},{2,17},{3,16},{4,23},{5,22},{6,21},{7,20},{8,27},{9,... | collective-permute-start | bytes 196616 | tf_op jit(solution)/shard_map/ppermute | solution.py:172
  45.5 3.8 %collective-permute-start.18 = (bf16[128,256]{1,0:T(8,128)(2,1)S(1)}, bf16[128,256]{1,0:T(8,128)(2,1)S(1)}, u32[]{:S(2)}, u32[]{:S(2)}) collective-permute-start(bf16[128,256]{1,0:T(8,128)(2,1)S(1)} %fusion.c0), channel_id=1, source_target_pairs={{0,3},{1,2},{2,1},{3,0},{4,7},{5,6},{6,5},{7,4},{8,11},{9,10},{10,... | collective-permute-start | bytes 196616 | tf_op jit(solution)/shard_map/ppermute | solution.py:165
  45.5 4.6 %collective-permute-start.17 = (bf16[128,256]{1,0:T(8,128)(2,1)S(1)}, bf16[128,256]{1,0:T(8,128)(2,1)S(1)}, u32[]{:S(2)}, u32[]{:S(2)}) collective-permute-start(bf16[128,256]{1,0:T(8,128)(2,1)S(1)} %fusion.c0), channel_id=1, source_target_pairs={{0,16},{16,0},{1,17},{17,1},{2,18},{18,2},{3,19},{19,3},{4,20},{20... | collective-permute-start | bytes 196616 | tf_op jit(solution)/shard_map/ppermute | solution.py:168
  46.1 4.0 %collective-permute-start.20 = (bf16[128,256]{1,0:T(8,128)(2,1)S(1)}, bf16[128,256]{1,0:T(8,128)(2,1)S(1)}, u32[]{:S(2)}, u32[]{:S(2)}) collective-permute-start(bf16[128,256]{1,0:T(8,128)(2,1)S(1)} %fusion.c0), channel_id=1, source_target_pairs={{0,1},{1,0},{2,3},{3,2},{4,5},{5,4},{6,7},{7,6},{8,9},{9,8},{10,11... | collective-permute-start | bytes 196616 | tf_op jit(solution)/shard_map/ppermute | solution.py:165
  48.0 2.1 %collective-permute-start.23 = (bf16[128,256]{1,0:T(8,128)(2,1)S(1)}, bf16[128,256]{1,0:T(8,128)(2,1)S(1)}, u32[]{:S(2)}, u32[]{:S(2)}) collective-permute-start(bf16[128,256]{1,0:T(8,128)(2,1)S(1)} %collective-permute-done.19.x1), channel_id=1, source_target_pairs={{0,1},{1,0},{2,3},{3,2},{4,5},{5,4},{6,7},{7,6},{8,9},{9,8},{10,11... | collective-permute-start | bytes 196616 | tf_op jit(solution)/shard_map/ppermute | solution.py:165
  54.4 4.0 %collective-permute-start.28 = (f32[16,128]{1,0:T(8,128)S(1)}, f32[16,128]{1,0:T(8,128)S(1)}, u32[]{:S(2)}, u32[]{:S(2)}) collective-permute-start(f32[16,128]{1,0:T(8,128)S(1)} %add.54), channel_id=1, source_target_pairs={{0,7},{1,6},{2,5},{3,4},{4,3},{5,2},{6,1},{7,0},{8,15},{9,14},{10,... | collective-permute-start | bytes 24584 | tf_op jit(solution)/shard_map/ppermute | solution.py:165
  56.0 3.1 %collective-permute-start.27 = (f32[16,128]{1,0:T(8,128)S(1)}, f32[16,128]{1,0:T(8,128)S(1)}, u32[]{:S(2)}, u32[]{:S(2)}) collective-permute-start(f32[16,128]{1,0:T(8,128)S(1)} %add.54), channel_id=1, source_target_pairs={{0,5},{1,4},{2,7},{3,6},{4,1},{5,0},{6,3},{7,2},{8,13},{9,12},{10,... | collective-permute-start | bytes 24584 | tf_op jit(solution)/shard_map/ppermute | solution.py:165
  57.3 3.1 %collective-permute-start.26 = (f32[16,128]{1,0:T(8,128)S(1)}, f32[16,128]{1,0:T(8,128)S(1)}, u32[]{:S(2)}, u32[]{:S(2)}) collective-permute-start(f32[16,128]{1,0:T(8,128)S(1)} %add.54), channel_id=1, source_target_pairs={{0,3},{1,2},{2,1},{3,0},{4,7},{5,6},{6,5},{7,4},{8,11},{9,10},{10,... | collective-permute-start | bytes 24584 | tf_op jit(solution)/shard_map/ppermute | solution.py:165
  60.4 4.0 %collective-permute-start.29 = (f32[16,128]{1,0:T(8,128)S(1)}, f32[16,128]{1,0:T(8,128)S(1)}, u32[]{:S(2)}, u32[]{:S(2)}) collective-permute-start(f32[16,128]{1,0:T(8,128)S(1)} %add_add_fusion.1), channel_id=1, source_target_pairs={{0,9},{1,8},{2,11},{3,10},{4,13},{5,12},{6,15},{7,14},{8,1},{9,0},... | collective-permute-start | bytes 24584 | tf_op jit(solution)/shard_map/ppermute | solution.py:165
  64.7 3.7 %collective-permute-start.30 = (f32[1,512]{1,0:T(1,128)S(1)}, f32[1,512]{1,0:T(1,128)S(1)}, u32[]{:S(2)}, u32[]{:S(2)}) collective-permute-start(f32[1,512]{1,0:T(1,128)S(1)} %shard_map.75.totals), channel_id=1, source_target_pairs={{0,16},{16,0},{1,17},{17,1},{2,18},{18,2},{3,19},{19,3},{4,20},{20... | collective-permute-start | bytes 6152 | tf_op jit(solution)/shard_map/ppermute | solution.py:168
  70.0 4.0 %collective-permute-start.34 = (f32[16,128]{1,0:T(8,128)S(1)}, f32[16,128]{1,0:T(8,128)S(1)}, u32[]{:S(2)}, u32[]{:S(2)}) collective-permute-start(f32[16,128]{1,0:T(8,128)S(1)} %add.59), channel_id=1, source_target_pairs={{0,7},{1,6},{2,5},{3,4},{4,3},{5,2},{6,1},{7,0},{8,15},{9,14},{10,... | collective-permute-start | bytes 24584 | tf_op jit(solution)/shard_map/ppermute | solution.py:165
  70.8 3.2 %collective-permute-start.33 = (f32[16,128]{1,0:T(8,128)S(1)}, f32[16,128]{1,0:T(8,128)S(1)}, u32[]{:S(2)}, u32[]{:S(2)}) collective-permute-start(f32[16,128]{1,0:T(8,128)S(1)} %add.59), channel_id=1, source_target_pairs={{0,5},{1,4},{2,7},{3,6},{4,1},{5,0},{6,3},{7,2},{8,13},{9,12},{10,... | collective-permute-start | bytes 24584 | tf_op jit(solution)/shard_map/ppermute | solution.py:165
  71.5 3.1 %collective-permute-start.32 = (f32[16,128]{1,0:T(8,128)S(1)}, f32[16,128]{1,0:T(8,128)S(1)}, u32[]{:S(2)}, u32[]{:S(2)}) collective-permute-start(f32[16,128]{1,0:T(8,128)S(1)} %add.59), channel_id=1, source_target_pairs={{0,3},{1,2},{2,1},{3,0},{4,7},{5,6},{6,5},{7,4},{8,11},{9,10},{10,... | collective-permute-start | bytes 24584 | tf_op jit(solution)/shard_map/ppermute | solution.py:165
  74.6 4.0 %collective-permute-start.35 = (f32[16,128]{1,0:T(8,128)S(1)}, f32[16,128]{1,0:T(8,128)S(1)}, u32[]{:S(2)}, u32[]{:S(2)}) collective-permute-start(f32[16,128]{1,0:T(8,128)S(1)} %add_add_fusion), channel_id=1, source_target_pairs={{0,9},{1,8},{2,11},{3,10},{4,13},{5,12},{6,15},{7,14},{8,1},{9,0},... | collective-permute-start | bytes 24584 | tf_op jit(solution)/shard_map/ppermute | solution.py:165
  79.0 3.7 %collective-permute-start.36 = (f32[1,512]{1,0:T(1,128)S(1)}, f32[1,512]{1,0:T(1,128)S(1)}, u32[]{:S(2)}, u32[]{:S(2)}) collective-permute-start(f32[1,512]{1,0:T(1,128)S(1)} %get-tuple-element.55.totals), channel_id=1, source_target_pairs={{0,16},{16,0},{1,17},{17,1},{2,18},{18,2},{3,19},{19,3},{4,20},{20... | collective-permute-start | bytes 6152 | tf_op jit(solution)/shard_map/ppermute | solution.py:168
  (11 other events, 22.5 us)

commit v4 on v3

--- a/solution.py
+++ b/solution.py
@@ -208,7 +208,7 @@
         loose=(0,),
     )
     weights, y0, z1, z2 = hold((weights, y0, z1, z2))
-    z3, yz2, yz1 = swap(z2, 5), swap(z2, 3), swap(z1, 3)
+    z3, yz2, yz1 = swap(z2, 5), swap(z2, 3), swap(y0, 5)
     target_x, z1 = hold((target_x, z1))
     (units,) = call(unit_targets, ((wide, BF16),), target, target_x, weights)
     units_far = swap(units, 1)
@@ -221,23 +221,23 @@
         units_far,
         flops=4 * part * targets * features,
     )
-    upper, yz1, z3 = hold((upper, yz1, z3))
+    upper, z3 = hold((upper, z3))
     yz3 = swap(z3, 3)
+    near_units, yz2 = hold((units, yz2))
     (lower,) = call(
         functools.partial(project, part),
         (((part, features), BF16),),
         plan,
         plan_far,
-        units,
+        near_units,
         units_far,
         flops=4 * part * targets * features,
     )
     (squares,) = call(sum_squares, (((1, sources), F32),), own, z2, z1, z3)
 
     squares += swap(squares, 1)
-    yz2, squares = hold((yz2, squares))
     squares_y = swap(squares, 3)
-    yz3, squares_y, lower = hold((yz3, squares_y, lower))
+    yz3, yz1, squares_y, lower = hold((yz3, yz1, squares_y, lower))
     pieces = [own, z2, z1, z3, y0, yz2, yz1, yz3]
     quarter = ((half, split), BF16)
     coupling, to_x, to_y, to_xy, xs = call(

time: 83.5 us -> 83.2 us (level)
  waiting for transfers between devices: 30.9 us -> 29.8 us
    ppermute x2, waiting for transfers between devices: 2.93 us -> 0.15 us  [both(): return lax.ppermute(value, ('rows', 'cols'), pairs)]
    ppermute x30, starting transfers between devices: 28.1 us -> 30.2 us  [swap(): return lax.ppermute(value, 'cols', [(i, i ^ bits) for i in range(n)])]
    ppermute x30, waiting for transfers between devices: 21.6 us -> 23.4 us  [swap(): return lax.ppermute(value, 'cols', [(i, i ^ bits) for i in range(n)])]
    ppermute x2, starting transfers between devices: 5.76 us -> 4.7 us  [both(): return lax.ppermute(value, ('rows', 'cols'), pairs)]
  transfers between devices with their start and end apart: 37 -> 37, of which waited for: 27 -> 25; matrix products, arithmetic and copies ran while one was open for 0% -> 0% of each run, Pallas kernels for 4% -> 4%
where the time goes in v4:
time: 83.2 us; the launch traced here: 82.9 us
  starting transfers between devices  40.7 us (49%)
  waiting for transfers between devices  29.8 us (36%)
  Pallas kernels  7.56 us (9%)
  local copies, waits for them, and re-layouts  3.95 us (5%)
    ppermute x30, starting transfers between devices, swap(): return lax.ppermute(value, 'cols', [(i, i ^ bits) for i in range(n)])  30.2 us
    ppermute x30, waiting for transfers between devices, swap(): return lax.ppermute(value, 'cols', [(i, i ^ bits) for i in range(n)])  23.4 us
    pallas_call x11, Pallas kernels, call(): pl.pallas_call(function, out_shape=outs, in_specs=[ANY if i in loose else...  7.56 us
    ppermute x5, waiting for transfers between devices, cross(): return lax.ppermute(value, 'rows', [(0, 1), (1, 0)])  6.29 us
    ppermute x5, starting transfers between devices, cross(): return lax.ppermute(value, 'rows', [(0, 1), (1, 0)])  5.76 us
    ppermute x2, starting transfers between devices, both(): return lax.ppermute(value, ('rows', 'cols'), pairs)  4.7 us
    unnamed x12, local copies, waits for them, and re-layouts  3.93 us
  transfers between devices with their start and end apart: 37, of which 25 were waited for; matrix products, arithmetic and copies ran while one was open for 0% of the time, Pallas kernels for 4%

profile of v4, /device:TPU:0, one launch (start us, length us, event | category | flops | bytes accessed | tf_op | source)
XLA Modules:
  0.0 82.9 jit_solution(5899963471831343718)
XLA Ops:
  1.1 2.6 %collective-permute-start = (bf16[512,256]{1,0:T(8,128)(2,1)}, bf16[512,256]{1,0:T(8,128)(2,1)S(1)}, u32[]{:S(2)}, u32[]{:S(2)}) collective-permute-start(bf16[512,256]{1,0:T(8,128)(2,1)} %near.3), channel_id=1, source_target_pairs={{0,16},{16,0},{1,17},{17,1},{2,18},{18,2},{3,19},{19,3},{4,20},{20... | collective-permute-start | bytes 786440 | tf_op jit(solution)/shard_map/ppermute | solution.py:168
  3.7 2.4 %collective-permute-start.3 = (bf16[32,2048]{1,0:T(8,128)(2,1)}, bf16[32,2048]{1,0:T(8,128)(2,1)S(1)}, u32[]{:S(2)}, u32[]{:S(2)}) collective-permute-start(bf16[32,2048]{1,0:T(8,128)(2,1)} %bitcast.5), channel_id=1, source_target_pairs={{0,9},{1,8},{2,11},{3,10},{4,13},{5,12},{6,15},{7,14},{8,1},{9,0},... | collective-permute-start | bytes 393224 | tf_op jit(solution)/shard_map/ppermute | solution.py:165
  6.1 1.5 %collective-permute-start.2 = (bf16[32,2048]{1,0:T(8,128)(2,1)}, bf16[32,2048]{1,0:T(8,128)(2,1)S(1)}, u32[]{:S(2)}, u32[]{:S(2)}) collective-permute-start(bf16[32,2048]{1,0:T(8,128)(2,1)} %bitcast.6), channel_id=1, source_target_pairs={{0,5},{1,4},{2,7},{3,6},{4,1},{5,0},{6,3},{7,2},{8,13},{9,12},{10,... | collective-permute-start | bytes 393224 | tf_op jit(solution)/shard_map/ppermute | solution.py:165
  7.6 1.3 %collective-permute-start.1 = (bf16[32,2048]{1,0:T(8,128)(2,1)}, bf16[32,2048]{1,0:T(8,128)(2,1)S(1)}, u32[]{:S(2)}, u32[]{:S(2)}) collective-permute-start(bf16[32,2048]{1,0:T(8,128)(2,1)} %bitcast.7), channel_id=1, source_target_pairs={{0,3},{1,2},{2,1},{3,0},{4,7},{5,6},{6,5},{7,4},{8,11},{9,10},{10,... | collective-permute-start | bytes 393224 | tf_op jit(solution)/shard_map/ppermute | solution.py:165
  8.9 1.6 %copy-done = bf16[2048,512]{1,0:T(8,128)(2,1)S(1)} copy-done((bf16[2048,512]{1,0:T(8,128)(2,1)S(1)}, bf16[2048,512]{1,0:T(8,128)(2,1)}, u32[]{:S(2)}) %copy-start) | copy-done | bytes 2097176
  13.9 1.4 %collective-permute-start.6 = (bf16[32,2048]{1,0:T(8,128)(2,1)S(1)}, bf16[32,2048]{1,0:T(8,128)(2,1)S(1)}, u32[]{:S(2)}, u32[]{:S(2)}) collective-permute-start(bf16[32,2048]{1,0:T(8,128)(2,1)S(1)} %collective-permute-done.3.refs_1_.p1), channel_id=1, source_target_pairs={{0,5},{1,4},{2,7},{3,6},{4,1},{5,0},{6,3},{7,2},{8,13},{9,12},{10,... | collective-permute-start | bytes 393224 | tf_op jit(solution)/shard_map/ppermute | solution.py:165
  15.4 1.3 %collective-permute-start.7 = (bf16[32,2048]{1,0:T(8,128)(2,1)S(1)}, bf16[32,2048]{1,0:T(8,128)(2,1)S(1)}, u32[]{:S(2)}, u32[]{:S(2)}) collective-permute-start(bf16[32,2048]{1,0:T(8,128)(2,1)S(1)} %collective-permute-done.3.refs_1_.p1), channel_id=1, source_target_pairs={{0,3},{1,2},{2,1},{3,0},{4,7},{5,6},{6,5},{7,4},{8,11},{9,10},{10,... | collective-permute-start | bytes 393224 | tf_op jit(solution)/shard_map/ppermute | solution.py:165
  17.1 1.4 %shard_map.70.upper = bf16[1024,512]{1,0:T(8,128)(2,1)S(1)} custom-call(bf16[2048,512]{1,0:T(8,128)(2,1)S(1)} %copy-done.1, bf16[2048,512]{1,0:T(8,128)(2,1)S(1)} %collective-permute-done.4.plan_far, bf16[512,512]{1,0:T(8,128)(2,1)S(1)} %shard_map.69.units.targets, bf16[512,512]{1,0:T(8,128)(2,1)S(1)} %collective-permute-done.5.units_far), custom_call_target="tpu_custom_call" | custom-call | flops 1073741824 | bytes 6291456 | tf_op jit(solution)/shard_map/pallas_call | solution.py:177
  19.4 1.9 %collective-permute-start.8 = (bf16[32,2048]{1,0:T(8,128)(2,1)S(1)}, bf16[32,2048]{1,0:T(8,128)(2,1)S(1)}, u32[]{:S(2)}, u32[]{:S(2)}) collective-permute-start(bf16[32,2048]{1,0:T(8,128)(2,1)S(1)} %collective-permute-done.6.refs_3_.p3), channel_id=1, source_target_pairs={{0,3},{1,2},{2,1},{3,0},{4,7},{5,6},{6,5},{7,4},{8,11},{9,10},{10,... | collective-permute-start | bytes 393224 | tf_op jit(solution)/shard_map/ppermute | solution.py:165
  22.8 1.4 %shard_map.72.lower = bf16[1024,512]{1,0:T(8,128)(2,1)S(1)} custom-call(bf16[2048,512]{1,0:T(8,128)(2,1)S(1)} %copy-done.1, bf16[2048,512]{1,0:T(8,128)(2,1)S(1)} %collective-permute-done.4.plan_far, bf16[512,512]{1,0:T(8,128)(2,1)S(1)} %shard_map.69.units.targets, bf16[512,512]{1,0:T(8,128)(2,1)S(1)} %collective-permute-done.5.units_far), custom_call_target="tpu_custom_call" | custom-call | flops 1073741824 | bytes 6291456 | tf_op jit(solution)/shard_map/pallas_call | solution.py:177
  24.2 1.6 %collective-permute-done.11.squares_y = f32[1,2048]{1,0:T(1,128)S(1)} collective-permute-done((f32[1,2048]{1,0:T(1,128)S(1)}, f32[1,2048]{1,0:T(1,128)S(1)}, u32[]{:S(2)}, u32[]{:S(2)}) %collective-permute-start.11) | collective-permute-done | bytes 8224 | tf_op jit(solution)/shard_map/ppermute | solution.py:165
  27.4 2.5 %collective-permute-start.14 = (bf16[128,256]{1,0:T(8,128)(2,1)S(1)}, bf16[128,256]{1,0:T(8,128)(2,1)S(1)}, u32[]{:S(2)}, u32[]{:S(2)}) collective-permute-start(bf16[128,256]{1,0:T(8,128)(2,1)S(1)} %get-tuple-element.48), channel_id=1, source_target_pairs={{0,19},{1,18},{2,17},{3,16},{4,23},{5,22},{6,21},{7,20},{8,27},{9,... | collective-permute-start | bytes 196616 | tf_op jit(solution)/shard_map/ppermute | solution.py:172
  30.9 2.0 %collective-permute-done.13 = bf16[128,256]{1,0:T(8,128)(2,1)S(1)} collective-permute-done((bf16[128,256]{1,0:T(8,128)(2,1)S(1)}, bf16[128,256]{1,0:T(8,128)(2,1)S(1)}, u32[]{:S(2)}, u32[]{:S(2)}) %collective-permute-start.13) | collective-permute-done | bytes 65568 | tf_op jit(solution)/shard_map/ppermute | solution.py:165
  32.9 1.4 %collective-permute-start.15 = (bf16[128,256]{1,0:T(8,128)(2,1)S(1)}, bf16[128,256]{1,0:T(8,128)(2,1)S(1)}, u32[]{:S(2)}, u32[]{:S(2)}) collective-permute-start(bf16[128,256]{1,0:T(8,128)(2,1)S(1)} %get-tuple-element.58), channel_id=1, source_target_pairs={{0,5},{1,4},{2,7},{3,6},{4,1},{5,0},{6,3},{7,2},{8,13},{9,12},{10,... | collective-permute-start | bytes 196616 | tf_op jit(solution)/shard_map/ppermute | solution.py:165
  34.7 2.4 %collective-permute-done.15 = bf16[128,256]{1,0:T(8,128)(2,1)S(1)} collective-permute-done((bf16[128,256]{1,0:T(8,128)(2,1)S(1)}, bf16[128,256]{1,0:T(8,128)(2,1)S(1)}, u32[]{:S(2)}, u32[]{:S(2)}) %collective-permute-start.15) | collective-permute-done | bytes 65568 | tf_op jit(solution)/shard_map/ppermute | solution.py:165
  37.1 1.9 %collective-permute-start.16 = (bf16[128,256]{1,0:T(8,128)(2,1)S(1)}, bf16[128,256]{1,0:T(8,128)(2,1)S(1)}, u32[]{:S(2)}, u32[]{:S(2)}) collective-permute-start(bf16[128,256]{1,0:T(8,128)(2,1)S(1)} %fusion.1), channel_id=1, source_target_pairs={{0,9},{1,8},{2,11},{3,10},{4,13},{5,12},{6,15},{7,14},{8,1},{9,0},... | collective-permute-start | bytes 196616 | tf_op jit(solution)/shard_map/ppermute | solution.py:165
  39.0 3.2 %collective-permute-done.16 = bf16[128,256]{1,0:T(8,128)(2,1)S(1)} collective-permute-done((bf16[128,256]{1,0:T(8,128)(2,1)S(1)}, bf16[128,256]{1,0:T(8,128)(2,1)S(1)}, u32[]{:S(2)}, u32[]{:S(2)}) %collective-permute-start.16) | collective-permute-done | bytes 65568 | tf_op jit(solution)/shard_map/ppermute | solution.py:165
  42.3 2.2 %collective-permute-start.19 = (bf16[128,256]{1,0:T(8,128)(2,1)S(1)}, bf16[128,256]{1,0:T(8,128)(2,1)S(1)}, u32[]{:S(2)}, u32[]{:S(2)}) collective-permute-start(bf16[128,256]{1,0:T(8,128)(2,1)S(1)} %fusion.c0), channel_id=1, source_target_pairs={{0,19},{1,18},{2,17},{3,16},{4,23},{5,22},{6,21},{7,20},{8,27},{9,... | collective-permute-start | bytes 196616 | tf_op jit(solution)/shard_map/ppermute | solution.py:172
  45.5 1.2 %collective-permute-start.20 = (bf16[128,256]{1,0:T(8,128)(2,1)S(1)}, bf16[128,256]{1,0:T(8,128)(2,1)S(1)}, u32[]{:S(2)}, u32[]{:S(2)}) collective-permute-start(bf16[128,256]{1,0:T(8,128)(2,1)S(1)} %fusion.c0), channel_id=1, source_target_pairs={{0,1},{1,0},{2,3},{3,2},{4,5},{5,4},{6,7},{7,6},{8,9},{9,8},{10,11... | collective-permute-start | bytes 196616 | tf_op jit(solution)/shard_map/ppermute | solution.py:165
  46.9 1.6 %collective-permute-start.23 = (bf16[128,256]{1,0:T(8,128)(2,1)S(1)}, bf16[128,256]{1,0:T(8,128)(2,1)S(1)}, u32[]{:S(2)}, u32[]{:S(2)}) collective-permute-start(bf16[128,256]{1,0:T(8,128)(2,1)S(1)} %collective-permute-done.19.x1), channel_id=1, source_target_pairs={{0,1},{1,0},{2,3},{3,2},{4,5},{5,4},{6,7},{7,6},{8,9},{9,8},{10,11... | collective-permute-start | bytes 196616 | tf_op jit(solution)/shard_map/ppermute | solution.py:165
  50.9 1.8 %shard_map.74 = (f32[512,2048]{1,0:T(8,128)S(1)}, f32[16,128]{1,0:T(8,128)S(1)}) custom-call(bf16[512,512]{1,0:T(8,128)(2,1)S(1)} %shard_map.69.units.targets, bf16[128,256]{1,0:T(8,128)(2,1)S(1)} %fusion.c0, bf16[128,256]{1,0:T(8,128)(2,1)S(1)} %collective-permute-done.17.x0, bf16[128,256]{1,0:T(8,128)(2,1)S(1)} %collective-permute-done.18.c1, ...), custom_call_target="tpu_custom_call" | custom-call | flops 1342177280 | bytes 7348224 | tf_op jit(solution)/shard_map/pallas_call | solution.py:177
  53.9 1.3 %collective-permute-start.28 = (f32[16,128]{1,0:T(8,128)S(1)}, f32[16,128]{1,0:T(8,128)S(1)}, u32[]{:S(2)}, u32[]{:S(2)}) collective-permute-start(f32[16,128]{1,0:T(8,128)S(1)} %add.54), channel_id=1, source_target_pairs={{0,7},{1,6},{2,5},{3,4},{4,3},{5,2},{6,1},{7,0},{8,15},{9,14},{10,... | collective-permute-start | bytes 24584 | tf_op jit(solution)/shard_map/ppermute | solution.py:165
  59.2 2.3 %collective-permute-start.29 = (f32[16,128]{1,0:T(8,128)S(1)}, f32[16,128]{1,0:T(8,128)S(1)}, u32[]{:S(2)}, u32[]{:S(2)}) collective-permute-start(f32[16,128]{1,0:T(8,128)S(1)} %add_add_fusion.1), channel_id=1, source_target_pairs={{0,9},{1,8},{2,11},{3,10},{4,13},{5,12},{6,15},{7,14},{8,1},{9,0},... | collective-permute-start | bytes 24584 | tf_op jit(solution)/shard_map/ppermute | solution.py:165
  61.5 1.7 %collective-permute-done.29 = f32[16,128]{1,0:T(8,128)S(1)} collective-permute-done((f32[16,128]{1,0:T(8,128)S(1)}, f32[16,128]{1,0:T(8,128)S(1)}, u32[]{:S(2)}, u32[]{:S(2)}) %collective-permute-start.29) | collective-permute-done | bytes 8224 | tf_op jit(solution)/shard_map/ppermute | solution.py:165
  63.6 1.3 %collective-permute-start.30 = (f32[1,512]{1,0:T(1,128)S(1)}, f32[1,512]{1,0:T(1,128)S(1)}, u32[]{:S(2)}, u32[]{:S(2)}) collective-permute-start(f32[1,512]{1,0:T(1,128)S(1)} %shard_map.75.totals), channel_id=1, source_target_pairs={{0,16},{16,0},{1,17},{17,1},{2,18},{18,2},{3,19},{19,3},{4,20},{20... | collective-permute-start | bytes 6152 | tf_op jit(solution)/shard_map/ppermute | solution.py:168
  64.8 2.4 %collective-permute-done.30.totals_x = f32[1,512]{1,0:T(1,128)S(1)} collective-permute-done((f32[1,512]{1,0:T(1,128)S(1)}, f32[1,512]{1,0:T(1,128)S(1)}, u32[]{:S(2)}, u32[]{:S(2)}) %collective-permute-start.30) | collective-permute-done | bytes 2080 | tf_op jit(solution)/shard_map/ppermute | solution.py:168
  67.7 1.2 %collective-permute-done.31 = f32[16,128]{1,0:T(8,128)S(1)} collective-permute-done((f32[16,128]{1,0:T(8,128)S(1)}, f32[16,128]{1,0:T(8,128)S(1)}, u32[]{:S(2)}, u32[]{:S(2)}) %collective-permute-start.31) | collective-permute-done | bytes 8224 | tf_op jit(solution)/shard_map/ppermute | solution.py:165
  68.9 2.1 %collective-permute-start.34 = (f32[16,128]{1,0:T(8,128)S(1)}, f32[16,128]{1,0:T(8,128)S(1)}, u32[]{:S(2)}, u32[]{:S(2)}) collective-permute-start(f32[16,128]{1,0:T(8,128)S(1)} %add.59), channel_id=1, source_target_pairs={{0,7},{1,6},{2,5},{3,4},{4,3},{5,2},{6,1},{7,0},{8,15},{9,14},{10,... | collective-permute-start | bytes 24584 | tf_op jit(solution)/shard_map/ppermute | solution.py:165
  72.9 1.2 %collective-permute-done.33 = f32[16,128]{1,0:T(8,128)S(1)} collective-permute-done((f32[16,128]{1,0:T(8,128)S(1)}, f32[16,128]{1,0:T(8,128)S(1)}, u32[]{:S(2)}, u32[]{:S(2)}) %collective-permute-start.33) | collective-permute-done | bytes 8224 | tf_op jit(solution)/shard_map/ppermute | solution.py:165
  74.3 2.6 %collective-permute-start.35 = (f32[16,128]{1,0:T(8,128)S(1)}, f32[16,128]{1,0:T(8,128)S(1)}, u32[]{:S(2)}, u32[]{:S(2)}) collective-permute-start(f32[16,128]{1,0:T(8,128)S(1)} %add_add_fusion), channel_id=1, source_target_pairs={{0,9},{1,8},{2,11},{3,10},{4,13},{5,12},{6,15},{7,14},{8,1},{9,0},... | collective-permute-start | bytes 24584 | tf_op jit(solution)/shard_map/ppermute | solution.py:165
  76.9 1.4 %collective-permute-done.35 = f32[16,128]{1,0:T(8,128)S(1)} collective-permute-done((f32[16,128]{1,0:T(8,128)S(1)}, f32[16,128]{1,0:T(8,128)S(1)}, u32[]{:S(2)}, u32[]{:S(2)}) %collective-permute-start.35) | collective-permute-done | bytes 8224 | tf_op jit(solution)/shard_map/ppermute | solution.py:165
  79.5 2.8 %collective-permute-done.36.totals_x = f32[1,512]{1,0:T(1,128)S(1)} collective-permute-done((f32[1,512]{1,0:T(1,128)S(1)}, f32[1,512]{1,0:T(1,128)S(1)}, u32[]{:S(2)}, u32[]{:S(2)}) %collective-permute-start.36) | collective-permute-done | bytes 2080 | tf_op jit(solution)/shard_map/ppermute | solution.py:168
  (77 shorter events, 23.3 us)
Async XLA Ops:
  0.6 16.5 %collective-permute-start.4 = (bf16[2048,512]{1,0:T(8,128)(2,1)}, bf16[2048,512]{1,0:T(8,128)(2,1)S(1)}, u32[]{:S(2)}, u32[]{:S(2)}) collective-permute-start(bf16[2048,512]{1,0:T(8,128)(2,1)} %plan.5), channel_id=1, source_target_pairs={{0,1},{1,0},{2,3},{3,2},{4,5},{5,4},{6,7},{7,6},{8,9},{9,8},{10,11... | collective-permute-start | bytes 6291464 | tf_op jit(solution)/shard_map/ppermute | solution.py:165
  1.1 12.2 %collective-permute-start = (bf16[512,256]{1,0:T(8,128)(2,1)}, bf16[512,256]{1,0:T(8,128)(2,1)S(1)}, u32[]{:S(2)}, u32[]{:S(2)}) collective-permute-start(bf16[512,256]{1,0:T(8,128)(2,1)} %near.3), channel_id=1, source_target_pairs={{0,16},{16,0},{1,17},{17,1},{2,18},{18,2},{3,19},{19,3},{4,20},{20... | collective-permute-start | bytes 786440 | tf_op jit(solution)/shard_map/ppermute | solution.py:168
  3.7 9.6 %collective-permute-start.3 = (bf16[32,2048]{1,0:T(8,128)(2,1)}, bf16[32,2048]{1,0:T(8,128)(2,1)S(1)}, u32[]{:S(2)}, u32[]{:S(2)}) collective-permute-start(bf16[32,2048]{1,0:T(8,128)(2,1)} %bitcast.5), channel_id=1, source_target_pairs={{0,9},{1,8},{2,11},{3,10},{4,13},{5,12},{6,15},{7,14},{8,1},{9,0},... | collective-permute-start | bytes 393224 | tf_op jit(solution)/shard_map/ppermute | solution.py:165
  6.1 7.2 %collective-permute-start.2 = (bf16[32,2048]{1,0:T(8,128)(2,1)}, bf16[32,2048]{1,0:T(8,128)(2,1)S(1)}, u32[]{:S(2)}, u32[]{:S(2)}) collective-permute-start(bf16[32,2048]{1,0:T(8,128)(2,1)} %bitcast.6), channel_id=1, source_target_pairs={{0,5},{1,4},{2,7},{3,6},{4,1},{5,0},{6,3},{7,2},{8,13},{9,12},{10,... | collective-permute-start | bytes 393224 | tf_op jit(solution)/shard_map/ppermute | solution.py:165
  7.6 5.8 %collective-permute-start.1 = (bf16[32,2048]{1,0:T(8,128)(2,1)}, bf16[32,2048]{1,0:T(8,128)(2,1)S(1)}, u32[]{:S(2)}, u32[]{:S(2)}) collective-permute-start(bf16[32,2048]{1,0:T(8,128)(2,1)} %bitcast.7), channel_id=1, source_target_pairs={{0,3},{1,2},{2,1},{3,0},{4,7},{5,6},{6,5},{7,4},{8,11},{9,10},{10,... | collective-permute-start | bytes 393224 | tf_op jit(solution)/shard_map/ppermute | solution.py:165
  13.6 3.5 %collective-permute-start.5 = (bf16[512,512]{1,0:T(8,128)(2,1)S(1)}, bf16[512,512]{1,0:T(8,128)(2,1)S(1)}, u32[]{:S(2)}, u32[]{:S(2)}) collective-permute-start(bf16[512,512]{1,0:T(8,128)(2,1)S(1)} %shard_map.69.units.targets), channel_id=1, source_target_pairs={{0,1},{1,0},{2,3},{3,2},{4,5},{5,4},{6,7},{7,6},{8,9},{9,8},{10,11... | collective-permute-start | bytes 1572872 | tf_op jit(solution)/shard_map/ppermute | solution.py:165
  13.9 5.4 %collective-permute-start.6 = (bf16[32,2048]{1,0:T(8,128)(2,1)S(1)}, bf16[32,2048]{1,0:T(8,128)(2,1)S(1)}, u32[]{:S(2)}, u32[]{:S(2)}) collective-permute-start(bf16[32,2048]{1,0:T(8,128)(2,1)S(1)} %collective-permute-done.3.refs_1_.p1), channel_id=1, source_target_pairs={{0,5},{1,4},{2,7},{3,6},{4,1},{5,0},{6,3},{7,2},{8,13},{9,12},{10,... | collective-permute-start | bytes 393224 | tf_op jit(solution)/shard_map/ppermute | solution.py:165
  15.4 6.2 %collective-permute-start.7 = (bf16[32,2048]{1,0:T(8,128)(2,1)S(1)}, bf16[32,2048]{1,0:T(8,128)(2,1)S(1)}, u32[]{:S(2)}, u32[]{:S(2)}) collective-permute-start(bf16[32,2048]{1,0:T(8,128)(2,1)S(1)} %collective-permute-done.3.refs_1_.p1), channel_id=1, source_target_pairs={{0,3},{1,2},{2,1},{3,0},{4,7},{5,6},{6,5},{7,4},{8,11},{9,10},{10,... | collective-permute-start | bytes 393224 | tf_op jit(solution)/shard_map/ppermute | solution.py:165
  16.6 7.6 %collective-permute-start.9 = (bf16[32,2048]{1,0:T(8,128)(2,1)S(1)}, bf16[32,2048]{1,0:T(8,128)(2,1)S(1)}, u32[]{:S(2)}, u32[]{:S(2)}) collective-permute-start(bf16[32,2048]{1,0:T(8,128)(2,1)S(1)} %collective-permute-done.1.p4), channel_id=1, source_target_pairs={{0,5},{1,4},{2,7},{3,6},{4,1},{5,0},{6,3},{7,2},{8,13},{9,12},{10,... | collective-permute-start | bytes 393224 | tf_op jit(solution)/shard_map/ppermute | solution.py:165
  19.4 6.5 %collective-permute-start.8 = (bf16[32,2048]{1,0:T(8,128)(2,1)S(1)}, bf16[32,2048]{1,0:T(8,128)(2,1)S(1)}, u32[]{:S(2)}, u32[]{:S(2)}) collective-permute-start(bf16[32,2048]{1,0:T(8,128)(2,1)S(1)} %collective-permute-done.6.refs_3_.p3), channel_id=1, source_target_pairs={{0,3},{1,2},{2,1},{3,0},{4,7},{5,6},{6,5},{7,4},{8,11},{9,10},{10,... | collective-permute-start | bytes 393224 | tf_op jit(solution)/shard_map/ppermute | solution.py:165
  22.7 3.1 %collective-permute-start.11 = (f32[1,2048]{1,0:T(1,128)S(1)}, f32[1,2048]{1,0:T(1,128)S(1)}, u32[]{:S(2)}, u32[]{:S(2)}) collective-permute-start(f32[1,2048]{1,0:T(1,128)S(1)} %add.48.squares), channel_id=1, source_target_pairs={{0,3},{1,2},{2,1},{3,0},{4,7},{5,6},{6,5},{7,4},{8,11},{9,10},{10,... | collective-permute-start | bytes 24584 | tf_op jit(solution)/shard_map/ppermute | solution.py:165
  26.6 4.3 %collective-permute-start.12 = (bf16[128,256]{1,0:T(8,128)(2,1)S(1)}, bf16[128,256]{1,0:T(8,128)(2,1)S(1)}, u32[]{:S(2)}, u32[]{:S(2)}) collective-permute-start(bf16[128,256]{1,0:T(8,128)(2,1)S(1)} %get-tuple-element.46), channel_id=1, source_target_pairs={{0,16},{16,0},{1,17},{17,1},{2,18},{18,2},{3,19},{19,3},{4,20},{20... | collective-permute-start | bytes 196616 | tf_op jit(solution)/shard_map/ppermute | solution.py:168
  27.2 5.7 %collective-permute-start.13 = (bf16[128,256]{1,0:T(8,128)(2,1)S(1)}, bf16[128,256]{1,0:T(8,128)(2,1)S(1)}, u32[]{:S(2)}, u32[]{:S(2)}) collective-permute-start(bf16[128,256]{1,0:T(8,128)(2,1)S(1)} %get-tuple-element.47), channel_id=1, source_target_pairs={{0,3},{1,2},{2,1},{3,0},{4,7},{5,6},{6,5},{7,4},{8,11},{9,10},{10,... | collective-permute-start | bytes 196616 | tf_op jit(solution)/shard_map/ppermute | solution.py:165
  27.4 5.5 %collective-permute-start.14 = (bf16[128,256]{1,0:T(8,128)(2,1)S(1)}, bf16[128,256]{1,0:T(8,128)(2,1)S(1)}, u32[]{:S(2)}, u32[]{:S(2)}) collective-permute-start(bf16[128,256]{1,0:T(8,128)(2,1)S(1)} %get-tuple-element.48), channel_id=1, source_target_pairs={{0,19},{1,18},{2,17},{3,16},{4,23},{5,22},{6,21},{7,20},{8,27},{9,... | collective-permute-start | bytes 196616 | tf_op jit(solution)/shard_map/ppermute | solution.py:172
  32.9 4.2 %collective-permute-start.15 = (bf16[128,256]{1,0:T(8,128)(2,1)S(1)}, bf16[128,256]{1,0:T(8,128)(2,1)S(1)}, u32[]{:S(2)}, u32[]{:S(2)}) collective-permute-start(bf16[128,256]{1,0:T(8,128)(2,1)S(1)} %get-tuple-element.58), channel_id=1, source_target_pairs={{0,5},{1,4},{2,7},{3,6},{4,1},{5,0},{6,3},{7,2},{8,13},{9,12},{10,... | collective-permute-start | bytes 196616 | tf_op jit(solution)/shard_map/ppermute | solution.py:165
  34.3 16.6 %collective-permute-start.24 = (bf16[256,2048]{1,0:T(8,128)(2,1)S(1)}, bf16[256,2048]{1,0:T(8,128)(2,1)S(1)}, u32[]{:S(2)}, u32[]{:S(2)}) collective-permute-start(bf16[256,2048]{1,0:T(8,128)(2,1)S(1)} %get-tuple-element.49.near), channel_id=1, source_target_pairs={{0,1},{1,0},{2,3},{3,2},{4,5},{5,4},{6,7},{7,6},{8,9},{9,8},{10,11... | collective-permute-start | bytes 3145736 | tf_op jit(solution)/shard_map/ppermute | solution.py:165
  37.1 5.1 %collective-permute-start.16 = (bf16[128,256]{1,0:T(8,128)(2,1)S(1)}, bf16[128,256]{1,0:T(8,128)(2,1)S(1)}, u32[]{:S(2)}, u32[]{:S(2)}) collective-permute-start(bf16[128,256]{1,0:T(8,128)(2,1)S(1)} %fusion.1), channel_id=1, source_target_pairs={{0,9},{1,8},{2,11},{3,10},{4,13},{5,12},{6,15},{7,14},{8,1},{9,0},... | collective-permute-start | bytes 196616 | tf_op jit(solution)/shard_map/ppermute | solution.py:165
  42.3 4.7 %collective-permute-start.19 = (bf16[128,256]{1,0:T(8,128)(2,1)S(1)}, bf16[128,256]{1,0:T(8,128)(2,1)S(1)}, u32[]{:S(2)}, u32[]{:S(2)}) collective-permute-start(bf16[128,256]{1,0:T(8,128)(2,1)S(1)} %fusion.c0), channel_id=1, source_target_pairs={{0,19},{1,18},{2,17},{3,16},{4,23},{5,22},{6,21},{7,20},{8,27},{9,... | collective-permute-start | bytes 196616 | tf_op jit(solution)/shard_map/ppermute | solution.py:172
  44.5 4.7 %collective-permute-start.18 = (bf16[128,256]{1,0:T(8,128)(2,1)S(1)}, bf16[128,256]{1,0:T(8,128)(2,1)S(1)}, u32[]{:S(2)}, u32[]{:S(2)}) collective-permute-start(bf16[128,256]{1,0:T(8,128)(2,1)S(1)} %fusion.c0), channel_id=1, source_target_pairs={{0,3},{1,2},{2,1},{3,0},{4,7},{5,6},{6,5},{7,4},{8,11},{9,10},{10,... | collective-permute-start | bytes 196616 | tf_op jit(solution)/shard_map/ppermute | solution.py:165
  45.0 4.6 %collective-permute-start.17 = (bf16[128,256]{1,0:T(8,128)(2,1)S(1)}, bf16[128,256]{1,0:T(8,128)(2,1)S(1)}, u32[]{:S(2)}, u32[]{:S(2)}) collective-permute-start(bf16[128,256]{1,0:T(8,128)(2,1)S(1)} %fusion.c0), channel_id=1, source_target_pairs={{0,16},{16,0},{1,17},{17,1},{2,18},{18,2},{3,19},{19,3},{4,20},{20... | collective-permute-start | bytes 196616 | tf_op jit(solution)/shard_map/ppermute | solution.py:168
  45.5 4.3 %collective-permute-start.20 = (bf16[128,256]{1,0:T(8,128)(2,1)S(1)}, bf16[128,256]{1,0:T(8,128)(2,1)S(1)}, u32[]{:S(2)}, u32[]{:S(2)}) collective-permute-start(bf16[128,256]{1,0:T(8,128)(2,1)S(1)} %fusion.c0), channel_id=1, source_target_pairs={{0,1},{1,0},{2,3},{3,2},{4,5},{5,4},{6,7},{7,6},{8,9},{9,8},{10,11... | collective-permute-start | bytes 196616 | tf_op jit(solution)/shard_map/ppermute | solution.py:165
  46.9 2.9 %collective-permute-start.23 = (bf16[128,256]{1,0:T(8,128)(2,1)S(1)}, bf16[128,256]{1,0:T(8,128)(2,1)S(1)}, u32[]{:S(2)}, u32[]{:S(2)}) collective-permute-start(bf16[128,256]{1,0:T(8,128)(2,1)S(1)} %collective-permute-done.19.x1), channel_id=1, source_target_pairs={{0,1},{1,0},{2,3},{3,2},{4,5},{5,4},{6,7},{7,6},{8,9},{9,8},{10,11... | collective-permute-start | bytes 196616 | tf_op jit(solution)/shard_map/ppermute | solution.py:165
  53.9 4.0 %collective-permute-start.28 = (f32[16,128]{1,0:T(8,128)S(1)}, f32[16,128]{1,0:T(8,128)S(1)}, u32[]{:S(2)}, u32[]{:S(2)}) collective-permute-start(f32[16,128]{1,0:T(8,128)S(1)} %add.54), channel_id=1, source_target_pairs={{0,7},{1,6},{2,5},{3,4},{4,3},{5,2},{6,1},{7,0},{8,15},{9,14},{10,... | collective-permute-start | bytes 24584 | tf_op jit(solution)/shard_map/ppermute | solution.py:165
  55.2 3.1 %collective-permute-start.27 = (f32[16,128]{1,0:T(8,128)S(1)}, f32[16,128]{1,0:T(8,128)S(1)}, u32[]{:S(2)}, u32[]{:S(2)}) collective-permute-start(f32[16,128]{1,0:T(8,128)S(1)} %add.54), channel_id=1, source_target_pairs={{0,5},{1,4},{2,7},{3,6},{4,1},{5,0},{6,3},{7,2},{8,13},{9,12},{10,... | collective-permute-start | bytes 24584 | tf_op jit(solution)/shard_map/ppermute | solution.py:165
  56.1 3.1 %collective-permute-start.26 = (f32[16,128]{1,0:T(8,128)S(1)}, f32[16,128]{1,0:T(8,128)S(1)}, u32[]{:S(2)}, u32[]{:S(2)}) collective-permute-start(f32[16,128]{1,0:T(8,128)S(1)} %add.54), channel_id=1, source_target_pairs={{0,3},{1,2},{2,1},{3,0},{4,7},{5,6},{6,5},{7,4},{8,11},{9,10},{10,... | collective-permute-start | bytes 24584 | tf_op jit(solution)/shard_map/ppermute | solution.py:165
  59.2 4.0 %collective-permute-start.29 = (f32[16,128]{1,0:T(8,128)S(1)}, f32[16,128]{1,0:T(8,128)S(1)}, u32[]{:S(2)}, u32[]{:S(2)}) collective-permute-start(f32[16,128]{1,0:T(8,128)S(1)} %add_add_fusion.1), channel_id=1, source_target_pairs={{0,9},{1,8},{2,11},{3,10},{4,13},{5,12},{6,15},{7,14},{8,1},{9,0},... | collective-permute-start | bytes 24584 | tf_op jit(solution)/shard_map/ppermute | solution.py:165
  63.6 3.7 %collective-permute-start.30 = (f32[1,512]{1,0:T(1,128)S(1)}, f32[1,512]{1,0:T(1,128)S(1)}, u32[]{:S(2)}, u32[]{:S(2)}) collective-permute-start(f32[1,512]{1,0:T(1,128)S(1)} %shard_map.75.totals), channel_id=1, source_target_pairs={{0,16},{16,0},{1,17},{17,1},{2,18},{18,2},{3,19},{19,3},{4,20},{20... | collective-permute-start | bytes 6152 | tf_op jit(solution)/shard_map/ppermute | solution.py:168
  68.9 4.0 %collective-permute-start.34 = (f32[16,128]{1,0:T(8,128)S(1)}, f32[16,128]{1,0:T(8,128)S(1)}, u32[]{:S(2)}, u32[]{:S(2)}) collective-permute-start(f32[16,128]{1,0:T(8,128)S(1)} %add.59), channel_id=1, source_target_pairs={{0,7},{1,6},{2,5},{3,4},{4,3},{5,2},{6,1},{7,0},{8,15},{9,14},{10,... | collective-permute-start | bytes 24584 | tf_op jit(solution)/shard_map/ppermute | solution.py:165
  71.0 3.1 %collective-permute-start.33 = (f32[16,128]{1,0:T(8,128)S(1)}, f32[16,128]{1,0:T(8,128)S(1)}, u32[]{:S(2)}, u32[]{:S(2)}) collective-permute-start(f32[16,128]{1,0:T(8,128)S(1)} %add.59), channel_id=1, source_target_pairs={{0,5},{1,4},{2,7},{3,6},{4,1},{5,0},{6,3},{7,2},{8,13},{9,12},{10,... | collective-permute-start | bytes 24584 | tf_op jit(solution)/shard_map/ppermute | solution.py:165
  71.2 3.1 %collective-permute-start.32 = (f32[16,128]{1,0:T(8,128)S(1)}, f32[16,128]{1,0:T(8,128)S(1)}, u32[]{:S(2)}, u32[]{:S(2)}) collective-permute-start(f32[16,128]{1,0:T(8,128)S(1)} %add.59), channel_id=1, source_target_pairs={{0,3},{1,2},{2,1},{3,0},{4,7},{5,6},{6,5},{7,4},{8,11},{9,10},{10,... | collective-permute-start | bytes 24584 | tf_op jit(solution)/shard_map/ppermute | solution.py:165
  74.3 4.0 %collective-permute-start.35 = (f32[16,128]{1,0:T(8,128)S(1)}, f32[16,128]{1,0:T(8,128)S(1)}, u32[]{:S(2)}, u32[]{:S(2)}) collective-permute-start(f32[16,128]{1,0:T(8,128)S(1)} %add_add_fusion), channel_id=1, source_target_pairs={{0,9},{1,8},{2,11},{3,10},{4,13},{5,12},{6,15},{7,14},{8,1},{9,0},... | collective-permute-start | bytes 24584 | tf_op jit(solution)/shard_map/ppermute | solution.py:165
  78.7 3.7 %collective-permute-start.36 = (f32[1,512]{1,0:T(1,128)S(1)}, f32[1,512]{1,0:T(1,128)S(1)}, u32[]{:S(2)}, u32[]{:S(2)}) collective-permute-start(f32[1,512]{1,0:T(1,128)S(1)} %get-tuple-element.55.totals), channel_id=1, source_target_pairs={{0,16},{16,0},{1,17},{17,1},{2,18},{18,2},{3,19},{19,3},{4,20},{20... | collective-permute-start | bytes 6152 | tf_op jit(solution)/shard_map/ppermute | solution.py:168
  (11 other events, 22.2 us)

commit v5 on v4

--- a/solution.py
+++ b/solution.py
@@ -58,6 +58,11 @@
     squares[...] = jnp.broadcast_to(total, squares.shape)
 
 
+def half_index():
+    index = lax.axis_index("cols")
+    return (index ^ (index >> 1) ^ (index >> 2) ^ (index >> 3)) & 1
+
+
 def unit_targets(near, near_x, squares, units):
     a, b = near[...].astype(F32), near_x[...].astype(F32)
     inverse = lax.rsqrt(squares[:, :1] + jnp.sum(b * b, axis=1, keepdims=True) + 1e-06)
@@ -86,7 +91,10 @@
     refs[-1][...] = total
 
 
-def couple(p0, p1, p2, p3, p4, p5, p6, p7, squares, squares_y, upper, lower, keep, to_x, to_y, to_xy, units):
+def couple(
+    p0, p1, p2, p3, p4, p5, p6, p7, squares, squares_y, upper, lower,
+    keep, to_x, to_y, to_xy, units,
+):
     inverse = lax.rsqrt(squares[...] + squares_y[...] + 1e-06)
     rows = p0.shape[0]
     for i, piece in enumerate((p0, p1, p2, p3, p4, p5, p6, p7)):
@@ -101,22 +109,26 @@
     to_xy[...] = product[half:, split:].astype(BF16)
 
 
-def kernel_block(targets, c0, x0, c1, x1, c2, x2, c3, x3, near, far, out, sums, left, whole):
+def kernel_block(targets, targets_far, c0, x0, c1, x1, c2, x2, c3, x3, near, far, out, sums, left, whole):
     rows, split = c0.shape
     for i, pair in enumerate(((c0, x0), (c1, x1), (c2, x2), (c3, x3))):
         for j, piece in enumerate(pair):
             whole[i * rows : (i + 1) * rows, j * split : (j + 1) * split] = piece[...]
     nt = (((1,), (1,)), ((), ()))
-    product = lax.dot_general(targets[...], whole[...], nt, preferred_element_type=F32)
     squares = jnp.sum(whole[...].astype(F32) ** 2)
     scale = lax.rsqrt(squares / 2048.0 + 1e-06) * (sharpness * LOG2E)
-    left[...] = (product * scale).astype(BF16)
+    count = targets.shape[0]
+    for i, points in enumerate((targets, targets_far)):
+        product = lax.dot_general(points[...], whole[...], nt, preferred_element_type=F32)
+        left[i * count : (i + 1) * count, :] = (product * scale).astype(BF16)
     half = 2 * rows
-    width = min(512, near.shape[1])
-    for start in range(0, near.shape[1], width):
+    count = out.shape[1]
+    width, first = min(512, count), half_index() * count
+    for start in range(0, count, width):
         here = slice(start, start + width)
-        scores = jnp.dot(left[:, :half], near[:, here], preferred_element_type=F32)
-        scores += jnp.dot(left[:, half:], far[:, here], preferred_element_type=F32)
+        there = pl.ds(pl.multiple_of(first + start, width), width)
+        scores = jnp.dot(left[:, :half], near[:, there], preferred_element_type=F32)
+        scores += jnp.dot(left[:, half:], far[:, there], preferred_element_type=F32)
         block = jnp.exp2(scores)
         out[:, here] = block
         total = jnp.sum(block, axis=0, keepdims=True)
@@ -126,7 +138,9 @@
 
 
 def sweep_rows(target_count, block, totals, mass, sums, rows, acc):
-    rows[...] = mass[...] / (totals[...] / target_count)
+    count = rows.shape[0]
+    start = pl.multiple_of(half_index() * count, count)
+    rows[...] = mass[pl.ds(start, count), :] / (totals[...] / target_count)
     for start in range(0, block.shape[0], 64):
         here = slice(start, start + 64)
         total = jnp.zeros((64, LANES), F32)
@@ -136,8 +150,16 @@
     sums[...] = jnp.sum(acc[...].T, axis=0, keepdims=True)
 
 
-def sweep_cols(source_count, block, totals, totals_x, mass, sums, acc, spread):
-    cols = mass[...] / ((totals[...] + totals_x[...]) / source_count)
+def chip_totals(own, core, both, x):
+    count = own.shape[1] // 2
+    other = core[...] + both[...]
+    other = jnp.concatenate([other[:, count:], other[:, :count]], axis=1)
+    return own[...] + x[...] + other
+
+
+def sweep_cols(source_count, block, own, core, both, x, mass, mass_far, sums, acc, spread):
+    masses = jnp.concatenate([mass[...], mass_far[...]], axis=1)
+    cols = masses / (chip_totals(own, core, both, x) / source_count)
     spread[...] = jnp.broadcast_to(cols, (LANES, block.shape[0])).T
     acc[...] = jnp.zeros_like(acc)
     for start in range(0, block.shape[0], 64):
@@ -148,9 +170,12 @@
     sums[...] = jnp.sum(acc[...], axis=1)
 
 
-def finish(source_count, rows_in, totals, totals_x, mass, rows, cols):
-    rows[...] = rows_in[...]
-    cols[...] = mass[...] / ((totals[...] + totals_x[...]) / source_count)
+def finish(source_count, rows_own, rows_far, own, core, both, x, mass, rows, cols):
+    count, mine = rows_own.shape[0], half_index()
+    rows[pl.ds(pl.multiple_of(mine * count, count), count), :] = rows_own[...]
+    rows[pl.ds(pl.multiple_of((1 - mine) * count, count), count), :] = rows_far[...]
+    totals = chip_totals(own, core, both, x)[:, : cols.shape[1]]
+    cols[...] = mass[...] / (totals / source_count)
 
 
 def turned(value, order):
@@ -167,8 +192,8 @@
     def cross(value):
         return lax.ppermute(value, "rows", [(0, 1), (1, 0)])
 
-    def both(value):
-        pairs = [(r * n + i, (1 - r) * n + (i ^ 3)) for r in range(2) for i in range(n)]
+    def both(value, bits):
+        pairs = [(r * n + i, (1 - r) * n + (i ^ bits)) for r in range(2) for i in range(n)]
         return lax.ppermute(value, ("rows", "cols"), pairs)
 
     def call(function, shapes, *values, scratch=(), mib=16, flops=0, loose=()):
@@ -221,7 +246,8 @@
         units_far,
         flops=4 * part * targets * features,
     )
-    upper, z3 = hold((upper, z3))
+    target_mass_far = swap(target_mass, 1)
+    upper, target_mass_far, z3 = hold((upper, target_mass_far, z3))
     yz3 = swap(z3, 3)
     near_units, yz2 = hold((units, yz2))
     (lower,) = call(
@@ -252,30 +278,32 @@
     )
     xs_far = swap(xs, 1)
 
-    for other in (cross(to_x), swap(to_y, 3), both(to_xy)):
+    for other in (cross(to_x), swap(to_y, 3), both(to_xy, 3)):
         coupling += other.astype(F32)
     coupling += turned(swap(coupling.astype(BF16), 5), (2, 3, 0, 1))
     coupling += turned(swap(coupling.astype(BF16), 9), (1, 0, 3, 2))
     coupling = coupling.astype(BF16)
-    blocks = [coupling, cross(coupling), swap(coupling, 3), both(coupling)]
+    blocks = [coupling, cross(coupling), swap(coupling, 3), both(coupling, 3)]
     blocks += [swap(block, 1) for block in blocks]
 
+    chip, count = 2 * targets, sources // 2
+    part, wide = (count // LANES, LANES), (1, chip)
     block, sums = call(
         kernel_block,
-        (((targets, sources), F32), (tall, F32)),
+        (((chip, count), F32), (part, F32)),
         units,
+        units_far,
         *blocks,
         xs,
         xs_far,
-        scratch=(((targets, features), BF16), ((features, features), BF16)),
-        flops=2 * targets * features * (sources + features),
+        scratch=(((chip, features), BF16), ((features, features), BF16)),
+        flops=2 * chip * features * (count + features),
     )
 
     for repeat in range(2):
-        sums = sums + swap(sums, 1)
-        sums = sums + swap(sums, 3) + swap(sums, 5) + swap(sums, 7)
+        sums = sums + swap(sums, 3) + swap(sums, 5) + swap(sums, 6)
         sums = sums + swap(sums, 9)
-        shapes, scratch = ((flat, F32), (tall, F32)), (((targets, LANES), F32),)
+        shapes, scratch = ((wide, F32), (part, F32)), (((chip, LANES), F32),)
         totals, *rows = call(
             functools.partial(sweep_rows, target_count),
             shapes[: 1 + repeat],
@@ -284,23 +312,23 @@
             mass,
             scratch=scratch if repeat else shapes[1:] + scratch,
         )
-        totals_x = cross(totals)
+        totals = (totals, swap(totals, 1), both(totals, 1), cross(totals))
         if repeat == 0:
             (sums,) = call(
                 functools.partial(sweep_cols, source_count),
-                ((tall, F32),),
+                ((part, F32),),
                 block,
-                totals,
-                totals_x,
+                *totals,
                 target_mass,
-                scratch=(((tall[0], 8, LANES), F32), ((targets, LANES), F32)),
+                target_mass_far,
+                scratch=(((part[0], 8, LANES), F32), ((chip, LANES), F32)),
             )
     rows, cols = call(
         functools.partial(finish, source_count),
         ((tall, F32), (flat, F32)),
         rows[0],
-        totals,
-        totals_x,
+        swap(rows[0], 1),
+        *totals,
         target_mass,
     )
     return (rows.reshape(-1), cols.reshape(-1))
@@ -311,7 +339,7 @@
     features = source[1] // n
     fits = (plan[0] // rows) * (plan[1] // n) * 4 <= 4 * MIB
     even = n == 16 and features % 16 == 0
-    whole = plan[0] % (rows * 512) == 0 and plan[1] % (n * 128) == 0
+    whole = plan[0] % (rows * 1024) == 0 and plan[1] % (n * 128) == 0
     return body if rows == 2 and fits and even and whole else plain_body
 
 

time: 83.2 us -> 82.1 us (0.987)
  waiting for transfers between devices: 29.8 us -> 25.4 us
  starting transfers between devices: 40.7 us -> 43.9 us
    ppermute x30 -> x32, waiting for transfers between devices: 23.4 us -> 20 us  [swap(): return lax.ppermute(value, 'cols', [(i, i ^ bits) for i in range(n)])]
    ppermute x5, waiting for transfers between devices: 6.29 us -> 3.99 us  [cross(): return lax.ppermute(value, 'rows', [(0, 1), (1, 0)])]
    ppermute x30 -> x32, starting transfers between devices: 30.2 us -> 32 us  [swap(): return lax.ppermute(value, 'cols', [(i, i ^ bits) for i in range(n)])]
    ppermute x2 -> x4, waiting for transfers between devices: 0.15 us -> 1.42 us  [both(): return lax.ppermute(value, ('rows', 'cols'), pairs)]
    ppermute x2 -> x4, starting transfers between devices: 4.7 us -> 5.75 us  [both(): return lax.ppermute(value, ('rows', 'cols'), pairs)]
  transfers between devices with their start and end apart: 37 -> 41, of which waited for: 25 -> 23; matrix products, arithmetic and copies ran while one was open for 0% -> 0% of each run, Pallas kernels for 4% -> 4%
where the time goes in v5:
time: 82.1 us; the launch traced here: 81.9 us
  starting transfers between devices  43.9 us (53%)
  waiting for transfers between devices  25.4 us (31%)
  Pallas kernels  7.71 us (9%)
  local copies, waits for them, and re-layouts  3.95 us (5%)
    ppermute x32, starting transfers between devices, swap(): return lax.ppermute(value, 'cols', [(i, i ^ bits) for i in range(n)])  32 us
    ppermute x32, waiting for transfers between devices, swap(): return lax.ppermute(value, 'cols', [(i, i ^ bits) for i in range(n)])  20 us
    pallas_call x11, Pallas kernels, call(): pl.pallas_call(function, out_shape=outs, in_specs=[ANY if i in loose else...  7.71 us
    ppermute x5, starting transfers between devices, cross(): return lax.ppermute(value, 'rows', [(0, 1), (1, 0)])  6.18 us
    ppermute x4, starting transfers between devices, both(): return lax.ppermute(value, ('rows', 'cols'), pairs)  5.75 us
    ppermute x5, waiting for transfers between devices, cross(): return lax.ppermute(value, 'rows', [(0, 1), (1, 0)])  3.99 us
    unnamed x12, local copies, waits for them, and re-layouts  3.92 us
  transfers between devices with their start and end apart: 41, of which 23 were waited for; matrix products, arithmetic and copies ran while one was open for 0% of the time, Pallas kernels for 4%

profile of v5, /device:TPU:0, one launch (start us, length us, event | category | flops | bytes accessed | tf_op | source)
XLA Modules:
  0.0 81.9 jit_solution(2364957103251787895)
XLA Ops:
  1.1 2.6 %collective-permute-start = (bf16[512,256]{1,0:T(8,128)(2,1)}, bf16[512,256]{1,0:T(8,128)(2,1)S(1)}, u32[]{:S(2)}, u32[]{:S(2)}) collective-permute-start(bf16[512,256]{1,0:T(8,128)(2,1)} %near.3), channel_id=1, source_target_pairs={{0,16},{16,0},{1,17},{17,1},{2,18},{18,2},{3,19},{19,3},{4,20},{20... | collective-permute-start | bytes 786440 | tf_op jit(solution)/shard_map/ppermute | solution.py:193
  3.7 2.4 %collective-permute-start.3 = (bf16[32,2048]{1,0:T(8,128)(2,1)}, bf16[32,2048]{1,0:T(8,128)(2,1)S(1)}, u32[]{:S(2)}, u32[]{:S(2)}) collective-permute-start(bf16[32,2048]{1,0:T(8,128)(2,1)} %bitcast.5), channel_id=1, source_target_pairs={{0,9},{1,8},{2,11},{3,10},{4,13},{5,12},{6,15},{7,14},{8,1},{9,0},... | collective-permute-start | bytes 393224 | tf_op jit(solution)/shard_map/ppermute | solution.py:190
  6.1 1.5 %collective-permute-start.2 = (bf16[32,2048]{1,0:T(8,128)(2,1)}, bf16[32,2048]{1,0:T(8,128)(2,1)S(1)}, u32[]{:S(2)}, u32[]{:S(2)}) collective-permute-start(bf16[32,2048]{1,0:T(8,128)(2,1)} %bitcast.6), channel_id=1, source_target_pairs={{0,5},{1,4},{2,7},{3,6},{4,1},{5,0},{6,3},{7,2},{8,13},{9,12},{10,... | collective-permute-start | bytes 393224 | tf_op jit(solution)/shard_map/ppermute | solution.py:190
  7.6 1.3 %collective-permute-start.1 = (bf16[32,2048]{1,0:T(8,128)(2,1)}, bf16[32,2048]{1,0:T(8,128)(2,1)S(1)}, u32[]{:S(2)}, u32[]{:S(2)}) collective-permute-start(bf16[32,2048]{1,0:T(8,128)(2,1)} %bitcast.7), channel_id=1, source_target_pairs={{0,3},{1,2},{2,1},{3,0},{4,7},{5,6},{6,5},{7,4},{8,11},{9,10},{10,... | collective-permute-start | bytes 393224 | tf_op jit(solution)/shard_map/ppermute | solution.py:190
  8.9 1.6 %copy-done = bf16[2048,512]{1,0:T(8,128)(2,1)S(1)} copy-done((bf16[2048,512]{1,0:T(8,128)(2,1)S(1)}, bf16[2048,512]{1,0:T(8,128)(2,1)}, u32[]{:S(2)}) %copy-start) | copy-done | bytes 2097176
  13.9 1.4 %collective-permute-start.7 = (bf16[32,2048]{1,0:T(8,128)(2,1)S(1)}, bf16[32,2048]{1,0:T(8,128)(2,1)S(1)}, u32[]{:S(2)}, u32[]{:S(2)}) collective-permute-start(bf16[32,2048]{1,0:T(8,128)(2,1)S(1)} %collective-permute-done.3.refs_1_.p1), channel_id=1, source_target_pairs={{0,5},{1,4},{2,7},{3,6},{4,1},{5,0},{6,3},{7,2},{8,13},{9,12},{10,... | collective-permute-start | bytes 393224 | tf_op jit(solution)/shard_map/ppermute | solution.py:190
  15.5 1.5 %collective-permute-start.8 = (bf16[32,2048]{1,0:T(8,128)(2,1)S(1)}, bf16[32,2048]{1,0:T(8,128)(2,1)S(1)}, u32[]{:S(2)}, u32[]{:S(2)}) collective-permute-start(bf16[32,2048]{1,0:T(8,128)(2,1)S(1)} %collective-permute-done.3.refs_1_.p1), channel_id=1, source_target_pairs={{0,3},{1,2},{2,1},{3,0},{4,7},{5,6},{6,5},{7,4},{8,11},{9,10},{10,... | collective-permute-start | bytes 393224 | tf_op jit(solution)/shard_map/ppermute | solution.py:190
  17.3 1.4 %shard_map.70.upper = bf16[1024,512]{1,0:T(8,128)(2,1)S(1)} custom-call(bf16[2048,512]{1,0:T(8,128)(2,1)S(1)} %copy-done.1, bf16[2048,512]{1,0:T(8,128)(2,1)S(1)} %collective-permute-done.5.plan_far, bf16[512,512]{1,0:T(8,128)(2,1)S(1)} %shard_map.69.units.targets, bf16[512,512]{1,0:T(8,128)(2,1)S(1)} %collective-permute-done.4.units_far.targets_far), custom_call_target="tpu_custom_call" | custom-call | flops 1073741824 | bytes 6291456 | tf_op jit(solution)/shard_map/pallas_call | solution.py:202
  19.4 1.9 %collective-permute-start.9 = (bf16[32,2048]{1,0:T(8,128)(2,1)S(1)}, bf16[32,2048]{1,0:T(8,128)(2,1)S(1)}, u32[]{:S(2)}, u32[]{:S(2)}) collective-permute-start(bf16[32,2048]{1,0:T(8,128)(2,1)S(1)} %collective-permute-done.7.refs_3_.p3), channel_id=1, source_target_pairs={{0,3},{1,2},{2,1},{3,0},{4,7},{5,6},{6,5},{7,4},{8,11},{9,10},{10,... | collective-permute-start | bytes 393224 | tf_op jit(solution)/shard_map/ppermute | solution.py:190
  22.8 1.4 %shard_map.72.lower = bf16[1024,512]{1,0:T(8,128)(2,1)S(1)} custom-call(bf16[2048,512]{1,0:T(8,128)(2,1)S(1)} %copy-done.1, bf16[2048,512]{1,0:T(8,128)(2,1)S(1)} %collective-permute-done.5.plan_far, bf16[512,512]{1,0:T(8,128)(2,1)S(1)} %shard_map.69.units.targets, bf16[512,512]{1,0:T(8,128)(2,1)S(1)} %collective-permute-done.4.units_far.targets_far), custom_call_target="tpu_custom_call" | custom-call | flops 1073741824 | bytes 6291456 | tf_op jit(solution)/shard_map/pallas_call | solution.py:202
  24.2 1.6 %collective-permute-done.12.squares_y = f32[1,2048]{1,0:T(1,128)S(1)} collective-permute-done((f32[1,2048]{1,0:T(1,128)S(1)}, f32[1,2048]{1,0:T(1,128)S(1)}, u32[]{:S(2)}, u32[]{:S(2)}) %collective-permute-start.12) | collective-permute-done | bytes 8224 | tf_op jit(solution)/shard_map/ppermute | solution.py:190
  27.4 2.5 %collective-permute-start.15 = (bf16[128,256]{1,0:T(8,128)(2,1)S(1)}, bf16[128,256]{1,0:T(8,128)(2,1)S(1)}, u32[]{:S(2)}, u32[]{:S(2)}) collective-permute-start(bf16[128,256]{1,0:T(8,128)(2,1)S(1)} %get-tuple-element.50), channel_id=1, source_target_pairs={{0,19},{1,18},{2,17},{3,16},{4,23},{5,22},{6,21},{7,20},{8,27},{9,... | collective-permute-start | bytes 196616 | tf_op jit(solution)/shard_map/ppermute | solution.py:197
  30.9 2.0 %collective-permute-done.14 = bf16[128,256]{1,0:T(8,128)(2,1)S(1)} collective-permute-done((bf16[128,256]{1,0:T(8,128)(2,1)S(1)}, bf16[128,256]{1,0:T(8,128)(2,1)S(1)}, u32[]{:S(2)}, u32[]{:S(2)}) %collective-permute-start.14) | collective-permute-done | bytes 65568 | tf_op jit(solution)/shard_map/ppermute | solution.py:190
  32.9 1.4 %collective-permute-start.16 = (bf16[128,256]{1,0:T(8,128)(2,1)S(1)}, bf16[128,256]{1,0:T(8,128)(2,1)S(1)}, u32[]{:S(2)}, u32[]{:S(2)}) collective-permute-start(bf16[128,256]{1,0:T(8,128)(2,1)S(1)} %get-tuple-element.60), channel_id=1, source_target_pairs={{0,5},{1,4},{2,7},{3,6},{4,1},{5,0},{6,3},{7,2},{8,13},{9,12},{10,... | collective-permute-start | bytes 196616 | tf_op jit(solution)/shard_map/ppermute | solution.py:190
  34.7 2.4 %collective-permute-done.16 = bf16[128,256]{1,0:T(8,128)(2,1)S(1)} collective-permute-done((bf16[128,256]{1,0:T(8,128)(2,1)S(1)}, bf16[128,256]{1,0:T(8,128)(2,1)S(1)}, u32[]{:S(2)}, u32[]{:S(2)}) %collective-permute-start.16) | collective-permute-done | bytes 65568 | tf_op jit(solution)/shard_map/ppermute | solution.py:190
  37.1 1.9 %collective-permute-start.17 = (bf16[128,256]{1,0:T(8,128)(2,1)S(1)}, bf16[128,256]{1,0:T(8,128)(2,1)S(1)}, u32[]{:S(2)}, u32[]{:S(2)}) collective-permute-start(bf16[128,256]{1,0:T(8,128)(2,1)S(1)} %fusion.1), channel_id=1, source_target_pairs={{0,9},{1,8},{2,11},{3,10},{4,13},{5,12},{6,15},{7,14},{8,1},{9,0},... | collective-permute-start | bytes 196616 | tf_op jit(solution)/shard_map/ppermute | solution.py:190
  39.0 3.2 %collective-permute-done.17 = bf16[128,256]{1,0:T(8,128)(2,1)S(1)} collective-permute-done((bf16[128,256]{1,0:T(8,128)(2,1)S(1)}, bf16[128,256]{1,0:T(8,128)(2,1)S(1)}, u32[]{:S(2)}, u32[]{:S(2)}) %collective-permute-start.17) | collective-permute-done | bytes 65568 | tf_op jit(solution)/shard_map/ppermute | solution.py:190
  42.2 2.2 %collective-permute-start.20 = (bf16[128,256]{1,0:T(8,128)(2,1)S(1)}, bf16[128,256]{1,0:T(8,128)(2,1)S(1)}, u32[]{:S(2)}, u32[]{:S(2)}) collective-permute-start(bf16[128,256]{1,0:T(8,128)(2,1)S(1)} %fusion.c0), channel_id=1, source_target_pairs={{0,19},{1,18},{2,17},{3,16},{4,23},{5,22},{6,21},{7,20},{8,27},{9,... | collective-permute-start | bytes 196616 | tf_op jit(solution)/shard_map/ppermute | solution.py:197
  45.5 1.2 %collective-permute-start.21 = (bf16[128,256]{1,0:T(8,128)(2,1)S(1)}, bf16[128,256]{1,0:T(8,128)(2,1)S(1)}, u32[]{:S(2)}, u32[]{:S(2)}) collective-permute-start(bf16[128,256]{1,0:T(8,128)(2,1)S(1)} %fusion.c0), channel_id=1, source_target_pairs={{0,1},{1,0},{2,3},{3,2},{4,5},{5,4},{6,7},{7,6},{8,9},{9,8},{10,11... | collective-permute-start | bytes 196616 | tf_op jit(solution)/shard_map/ppermute | solution.py:190
  46.9 1.6 %collective-permute-start.24 = (bf16[128,256]{1,0:T(8,128)(2,1)S(1)}, bf16[128,256]{1,0:T(8,128)(2,1)S(1)}, u32[]{:S(2)}, u32[]{:S(2)}) collective-permute-start(bf16[128,256]{1,0:T(8,128)(2,1)S(1)} %collective-permute-done.20.x1), channel_id=1, source_target_pairs={{0,1},{1,0},{2,3},{3,2},{4,5},{5,4},{6,7},{7,6},{8,9},{9,8},{10,11... | collective-permute-start | bytes 196616 | tf_op jit(solution)/shard_map/ppermute | solution.py:190
  50.9 1.9 %shard_map.74 = (f32[1024,1024]{1,0:T(8,128)S(1)}, f32[8,128]{1,0:T(8,128)S(1)}) custom-call(bf16[512,512]{1,0:T(8,128)(2,1)S(1)} %shard_map.69.units.targets, bf16[512,512]{1,0:T(8,128)(2,1)S(1)} %collective-permute-done.4.units_far.targets_far, bf16[128,256]{1,0:T(8,128)(2,1)S(1)} %fusion.c0, bf16[128,256]{1,0:T(8,128)(2,1)S(1)} %collective-permute-done.18.x0, ...), custom_call_target="tpu_custom_call" | custom-call | flops 1610612736 | bytes 7868416 | tf_op jit(solution)/shard_map/pallas_call | solution.py:202
  52.8 1.6 %collective-permute-start.28 = (f32[8,128]{1,0:T(8,128)S(1)}, f32[8,128]{1,0:T(8,128)S(1)}, u32[]{:S(2)}, u32[]{:S(2)}) collective-permute-start(f32[8,128]{1,0:T(8,128)S(1)} %get-tuple-element.53), channel_id=1, source_target_pairs={{0,6},{1,7},{2,4},{3,5},{4,2},{5,3},{6,0},{7,1},{8,14},{9,15},{10,... | collective-permute-start | bytes 12296 | tf_op jit(solution)/shard_map/ppermute | solution.py:190
  56.1 1.3 %collective-permute-done.28 = f32[8,128]{1,0:T(8,128)S(1)} collective-permute-done((f32[8,128]{1,0:T(8,128)S(1)}, f32[8,128]{1,0:T(8,128)S(1)}, u32[]{:S(2)}, u32[]{:S(2)}) %collective-permute-start.28) | collective-permute-done | bytes 4128 | tf_op jit(solution)/shard_map/ppermute | solution.py:190
  58.1 2.4 %collective-permute-start.29 = (f32[8,128]{1,0:T(8,128)S(1)}, f32[8,128]{1,0:T(8,128)S(1)}, u32[]{:S(2)}, u32[]{:S(2)}) collective-permute-start(f32[8,128]{1,0:T(8,128)S(1)} %add_add_fusion.1), channel_id=1, source_target_pairs={{0,9},{1,8},{2,11},{3,10},{4,13},{5,12},{6,15},{7,14},{8,1},{9,0},... | collective-permute-start | bytes 12296 | tf_op jit(solution)/shard_map/ppermute | solution.py:190
  60.5 1.5 %collective-permute-done.29 = f32[8,128]{1,0:T(8,128)S(1)} collective-permute-done((f32[8,128]{1,0:T(8,128)S(1)}, f32[8,128]{1,0:T(8,128)S(1)}, u32[]{:S(2)}, u32[]{:S(2)}) %collective-permute-start.29) | collective-permute-done | bytes 4128 | tf_op jit(solution)/shard_map/ppermute | solution.py:190
  64.6 1.5 %collective-permute-done.32.x = f32[1,1024]{1,0:T(1,128)S(1)} collective-permute-done((f32[1,1024]{1,0:T(1,128)S(1)}, f32[1,1024]{1,0:T(1,128)S(1)}, u32[]{:S(2)}, u32[]{:S(2)}) %collective-permute-start.32) | collective-permute-done | bytes 4128 | tf_op jit(solution)/shard_map/ppermute | solution.py:193
  66.9 2.2 %collective-permute-start.35 = (f32[8,128]{1,0:T(8,128)S(1)}, f32[8,128]{1,0:T(8,128)S(1)}, u32[]{:S(2)}, u32[]{:S(2)}) collective-permute-start(f32[8,128]{1,0:T(8,128)S(1)} %shard_map.76), channel_id=1, source_target_pairs={{0,6},{1,7},{2,4},{3,5},{4,2},{5,3},{6,0},{7,1},{8,14},{9,15},{10,... | collective-permute-start | bytes 12296 | tf_op jit(solution)/shard_map/ppermute | solution.py:190
  70.2 1.3 %collective-permute-done.35 = f32[8,128]{1,0:T(8,128)S(1)} collective-permute-done((f32[8,128]{1,0:T(8,128)S(1)}, f32[8,128]{1,0:T(8,128)S(1)}, u32[]{:S(2)}, u32[]{:S(2)}) %collective-permute-start.35) | collective-permute-done | bytes 4128 | tf_op jit(solution)/shard_map/ppermute | solution.py:190
  72.2 2.7 %collective-permute-start.36 = (f32[8,128]{1,0:T(8,128)S(1)}, f32[8,128]{1,0:T(8,128)S(1)}, u32[]{:S(2)}, u32[]{:S(2)}) collective-permute-start(f32[8,128]{1,0:T(8,128)S(1)} %add_add_fusion), channel_id=1, source_target_pairs={{0,9},{1,8},{2,11},{3,10},{4,13},{5,12},{6,15},{7,14},{8,1},{9,0},... | collective-permute-start | bytes 12296 | tf_op jit(solution)/shard_map/ppermute | solution.py:190
  74.9 1.3 %collective-permute-done.36 = f32[8,128]{1,0:T(8,128)S(1)} collective-permute-done((f32[8,128]{1,0:T(8,128)S(1)}, f32[8,128]{1,0:T(8,128)S(1)}, u32[]{:S(2)}, u32[]{:S(2)}) %collective-permute-start.36) | collective-permute-done | bytes 4128 | tf_op jit(solution)/shard_map/ppermute | solution.py:190
  76.9 1.4 %collective-permute-start.40 = (f32[1,1024]{1,0:T(1,128)S(1)}, f32[1,1024]{1,0:T(1,128)S(1)}, u32[]{:S(2)}, u32[]{:S(2)}) collective-permute-start(f32[1,1024]{1,0:T(1,128)S(1)} %get-tuple-element.57.own), channel_id=1, source_target_pairs={{0,16},{16,0},{1,17},{17,1},{2,18},{18,2},{3,19},{19,3},{4,20},{20... | collective-permute-start | bytes 12296 | tf_op jit(solution)/shard_map/ppermute | solution.py:193
  79.0 1.5 %collective-permute-done.40.x = f32[1,1024]{1,0:T(1,128)S(1)} collective-permute-done((f32[1,1024]{1,0:T(1,128)S(1)}, f32[1,1024]{1,0:T(1,128)S(1)}, u32[]{:S(2)}, u32[]{:S(2)}) %collective-permute-start.40) | collective-permute-done | bytes 4128 | tf_op jit(solution)/shard_map/ppermute | solution.py:193
  (83 shorter events, 23.5 us)
Async XLA Ops:
  0.6 16.7 %collective-permute-start.5 = (bf16[2048,512]{1,0:T(8,128)(2,1)}, bf16[2048,512]{1,0:T(8,128)(2,1)S(1)}, u32[]{:S(2)}, u32[]{:S(2)}) collective-permute-start(bf16[2048,512]{1,0:T(8,128)(2,1)} %plan.5), channel_id=1, source_target_pairs={{0,1},{1,0},{2,3},{3,2},{4,5},{5,4},{6,7},{7,6},{8,9},{9,8},{10,11... | collective-permute-start | bytes 6291464 | tf_op jit(solution)/shard_map/ppermute | solution.py:190
  1.1 12.2 %collective-permute-start = (bf16[512,256]{1,0:T(8,128)(2,1)}, bf16[512,256]{1,0:T(8,128)(2,1)S(1)}, u32[]{:S(2)}, u32[]{:S(2)}) collective-permute-start(bf16[512,256]{1,0:T(8,128)(2,1)} %near.3), channel_id=1, source_target_pairs={{0,16},{16,0},{1,17},{17,1},{2,18},{18,2},{3,19},{19,3},{4,20},{20... | collective-permute-start | bytes 786440 | tf_op jit(solution)/shard_map/ppermute | solution.py:193
  3.7 9.6 %collective-permute-start.3 = (bf16[32,2048]{1,0:T(8,128)(2,1)}, bf16[32,2048]{1,0:T(8,128)(2,1)S(1)}, u32[]{:S(2)}, u32[]{:S(2)}) collective-permute-start(bf16[32,2048]{1,0:T(8,128)(2,1)} %bitcast.5), channel_id=1, source_target_pairs={{0,9},{1,8},{2,11},{3,10},{4,13},{5,12},{6,15},{7,14},{8,1},{9,0},... | collective-permute-start | bytes 393224 | tf_op jit(solution)/shard_map/ppermute | solution.py:190
  6.1 7.2 %collective-permute-start.2 = (bf16[32,2048]{1,0:T(8,128)(2,1)}, bf16[32,2048]{1,0:T(8,128)(2,1)S(1)}, u32[]{:S(2)}, u32[]{:S(2)}) collective-permute-start(bf16[32,2048]{1,0:T(8,128)(2,1)} %bitcast.6), channel_id=1, source_target_pairs={{0,5},{1,4},{2,7},{3,6},{4,1},{5,0},{6,3},{7,2},{8,13},{9,12},{10,... | collective-permute-start | bytes 393224 | tf_op jit(solution)/shard_map/ppermute | solution.py:190
  7.6 5.8 %collective-permute-start.1 = (bf16[32,2048]{1,0:T(8,128)(2,1)}, bf16[32,2048]{1,0:T(8,128)(2,1)S(1)}, u32[]{:S(2)}, u32[]{:S(2)}) collective-permute-start(bf16[32,2048]{1,0:T(8,128)(2,1)} %bitcast.7), channel_id=1, source_target_pairs={{0,3},{1,2},{2,1},{3,0},{4,7},{5,6},{6,5},{7,4},{8,11},{9,10},{10,... | collective-permute-start | bytes 393224 | tf_op jit(solution)/shard_map/ppermute | solution.py:190
  13.6 3.4 %collective-permute-start.4 = (bf16[512,512]{1,0:T(8,128)(2,1)S(1)}, bf16[512,512]{1,0:T(8,128)(2,1)S(1)}, u32[]{:S(2)}, u32[]{:S(2)}) collective-permute-start(bf16[512,512]{1,0:T(8,128)(2,1)S(1)} %shard_map.69.units.targets), channel_id=1, source_target_pairs={{0,1},{1,0},{2,3},{3,2},{4,5},{5,4},{6,7},{7,6},{8,9},{9,8},{10,11... | collective-permute-start | bytes 1572872 | tf_op jit(solution)/shard_map/ppermute | solution.py:190
  13.9 5.4 %collective-permute-start.7 = (bf16[32,2048]{1,0:T(8,128)(2,1)S(1)}, bf16[32,2048]{1,0:T(8,128)(2,1)S(1)}, u32[]{:S(2)}, u32[]{:S(2)}) collective-permute-start(bf16[32,2048]{1,0:T(8,128)(2,1)S(1)} %collective-permute-done.3.refs_1_.p1), channel_id=1, source_target_pairs={{0,5},{1,4},{2,7},{3,6},{4,1},{5,0},{6,3},{7,2},{8,13},{9,12},{10,... | collective-permute-start | bytes 393224 | tf_op jit(solution)/shard_map/ppermute | solution.py:190
  15.4 3.4 %collective-permute-start.6 = (f32[1,512]{1,0:T(1,128)S(1)}, f32[1,512]{1,0:T(1,128)S(1)}, u32[]{:S(2)}, u32[]{:S(2)}) collective-permute-start(f32[1,512]{1,0:T(1,128)S(1)} %get-tuple-element.37.mass), channel_id=1, source_target_pairs={{0,1},{1,0},{2,3},{3,2},{4,5},{5,4},{6,7},{7,6},{8,9},{9,8},{10,11... | collective-permute-start | bytes 6152 | tf_op jit(solution)/shard_map/ppermute | solution.py:190
  15.5 6.0 %collective-permute-start.8 = (bf16[32,2048]{1,0:T(8,128)(2,1)S(1)}, bf16[32,2048]{1,0:T(8,128)(2,1)S(1)}, u32[]{:S(2)}, u32[]{:S(2)}) collective-permute-start(bf16[32,2048]{1,0:T(8,128)(2,1)S(1)} %collective-permute-done.3.refs_1_.p1), channel_id=1, source_target_pairs={{0,3},{1,2},{2,1},{3,0},{4,7},{5,6},{6,5},{7,4},{8,11},{9,10},{10,... | collective-permute-start | bytes 393224 | tf_op jit(solution)/shard_map/ppermute | solution.py:190
  17.0 7.2 %collective-permute-start.10 = (bf16[32,2048]{1,0:T(8,128)(2,1)S(1)}, bf16[32,2048]{1,0:T(8,128)(2,1)S(1)}, u32[]{:S(2)}, u32[]{:S(2)}) collective-permute-start(bf16[32,2048]{1,0:T(8,128)(2,1)S(1)} %collective-permute-done.1.p4), channel_id=1, source_target_pairs={{0,5},{1,4},{2,7},{3,6},{4,1},{5,0},{6,3},{7,2},{8,13},{9,12},{10,... | collective-permute-start | bytes 393224 | tf_op jit(solution)/shard_map/ppermute | solution.py:190
  19.4 6.5 %collective-permute-start.9 = (bf16[32,2048]{1,0:T(8,128)(2,1)S(1)}, bf16[32,2048]{1,0:T(8,128)(2,1)S(1)}, u32[]{:S(2)}, u32[]{:S(2)}) collective-permute-start(bf16[32,2048]{1,0:T(8,128)(2,1)S(1)} %collective-permute-done.7.refs_3_.p3), channel_id=1, source_target_pairs={{0,3},{1,2},{2,1},{3,0},{4,7},{5,6},{6,5},{7,4},{8,11},{9,10},{10,... | collective-permute-start | bytes 393224 | tf_op jit(solution)/shard_map/ppermute | solution.py:190
  22.7 3.1 %collective-permute-start.12 = (f32[1,2048]{1,0:T(1,128)S(1)}, f32[1,2048]{1,0:T(1,128)S(1)}, u32[]{:S(2)}, u32[]{:S(2)}) collective-permute-start(f32[1,2048]{1,0:T(1,128)S(1)} %add.42.squares), channel_id=1, source_target_pairs={{0,3},{1,2},{2,1},{3,0},{4,7},{5,6},{6,5},{7,4},{8,11},{9,10},{10,... | collective-permute-start | bytes 24584 | tf_op jit(solution)/shard_map/ppermute | solution.py:190
  26.6 4.3 %collective-permute-start.13 = (bf16[128,256]{1,0:T(8,128)(2,1)S(1)}, bf16[128,256]{1,0:T(8,128)(2,1)S(1)}, u32[]{:S(2)}, u32[]{:S(2)}) collective-permute-start(bf16[128,256]{1,0:T(8,128)(2,1)S(1)} %get-tuple-element.48), channel_id=1, source_target_pairs={{0,16},{16,0},{1,17},{17,1},{2,18},{18,2},{3,19},{19,3},{4,20},{20... | collective-permute-start | bytes 196616 | tf_op jit(solution)/shard_map/ppermute | solution.py:193
  27.2 5.7 %collective-permute-start.14 = (bf16[128,256]{1,0:T(8,128)(2,1)S(1)}, bf16[128,256]{1,0:T(8,128)(2,1)S(1)}, u32[]{:S(2)}, u32[]{:S(2)}) collective-permute-start(bf16[128,256]{1,0:T(8,128)(2,1)S(1)} %get-tuple-element.49), channel_id=1, source_target_pairs={{0,3},{1,2},{2,1},{3,0},{4,7},{5,6},{6,5},{7,4},{8,11},{9,10},{10,... | collective-permute-start | bytes 196616 | tf_op jit(solution)/shard_map/ppermute | solution.py:190
  27.4 5.5 %collective-permute-start.15 = (bf16[128,256]{1,0:T(8,128)(2,1)S(1)}, bf16[128,256]{1,0:T(8,128)(2,1)S(1)}, u32[]{:S(2)}, u32[]{:S(2)}) collective-permute-start(bf16[128,256]{1,0:T(8,128)(2,1)S(1)} %get-tuple-element.50), channel_id=1, source_target_pairs={{0,19},{1,18},{2,17},{3,16},{4,23},{5,22},{6,21},{7,20},{8,27},{9,... | collective-permute-start | bytes 196616 | tf_op jit(solution)/shard_map/ppermute | solution.py:197
  32.9 4.2 %collective-permute-start.16 = (bf16[128,256]{1,0:T(8,128)(2,1)S(1)}, bf16[128,256]{1,0:T(8,128)(2,1)S(1)}, u32[]{:S(2)}, u32[]{:S(2)}) collective-permute-start(bf16[128,256]{1,0:T(8,128)(2,1)S(1)} %get-tuple-element.60), channel_id=1, source_target_pairs={{0,5},{1,4},{2,7},{3,6},{4,1},{5,0},{6,3},{7,2},{8,13},{9,12},{10,... | collective-permute-start | bytes 196616 | tf_op jit(solution)/shard_map/ppermute | solution.py:190
  34.3 16.6 %collective-permute-start.25 = (bf16[256,2048]{1,0:T(8,128)(2,1)S(1)}, bf16[256,2048]{1,0:T(8,128)(2,1)S(1)}, u32[]{:S(2)}, u32[]{:S(2)}) collective-permute-start(bf16[256,2048]{1,0:T(8,128)(2,1)S(1)} %get-tuple-element.51.near), channel_id=1, source_target_pairs={{0,1},{1,0},{2,3},{3,2},{4,5},{5,4},{6,7},{7,6},{8,9},{9,8},{10,11... | collective-permute-start | bytes 3145736 | tf_op jit(solution)/shard_map/ppermute | solution.py:190
  37.1 5.1 %collective-permute-start.17 = (bf16[128,256]{1,0:T(8,128)(2,1)S(1)}, bf16[128,256]{1,0:T(8,128)(2,1)S(1)}, u32[]{:S(2)}, u32[]{:S(2)}) collective-permute-start(bf16[128,256]{1,0:T(8,128)(2,1)S(1)} %fusion.1), channel_id=1, source_target_pairs={{0,9},{1,8},{2,11},{3,10},{4,13},{5,12},{6,15},{7,14},{8,1},{9,0},... | collective-permute-start | bytes 196616 | tf_op jit(solution)/shard_map/ppermute | solution.py:190
  42.2 4.7 %collective-permute-start.20 = (bf16[128,256]{1,0:T(8,128)(2,1)S(1)}, bf16[128,256]{1,0:T(8,128)(2,1)S(1)}, u32[]{:S(2)}, u32[]{:S(2)}) collective-permute-start(bf16[128,256]{1,0:T(8,128)(2,1)S(1)} %fusion.c0), channel_id=1, source_target_pairs={{0,19},{1,18},{2,17},{3,16},{4,23},{5,22},{6,21},{7,20},{8,27},{9,... | collective-permute-start | bytes 196616 | tf_op jit(solution)/shard_map/ppermute | solution.py:197
  44.5 4.7 %collective-permute-start.19 = (bf16[128,256]{1,0:T(8,128)(2,1)S(1)}, bf16[128,256]{1,0:T(8,128)(2,1)S(1)}, u32[]{:S(2)}, u32[]{:S(2)}) collective-permute-start(bf16[128,256]{1,0:T(8,128)(2,1)S(1)} %fusion.c0), channel_id=1, source_target_pairs={{0,3},{1,2},{2,1},{3,0},{4,7},{5,6},{6,5},{7,4},{8,11},{9,10},{10,... | collective-permute-start | bytes 196616 | tf_op jit(solution)/shard_map/ppermute | solution.py:190
  45.0 4.6 %collective-permute-start.18 = (bf16[128,256]{1,0:T(8,128)(2,1)S(1)}, bf16[128,256]{1,0:T(8,128)(2,1)S(1)}, u32[]{:S(2)}, u32[]{:S(2)}) collective-permute-start(bf16[128,256]{1,0:T(8,128)(2,1)S(1)} %fusion.c0), channel_id=1, source_target_pairs={{0,16},{16,0},{1,17},{17,1},{2,18},{18,2},{3,19},{19,3},{4,20},{20... | collective-permute-start | bytes 196616 | tf_op jit(solution)/shard_map/ppermute | solution.py:193
  45.5 4.3 %collective-permute-start.21 = (bf16[128,256]{1,0:T(8,128)(2,1)S(1)}, bf16[128,256]{1,0:T(8,128)(2,1)S(1)}, u32[]{:S(2)}, u32[]{:S(2)}) collective-permute-start(bf16[128,256]{1,0:T(8,128)(2,1)S(1)} %fusion.c0), channel_id=1, source_target_pairs={{0,1},{1,0},{2,3},{3,2},{4,5},{5,4},{6,7},{7,6},{8,9},{9,8},{10,11... | collective-permute-start | bytes 196616 | tf_op jit(solution)/shard_map/ppermute | solution.py:190
  52.8 4.6 %collective-permute-start.28 = (f32[8,128]{1,0:T(8,128)S(1)}, f32[8,128]{1,0:T(8,128)S(1)}, u32[]{:S(2)}, u32[]{:S(2)}) collective-permute-start(f32[8,128]{1,0:T(8,128)S(1)} %get-tuple-element.53), channel_id=1, source_target_pairs={{0,6},{1,7},{2,4},{3,5},{4,2},{5,3},{6,0},{7,1},{8,14},{9,15},{10,... | collective-permute-start | bytes 12296 | tf_op jit(solution)/shard_map/ppermute | solution.py:190
  54.4 3.0 %collective-permute-start.27 = (f32[8,128]{1,0:T(8,128)S(1)}, f32[8,128]{1,0:T(8,128)S(1)}, u32[]{:S(2)}, u32[]{:S(2)}) collective-permute-start(f32[8,128]{1,0:T(8,128)S(1)} %get-tuple-element.53), channel_id=1, source_target_pairs={{0,5},{1,4},{2,7},{3,6},{4,1},{5,0},{6,3},{7,2},{8,13},{9,12},{10,... | collective-permute-start | bytes 12296 | tf_op jit(solution)/shard_map/ppermute | solution.py:190
  55.0 3.0 %collective-permute-start.26 = (f32[8,128]{1,0:T(8,128)S(1)}, f32[8,128]{1,0:T(8,128)S(1)}, u32[]{:S(2)}, u32[]{:S(2)}) collective-permute-start(f32[8,128]{1,0:T(8,128)S(1)} %get-tuple-element.53), channel_id=1, source_target_pairs={{0,3},{1,2},{2,1},{3,0},{4,7},{5,6},{6,5},{7,4},{8,11},{9,10},{10,... | collective-permute-start | bytes 12296 | tf_op jit(solution)/shard_map/ppermute | solution.py:190
  58.1 3.9 %collective-permute-start.29 = (f32[8,128]{1,0:T(8,128)S(1)}, f32[8,128]{1,0:T(8,128)S(1)}, u32[]{:S(2)}, u32[]{:S(2)}) collective-permute-start(f32[8,128]{1,0:T(8,128)S(1)} %add_add_fusion.1), channel_id=1, source_target_pairs={{0,9},{1,8},{2,11},{3,10},{4,13},{5,12},{6,15},{7,14},{8,1},{9,0},... | collective-permute-start | bytes 12296 | tf_op jit(solution)/shard_map/ppermute | solution.py:190
  62.4 3.7 %collective-permute-start.32 = (f32[1,1024]{1,0:T(1,128)S(1)}, f32[1,1024]{1,0:T(1,128)S(1)}, u32[]{:S(2)}, u32[]{:S(2)}) collective-permute-start(f32[1,1024]{1,0:T(1,128)S(1)} %shard_map.75.own), channel_id=1, source_target_pairs={{0,16},{16,0},{1,17},{17,1},{2,18},{18,2},{3,19},{19,3},{4,20},{20... | collective-permute-start | bytes 12296 | tf_op jit(solution)/shard_map/ppermute | solution.py:193
  66.9 4.6 %collective-permute-start.35 = (f32[8,128]{1,0:T(8,128)S(1)}, f32[8,128]{1,0:T(8,128)S(1)}, u32[]{:S(2)}, u32[]{:S(2)}) collective-permute-start(f32[8,128]{1,0:T(8,128)S(1)} %shard_map.76), channel_id=1, source_target_pairs={{0,6},{1,7},{2,4},{3,5},{4,2},{5,3},{6,0},{7,1},{8,14},{9,15},{10,... | collective-permute-start | bytes 12296 | tf_op jit(solution)/shard_map/ppermute | solution.py:190
  69.2 3.1 %collective-permute-start.34 = (f32[8,128]{1,0:T(8,128)S(1)}, f32[8,128]{1,0:T(8,128)S(1)}, u32[]{:S(2)}, u32[]{:S(2)}) collective-permute-start(f32[8,128]{1,0:T(8,128)S(1)} %shard_map.76), channel_id=1, source_target_pairs={{0,5},{1,4},{2,7},{3,6},{4,1},{5,0},{6,3},{7,2},{8,13},{9,12},{10,... | collective-permute-start | bytes 12296 | tf_op jit(solution)/shard_map/ppermute | solution.py:190
  69.2 3.1 %collective-permute-start.33 = (f32[8,128]{1,0:T(8,128)S(1)}, f32[8,128]{1,0:T(8,128)S(1)}, u32[]{:S(2)}, u32[]{:S(2)}) collective-permute-start(f32[8,128]{1,0:T(8,128)S(1)} %shard_map.76), channel_id=1, source_target_pairs={{0,3},{1,2},{2,1},{3,0},{4,7},{5,6},{6,5},{7,4},{8,11},{9,10},{10,... | collective-permute-start | bytes 12296 | tf_op jit(solution)/shard_map/ppermute | solution.py:190
  72.2 4.0 %collective-permute-start.36 = (f32[8,128]{1,0:T(8,128)S(1)}, f32[8,128]{1,0:T(8,128)S(1)}, u32[]{:S(2)}, u32[]{:S(2)}) collective-permute-start(f32[8,128]{1,0:T(8,128)S(1)} %add_add_fusion), channel_id=1, source_target_pairs={{0,9},{1,8},{2,11},{3,10},{4,13},{5,12},{6,15},{7,14},{8,1},{9,0},... | collective-permute-start | bytes 12296 | tf_op jit(solution)/shard_map/ppermute | solution.py:190
  76.9 3.6 %collective-permute-start.40 = (f32[1,1024]{1,0:T(1,128)S(1)}, f32[1,1024]{1,0:T(1,128)S(1)}, u32[]{:S(2)}, u32[]{:S(2)}) collective-permute-start(f32[1,1024]{1,0:T(1,128)S(1)} %get-tuple-element.57.own), channel_id=1, source_target_pairs={{0,16},{16,0},{1,17},{17,1},{2,18},{18,2},{3,19},{19,3},{4,20},{20... | collective-permute-start | bytes 12296 | tf_op jit(solution)/shard_map/ppermute | solution.py:193
  (15 other events, 34.6 us)

commit v6 on v5

--- a/solution.py
+++ b/solution.py
@@ -109,27 +109,34 @@
     to_xy[...] = product[half:, split:].astype(BF16)
 
 
-def kernel_block(targets, targets_far, c0, x0, c1, x1, c2, x2, c3, x3, near, far, out, sums, left, whole):
+def left_part(targets, targets_far, c0, x0, c1, x1, left, squares, whole):
     rows, split = c0.shape
-    for i, pair in enumerate(((c0, x0), (c1, x1), (c2, x2), (c3, x3))):
+    for i, pair in enumerate(((c0, x0), (c1, x1))):
         for j, piece in enumerate(pair):
             whole[i * rows : (i + 1) * rows, j * split : (j + 1) * split] = piece[...]
     nt = (((1,), (1,)), ((), ()))
-    squares = jnp.sum(whole[...].astype(F32) ** 2)
-    scale = lax.rsqrt(squares / 2048.0 + 1e-06) * (sharpness * LOG2E)
     count = targets.shape[0]
     for i, points in enumerate((targets, targets_far)):
         product = lax.dot_general(points[...], whole[...], nt, preferred_element_type=F32)
-        left[i * count : (i + 1) * count, :] = (product * scale).astype(BF16)
-    half = 2 * rows
+        left[i * count : (i + 1) * count, :] = product.astype(BF16)
+    squares[...] = jnp.broadcast_to(jnp.sum(whole[...].astype(F32) ** 2), squares.shape)
+
+
+def kernel_block(
+    left, squares, targets, targets_far, c2, x2, c3, x3, near, far,
+    out, sums, left_far, squares_far, whole,
+):
+    left_part(targets, targets_far, c2, x2, c3, x3, left_far, squares_far, whole)
+    total = squares[:1, :1] + squares_far[:1, :1]
+    scale = lax.rsqrt(total / 2048.0 + 1e-06) * (sharpness * LOG2E)
     count = out.shape[1]
     width, first = min(512, count), half_index() * count
     for start in range(0, count, width):
         here = slice(start, start + width)
         there = pl.ds(pl.multiple_of(first + start, width), width)
-        scores = jnp.dot(left[:, :half], near[:, there], preferred_element_type=F32)
-        scores += jnp.dot(left[:, half:], far[:, there], preferred_element_type=F32)
-        block = jnp.exp2(scores)
+        scores = jnp.dot(left[...], near[:, there], preferred_element_type=F32)
+        scores += jnp.dot(left_far[...], far[:, there], preferred_element_type=F32)
+        block = jnp.exp2(scores * scale)
         out[:, here] = block
         total = jnp.sum(block, axis=0, keepdims=True)
         for j in range(width // LANES):
@@ -288,16 +295,28 @@
 
     chip, count = 2 * targets, sources // 2
     part, wide = (count // LANES, LANES), (1, chip)
+    squares_shape = ((8, LANES), F32)
+    left, left_squares = call(
+        left_part,
+        (((chip, split), BF16), squares_shape),
+        units,
+        units_far,
+        *blocks[:4],
+        scratch=(((split, features), BF16),),
+        flops=2 * chip * features * split,
+    )
     block, sums = call(
         kernel_block,
         (((chip, count), F32), (part, F32)),
+        left,
+        left_squares,
         units,
         units_far,
-        *blocks,
+        *blocks[4:],
         xs,
         xs_far,
-        scratch=(((chip, features), BF16), ((features, features), BF16)),
-        flops=2 * chip * features * (count + features),
+        scratch=(((chip, split), BF16), squares_shape, ((split, features), BF16)),
+        flops=2 * chip * features * (count + split),
     )
 
     for repeat in range(2):

time: 82.1 us -> 81.8 us (level)
    pallas_call x11 -> x12, Pallas kernels: 7.71 us -> 7.85 us  [call(): pl.pallas_call(function, out_shape=outs, in_specs=[ANY if i in loose else...]
  transfers between devices with their start and end apart: 41 -> 41, of which waited for: 23 -> 23; matrix products, arithmetic and copies ran while one was open for 0% -> 0% of each run, Pallas kernels for 4% -> 5%
where the time goes in v6:
time: 81.8 us; the launch traced here: 81.6 us
  starting transfers between devices  43.9 us (54%)
  waiting for transfers between devices  24.9 us (30%)
  Pallas kernels  7.85 us (10%)
  local copies, waits for them, and re-layouts  3.95 us (5%)
  between operations  0.82 us (1%)
    ppermute x32, starting transfers between devices, swap(): return lax.ppermute(value, 'cols', [(i, i ^ bits) for i in range(n)])  32 us
    ppermute x32, waiting for transfers between devices, swap(): return lax.ppermute(value, 'cols', [(i, i ^ bits) for i in range(n)])  19.5 us
    pallas_call x12, Pallas kernels, call(): pl.pallas_call(function, out_shape=outs, in_specs=[ANY if i in loose else...  7.85 us
    ppermute x5, starting transfers between devices, cross(): return lax.ppermute(value, 'rows', [(0, 1), (1, 0)])  6.19 us
    ppermute x4, starting transfers between devices, both(): return lax.ppermute(value, ('rows', 'cols'), pairs)  5.75 us
    ppermute x5, waiting for transfers between devices, cross(): return lax.ppermute(value, 'rows', [(0, 1), (1, 0)])  3.99 us
    unnamed x12, local copies, waits for them, and re-layouts  3.92 us
  transfers between devices with their start and end apart: 41, of which 23 were waited for; matrix products, arithmetic and copies ran while one was open for 0% of the time, Pallas kernels for 5%

profile of v6, /device:TPU:0, one launch (start us, length us, event | category | flops | bytes accessed | tf_op | source)
XLA Modules:
  0.0 81.6 jit_solution(10110199082443100510)
XLA Ops:
  1.1 2.6 %collective-permute-start = (bf16[512,256]{1,0:T(8,128)(2,1)}, bf16[512,256]{1,0:T(8,128)(2,1)S(1)}, u32[]{:S(2)}, u32[]{:S(2)}) collective-permute-start(bf16[512,256]{1,0:T(8,128)(2,1)} %near.3), channel_id=1, source_target_pairs={{0,16},{16,0},{1,17},{17,1},{2,18},{18,2},{3,19},{19,3},{4,20},{20... | collective-permute-start | bytes 786440 | tf_op jit(solution)/shard_map/ppermute | solution.py:200
  3.7 2.4 %collective-permute-start.3 = (bf16[32,2048]{1,0:T(8,128)(2,1)}, bf16[32,2048]{1,0:T(8,128)(2,1)S(1)}, u32[]{:S(2)}, u32[]{:S(2)}) collective-permute-start(bf16[32,2048]{1,0:T(8,128)(2,1)} %bitcast.5), channel_id=1, source_target_pairs={{0,9},{1,8},{2,11},{3,10},{4,13},{5,12},{6,15},{7,14},{8,1},{9,0},... | collective-permute-start | bytes 393224 | tf_op jit(solution)/shard_map/ppermute | solution.py:197
  6.1 1.5 %collective-permute-start.2 = (bf16[32,2048]{1,0:T(8,128)(2,1)}, bf16[32,2048]{1,0:T(8,128)(2,1)S(1)}, u32[]{:S(2)}, u32[]{:S(2)}) collective-permute-start(bf16[32,2048]{1,0:T(8,128)(2,1)} %bitcast.6), channel_id=1, source_target_pairs={{0,5},{1,4},{2,7},{3,6},{4,1},{5,0},{6,3},{7,2},{8,13},{9,12},{10,... | collective-permute-start | bytes 393224 | tf_op jit(solution)/shard_map/ppermute | solution.py:197
  7.6 1.3 %collective-permute-start.1 = (bf16[32,2048]{1,0:T(8,128)(2,1)}, bf16[32,2048]{1,0:T(8,128)(2,1)S(1)}, u32[]{:S(2)}, u32[]{:S(2)}) collective-permute-start(bf16[32,2048]{1,0:T(8,128)(2,1)} %bitcast.7), channel_id=1, source_target_pairs={{0,3},{1,2},{2,1},{3,0},{4,7},{5,6},{6,5},{7,4},{8,11},{9,10},{10,... | collective-permute-start | bytes 393224 | tf_op jit(solution)/shard_map/ppermute | solution.py:197
  8.9 1.6 %copy-done = bf16[2048,512]{1,0:T(8,128)(2,1)S(1)} copy-done((bf16[2048,512]{1,0:T(8,128)(2,1)S(1)}, bf16[2048,512]{1,0:T(8,128)(2,1)}, u32[]{:S(2)}) %copy-start) | copy-done | bytes 2097176
  13.9 1.4 %collective-permute-start.7 = (bf16[32,2048]{1,0:T(8,128)(2,1)S(1)}, bf16[32,2048]{1,0:T(8,128)(2,1)S(1)}, u32[]{:S(2)}, u32[]{:S(2)}) collective-permute-start(bf16[32,2048]{1,0:T(8,128)(2,1)S(1)} %collective-permute-done.3.refs_1_.p1), channel_id=1, source_target_pairs={{0,5},{1,4},{2,7},{3,6},{4,1},{5,0},{6,3},{7,2},{8,13},{9,12},{10,... | collective-permute-start | bytes 393224 | tf_op jit(solution)/shard_map/ppermute | solution.py:197
  15.5 1.5 %collective-permute-start.8 = (bf16[32,2048]{1,0:T(8,128)(2,1)S(1)}, bf16[32,2048]{1,0:T(8,128)(2,1)S(1)}, u32[]{:S(2)}, u32[]{:S(2)}) collective-permute-start(bf16[32,2048]{1,0:T(8,128)(2,1)S(1)} %collective-permute-done.3.refs_1_.p1), channel_id=1, source_target_pairs={{0,3},{1,2},{2,1},{3,0},{4,7},{5,6},{6,5},{7,4},{8,11},{9,10},{10,... | collective-permute-start | bytes 393224 | tf_op jit(solution)/shard_map/ppermute | solution.py:197
  17.3 1.4 %shard_map.70.upper = bf16[1024,512]{1,0:T(8,128)(2,1)S(1)} custom-call(bf16[2048,512]{1,0:T(8,128)(2,1)S(1)} %copy-done.1, bf16[2048,512]{1,0:T(8,128)(2,1)S(1)} %collective-permute-done.5.plan_far, bf16[512,512]{1,0:T(8,128)(2,1)S(1)} %shard_map.69.units.targets, bf16[512,512]{1,0:T(8,128)(2,1)S(1)} %collective-permute-done.4.units_far.targets_far), custom_call_target="tpu_custom_call" | custom-call | flops 1073741824 | bytes 6291456 | tf_op jit(solution)/shard_map/pallas_call | solution.py:209
  19.4 1.9 %collective-permute-start.9 = (bf16[32,2048]{1,0:T(8,128)(2,1)S(1)}, bf16[32,2048]{1,0:T(8,128)(2,1)S(1)}, u32[]{:S(2)}, u32[]{:S(2)}) collective-permute-start(bf16[32,2048]{1,0:T(8,128)(2,1)S(1)} %collective-permute-done.7.refs_3_.p3), channel_id=1, source_target_pairs={{0,3},{1,2},{2,1},{3,0},{4,7},{5,6},{6,5},{7,4},{8,11},{9,10},{10,... | collective-permute-start | bytes 393224 | tf_op jit(solution)/shard_map/ppermute | solution.py:197
  22.8 1.4 %shard_map.72.lower = bf16[1024,512]{1,0:T(8,128)(2,1)S(1)} custom-call(bf16[2048,512]{1,0:T(8,128)(2,1)S(1)} %copy-done.1, bf16[2048,512]{1,0:T(8,128)(2,1)S(1)} %collective-permute-done.5.plan_far, bf16[512,512]{1,0:T(8,128)(2,1)S(1)} %shard_map.69.units.targets, bf16[512,512]{1,0:T(8,128)(2,1)S(1)} %collective-permute-done.4.units_far.targets_far), custom_call_target="tpu_custom_call" | custom-call | flops 1073741824 | bytes 6291456 | tf_op jit(solution)/shard_map/pallas_call | solution.py:209
  24.2 1.6 %collective-permute-done.12.squares_y = f32[1,2048]{1,0:T(1,128)S(1)} collective-permute-done((f32[1,2048]{1,0:T(1,128)S(1)}, f32[1,2048]{1,0:T(1,128)S(1)}, u32[]{:S(2)}, u32[]{:S(2)}) %collective-permute-start.12) | collective-permute-done | bytes 8224 | tf_op jit(solution)/shard_map/ppermute | solution.py:197
  27.4 2.5 %collective-permute-start.15 = (bf16[128,256]{1,0:T(8,128)(2,1)S(1)}, bf16[128,256]{1,0:T(8,128)(2,1)S(1)}, u32[]{:S(2)}, u32[]{:S(2)}) collective-permute-start(bf16[128,256]{1,0:T(8,128)(2,1)S(1)} %get-tuple-element.52), channel_id=1, source_target_pairs={{0,19},{1,18},{2,17},{3,16},{4,23},{5,22},{6,21},{7,20},{8,27},{9,... | collective-permute-start | bytes 196616 | tf_op jit(solution)/shard_map/ppermute | solution.py:204
  30.9 2.0 %collective-permute-done.14 = bf16[128,256]{1,0:T(8,128)(2,1)S(1)} collective-permute-done((bf16[128,256]{1,0:T(8,128)(2,1)S(1)}, bf16[128,256]{1,0:T(8,128)(2,1)S(1)}, u32[]{:S(2)}, u32[]{:S(2)}) %collective-permute-start.14) | collective-permute-done | bytes 65568 | tf_op jit(solution)/shard_map/ppermute | solution.py:197
  32.9 1.4 %collective-permute-start.16 = (bf16[128,256]{1,0:T(8,128)(2,1)S(1)}, bf16[128,256]{1,0:T(8,128)(2,1)S(1)}, u32[]{:S(2)}, u32[]{:S(2)}) collective-permute-start(bf16[128,256]{1,0:T(8,128)(2,1)S(1)} %get-tuple-element.64), channel_id=1, source_target_pairs={{0,5},{1,4},{2,7},{3,6},{4,1},{5,0},{6,3},{7,2},{8,13},{9,12},{10,... | collective-permute-start | bytes 196616 | tf_op jit(solution)/shard_map/ppermute | solution.py:197
  34.7 2.4 %collective-permute-done.16 = bf16[128,256]{1,0:T(8,128)(2,1)S(1)} collective-permute-done((bf16[128,256]{1,0:T(8,128)(2,1)S(1)}, bf16[128,256]{1,0:T(8,128)(2,1)S(1)}, u32[]{:S(2)}, u32[]{:S(2)}) %collective-permute-start.16) | collective-permute-done | bytes 65568 | tf_op jit(solution)/shard_map/ppermute | solution.py:197
  37.1 1.9 %collective-permute-start.17 = (bf16[128,256]{1,0:T(8,128)(2,1)S(1)}, bf16[128,256]{1,0:T(8,128)(2,1)S(1)}, u32[]{:S(2)}, u32[]{:S(2)}) collective-permute-start(bf16[128,256]{1,0:T(8,128)(2,1)S(1)} %fusion.1), channel_id=1, source_target_pairs={{0,9},{1,8},{2,11},{3,10},{4,13},{5,12},{6,15},{7,14},{8,1},{9,0},... | collective-permute-start | bytes 196616 | tf_op jit(solution)/shard_map/ppermute | solution.py:197
  39.0 3.2 %collective-permute-done.17 = bf16[128,256]{1,0:T(8,128)(2,1)S(1)} collective-permute-done((bf16[128,256]{1,0:T(8,128)(2,1)S(1)}, bf16[128,256]{1,0:T(8,128)(2,1)S(1)}, u32[]{:S(2)}, u32[]{:S(2)}) %collective-permute-start.17) | collective-permute-done | bytes 65568 | tf_op jit(solution)/shard_map/ppermute | solution.py:197
  42.2 2.2 %collective-permute-start.20 = (bf16[128,256]{1,0:T(8,128)(2,1)S(1)}, bf16[128,256]{1,0:T(8,128)(2,1)S(1)}, u32[]{:S(2)}, u32[]{:S(2)}) collective-permute-start(bf16[128,256]{1,0:T(8,128)(2,1)S(1)} %fusion.c0), channel_id=1, source_target_pairs={{0,19},{1,18},{2,17},{3,16},{4,23},{5,22},{6,21},{7,20},{8,27},{9,... | collective-permute-start | bytes 196616 | tf_op jit(solution)/shard_map/ppermute | solution.py:204
  45.5 1.2 %collective-permute-start.21 = (bf16[128,256]{1,0:T(8,128)(2,1)S(1)}, bf16[128,256]{1,0:T(8,128)(2,1)S(1)}, u32[]{:S(2)}, u32[]{:S(2)}) collective-permute-start(bf16[128,256]{1,0:T(8,128)(2,1)S(1)} %fusion.c0), channel_id=1, source_target_pairs={{0,1},{1,0},{2,3},{3,2},{4,5},{5,4},{6,7},{7,6},{8,9},{9,8},{10,11... | collective-permute-start | bytes 196616 | tf_op jit(solution)/shard_map/ppermute | solution.py:197
  46.9 1.6 %collective-permute-start.24 = (bf16[128,256]{1,0:T(8,128)(2,1)S(1)}, bf16[128,256]{1,0:T(8,128)(2,1)S(1)}, u32[]{:S(2)}, u32[]{:S(2)}) collective-permute-start(bf16[128,256]{1,0:T(8,128)(2,1)S(1)} %collective-permute-done.20.x1), channel_id=1, source_target_pairs={{0,1},{1,0},{2,3},{3,2},{4,5},{5,4},{6,7},{7,6},{8,9},{9,8},{10,11... | collective-permute-start | bytes 196616 | tf_op jit(solution)/shard_map/ppermute | solution.py:197
  50.8 1.6 %shard_map.75 = (f32[1024,1024]{1,0:T(8,128)S(1)}, f32[8,128]{1,0:T(8,128)S(1)}) custom-call(bf16[1024,256]{1,0:T(8,128)(2,1)S(1)} %get-tuple-element.53.left, f32[8,128]{1,0:T(8,128)S(1)} %get-tuple-element.54.squares, bf16[512,512]{1,0:T(8,128)(2,1)S(1)} %shard_map.69.units.targets, bf16[512,512]{1,0:T(8,128)(2,1)S(1)} %collective-permute-done.4.units_far.targets_far, ...), custom_call_target="tpu_custom_call" | custom-call | flops 1342177280 | bytes 8134656 | tf_op jit(solution)/shard_map/pallas_call | solution.py:209
  52.5 1.6 %collective-permute-start.28 = (f32[8,128]{1,0:T(8,128)S(1)}, f32[8,128]{1,0:T(8,128)S(1)}, u32[]{:S(2)}, u32[]{:S(2)}) collective-permute-start(f32[8,128]{1,0:T(8,128)S(1)} %get-tuple-element.57), channel_id=1, source_target_pairs={{0,6},{1,7},{2,4},{3,5},{4,2},{5,3},{6,0},{7,1},{8,14},{9,15},{10,... | collective-permute-start | bytes 12296 | tf_op jit(solution)/shard_map/ppermute | solution.py:197
  55.7 1.3 %collective-permute-done.28 = f32[8,128]{1,0:T(8,128)S(1)} collective-permute-done((f32[8,128]{1,0:T(8,128)S(1)}, f32[8,128]{1,0:T(8,128)S(1)}, u32[]{:S(2)}, u32[]{:S(2)}) %collective-permute-start.28) | collective-permute-done | bytes 4128 | tf_op jit(solution)/shard_map/ppermute | solution.py:197
  57.7 2.4 %collective-permute-start.29 = (f32[8,128]{1,0:T(8,128)S(1)}, f32[8,128]{1,0:T(8,128)S(1)}, u32[]{:S(2)}, u32[]{:S(2)}) collective-permute-start(f32[8,128]{1,0:T(8,128)S(1)} %add_add_fusion.1), channel_id=1, source_target_pairs={{0,9},{1,8},{2,11},{3,10},{4,13},{5,12},{6,15},{7,14},{8,1},{9,0},... | collective-permute-start | bytes 12296 | tf_op jit(solution)/shard_map/ppermute | solution.py:197
  60.1 1.5 %collective-permute-done.29 = f32[8,128]{1,0:T(8,128)S(1)} collective-permute-done((f32[8,128]{1,0:T(8,128)S(1)}, f32[8,128]{1,0:T(8,128)S(1)}, u32[]{:S(2)}, u32[]{:S(2)}) %collective-permute-start.29) | collective-permute-done | bytes 4128 | tf_op jit(solution)/shard_map/ppermute | solution.py:197
  64.2 1.5 %collective-permute-done.32.x = f32[1,1024]{1,0:T(1,128)S(1)} collective-permute-done((f32[1,1024]{1,0:T(1,128)S(1)}, f32[1,1024]{1,0:T(1,128)S(1)}, u32[]{:S(2)}, u32[]{:S(2)}) %collective-permute-start.32) | collective-permute-done | bytes 4128 | tf_op jit(solution)/shard_map/ppermute | solution.py:200
  66.6 2.3 %collective-permute-start.35 = (f32[8,128]{1,0:T(8,128)S(1)}, f32[8,128]{1,0:T(8,128)S(1)}, u32[]{:S(2)}, u32[]{:S(2)}) collective-permute-start(f32[8,128]{1,0:T(8,128)S(1)} %shard_map.77), channel_id=1, source_target_pairs={{0,6},{1,7},{2,4},{3,5},{4,2},{5,3},{6,0},{7,1},{8,14},{9,15},{10,... | collective-permute-start | bytes 12296 | tf_op jit(solution)/shard_map/ppermute | solution.py:197
  69.8 1.3 %collective-permute-done.35 = f32[8,128]{1,0:T(8,128)S(1)} collective-permute-done((f32[8,128]{1,0:T(8,128)S(1)}, f32[8,128]{1,0:T(8,128)S(1)}, u32[]{:S(2)}, u32[]{:S(2)}) %collective-permute-start.35) | collective-permute-done | bytes 4128 | tf_op jit(solution)/shard_map/ppermute | solution.py:197
  71.9 2.7 %collective-permute-start.36 = (f32[8,128]{1,0:T(8,128)S(1)}, f32[8,128]{1,0:T(8,128)S(1)}, u32[]{:S(2)}, u32[]{:S(2)}) collective-permute-start(f32[8,128]{1,0:T(8,128)S(1)} %add_add_fusion), channel_id=1, source_target_pairs={{0,9},{1,8},{2,11},{3,10},{4,13},{5,12},{6,15},{7,14},{8,1},{9,0},... | collective-permute-start | bytes 12296 | tf_op jit(solution)/shard_map/ppermute | solution.py:197
  74.6 1.3 %collective-permute-done.36 = f32[8,128]{1,0:T(8,128)S(1)} collective-permute-done((f32[8,128]{1,0:T(8,128)S(1)}, f32[8,128]{1,0:T(8,128)S(1)}, u32[]{:S(2)}, u32[]{:S(2)}) %collective-permute-start.36) | collective-permute-done | bytes 4128 | tf_op jit(solution)/shard_map/ppermute | solution.py:197
  76.5 1.4 %collective-permute-start.40 = (f32[1,1024]{1,0:T(1,128)S(1)}, f32[1,1024]{1,0:T(1,128)S(1)}, u32[]{:S(2)}, u32[]{:S(2)}) collective-permute-start(f32[1,1024]{1,0:T(1,128)S(1)} %get-tuple-element.61.own), channel_id=1, source_target_pairs={{0,16},{16,0},{1,17},{17,1},{2,18},{18,2},{3,19},{19,3},{4,20},{20... | collective-permute-start | bytes 12296 | tf_op jit(solution)/shard_map/ppermute | solution.py:200
  78.7 1.5 %collective-permute-done.40.x = f32[1,1024]{1,0:T(1,128)S(1)} collective-permute-done((f32[1,1024]{1,0:T(1,128)S(1)}, f32[1,1024]{1,0:T(1,128)S(1)}, u32[]{:S(2)}, u32[]{:S(2)}) %collective-permute-start.40) | collective-permute-done | bytes 4128 | tf_op jit(solution)/shard_map/ppermute | solution.py:200
  (84 shorter events, 23.5 us)
Async XLA Ops:
  0.6 16.7 %collective-permute-start.5 = (bf16[2048,512]{1,0:T(8,128)(2,1)}, bf16[2048,512]{1,0:T(8,128)(2,1)S(1)}, u32[]{:S(2)}, u32[]{:S(2)}) collective-permute-start(bf16[2048,512]{1,0:T(8,128)(2,1)} %plan.5), channel_id=1, source_target_pairs={{0,1},{1,0},{2,3},{3,2},{4,5},{5,4},{6,7},{7,6},{8,9},{9,8},{10,11... | collective-permute-start | bytes 6291464 | tf_op jit(solution)/shard_map/ppermute | solution.py:197
  1.1 12.2 %collective-permute-start = (bf16[512,256]{1,0:T(8,128)(2,1)}, bf16[512,256]{1,0:T(8,128)(2,1)S(1)}, u32[]{:S(2)}, u32[]{:S(2)}) collective-permute-start(bf16[512,256]{1,0:T(8,128)(2,1)} %near.3), channel_id=1, source_target_pairs={{0,16},{16,0},{1,17},{17,1},{2,18},{18,2},{3,19},{19,3},{4,20},{20... | collective-permute-start | bytes 786440 | tf_op jit(solution)/shard_map/ppermute | solution.py:200
  3.7 9.6 %collective-permute-start.3 = (bf16[32,2048]{1,0:T(8,128)(2,1)}, bf16[32,2048]{1,0:T(8,128)(2,1)S(1)}, u32[]{:S(2)}, u32[]{:S(2)}) collective-permute-start(bf16[32,2048]{1,0:T(8,128)(2,1)} %bitcast.5), channel_id=1, source_target_pairs={{0,9},{1,8},{2,11},{3,10},{4,13},{5,12},{6,15},{7,14},{8,1},{9,0},... | collective-permute-start | bytes 393224 | tf_op jit(solution)/shard_map/ppermute | solution.py:197
  6.1 7.2 %collective-permute-start.2 = (bf16[32,2048]{1,0:T(8,128)(2,1)}, bf16[32,2048]{1,0:T(8,128)(2,1)S(1)}, u32[]{:S(2)}, u32[]{:S(2)}) collective-permute-start(bf16[32,2048]{1,0:T(8,128)(2,1)} %bitcast.6), channel_id=1, source_target_pairs={{0,5},{1,4},{2,7},{3,6},{4,1},{5,0},{6,3},{7,2},{8,13},{9,12},{10,... | collective-permute-start | bytes 393224 | tf_op jit(solution)/shard_map/ppermute | solution.py:197
  7.6 5.8 %collective-permute-start.1 = (bf16[32,2048]{1,0:T(8,128)(2,1)}, bf16[32,2048]{1,0:T(8,128)(2,1)S(1)}, u32[]{:S(2)}, u32[]{:S(2)}) collective-permute-start(bf16[32,2048]{1,0:T(8,128)(2,1)} %bitcast.7), channel_id=1, source_target_pairs={{0,3},{1,2},{2,1},{3,0},{4,7},{5,6},{6,5},{7,4},{8,11},{9,10},{10,... | collective-permute-start | bytes 393224 | tf_op jit(solution)/shard_map/ppermute | solution.py:197
  13.6 3.4 %collective-permute-start.4 = (bf16[512,512]{1,0:T(8,128)(2,1)S(1)}, bf16[512,512]{1,0:T(8,128)(2,1)S(1)}, u32[]{:S(2)}, u32[]{:S(2)}) collective-permute-start(bf16[512,512]{1,0:T(8,128)(2,1)S(1)} %shard_map.69.units.targets), channel_id=1, source_target_pairs={{0,1},{1,0},{2,3},{3,2},{4,5},{5,4},{6,7},{7,6},{8,9},{9,8},{10,11... | collective-permute-start | bytes 1572872 | tf_op jit(solution)/shard_map/ppermute | solution.py:197
  13.9 5.4 %collective-permute-start.7 = (bf16[32,2048]{1,0:T(8,128)(2,1)S(1)}, bf16[32,2048]{1,0:T(8,128)(2,1)S(1)}, u32[]{:S(2)}, u32[]{:S(2)}) collective-permute-start(bf16[32,2048]{1,0:T(8,128)(2,1)S(1)} %collective-permute-done.3.refs_1_.p1), channel_id=1, source_target_pairs={{0,5},{1,4},{2,7},{3,6},{4,1},{5,0},{6,3},{7,2},{8,13},{9,12},{10,... | collective-permute-start | bytes 393224 | tf_op jit(solution)/shard_map/ppermute | solution.py:197
  15.4 3.4 %collective-permute-start.6 = (f32[1,512]{1,0:T(1,128)S(1)}, f32[1,512]{1,0:T(1,128)S(1)}, u32[]{:S(2)}, u32[]{:S(2)}) collective-permute-start(f32[1,512]{1,0:T(1,128)S(1)} %get-tuple-element.39.mass), channel_id=1, source_target_pairs={{0,1},{1,0},{2,3},{3,2},{4,5},{5,4},{6,7},{7,6},{8,9},{9,8},{10,11... | collective-permute-start | bytes 6152 | tf_op jit(solution)/shard_map/ppermute | solution.py:197
  15.5 6.0 %collective-permute-start.8 = (bf16[32,2048]{1,0:T(8,128)(2,1)S(1)}, bf16[32,2048]{1,0:T(8,128)(2,1)S(1)}, u32[]{:S(2)}, u32[]{:S(2)}) collective-permute-start(bf16[32,2048]{1,0:T(8,128)(2,1)S(1)} %collective-permute-done.3.refs_1_.p1), channel_id=1, source_target_pairs={{0,3},{1,2},{2,1},{3,0},{4,7},{5,6},{6,5},{7,4},{8,11},{9,10},{10,... | collective-permute-start | bytes 393224 | tf_op jit(solution)/shard_map/ppermute | solution.py:197
  17.0 7.2 %collective-permute-start.10 = (bf16[32,2048]{1,0:T(8,128)(2,1)S(1)}, bf16[32,2048]{1,0:T(8,128)(2,1)S(1)}, u32[]{:S(2)}, u32[]{:S(2)}) collective-permute-start(bf16[32,2048]{1,0:T(8,128)(2,1)S(1)} %collective-permute-done.1.p4), channel_id=1, source_target_pairs={{0,5},{1,4},{2,7},{3,6},{4,1},{5,0},{6,3},{7,2},{8,13},{9,12},{10,... | collective-permute-start | bytes 393224 | tf_op jit(solution)/shard_map/ppermute | solution.py:197
  19.4 6.5 %collective-permute-start.9 = (bf16[32,2048]{1,0:T(8,128)(2,1)S(1)}, bf16[32,2048]{1,0:T(8,128)(2,1)S(1)}, u32[]{:S(2)}, u32[]{:S(2)}) collective-permute-start(bf16[32,2048]{1,0:T(8,128)(2,1)S(1)} %collective-permute-done.7.refs_3_.p3), channel_id=1, source_target_pairs={{0,3},{1,2},{2,1},{3,0},{4,7},{5,6},{6,5},{7,4},{8,11},{9,10},{10,... | collective-permute-start | bytes 393224 | tf_op jit(solution)/shard_map/ppermute | solution.py:197
  22.7 3.1 %collective-permute-start.12 = (f32[1,2048]{1,0:T(1,128)S(1)}, f32[1,2048]{1,0:T(1,128)S(1)}, u32[]{:S(2)}, u32[]{:S(2)}) collective-permute-start(f32[1,2048]{1,0:T(1,128)S(1)} %add.42.squares), channel_id=1, source_target_pairs={{0,3},{1,2},{2,1},{3,0},{4,7},{5,6},{6,5},{7,4},{8,11},{9,10},{10,... | collective-permute-start | bytes 24584 | tf_op jit(solution)/shard_map/ppermute | solution.py:197
  26.6 4.3 %collective-permute-start.13 = (bf16[128,256]{1,0:T(8,128)(2,1)S(1)}, bf16[128,256]{1,0:T(8,128)(2,1)S(1)}, u32[]{:S(2)}, u32[]{:S(2)}) collective-permute-start(bf16[128,256]{1,0:T(8,128)(2,1)S(1)} %get-tuple-element.50), channel_id=1, source_target_pairs={{0,16},{16,0},{1,17},{17,1},{2,18},{18,2},{3,19},{19,3},{4,20},{20... | collective-permute-start | bytes 196616 | tf_op jit(solution)/shard_map/ppermute | solution.py:200
  27.2 5.7 %collective-permute-start.14 = (bf16[128,256]{1,0:T(8,128)(2,1)S(1)}, bf16[128,256]{1,0:T(8,128)(2,1)S(1)}, u32[]{:S(2)}, u32[]{:S(2)}) collective-permute-start(bf16[128,256]{1,0:T(8,128)(2,1)S(1)} %get-tuple-element.51), channel_id=1, source_target_pairs={{0,3},{1,2},{2,1},{3,0},{4,7},{5,6},{6,5},{7,4},{8,11},{9,10},{10,... | collective-permute-start | bytes 196616 | tf_op jit(solution)/shard_map/ppermute | solution.py:197
  27.4 5.5 %collective-permute-start.15 = (bf16[128,256]{1,0:T(8,128)(2,1)S(1)}, bf16[128,256]{1,0:T(8,128)(2,1)S(1)}, u32[]{:S(2)}, u32[]{:S(2)}) collective-permute-start(bf16[128,256]{1,0:T(8,128)(2,1)S(1)} %get-tuple-element.52), channel_id=1, source_target_pairs={{0,19},{1,18},{2,17},{3,16},{4,23},{5,22},{6,21},{7,20},{8,27},{9,... | collective-permute-start | bytes 196616 | tf_op jit(solution)/shard_map/ppermute | solution.py:204
  32.9 4.2 %collective-permute-start.16 = (bf16[128,256]{1,0:T(8,128)(2,1)S(1)}, bf16[128,256]{1,0:T(8,128)(2,1)S(1)}, u32[]{:S(2)}, u32[]{:S(2)}) collective-permute-start(bf16[128,256]{1,0:T(8,128)(2,1)S(1)} %get-tuple-element.64), channel_id=1, source_target_pairs={{0,5},{1,4},{2,7},{3,6},{4,1},{5,0},{6,3},{7,2},{8,13},{9,12},{10,... | collective-permute-start | bytes 196616 | tf_op jit(solution)/shard_map/ppermute | solution.py:197
  34.3 16.6 %collective-permute-start.25 = (bf16[256,2048]{1,0:T(8,128)(2,1)S(1)}, bf16[256,2048]{1,0:T(8,128)(2,1)S(1)}, u32[]{:S(2)}, u32[]{:S(2)}) collective-permute-start(bf16[256,2048]{1,0:T(8,128)(2,1)S(1)} %get-tuple-element.55.near), channel_id=1, source_target_pairs={{0,1},{1,0},{2,3},{3,2},{4,5},{5,4},{6,7},{7,6},{8,9},{9,8},{10,11... | collective-permute-start | bytes 3145736 | tf_op jit(solution)/shard_map/ppermute | solution.py:197
  37.1 5.1 %collective-permute-start.17 = (bf16[128,256]{1,0:T(8,128)(2,1)S(1)}, bf16[128,256]{1,0:T(8,128)(2,1)S(1)}, u32[]{:S(2)}, u32[]{:S(2)}) collective-permute-start(bf16[128,256]{1,0:T(8,128)(2,1)S(1)} %fusion.1), channel_id=1, source_target_pairs={{0,9},{1,8},{2,11},{3,10},{4,13},{5,12},{6,15},{7,14},{8,1},{9,0},... | collective-permute-start | bytes 196616 | tf_op jit(solution)/shard_map/ppermute | solution.py:197
  42.2 4.7 %collective-permute-start.20 = (bf16[128,256]{1,0:T(8,128)(2,1)S(1)}, bf16[128,256]{1,0:T(8,128)(2,1)S(1)}, u32[]{:S(2)}, u32[]{:S(2)}) collective-permute-start(bf16[128,256]{1,0:T(8,128)(2,1)S(1)} %fusion.c0), channel_id=1, source_target_pairs={{0,19},{1,18},{2,17},{3,16},{4,23},{5,22},{6,21},{7,20},{8,27},{9,... | collective-permute-start | bytes 196616 | tf_op jit(solution)/shard_map/ppermute | solution.py:204
  44.5 4.7 %collective-permute-start.19 = (bf16[128,256]{1,0:T(8,128)(2,1)S(1)}, bf16[128,256]{1,0:T(8,128)(2,1)S(1)}, u32[]{:S(2)}, u32[]{:S(2)}) collective-permute-start(bf16[128,256]{1,0:T(8,128)(2,1)S(1)} %fusion.c0), channel_id=1, source_target_pairs={{0,3},{1,2},{2,1},{3,0},{4,7},{5,6},{6,5},{7,4},{8,11},{9,10},{10,... | collective-permute-start | bytes 196616 | tf_op jit(solution)/shard_map/ppermute | solution.py:197
  45.0 4.6 %collective-permute-start.18 = (bf16[128,256]{1,0:T(8,128)(2,1)S(1)}, bf16[128,256]{1,0:T(8,128)(2,1)S(1)}, u32[]{:S(2)}, u32[]{:S(2)}) collective-permute-start(bf16[128,256]{1,0:T(8,128)(2,1)S(1)} %fusion.c0), channel_id=1, source_target_pairs={{0,16},{16,0},{1,17},{17,1},{2,18},{18,2},{3,19},{19,3},{4,20},{20... | collective-permute-start | bytes 196616 | tf_op jit(solution)/shard_map/ppermute | solution.py:200
  45.5 4.7 %collective-permute-start.21 = (bf16[128,256]{1,0:T(8,128)(2,1)S(1)}, bf16[128,256]{1,0:T(8,128)(2,1)S(1)}, u32[]{:S(2)}, u32[]{:S(2)}) collective-permute-start(bf16[128,256]{1,0:T(8,128)(2,1)S(1)} %fusion.c0), channel_id=1, source_target_pairs={{0,1},{1,0},{2,3},{3,2},{4,5},{5,4},{6,7},{7,6},{8,9},{9,8},{10,11... | collective-permute-start | bytes 196616 | tf_op jit(solution)/shard_map/ppermute | solution.py:197
  46.9 3.4 %collective-permute-start.24 = (bf16[128,256]{1,0:T(8,128)(2,1)S(1)}, bf16[128,256]{1,0:T(8,128)(2,1)S(1)}, u32[]{:S(2)}, u32[]{:S(2)}) collective-permute-start(bf16[128,256]{1,0:T(8,128)(2,1)S(1)} %collective-permute-done.20.x1), channel_id=1, source_target_pairs={{0,1},{1,0},{2,3},{3,2},{4,5},{5,4},{6,7},{7,6},{8,9},{9,8},{10,11... | collective-permute-start | bytes 196616 | tf_op jit(solution)/shard_map/ppermute | solution.py:197
  52.5 4.6 %collective-permute-start.28 = (f32[8,128]{1,0:T(8,128)S(1)}, f32[8,128]{1,0:T(8,128)S(1)}, u32[]{:S(2)}, u32[]{:S(2)}) collective-permute-start(f32[8,128]{1,0:T(8,128)S(1)} %get-tuple-element.57), channel_id=1, source_target_pairs={{0,6},{1,7},{2,4},{3,5},{4,2},{5,3},{6,0},{7,1},{8,14},{9,15},{10,... | collective-permute-start | bytes 12296 | tf_op jit(solution)/shard_map/ppermute | solution.py:197
  54.7 3.0 %collective-permute-start.26 = (f32[8,128]{1,0:T(8,128)S(1)}, f32[8,128]{1,0:T(8,128)S(1)}, u32[]{:S(2)}, u32[]{:S(2)}) collective-permute-start(f32[8,128]{1,0:T(8,128)S(1)} %get-tuple-element.57), channel_id=1, source_target_pairs={{0,3},{1,2},{2,1},{3,0},{4,7},{5,6},{6,5},{7,4},{8,11},{9,10},{10,... | collective-permute-start | bytes 12296 | tf_op jit(solution)/shard_map/ppermute | solution.py:197
  57.7 3.9 %collective-permute-start.29 = (f32[8,128]{1,0:T(8,128)S(1)}, f32[8,128]{1,0:T(8,128)S(1)}, u32[]{:S(2)}, u32[]{:S(2)}) collective-permute-start(f32[8,128]{1,0:T(8,128)S(1)} %add_add_fusion.1), channel_id=1, source_target_pairs={{0,9},{1,8},{2,11},{3,10},{4,13},{5,12},{6,15},{7,14},{8,1},{9,0},... | collective-permute-start | bytes 12296 | tf_op jit(solution)/shard_map/ppermute | solution.py:197
  62.0 3.7 %collective-permute-start.32 = (f32[1,1024]{1,0:T(1,128)S(1)}, f32[1,1024]{1,0:T(1,128)S(1)}, u32[]{:S(2)}, u32[]{:S(2)}) collective-permute-start(f32[1,1024]{1,0:T(1,128)S(1)} %shard_map.76.own), channel_id=1, source_target_pairs={{0,16},{16,0},{1,17},{17,1},{2,18},{18,2},{3,19},{19,3},{4,20},{20... | collective-permute-start | bytes 12296 | tf_op jit(solution)/shard_map/ppermute | solution.py:200
  66.6 4.6 %collective-permute-start.35 = (f32[8,128]{1,0:T(8,128)S(1)}, f32[8,128]{1,0:T(8,128)S(1)}, u32[]{:S(2)}, u32[]{:S(2)}) collective-permute-start(f32[8,128]{1,0:T(8,128)S(1)} %shard_map.77), channel_id=1, source_target_pairs={{0,6},{1,7},{2,4},{3,5},{4,2},{5,3},{6,0},{7,1},{8,14},{9,15},{10,... | collective-permute-start | bytes 12296 | tf_op jit(solution)/shard_map/ppermute | solution.py:197
  68.8 3.1 %collective-permute-start.34 = (f32[8,128]{1,0:T(8,128)S(1)}, f32[8,128]{1,0:T(8,128)S(1)}, u32[]{:S(2)}, u32[]{:S(2)}) collective-permute-start(f32[8,128]{1,0:T(8,128)S(1)} %shard_map.77), channel_id=1, source_target_pairs={{0,5},{1,4},{2,7},{3,6},{4,1},{5,0},{6,3},{7,2},{8,13},{9,12},{10,... | collective-permute-start | bytes 12296 | tf_op jit(solution)/shard_map/ppermute | solution.py:197
  68.8 3.1 %collective-permute-start.33 = (f32[8,128]{1,0:T(8,128)S(1)}, f32[8,128]{1,0:T(8,128)S(1)}, u32[]{:S(2)}, u32[]{:S(2)}) collective-permute-start(f32[8,128]{1,0:T(8,128)S(1)} %shard_map.77), channel_id=1, source_target_pairs={{0,3},{1,2},{2,1},{3,0},{4,7},{5,6},{6,5},{7,4},{8,11},{9,10},{10,... | collective-permute-start | bytes 12296 | tf_op jit(solution)/shard_map/ppermute | solution.py:197
  71.9 4.0 %collective-permute-start.36 = (f32[8,128]{1,0:T(8,128)S(1)}, f32[8,128]{1,0:T(8,128)S(1)}, u32[]{:S(2)}, u32[]{:S(2)}) collective-permute-start(f32[8,128]{1,0:T(8,128)S(1)} %add_add_fusion), channel_id=1, source_target_pairs={{0,9},{1,8},{2,11},{3,10},{4,13},{5,12},{6,15},{7,14},{8,1},{9,0},... | collective-permute-start | bytes 12296 | tf_op jit(solution)/shard_map/ppermute | solution.py:197
  76.5 3.6 %collective-permute-start.40 = (f32[1,1024]{1,0:T(1,128)S(1)}, f32[1,1024]{1,0:T(1,128)S(1)}, u32[]{:S(2)}, u32[]{:S(2)}) collective-permute-start(f32[1,1024]{1,0:T(1,128)S(1)} %get-tuple-element.61.own), channel_id=1, source_target_pairs={{0,16},{16,0},{1,17},{17,1},{2,18},{18,2},{3,19},{19,3},{4,20},{20... | collective-permute-start | bytes 12296 | tf_op jit(solution)/shard_map/ppermute | solution.py:200
  (15 other events, 34.7 us)

commit v7 on v6

--- a/solution.py
+++ b/solution.py
@@ -157,16 +157,24 @@
     sums[...] = jnp.sum(acc[...].T, axis=0, keepdims=True)
 
 
+def last_rows(target_count, block, totals, mass, sums, rows, packed, acc):
+    sweep_rows(target_count, block, totals, mass, sums, rows, acc)
+    count = rows.shape[0]
+    for j in range(sums.shape[1] // LANES):
+        packed[j : j + 1, :] = sums[:, j * LANES : (j + 1) * LANES]
+    packed[packed.shape[0] - count :, :] = rows[...]
+
+
 def chip_totals(own, core, both, x):
     count = own.shape[1] // 2
-    other = core[...] + both[...]
+    other = core + both
     other = jnp.concatenate([other[:, count:], other[:, :count]], axis=1)
-    return own[...] + x[...] + other
+    return own + x + other
 
 
 def sweep_cols(source_count, block, own, core, both, x, mass, mass_far, sums, acc, spread):
     masses = jnp.concatenate([mass[...], mass_far[...]], axis=1)
-    cols = masses / (chip_totals(own, core, both, x) / source_count)
+    cols = masses / (chip_totals(own[...], core[...], both[...], x[...]) / source_count)
     spread[...] = jnp.broadcast_to(cols, (LANES, block.shape[0])).T
     acc[...] = jnp.zeros_like(acc)
     for start in range(0, block.shape[0], 64):
@@ -177,11 +185,15 @@
     sums[...] = jnp.sum(acc[...], axis=1)
 
 
-def finish(source_count, rows_own, rows_far, own, core, both, x, mass, rows, cols):
+def finish(source_count, rows_own, own, core, both, x, mass, rows, cols):
     count, mine = rows_own.shape[0], half_index()
+    rest = core.shape[0] - count
     rows[pl.ds(pl.multiple_of(mine * count, count), count), :] = rows_own[...]
-    rows[pl.ds(pl.multiple_of((1 - mine) * count, count), count), :] = rows_far[...]
-    totals = chip_totals(own, core, both, x)[:, : cols.shape[1]]
+    rows[pl.ds(pl.multiple_of((1 - mine) * count, count), count), :] = core[rest:, :]
+    parts = [
+        jnp.concatenate([ref[j : j + 1, :] for j in range(rest)], axis=1) for ref in (core, both, x)
+    ]
+    totals = chip_totals(own[...], *parts)[:, : cols.shape[1]]
     cols[...] = mass[...] / (totals / source_count)
 
 
@@ -322,32 +334,45 @@
     for repeat in range(2):
         sums = sums + swap(sums, 3) + swap(sums, 5) + swap(sums, 6)
         sums = sums + swap(sums, 9)
-        shapes, scratch = ((wide, F32), (part, F32)), (((chip, LANES), F32),)
-        totals, *rows = call(
-            functools.partial(sweep_rows, target_count),
-            shapes[: 1 + repeat],
-            block,
-            sums,
-            mass,
-            scratch=scratch if repeat else shapes[1:] + scratch,
-        )
-        totals = (totals, swap(totals, 1), both(totals, 1), cross(totals))
+        scratch = (((chip, LANES), F32),)
         if repeat == 0:
+            (totals,) = call(
+                functools.partial(sweep_rows, target_count),
+                ((wide, F32),),
+                block,
+                sums,
+                mass,
+                scratch=((part, F32),) + scratch,
+            )
             (sums,) = call(
                 functools.partial(sweep_cols, source_count),
                 ((part, F32),),
                 block,
-                *totals,
+                totals,
+                swap(totals, 1),
+                both(totals, 1),
+                cross(totals),
                 target_mass,
                 target_mass_far,
                 scratch=(((part[0], 8, LANES), F32), ((chip, LANES), F32)),
             )
+        else:
+            totals, rows, packed = call(
+                functools.partial(last_rows, target_count),
+                ((wide, F32), (part, F32), ((chip // LANES + part[0], LANES), F32)),
+                block,
+                sums,
+                mass,
+                scratch=scratch,
+            )
     rows, cols = call(
         functools.partial(finish, source_count),
         ((tall, F32), (flat, F32)),
-        rows[0],
-        swap(rows[0], 1),
-        *totals,
+        rows,
+        totals,
+        swap(packed, 1),
+        both(packed, 1),
+        cross(packed),
         target_mass,
     )
     return (rows.reshape(-1), cols.reshape(-1))

time: 81.8 us -> 81.8 us (level)
    ppermute x32 -> x31, starting transfers between devices: 32 us -> 31.8 us  [swap(): return lax.ppermute(value, 'cols', [(i, i ^ bits) for i in range(n)])]
    ppermute x32 -> x31, waiting for transfers between devices: 19.5 us -> 19.5 us  [swap(): return lax.ppermute(value, 'cols', [(i, i ^ bits) for i in range(n)])]
  transfers between devices with their start and end apart: 41 -> 40, of which waited for: 23 -> 23; matrix products, arithmetic and copies ran while one was open for 0% -> 0% of each run, Pallas kernels for 5% -> 5%
where the time goes in v7:
time: 81.8 us; the launch traced here: 81.6 us
  starting transfers between devices  43.7 us (53%)
  waiting for transfers between devices  25.1 us (31%)
  Pallas kernels  7.85 us (10%)
  local copies, waits for them, and re-layouts  3.95 us (5%)
  between operations  0.82 us (1%)
    ppermute x31, starting transfers between devices, swap(): return lax.ppermute(value, 'cols', [(i, i ^ bits) for i in range(n)])  31.8 us
    ppermute x31, waiting for transfers between devices, swap(): return lax.ppermute(value, 'cols', [(i, i ^ bits) for i in range(n)])  19.5 us
    pallas_call x12, Pallas kernels, call(): pl.pallas_call(function, out_shape=outs, in_specs=[ANY if i in loose else...  7.85 us
    ppermute x5, starting transfers between devices, cross(): return lax.ppermute(value, 'rows', [(0, 1), (1, 0)])  6.35 us
    ppermute x4, starting transfers between devices, both(): return lax.ppermute(value, ('rows', 'cols'), pairs)  5.55 us
    ppermute x5, waiting for transfers between devices, cross(): return lax.ppermute(value, 'rows', [(0, 1), (1, 0)])  4.03 us
    unnamed x12, local copies, waits for them, and re-layouts  3.92 us
  transfers between devices with their start and end apart: 40, of which 23 were waited for; matrix products, arithmetic and copies ran while one was open for 0% of the time, Pallas kernels for 5%

profile of v7, /device:TPU:0, one launch (start us, length us, event | category | flops | bytes accessed | tf_op | source)
XLA Modules:
  0.0 81.6 jit_solution(7084921420989242727)
XLA Ops:
  1.1 2.6 %collective-permute-start = (bf16[512,256]{1,0:T(8,128)(2,1)}, bf16[512,256]{1,0:T(8,128)(2,1)S(1)}, u32[]{:S(2)}, u32[]{:S(2)}) collective-permute-start(bf16[512,256]{1,0:T(8,128)(2,1)} %near.3), channel_id=1, source_target_pairs={{0,16},{16,0},{1,17},{17,1},{2,18},{18,2},{3,19},{19,3},{4,20},{20... | collective-permute-start | bytes 786440 | tf_op jit(solution)/shard_map/ppermute | solution.py:212
  3.7 2.4 %collective-permute-start.3 = (bf16[32,2048]{1,0:T(8,128)(2,1)}, bf16[32,2048]{1,0:T(8,128)(2,1)S(1)}, u32[]{:S(2)}, u32[]{:S(2)}) collective-permute-start(bf16[32,2048]{1,0:T(8,128)(2,1)} %bitcast.5), channel_id=1, source_target_pairs={{0,9},{1,8},{2,11},{3,10},{4,13},{5,12},{6,15},{7,14},{8,1},{9,0},... | collective-permute-start | bytes 393224 | tf_op jit(solution)/shard_map/ppermute | solution.py:209
  6.1 1.5 %collective-permute-start.2 = (bf16[32,2048]{1,0:T(8,128)(2,1)}, bf16[32,2048]{1,0:T(8,128)(2,1)S(1)}, u32[]{:S(2)}, u32[]{:S(2)}) collective-permute-start(bf16[32,2048]{1,0:T(8,128)(2,1)} %bitcast.6), channel_id=1, source_target_pairs={{0,5},{1,4},{2,7},{3,6},{4,1},{5,0},{6,3},{7,2},{8,13},{9,12},{10,... | collective-permute-start | bytes 393224 | tf_op jit(solution)/shard_map/ppermute | solution.py:209
  7.6 1.3 %collective-permute-start.1 = (bf16[32,2048]{1,0:T(8,128)(2,1)}, bf16[32,2048]{1,0:T(8,128)(2,1)S(1)}, u32[]{:S(2)}, u32[]{:S(2)}) collective-permute-start(bf16[32,2048]{1,0:T(8,128)(2,1)} %bitcast.7), channel_id=1, source_target_pairs={{0,3},{1,2},{2,1},{3,0},{4,7},{5,6},{6,5},{7,4},{8,11},{9,10},{10,... | collective-permute-start | bytes 393224 | tf_op jit(solution)/shard_map/ppermute | solution.py:209
  8.9 1.6 %copy-done = bf16[2048,512]{1,0:T(8,128)(2,1)S(1)} copy-done((bf16[2048,512]{1,0:T(8,128)(2,1)S(1)}, bf16[2048,512]{1,0:T(8,128)(2,1)}, u32[]{:S(2)}) %copy-start) | copy-done | bytes 2097176
  13.9 1.4 %collective-permute-start.7 = (bf16[32,2048]{1,0:T(8,128)(2,1)S(1)}, bf16[32,2048]{1,0:T(8,128)(2,1)S(1)}, u32[]{:S(2)}, u32[]{:S(2)}) collective-permute-start(bf16[32,2048]{1,0:T(8,128)(2,1)S(1)} %collective-permute-done.3.refs_1_.p1), channel_id=1, source_target_pairs={{0,5},{1,4},{2,7},{3,6},{4,1},{5,0},{6,3},{7,2},{8,13},{9,12},{10,... | collective-permute-start | bytes 393224 | tf_op jit(solution)/shard_map/ppermute | solution.py:209
  15.5 1.5 %collective-permute-start.8 = (bf16[32,2048]{1,0:T(8,128)(2,1)S(1)}, bf16[32,2048]{1,0:T(8,128)(2,1)S(1)}, u32[]{:S(2)}, u32[]{:S(2)}) collective-permute-start(bf16[32,2048]{1,0:T(8,128)(2,1)S(1)} %collective-permute-done.3.refs_1_.p1), channel_id=1, source_target_pairs={{0,3},{1,2},{2,1},{3,0},{4,7},{5,6},{6,5},{7,4},{8,11},{9,10},{10,... | collective-permute-start | bytes 393224 | tf_op jit(solution)/shard_map/ppermute | solution.py:209
  17.3 1.4 %shard_map.70.upper = bf16[1024,512]{1,0:T(8,128)(2,1)S(1)} custom-call(bf16[2048,512]{1,0:T(8,128)(2,1)S(1)} %copy-done.1, bf16[2048,512]{1,0:T(8,128)(2,1)S(1)} %collective-permute-done.5.plan_far, bf16[512,512]{1,0:T(8,128)(2,1)S(1)} %shard_map.69.units.targets, bf16[512,512]{1,0:T(8,128)(2,1)S(1)} %collective-permute-done.4.units_far.targets_far), custom_call_target="tpu_custom_call" | custom-call | flops 1073741824 | bytes 6291456 | tf_op jit(solution)/shard_map/pallas_call | solution.py:221
  19.4 1.9 %collective-permute-start.9 = (bf16[32,2048]{1,0:T(8,128)(2,1)S(1)}, bf16[32,2048]{1,0:T(8,128)(2,1)S(1)}, u32[]{:S(2)}, u32[]{:S(2)}) collective-permute-start(bf16[32,2048]{1,0:T(8,128)(2,1)S(1)} %collective-permute-done.7.refs_3_.p3), channel_id=1, source_target_pairs={{0,3},{1,2},{2,1},{3,0},{4,7},{5,6},{6,5},{7,4},{8,11},{9,10},{10,... | collective-permute-start | bytes 393224 | tf_op jit(solution)/shard_map/ppermute | solution.py:209
  22.8 1.4 %shard_map.72.lower = bf16[1024,512]{1,0:T(8,128)(2,1)S(1)} custom-call(bf16[2048,512]{1,0:T(8,128)(2,1)S(1)} %copy-done.1, bf16[2048,512]{1,0:T(8,128)(2,1)S(1)} %collective-permute-done.5.plan_far, bf16[512,512]{1,0:T(8,128)(2,1)S(1)} %shard_map.69.units.targets, bf16[512,512]{1,0:T(8,128)(2,1)S(1)} %collective-permute-done.4.units_far.targets_far), custom_call_target="tpu_custom_call" | custom-call | flops 1073741824 | bytes 6291456 | tf_op jit(solution)/shard_map/pallas_call | solution.py:221
  24.2 1.6 %collective-permute-done.12.squares_y = f32[1,2048]{1,0:T(1,128)S(1)} collective-permute-done((f32[1,2048]{1,0:T(1,128)S(1)}, f32[1,2048]{1,0:T(1,128)S(1)}, u32[]{:S(2)}, u32[]{:S(2)}) %collective-permute-start.12) | collective-permute-done | bytes 8224 | tf_op jit(solution)/shard_map/ppermute | solution.py:209
  27.4 2.5 %collective-permute-start.15 = (bf16[128,256]{1,0:T(8,128)(2,1)S(1)}, bf16[128,256]{1,0:T(8,128)(2,1)S(1)}, u32[]{:S(2)}, u32[]{:S(2)}) collective-permute-start(bf16[128,256]{1,0:T(8,128)(2,1)S(1)} %get-tuple-element.53), channel_id=1, source_target_pairs={{0,19},{1,18},{2,17},{3,16},{4,23},{5,22},{6,21},{7,20},{8,27},{9,... | collective-permute-start | bytes 196616 | tf_op jit(solution)/shard_map/ppermute | solution.py:216
  30.9 2.0 %collective-permute-done.14 = bf16[128,256]{1,0:T(8,128)(2,1)S(1)} collective-permute-done((bf16[128,256]{1,0:T(8,128)(2,1)S(1)}, bf16[128,256]{1,0:T(8,128)(2,1)S(1)}, u32[]{:S(2)}, u32[]{:S(2)}) %collective-permute-start.14) | collective-permute-done | bytes 65568 | tf_op jit(solution)/shard_map/ppermute | solution.py:209
  32.9 1.4 %collective-permute-start.16 = (bf16[128,256]{1,0:T(8,128)(2,1)S(1)}, bf16[128,256]{1,0:T(8,128)(2,1)S(1)}, u32[]{:S(2)}, u32[]{:S(2)}) collective-permute-start(bf16[128,256]{1,0:T(8,128)(2,1)S(1)} %get-tuple-element.66), channel_id=1, source_target_pairs={{0,5},{1,4},{2,7},{3,6},{4,1},{5,0},{6,3},{7,2},{8,13},{9,12},{10,... | collective-permute-start | bytes 196616 | tf_op jit(solution)/shard_map/ppermute | solution.py:209
  34.7 2.4 %collective-permute-done.16 = bf16[128,256]{1,0:T(8,128)(2,1)S(1)} collective-permute-done((bf16[128,256]{1,0:T(8,128)(2,1)S(1)}, bf16[128,256]{1,0:T(8,128)(2,1)S(1)}, u32[]{:S(2)}, u32[]{:S(2)}) %collective-permute-start.16) | collective-permute-done | bytes 65568 | tf_op jit(solution)/shard_map/ppermute | solution.py:209
  37.1 1.9 %collective-permute-start.17 = (bf16[128,256]{1,0:T(8,128)(2,1)S(1)}, bf16[128,256]{1,0:T(8,128)(2,1)S(1)}, u32[]{:S(2)}, u32[]{:S(2)}) collective-permute-start(bf16[128,256]{1,0:T(8,128)(2,1)S(1)} %fusion.1), channel_id=1, source_target_pairs={{0,9},{1,8},{2,11},{3,10},{4,13},{5,12},{6,15},{7,14},{8,1},{9,0},... | collective-permute-start | bytes 196616 | tf_op jit(solution)/shard_map/ppermute | solution.py:209
  39.0 3.2 %collective-permute-done.17 = bf16[128,256]{1,0:T(8,128)(2,1)S(1)} collective-permute-done((bf16[128,256]{1,0:T(8,128)(2,1)S(1)}, bf16[128,256]{1,0:T(8,128)(2,1)S(1)}, u32[]{:S(2)}, u32[]{:S(2)}) %collective-permute-start.17) | collective-permute-done | bytes 65568 | tf_op jit(solution)/shard_map/ppermute | solution.py:209
  42.2 2.2 %collective-permute-start.20 = (bf16[128,256]{1,0:T(8,128)(2,1)S(1)}, bf16[128,256]{1,0:T(8,128)(2,1)S(1)}, u32[]{:S(2)}, u32[]{:S(2)}) collective-permute-start(bf16[128,256]{1,0:T(8,128)(2,1)S(1)} %fusion.c0), channel_id=1, source_target_pairs={{0,19},{1,18},{2,17},{3,16},{4,23},{5,22},{6,21},{7,20},{8,27},{9,... | collective-permute-start | bytes 196616 | tf_op jit(solution)/shard_map/ppermute | solution.py:216
  45.5 1.2 %collective-permute-start.21 = (bf16[128,256]{1,0:T(8,128)(2,1)S(1)}, bf16[128,256]{1,0:T(8,128)(2,1)S(1)}, u32[]{:S(2)}, u32[]{:S(2)}) collective-permute-start(bf16[128,256]{1,0:T(8,128)(2,1)S(1)} %fusion.c0), channel_id=1, source_target_pairs={{0,1},{1,0},{2,3},{3,2},{4,5},{5,4},{6,7},{7,6},{8,9},{9,8},{10,11... | collective-permute-start | bytes 196616 | tf_op jit(solution)/shard_map/ppermute | solution.py:209
  46.9 1.6 %collective-permute-start.24 = (bf16[128,256]{1,0:T(8,128)(2,1)S(1)}, bf16[128,256]{1,0:T(8,128)(2,1)S(1)}, u32[]{:S(2)}, u32[]{:S(2)}) collective-permute-start(bf16[128,256]{1,0:T(8,128)(2,1)S(1)} %collective-permute-done.20.x1), channel_id=1, source_target_pairs={{0,1},{1,0},{2,3},{3,2},{4,5},{5,4},{6,7},{7,6},{8,9},{9,8},{10,11... | collective-permute-start | bytes 196616 | tf_op jit(solution)/shard_map/ppermute | solution.py:209
  50.8 1.6 %shard_map.75 = (f32[1024,1024]{1,0:T(8,128)S(1)}, f32[8,128]{1,0:T(8,128)S(1)}) custom-call(bf16[1024,256]{1,0:T(8,128)(2,1)S(1)} %get-tuple-element.54.left, f32[8,128]{1,0:T(8,128)S(1)} %get-tuple-element.55.squares, bf16[512,512]{1,0:T(8,128)(2,1)S(1)} %shard_map.69.units.targets, bf16[512,512]{1,0:T(8,128)(2,1)S(1)} %collective-permute-done.4.units_far.targets_far, ...), custom_call_target="tpu_custom_call" | custom-call | flops 1342177280 | bytes 8134656 | tf_op jit(solution)/shard_map/pallas_call | solution.py:221
  52.5 1.6 %collective-permute-start.28 = (f32[8,128]{1,0:T(8,128)S(1)}, f32[8,128]{1,0:T(8,128)S(1)}, u32[]{:S(2)}, u32[]{:S(2)}) collective-permute-start(f32[8,128]{1,0:T(8,128)S(1)} %get-tuple-element.58), channel_id=1, source_target_pairs={{0,6},{1,7},{2,4},{3,5},{4,2},{5,3},{6,0},{7,1},{8,14},{9,15},{10,... | collective-permute-start | bytes 12296 | tf_op jit(solution)/shard_map/ppermute | solution.py:209
  55.7 1.3 %collective-permute-done.28 = f32[8,128]{1,0:T(8,128)S(1)} collective-permute-done((f32[8,128]{1,0:T(8,128)S(1)}, f32[8,128]{1,0:T(8,128)S(1)}, u32[]{:S(2)}, u32[]{:S(2)}) %collective-permute-start.28) | collective-permute-done | bytes 4128 | tf_op jit(solution)/shard_map/ppermute | solution.py:209
  57.7 2.4 %collective-permute-start.29 = (f32[8,128]{1,0:T(8,128)S(1)}, f32[8,128]{1,0:T(8,128)S(1)}, u32[]{:S(2)}, u32[]{:S(2)}) collective-permute-start(f32[8,128]{1,0:T(8,128)S(1)} %add_add_fusion.1), channel_id=1, source_target_pairs={{0,9},{1,8},{2,11},{3,10},{4,13},{5,12},{6,15},{7,14},{8,1},{9,0},... | collective-permute-start | bytes 12296 | tf_op jit(solution)/shard_map/ppermute | solution.py:209
  60.1 1.5 %collective-permute-done.29 = f32[8,128]{1,0:T(8,128)S(1)} collective-permute-done((f32[8,128]{1,0:T(8,128)S(1)}, f32[8,128]{1,0:T(8,128)S(1)}, u32[]{:S(2)}, u32[]{:S(2)}) %collective-permute-start.29) | collective-permute-done | bytes 4128 | tf_op jit(solution)/shard_map/ppermute | solution.py:209
  64.2 1.5 %collective-permute-done.32.x = f32[1,1024]{1,0:T(1,128)S(1)} collective-permute-done((f32[1,1024]{1,0:T(1,128)S(1)}, f32[1,1024]{1,0:T(1,128)S(1)}, u32[]{:S(2)}, u32[]{:S(2)}) %collective-permute-start.32) | collective-permute-done | bytes 4128 | tf_op jit(solution)/shard_map/ppermute | solution.py:212
  66.6 2.3 %collective-permute-start.35 = (f32[8,128]{1,0:T(8,128)S(1)}, f32[8,128]{1,0:T(8,128)S(1)}, u32[]{:S(2)}, u32[]{:S(2)}) collective-permute-start(f32[8,128]{1,0:T(8,128)S(1)} %shard_map.77), channel_id=1, source_target_pairs={{0,6},{1,7},{2,4},{3,5},{4,2},{5,3},{6,0},{7,1},{8,14},{9,15},{10,... | collective-permute-start | bytes 12296 | tf_op jit(solution)/shard_map/ppermute | solution.py:209
  69.8 1.3 %collective-permute-done.35 = f32[8,128]{1,0:T(8,128)S(1)} collective-permute-done((f32[8,128]{1,0:T(8,128)S(1)}, f32[8,128]{1,0:T(8,128)S(1)}, u32[]{:S(2)}, u32[]{:S(2)}) %collective-permute-start.35) | collective-permute-done | bytes 4128 | tf_op jit(solution)/shard_map/ppermute | solution.py:209
  71.9 2.7 %collective-permute-start.36 = (f32[8,128]{1,0:T(8,128)S(1)}, f32[8,128]{1,0:T(8,128)S(1)}, u32[]{:S(2)}, u32[]{:S(2)}) collective-permute-start(f32[8,128]{1,0:T(8,128)S(1)} %add_add_fusion), channel_id=1, source_target_pairs={{0,9},{1,8},{2,11},{3,10},{4,13},{5,12},{6,15},{7,14},{8,1},{9,0},... | collective-permute-start | bytes 12296 | tf_op jit(solution)/shard_map/ppermute | solution.py:209
  74.6 1.3 %collective-permute-done.36 = f32[8,128]{1,0:T(8,128)S(1)} collective-permute-done((f32[8,128]{1,0:T(8,128)S(1)}, f32[8,128]{1,0:T(8,128)S(1)}, u32[]{:S(2)}, u32[]{:S(2)}) %collective-permute-start.36) | collective-permute-done | bytes 4128 | tf_op jit(solution)/shard_map/ppermute | solution.py:209
  76.3 1.5 %collective-permute-start.39 = (f32[16,128]{1,0:T(8,128)S(1)}, f32[16,128]{1,0:T(8,128)S(1)}, u32[]{:S(2)}, u32[]{:S(2)}) collective-permute-start(f32[16,128]{1,0:T(8,128)S(1)} %get-tuple-element.63), channel_id=1, source_target_pairs={{0,16},{16,0},{1,17},{17,1},{2,18},{18,2},{3,19},{19,3},{4,20},{20... | collective-permute-start | bytes 24584 | tf_op jit(solution)/shard_map/ppermute | solution.py:212
  78.5 1.5 %collective-permute-done.39.x = f32[16,128]{1,0:T(8,128)S(1)} collective-permute-done((f32[16,128]{1,0:T(8,128)S(1)}, f32[16,128]{1,0:T(8,128)S(1)}, u32[]{:S(2)}, u32[]{:S(2)}) %collective-permute-start.39) | collective-permute-done | bytes 8224 | tf_op jit(solution)/shard_map/ppermute | solution.py:212
  (82 shorter events, 23.3 us)
Async XLA Ops:
  0.6 16.7 %collective-permute-start.5 = (bf16[2048,512]{1,0:T(8,128)(2,1)}, bf16[2048,512]{1,0:T(8,128)(2,1)S(1)}, u32[]{:S(2)}, u32[]{:S(2)}) collective-permute-start(bf16[2048,512]{1,0:T(8,128)(2,1)} %plan.5), channel_id=1, source_target_pairs={{0,1},{1,0},{2,3},{3,2},{4,5},{5,4},{6,7},{7,6},{8,9},{9,8},{10,11... | collective-permute-start | bytes 6291464 | tf_op jit(solution)/shard_map/ppermute | solution.py:209
  1.1 12.2 %collective-permute-start = (bf16[512,256]{1,0:T(8,128)(2,1)}, bf16[512,256]{1,0:T(8,128)(2,1)S(1)}, u32[]{:S(2)}, u32[]{:S(2)}) collective-permute-start(bf16[512,256]{1,0:T(8,128)(2,1)} %near.3), channel_id=1, source_target_pairs={{0,16},{16,0},{1,17},{17,1},{2,18},{18,2},{3,19},{19,3},{4,20},{20... | collective-permute-start | bytes 786440 | tf_op jit(solution)/shard_map/ppermute | solution.py:212
  3.7 9.6 %collective-permute-start.3 = (bf16[32,2048]{1,0:T(8,128)(2,1)}, bf16[32,2048]{1,0:T(8,128)(2,1)S(1)}, u32[]{:S(2)}, u32[]{:S(2)}) collective-permute-start(bf16[32,2048]{1,0:T(8,128)(2,1)} %bitcast.5), channel_id=1, source_target_pairs={{0,9},{1,8},{2,11},{3,10},{4,13},{5,12},{6,15},{7,14},{8,1},{9,0},... | collective-permute-start | bytes 393224 | tf_op jit(solution)/shard_map/ppermute | solution.py:209
  6.1 7.2 %collective-permute-start.2 = (bf16[32,2048]{1,0:T(8,128)(2,1)}, bf16[32,2048]{1,0:T(8,128)(2,1)S(1)}, u32[]{:S(2)}, u32[]{:S(2)}) collective-permute-start(bf16[32,2048]{1,0:T(8,128)(2,1)} %bitcast.6), channel_id=1, source_target_pairs={{0,5},{1,4},{2,7},{3,6},{4,1},{5,0},{6,3},{7,2},{8,13},{9,12},{10,... | collective-permute-start | bytes 393224 | tf_op jit(solution)/shard_map/ppermute | solution.py:209
  7.6 5.8 %collective-permute-start.1 = (bf16[32,2048]{1,0:T(8,128)(2,1)}, bf16[32,2048]{1,0:T(8,128)(2,1)S(1)}, u32[]{:S(2)}, u32[]{:S(2)}) collective-permute-start(bf16[32,2048]{1,0:T(8,128)(2,1)} %bitcast.7), channel_id=1, source_target_pairs={{0,3},{1,2},{2,1},{3,0},{4,7},{5,6},{6,5},{7,4},{8,11},{9,10},{10,... | collective-permute-start | bytes 393224 | tf_op jit(solution)/shard_map/ppermute | solution.py:209
  13.6 3.4 %collective-permute-start.4 = (bf16[512,512]{1,0:T(8,128)(2,1)S(1)}, bf16[512,512]{1,0:T(8,128)(2,1)S(1)}, u32[]{:S(2)}, u32[]{:S(2)}) collective-permute-start(bf16[512,512]{1,0:T(8,128)(2,1)S(1)} %shard_map.69.units.targets), channel_id=1, source_target_pairs={{0,1},{1,0},{2,3},{3,2},{4,5},{5,4},{6,7},{7,6},{8,9},{9,8},{10,11... | collective-permute-start | bytes 1572872 | tf_op jit(solution)/shard_map/ppermute | solution.py:209
  13.9 5.4 %collective-permute-start.7 = (bf16[32,2048]{1,0:T(8,128)(2,1)S(1)}, bf16[32,2048]{1,0:T(8,128)(2,1)S(1)}, u32[]{:S(2)}, u32[]{:S(2)}) collective-permute-start(bf16[32,2048]{1,0:T(8,128)(2,1)S(1)} %collective-permute-done.3.refs_1_.p1), channel_id=1, source_target_pairs={{0,5},{1,4},{2,7},{3,6},{4,1},{5,0},{6,3},{7,2},{8,13},{9,12},{10,... | collective-permute-start | bytes 393224 | tf_op jit(solution)/shard_map/ppermute | solution.py:209
  15.4 3.4 %collective-permute-start.6 = (f32[1,512]{1,0:T(1,128)S(1)}, f32[1,512]{1,0:T(1,128)S(1)}, u32[]{:S(2)}, u32[]{:S(2)}) collective-permute-start(f32[1,512]{1,0:T(1,128)S(1)} %get-tuple-element.40.mass), channel_id=1, source_target_pairs={{0,1},{1,0},{2,3},{3,2},{4,5},{5,4},{6,7},{7,6},{8,9},{9,8},{10,11... | collective-permute-start | bytes 6152 | tf_op jit(solution)/shard_map/ppermute | solution.py:209
  15.5 6.0 %collective-permute-start.8 = (bf16[32,2048]{1,0:T(8,128)(2,1)S(1)}, bf16[32,2048]{1,0:T(8,128)(2,1)S(1)}, u32[]{:S(2)}, u32[]{:S(2)}) collective-permute-start(bf16[32,2048]{1,0:T(8,128)(2,1)S(1)} %collective-permute-done.3.refs_1_.p1), channel_id=1, source_target_pairs={{0,3},{1,2},{2,1},{3,0},{4,7},{5,6},{6,5},{7,4},{8,11},{9,10},{10,... | collective-permute-start | bytes 393224 | tf_op jit(solution)/shard_map/ppermute | solution.py:209
  17.0 7.2 %collective-permute-start.10 = (bf16[32,2048]{1,0:T(8,128)(2,1)S(1)}, bf16[32,2048]{1,0:T(8,128)(2,1)S(1)}, u32[]{:S(2)}, u32[]{:S(2)}) collective-permute-start(bf16[32,2048]{1,0:T(8,128)(2,1)S(1)} %collective-permute-done.1.p4), channel_id=1, source_target_pairs={{0,5},{1,4},{2,7},{3,6},{4,1},{5,0},{6,3},{7,2},{8,13},{9,12},{10,... | collective-permute-start | bytes 393224 | tf_op jit(solution)/shard_map/ppermute | solution.py:209
  19.4 6.5 %collective-permute-start.9 = (bf16[32,2048]{1,0:T(8,128)(2,1)S(1)}, bf16[32,2048]{1,0:T(8,128)(2,1)S(1)}, u32[]{:S(2)}, u32[]{:S(2)}) collective-permute-start(bf16[32,2048]{1,0:T(8,128)(2,1)S(1)} %collective-permute-done.7.refs_3_.p3), channel_id=1, source_target_pairs={{0,3},{1,2},{2,1},{3,0},{4,7},{5,6},{6,5},{7,4},{8,11},{9,10},{10,... | collective-permute-start | bytes 393224 | tf_op jit(solution)/shard_map/ppermute | solution.py:209
  22.7 3.1 %collective-permute-start.12 = (f32[1,2048]{1,0:T(1,128)S(1)}, f32[1,2048]{1,0:T(1,128)S(1)}, u32[]{:S(2)}, u32[]{:S(2)}) collective-permute-start(f32[1,2048]{1,0:T(1,128)S(1)} %add.42.squares), channel_id=1, source_target_pairs={{0,3},{1,2},{2,1},{3,0},{4,7},{5,6},{6,5},{7,4},{8,11},{9,10},{10,... | collective-permute-start | bytes 24584 | tf_op jit(solution)/shard_map/ppermute | solution.py:209
  26.6 4.3 %collective-permute-start.13 = (bf16[128,256]{1,0:T(8,128)(2,1)S(1)}, bf16[128,256]{1,0:T(8,128)(2,1)S(1)}, u32[]{:S(2)}, u32[]{:S(2)}) collective-permute-start(bf16[128,256]{1,0:T(8,128)(2,1)S(1)} %get-tuple-element.51), channel_id=1, source_target_pairs={{0,16},{16,0},{1,17},{17,1},{2,18},{18,2},{3,19},{19,3},{4,20},{20... | collective-permute-start | bytes 196616 | tf_op jit(solution)/shard_map/ppermute | solution.py:212
  27.2 5.7 %collective-permute-start.14 = (bf16[128,256]{1,0:T(8,128)(2,1)S(1)}, bf16[128,256]{1,0:T(8,128)(2,1)S(1)}, u32[]{:S(2)}, u32[]{:S(2)}) collective-permute-start(bf16[128,256]{1,0:T(8,128)(2,1)S(1)} %get-tuple-element.52), channel_id=1, source_target_pairs={{0,3},{1,2},{2,1},{3,0},{4,7},{5,6},{6,5},{7,4},{8,11},{9,10},{10,... | collective-permute-start | bytes 196616 | tf_op jit(solution)/shard_map/ppermute | solution.py:209
  27.4 5.5 %collective-permute-start.15 = (bf16[128,256]{1,0:T(8,128)(2,1)S(1)}, bf16[128,256]{1,0:T(8,128)(2,1)S(1)}, u32[]{:S(2)}, u32[]{:S(2)}) collective-permute-start(bf16[128,256]{1,0:T(8,128)(2,1)S(1)} %get-tuple-element.53), channel_id=1, source_target_pairs={{0,19},{1,18},{2,17},{3,16},{4,23},{5,22},{6,21},{7,20},{8,27},{9,... | collective-permute-start | bytes 196616 | tf_op jit(solution)/shard_map/ppermute | solution.py:216
  32.9 4.2 %collective-permute-start.16 = (bf16[128,256]{1,0:T(8,128)(2,1)S(1)}, bf16[128,256]{1,0:T(8,128)(2,1)S(1)}, u32[]{:S(2)}, u32[]{:S(2)}) collective-permute-start(bf16[128,256]{1,0:T(8,128)(2,1)S(1)} %get-tuple-element.66), channel_id=1, source_target_pairs={{0,5},{1,4},{2,7},{3,6},{4,1},{5,0},{6,3},{7,2},{8,13},{9,12},{10,... | collective-permute-start | bytes 196616 | tf_op jit(solution)/shard_map/ppermute | solution.py:209
  34.3 16.6 %collective-permute-start.25 = (bf16[256,2048]{1,0:T(8,128)(2,1)S(1)}, bf16[256,2048]{1,0:T(8,128)(2,1)S(1)}, u32[]{:S(2)}, u32[]{:S(2)}) collective-permute-start(bf16[256,2048]{1,0:T(8,128)(2,1)S(1)} %get-tuple-element.56.near), channel_id=1, source_target_pairs={{0,1},{1,0},{2,3},{3,2},{4,5},{5,4},{6,7},{7,6},{8,9},{9,8},{10,11... | collective-permute-start | bytes 3145736 | tf_op jit(solution)/shard_map/ppermute | solution.py:209
  37.1 5.1 %collective-permute-start.17 = (bf16[128,256]{1,0:T(8,128)(2,1)S(1)}, bf16[128,256]{1,0:T(8,128)(2,1)S(1)}, u32[]{:S(2)}, u32[]{:S(2)}) collective-permute-start(bf16[128,256]{1,0:T(8,128)(2,1)S(1)} %fusion.1), channel_id=1, source_target_pairs={{0,9},{1,8},{2,11},{3,10},{4,13},{5,12},{6,15},{7,14},{8,1},{9,0},... | collective-permute-start | bytes 196616 | tf_op jit(solution)/shard_map/ppermute | solution.py:209
  42.2 4.7 %collective-permute-start.20 = (bf16[128,256]{1,0:T(8,128)(2,1)S(1)}, bf16[128,256]{1,0:T(8,128)(2,1)S(1)}, u32[]{:S(2)}, u32[]{:S(2)}) collective-permute-start(bf16[128,256]{1,0:T(8,128)(2,1)S(1)} %fusion.c0), channel_id=1, source_target_pairs={{0,19},{1,18},{2,17},{3,16},{4,23},{5,22},{6,21},{7,20},{8,27},{9,... | collective-permute-start | bytes 196616 | tf_op jit(solution)/shard_map/ppermute | solution.py:216
  44.5 4.7 %collective-permute-start.19 = (bf16[128,256]{1,0:T(8,128)(2,1)S(1)}, bf16[128,256]{1,0:T(8,128)(2,1)S(1)}, u32[]{:S(2)}, u32[]{:S(2)}) collective-permute-start(bf16[128,256]{1,0:T(8,128)(2,1)S(1)} %fusion.c0), channel_id=1, source_target_pairs={{0,3},{1,2},{2,1},{3,0},{4,7},{5,6},{6,5},{7,4},{8,11},{9,10},{10,... | collective-permute-start | bytes 196616 | tf_op jit(solution)/shard_map/ppermute | solution.py:209
  45.0 4.6 %collective-permute-start.18 = (bf16[128,256]{1,0:T(8,128)(2,1)S(1)}, bf16[128,256]{1,0:T(8,128)(2,1)S(1)}, u32[]{:S(2)}, u32[]{:S(2)}) collective-permute-start(bf16[128,256]{1,0:T(8,128)(2,1)S(1)} %fusion.c0), channel_id=1, source_target_pairs={{0,16},{16,0},{1,17},{17,1},{2,18},{18,2},{3,19},{19,3},{4,20},{20... | collective-permute-start | bytes 196616 | tf_op jit(solution)/shard_map/ppermute | solution.py:212
  45.5 4.7 %collective-permute-start.21 = (bf16[128,256]{1,0:T(8,128)(2,1)S(1)}, bf16[128,256]{1,0:T(8,128)(2,1)S(1)}, u32[]{:S(2)}, u32[]{:S(2)}) collective-permute-start(bf16[128,256]{1,0:T(8,128)(2,1)S(1)} %fusion.c0), channel_id=1, source_target_pairs={{0,1},{1,0},{2,3},{3,2},{4,5},{5,4},{6,7},{7,6},{8,9},{9,8},{10,11... | collective-permute-start | bytes 196616 | tf_op jit(solution)/shard_map/ppermute | solution.py:209
  46.9 3.4 %collective-permute-start.24 = (bf16[128,256]{1,0:T(8,128)(2,1)S(1)}, bf16[128,256]{1,0:T(8,128)(2,1)S(1)}, u32[]{:S(2)}, u32[]{:S(2)}) collective-permute-start(bf16[128,256]{1,0:T(8,128)(2,1)S(1)} %collective-permute-done.20.x1), channel_id=1, source_target_pairs={{0,1},{1,0},{2,3},{3,2},{4,5},{5,4},{6,7},{7,6},{8,9},{9,8},{10,11... | collective-permute-start | bytes 196616 | tf_op jit(solution)/shard_map/ppermute | solution.py:209
  52.5 4.6 %collective-permute-start.28 = (f32[8,128]{1,0:T(8,128)S(1)}, f32[8,128]{1,0:T(8,128)S(1)}, u32[]{:S(2)}, u32[]{:S(2)}) collective-permute-start(f32[8,128]{1,0:T(8,128)S(1)} %get-tuple-element.58), channel_id=1, source_target_pairs={{0,6},{1,7},{2,4},{3,5},{4,2},{5,3},{6,0},{7,1},{8,14},{9,15},{10,... | collective-permute-start | bytes 12296 | tf_op jit(solution)/shard_map/ppermute | solution.py:209
  57.7 3.9 %collective-permute-start.29 = (f32[8,128]{1,0:T(8,128)S(1)}, f32[8,128]{1,0:T(8,128)S(1)}, u32[]{:S(2)}, u32[]{:S(2)}) collective-permute-start(f32[8,128]{1,0:T(8,128)S(1)} %add_add_fusion.1), channel_id=1, source_target_pairs={{0,9},{1,8},{2,11},{3,10},{4,13},{5,12},{6,15},{7,14},{8,1},{9,0},... | collective-permute-start | bytes 12296 | tf_op jit(solution)/shard_map/ppermute | solution.py:209
  62.0 3.7 %collective-permute-start.32 = (f32[1,1024]{1,0:T(1,128)S(1)}, f32[1,1024]{1,0:T(1,128)S(1)}, u32[]{:S(2)}, u32[]{:S(2)}) collective-permute-start(f32[1,1024]{1,0:T(1,128)S(1)} %shard_map.76.own), channel_id=1, source_target_pairs={{0,16},{16,0},{1,17},{17,1},{2,18},{18,2},{3,19},{19,3},{4,20},{20... | collective-permute-start | bytes 12296 | tf_op jit(solution)/shard_map/ppermute | solution.py:212
  66.6 4.6 %collective-permute-start.35 = (f32[8,128]{1,0:T(8,128)S(1)}, f32[8,128]{1,0:T(8,128)S(1)}, u32[]{:S(2)}, u32[]{:S(2)}) collective-permute-start(f32[8,128]{1,0:T(8,128)S(1)} %shard_map.77), channel_id=1, source_target_pairs={{0,6},{1,7},{2,4},{3,5},{4,2},{5,3},{6,0},{7,1},{8,14},{9,15},{10,... | collective-permute-start | bytes 12296 | tf_op jit(solution)/shard_map/ppermute | solution.py:209
  68.8 3.1 %collective-permute-start.34 = (f32[8,128]{1,0:T(8,128)S(1)}, f32[8,128]{1,0:T(8,128)S(1)}, u32[]{:S(2)}, u32[]{:S(2)}) collective-permute-start(f32[8,128]{1,0:T(8,128)S(1)} %shard_map.77), channel_id=1, source_target_pairs={{0,5},{1,4},{2,7},{3,6},{4,1},{5,0},{6,3},{7,2},{8,13},{9,12},{10,... | collective-permute-start | bytes 12296 | tf_op jit(solution)/shard_map/ppermute | solution.py:209
  71.9 4.0 %collective-permute-start.36 = (f32[8,128]{1,0:T(8,128)S(1)}, f32[8,128]{1,0:T(8,128)S(1)}, u32[]{:S(2)}, u32[]{:S(2)}) collective-permute-start(f32[8,128]{1,0:T(8,128)S(1)} %add_add_fusion), channel_id=1, source_target_pairs={{0,9},{1,8},{2,11},{3,10},{4,13},{5,12},{6,15},{7,14},{8,1},{9,0},... | collective-permute-start | bytes 12296 | tf_op jit(solution)/shard_map/ppermute | solution.py:209
  76.3 3.7 %collective-permute-start.39 = (f32[16,128]{1,0:T(8,128)S(1)}, f32[16,128]{1,0:T(8,128)S(1)}, u32[]{:S(2)}, u32[]{:S(2)}) collective-permute-start(f32[16,128]{1,0:T(8,128)S(1)} %get-tuple-element.63), channel_id=1, source_target_pairs={{0,16},{16,0},{1,17},{17,1},{2,18},{18,2},{3,19},{19,3},{4,20},{20... | collective-permute-start | bytes 24584 | tf_op jit(solution)/shard_map/ppermute | solution.py:212
  77.8 3.2 %collective-permute-start.38 = (f32[16,128]{1,0:T(8,128)S(1)}, f32[16,128]{1,0:T(8,128)S(1)}, u32[]{:S(2)}, u32[]{:S(2)}) collective-permute-start(f32[16,128]{1,0:T(8,128)S(1)} %get-tuple-element.63), channel_id=1, source_target_pairs={{0,17},{1,16},{2,19},{3,18},{4,21},{5,20},{6,23},{7,22},{8,25},{9,... | collective-permute-start | bytes 24584 | tf_op jit(solution)/shard_map/ppermute | solution.py:216
  77.9 3.1 %collective-permute-start.37 = (f32[16,128]{1,0:T(8,128)S(1)}, f32[16,128]{1,0:T(8,128)S(1)}, u32[]{:S(2)}, u32[]{:S(2)}) collective-permute-start(f32[16,128]{1,0:T(8,128)S(1)} %get-tuple-element.63), channel_id=1, source_target_pairs={{0,1},{1,0},{2,3},{3,2},{4,5},{5,4},{6,7},{7,6},{8,9},{9,8},{10,11... | collective-permute-start | bytes 24584 | tf_op jit(solution)/shard_map/ppermute | solution.py:209
  (14 other events, 32.6 us)

commit v8 on v7

--- a/solution.py
+++ b/solution.py
@@ -93,20 +93,33 @@
 
 def couple(
     p0, p1, p2, p3, p4, p5, p6, p7, squares, squares_y, upper, lower,
-    keep, to_x, to_y, to_xy, units,
+    to_x, to_y, to_xy, units,
 ):
     inverse = lax.rsqrt(squares[...] + squares_y[...] + 1e-06)
     rows = p0.shape[0]
     for i, piece in enumerate((p0, p1, p2, p3, p4, p5, p6, p7)):
         units[i * rows : (i + 1) * rows, :] = (piece[...].astype(F32) * inverse).astype(BF16)
+    half, split = to_x.shape
+    part = upper.shape[0]
+    for rows, cols, out in (
+        (slice(half, None), slice(None), None),
+        (slice(0, half), slice(split, None), to_x),
+    ):
+        product = jnp.dot(units[rows, :part], upper[:, cols], preferred_element_type=F32)
+        product += jnp.dot(units[rows, part:], lower[:, cols], preferred_element_type=F32)
+        if out is None:
+            to_y[...] = product[:, :split].astype(BF16)
+            to_xy[...] = product[:, split:].astype(BF16)
+        else:
+            out[...] = product.astype(BF16)
+
+
+def couple_own(units, upper, lower, keep):
     half, split = keep.shape
     part = upper.shape[0]
-    product = jnp.dot(units[:, :part], upper[...], preferred_element_type=F32)
-    product += jnp.dot(units[:, part:], lower[...], preferred_element_type=F32)
-    keep[...] = product[:half, :split]
-    to_x[...] = product[:half, split:].astype(BF16)
-    to_y[...] = product[half:, :split].astype(BF16)
-    to_xy[...] = product[half:, split:].astype(BF16)
+    product = jnp.dot(units[:half, :part], upper[:, :split], preferred_element_type=F32)
+    product += jnp.dot(units[:half, part:], lower[:, :split], preferred_element_type=F32)
+    keep[...] = product
 
 
 def left_part(targets, targets_far, c0, x0, c1, x1, left, squares, whole):
@@ -285,15 +298,18 @@
     yz3, yz1, squares_y, lower = hold((yz3, yz1, squares_y, lower))
     pieces = [own, z2, z1, z3, y0, yz2, yz1, yz3]
     quarter = ((half, split), BF16)
-    coupling, to_x, to_y, to_xy, xs = call(
+    to_x, to_y, to_xy, xs = call(
         couple,
-        (((half, split), F32), quarter, quarter, quarter, ((split, sources), BF16)),
+        (quarter, quarter, quarter, ((split, sources), BF16)),
         *pieces,
         squares,
         squares_y,
         upper,
         lower,
         flops=2 * sources * split * features,
+    )
+    (coupling,) = call(
+        couple_own, (((half, split), F32),), xs, upper, lower, flops=2 * sources * half * split
     )
     xs_far = swap(xs, 1)
 

time: 81.8 us -> 81.7 us (level)
    pallas_call x12 -> x13, Pallas kernels: 7.85 us -> 8.04 us  [call(): pl.pallas_call(function, out_shape=outs, in_specs=[ANY if i in loose else...]
where the time goes in v8:
time: 81.7 us; the launch traced here: 81.5 us
  starting transfers between devices  43.8 us (54%)
  waiting for transfers between devices  24.8 us (30%)
  Pallas kernels  8.04 us (10%)
  local copies, waits for them, and re-layouts  3.95 us (5%)
  between operations  0.82 us (1%)
    ppermute x31, starting transfers between devices, swap(): return lax.ppermute(value, 'cols', [(i, i ^ bits) for i in range(n)])  31.9 us
    ppermute x31, waiting for transfers between devices, swap(): return lax.ppermute(value, 'cols', [(i, i ^ bits) for i in range(n)])  19.5 us
    pallas_call x13, Pallas kernels, call(): pl.pallas_call(function, out_shape=outs, in_specs=[ANY if i in loose else...  8.04 us
    ppermute x5, starting transfers between devices, cross(): return lax.ppermute(value, 'rows', [(0, 1), (1, 0)])  6.34 us
    ppermute x4, starting transfers between devices, both(): return lax.ppermute(value, ('rows', 'cols'), pairs)  5.55 us
    unnamed x12, local copies, waits for them, and re-layouts  3.92 us
    ppermute x5, waiting for transfers between devices, cross(): return lax.ppermute(value, 'rows', [(0, 1), (1, 0)])  3.72 us
  transfers between devices with their start and end apart: 40, of which 23 were waited for; matrix products, arithmetic and copies ran while one was open for 0% of the time, Pallas kernels for 5%

profile of v8, /device:TPU:0, one launch (start us, length us, event | category | flops | bytes accessed | tf_op | source)
XLA Modules:
  0.0 81.5 jit_solution(15449381402364382434)
XLA Ops:
  1.1 2.6 %collective-permute-start = (bf16[512,256]{1,0:T(8,128)(2,1)}, bf16[512,256]{1,0:T(8,128)(2,1)S(1)}, u32[]{:S(2)}, u32[]{:S(2)}) collective-permute-start(bf16[512,256]{1,0:T(8,128)(2,1)} %near.3), channel_id=1, source_target_pairs={{0,16},{16,0},{1,17},{17,1},{2,18},{18,2},{3,19},{19,3},{4,20},{20... | collective-permute-start | bytes 786440 | tf_op jit(solution)/shard_map/ppermute | solution.py:225
  3.7 2.4 %collective-permute-start.3 = (bf16[32,2048]{1,0:T(8,128)(2,1)}, bf16[32,2048]{1,0:T(8,128)(2,1)S(1)}, u32[]{:S(2)}, u32[]{:S(2)}) collective-permute-start(bf16[32,2048]{1,0:T(8,128)(2,1)} %bitcast.5), channel_id=1, source_target_pairs={{0,9},{1,8},{2,11},{3,10},{4,13},{5,12},{6,15},{7,14},{8,1},{9,0},... | collective-permute-start | bytes 393224 | tf_op jit(solution)/shard_map/ppermute | solution.py:222
  6.1 1.5 %collective-permute-start.2 = (bf16[32,2048]{1,0:T(8,128)(2,1)}, bf16[32,2048]{1,0:T(8,128)(2,1)S(1)}, u32[]{:S(2)}, u32[]{:S(2)}) collective-permute-start(bf16[32,2048]{1,0:T(8,128)(2,1)} %bitcast.6), channel_id=1, source_target_pairs={{0,5},{1,4},{2,7},{3,6},{4,1},{5,0},{6,3},{7,2},{8,13},{9,12},{10,... | collective-permute-start | bytes 393224 | tf_op jit(solution)/shard_map/ppermute | solution.py:222
  7.6 1.3 %collective-permute-start.1 = (bf16[32,2048]{1,0:T(8,128)(2,1)}, bf16[32,2048]{1,0:T(8,128)(2,1)S(1)}, u32[]{:S(2)}, u32[]{:S(2)}) collective-permute-start(bf16[32,2048]{1,0:T(8,128)(2,1)} %bitcast.7), channel_id=1, source_target_pairs={{0,3},{1,2},{2,1},{3,0},{4,7},{5,6},{6,5},{7,4},{8,11},{9,10},{10,... | collective-permute-start | bytes 393224 | tf_op jit(solution)/shard_map/ppermute | solution.py:222
  8.9 1.6 %copy-done = bf16[2048,512]{1,0:T(8,128)(2,1)S(1)} copy-done((bf16[2048,512]{1,0:T(8,128)(2,1)S(1)}, bf16[2048,512]{1,0:T(8,128)(2,1)}, u32[]{:S(2)}) %copy-start) | copy-done | bytes 2097176
  13.9 1.4 %collective-permute-start.7 = (bf16[32,2048]{1,0:T(8,128)(2,1)S(1)}, bf16[32,2048]{1,0:T(8,128)(2,1)S(1)}, u32[]{:S(2)}, u32[]{:S(2)}) collective-permute-start(bf16[32,2048]{1,0:T(8,128)(2,1)S(1)} %collective-permute-done.3.refs_1_.p1), channel_id=1, source_target_pairs={{0,5},{1,4},{2,7},{3,6},{4,1},{5,0},{6,3},{7,2},{8,13},{9,12},{10,... | collective-permute-start | bytes 393224 | tf_op jit(solution)/shard_map/ppermute | solution.py:222
  15.5 1.5 %collective-permute-start.8 = (bf16[32,2048]{1,0:T(8,128)(2,1)S(1)}, bf16[32,2048]{1,0:T(8,128)(2,1)S(1)}, u32[]{:S(2)}, u32[]{:S(2)}) collective-permute-start(bf16[32,2048]{1,0:T(8,128)(2,1)S(1)} %collective-permute-done.3.refs_1_.p1), channel_id=1, source_target_pairs={{0,3},{1,2},{2,1},{3,0},{4,7},{5,6},{6,5},{7,4},{8,11},{9,10},{10,... | collective-permute-start | bytes 393224 | tf_op jit(solution)/shard_map/ppermute | solution.py:222
  17.3 1.4 %shard_map.70.upper = bf16[1024,512]{1,0:T(8,128)(2,1)S(1)} custom-call(bf16[2048,512]{1,0:T(8,128)(2,1)S(1)} %copy-done.1, bf16[2048,512]{1,0:T(8,128)(2,1)S(1)} %collective-permute-done.5.plan_far, bf16[512,512]{1,0:T(8,128)(2,1)S(1)} %shard_map.69.units.targets, bf16[512,512]{1,0:T(8,128)(2,1)S(1)} %collective-permute-done.4.units_far.targets_far), custom_call_target="tpu_custom_call" | custom-call | flops 1073741824 | bytes 6291456 | tf_op jit(solution)/shard_map/pallas_call | solution.py:234
  19.4 1.9 %collective-permute-start.9 = (bf16[32,2048]{1,0:T(8,128)(2,1)S(1)}, bf16[32,2048]{1,0:T(8,128)(2,1)S(1)}, u32[]{:S(2)}, u32[]{:S(2)}) collective-permute-start(bf16[32,2048]{1,0:T(8,128)(2,1)S(1)} %collective-permute-done.7.refs_3_.p3), channel_id=1, source_target_pairs={{0,3},{1,2},{2,1},{3,0},{4,7},{5,6},{6,5},{7,4},{8,11},{9,10},{10,... | collective-permute-start | bytes 393224 | tf_op jit(solution)/shard_map/ppermute | solution.py:222
  22.8 1.4 %shard_map.72.lower = bf16[1024,512]{1,0:T(8,128)(2,1)S(1)} custom-call(bf16[2048,512]{1,0:T(8,128)(2,1)S(1)} %copy-done.1, bf16[2048,512]{1,0:T(8,128)(2,1)S(1)} %collective-permute-done.5.plan_far, bf16[512,512]{1,0:T(8,128)(2,1)S(1)} %shard_map.69.units.targets, bf16[512,512]{1,0:T(8,128)(2,1)S(1)} %collective-permute-done.4.units_far.targets_far), custom_call_target="tpu_custom_call" | custom-call | flops 1073741824 | bytes 6291456 | tf_op jit(solution)/shard_map/pallas_call | solution.py:234
  24.2 1.6 %collective-permute-done.12.squares_y = f32[1,2048]{1,0:T(1,128)S(1)} collective-permute-done((f32[1,2048]{1,0:T(1,128)S(1)}, f32[1,2048]{1,0:T(1,128)S(1)}, u32[]{:S(2)}, u32[]{:S(2)}) %collective-permute-start.12) | collective-permute-done | bytes 8224 | tf_op jit(solution)/shard_map/ppermute | solution.py:222
  27.2 2.5 %collective-permute-start.15 = (bf16[128,256]{1,0:T(8,128)(2,1)S(1)}, bf16[128,256]{1,0:T(8,128)(2,1)S(1)}, u32[]{:S(2)}, u32[]{:S(2)}) collective-permute-start(bf16[128,256]{1,0:T(8,128)(2,1)S(1)} %get-tuple-element.52), channel_id=1, source_target_pairs={{0,19},{1,18},{2,17},{3,16},{4,23},{5,22},{6,21},{7,20},{8,27},{9,... | collective-permute-start | bytes 196616 | tf_op jit(solution)/shard_map/ppermute | solution.py:229
  30.8 2.0 %collective-permute-done.14 = bf16[128,256]{1,0:T(8,128)(2,1)S(1)} collective-permute-done((bf16[128,256]{1,0:T(8,128)(2,1)S(1)}, bf16[128,256]{1,0:T(8,128)(2,1)S(1)}, u32[]{:S(2)}, u32[]{:S(2)}) %collective-permute-start.14) | collective-permute-done | bytes 65568 | tf_op jit(solution)/shard_map/ppermute | solution.py:222
  32.8 1.4 %collective-permute-start.16 = (bf16[128,256]{1,0:T(8,128)(2,1)S(1)}, bf16[128,256]{1,0:T(8,128)(2,1)S(1)}, u32[]{:S(2)}, u32[]{:S(2)}) collective-permute-start(bf16[128,256]{1,0:T(8,128)(2,1)S(1)} %get-tuple-element.64), channel_id=1, source_target_pairs={{0,5},{1,4},{2,7},{3,6},{4,1},{5,0},{6,3},{7,2},{8,13},{9,12},{10,... | collective-permute-start | bytes 196616 | tf_op jit(solution)/shard_map/ppermute | solution.py:222
  34.6 2.4 %collective-permute-done.16 = bf16[128,256]{1,0:T(8,128)(2,1)S(1)} collective-permute-done((bf16[128,256]{1,0:T(8,128)(2,1)S(1)}, bf16[128,256]{1,0:T(8,128)(2,1)S(1)}, u32[]{:S(2)}, u32[]{:S(2)}) %collective-permute-start.16) | collective-permute-done | bytes 65568 | tf_op jit(solution)/shard_map/ppermute | solution.py:222
  37.0 1.9 %collective-permute-start.17 = (bf16[128,256]{1,0:T(8,128)(2,1)S(1)}, bf16[128,256]{1,0:T(8,128)(2,1)S(1)}, u32[]{:S(2)}, u32[]{:S(2)}) collective-permute-start(bf16[128,256]{1,0:T(8,128)(2,1)S(1)} %fusion.1), channel_id=1, source_target_pairs={{0,9},{1,8},{2,11},{3,10},{4,13},{5,12},{6,15},{7,14},{8,1},{9,0},... | collective-permute-start | bytes 196616 | tf_op jit(solution)/shard_map/ppermute | solution.py:222
  38.9 3.2 %collective-permute-done.17 = bf16[128,256]{1,0:T(8,128)(2,1)S(1)} collective-permute-done((bf16[128,256]{1,0:T(8,128)(2,1)S(1)}, bf16[128,256]{1,0:T(8,128)(2,1)S(1)}, u32[]{:S(2)}, u32[]{:S(2)}) %collective-permute-start.17) | collective-permute-done | bytes 65568 | tf_op jit(solution)/shard_map/ppermute | solution.py:222
  42.1 2.2 %collective-permute-start.20 = (bf16[128,256]{1,0:T(8,128)(2,1)S(1)}, bf16[128,256]{1,0:T(8,128)(2,1)S(1)}, u32[]{:S(2)}, u32[]{:S(2)}) collective-permute-start(bf16[128,256]{1,0:T(8,128)(2,1)S(1)} %fusion.c0), channel_id=1, source_target_pairs={{0,19},{1,18},{2,17},{3,16},{4,23},{5,22},{6,21},{7,20},{8,27},{9,... | collective-permute-start | bytes 196616 | tf_op jit(solution)/shard_map/ppermute | solution.py:229
  45.4 1.2 %collective-permute-start.21 = (bf16[128,256]{1,0:T(8,128)(2,1)S(1)}, bf16[128,256]{1,0:T(8,128)(2,1)S(1)}, u32[]{:S(2)}, u32[]{:S(2)}) collective-permute-start(bf16[128,256]{1,0:T(8,128)(2,1)S(1)} %fusion.c0), channel_id=1, source_target_pairs={{0,1},{1,0},{2,3},{3,2},{4,5},{5,4},{6,7},{7,6},{8,9},{9,8},{10,11... | collective-permute-start | bytes 196616 | tf_op jit(solution)/shard_map/ppermute | solution.py:222
  46.8 1.6 %collective-permute-start.24 = (bf16[128,256]{1,0:T(8,128)(2,1)S(1)}, bf16[128,256]{1,0:T(8,128)(2,1)S(1)}, u32[]{:S(2)}, u32[]{:S(2)}) collective-permute-start(bf16[128,256]{1,0:T(8,128)(2,1)S(1)} %collective-permute-done.20.x1), channel_id=1, source_target_pairs={{0,1},{1,0},{2,3},{3,2},{4,5},{5,4},{6,7},{7,6},{8,9},{9,8},{10,11... | collective-permute-start | bytes 196616 | tf_op jit(solution)/shard_map/ppermute | solution.py:222
  50.7 1.6 %shard_map.76 = (f32[1024,1024]{1,0:T(8,128)S(1)}, f32[8,128]{1,0:T(8,128)S(1)}) custom-call(bf16[1024,256]{1,0:T(8,128)(2,1)S(1)} %get-tuple-element.53.left, f32[8,128]{1,0:T(8,128)S(1)} %get-tuple-element.54.squares, bf16[512,512]{1,0:T(8,128)(2,1)S(1)} %shard_map.69.units.targets, bf16[512,512]{1,0:T(8,128)(2,1)S(1)} %collective-permute-done.4.units_far.targets_far, ...), custom_call_target="tpu_custom_call" | custom-call | flops 1342177280 | bytes 8134656 | tf_op jit(solution)/shard_map/pallas_call | solution.py:234
  52.3 1.6 %collective-permute-start.28 = (f32[8,128]{1,0:T(8,128)S(1)}, f32[8,128]{1,0:T(8,128)S(1)}, u32[]{:S(2)}, u32[]{:S(2)}) collective-permute-start(f32[8,128]{1,0:T(8,128)S(1)} %get-tuple-element.56), channel_id=1, source_target_pairs={{0,6},{1,7},{2,4},{3,5},{4,2},{5,3},{6,0},{7,1},{8,14},{9,15},{10,... | collective-permute-start | bytes 12296 | tf_op jit(solution)/shard_map/ppermute | solution.py:222
  55.6 1.3 %collective-permute-done.28 = f32[8,128]{1,0:T(8,128)S(1)} collective-permute-done((f32[8,128]{1,0:T(8,128)S(1)}, f32[8,128]{1,0:T(8,128)S(1)}, u32[]{:S(2)}, u32[]{:S(2)}) %collective-permute-start.28) | collective-permute-done | bytes 4128 | tf_op jit(solution)/shard_map/ppermute | solution.py:222
  57.6 2.4 %collective-permute-start.29 = (f32[8,128]{1,0:T(8,128)S(1)}, f32[8,128]{1,0:T(8,128)S(1)}, u32[]{:S(2)}, u32[]{:S(2)}) collective-permute-start(f32[8,128]{1,0:T(8,128)S(1)} %add_add_fusion.1), channel_id=1, source_target_pairs={{0,9},{1,8},{2,11},{3,10},{4,13},{5,12},{6,15},{7,14},{8,1},{9,0},... | collective-permute-start | bytes 12296 | tf_op jit(solution)/shard_map/ppermute | solution.py:222
  60.0 1.5 %collective-permute-done.29 = f32[8,128]{1,0:T(8,128)S(1)} collective-permute-done((f32[8,128]{1,0:T(8,128)S(1)}, f32[8,128]{1,0:T(8,128)S(1)}, u32[]{:S(2)}, u32[]{:S(2)}) %collective-permute-start.29) | collective-permute-done | bytes 4128 | tf_op jit(solution)/shard_map/ppermute | solution.py:222
  64.1 1.5 %collective-permute-done.32.x = f32[1,1024]{1,0:T(1,128)S(1)} collective-permute-done((f32[1,1024]{1,0:T(1,128)S(1)}, f32[1,1024]{1,0:T(1,128)S(1)}, u32[]{:S(2)}, u32[]{:S(2)}) %collective-permute-start.32) | collective-permute-done | bytes 4128 | tf_op jit(solution)/shard_map/ppermute | solution.py:225
  66.5 2.3 %collective-permute-start.35 = (f32[8,128]{1,0:T(8,128)S(1)}, f32[8,128]{1,0:T(8,128)S(1)}, u32[]{:S(2)}, u32[]{:S(2)}) collective-permute-start(f32[8,128]{1,0:T(8,128)S(1)} %shard_map.78), channel_id=1, source_target_pairs={{0,6},{1,7},{2,4},{3,5},{4,2},{5,3},{6,0},{7,1},{8,14},{9,15},{10,... | collective-permute-start | bytes 12296 | tf_op jit(solution)/shard_map/ppermute | solution.py:222
  69.7 1.3 %collective-permute-done.35 = f32[8,128]{1,0:T(8,128)S(1)} collective-permute-done((f32[8,128]{1,0:T(8,128)S(1)}, f32[8,128]{1,0:T(8,128)S(1)}, u32[]{:S(2)}, u32[]{:S(2)}) %collective-permute-start.35) | collective-permute-done | bytes 4128 | tf_op jit(solution)/shard_map/ppermute | solution.py:222
  71.8 2.7 %collective-permute-start.36 = (f32[8,128]{1,0:T(8,128)S(1)}, f32[8,128]{1,0:T(8,128)S(1)}, u32[]{:S(2)}, u32[]{:S(2)}) collective-permute-start(f32[8,128]{1,0:T(8,128)S(1)} %add_add_fusion), channel_id=1, source_target_pairs={{0,9},{1,8},{2,11},{3,10},{4,13},{5,12},{6,15},{7,14},{8,1},{9,0},... | collective-permute-start | bytes 12296 | tf_op jit(solution)/shard_map/ppermute | solution.py:222
  74.4 1.3 %collective-permute-done.36 = f32[8,128]{1,0:T(8,128)S(1)} collective-permute-done((f32[8,128]{1,0:T(8,128)S(1)}, f32[8,128]{1,0:T(8,128)S(1)}, u32[]{:S(2)}, u32[]{:S(2)}) %collective-permute-start.36) | collective-permute-done | bytes 4128 | tf_op jit(solution)/shard_map/ppermute | solution.py:222
  76.2 1.5 %collective-permute-start.39 = (f32[16,128]{1,0:T(8,128)S(1)}, f32[16,128]{1,0:T(8,128)S(1)}, u32[]{:S(2)}, u32[]{:S(2)}) collective-permute-start(f32[16,128]{1,0:T(8,128)S(1)} %get-tuple-element.61), channel_id=1, source_target_pairs={{0,16},{16,0},{1,17},{17,1},{2,18},{18,2},{3,19},{19,3},{4,20},{20... | collective-permute-start | bytes 24584 | tf_op jit(solution)/shard_map/ppermute | solution.py:225
  78.4 1.5 %collective-permute-done.39.x = f32[16,128]{1,0:T(8,128)S(1)} collective-permute-done((f32[16,128]{1,0:T(8,128)S(1)}, f32[16,128]{1,0:T(8,128)S(1)}, u32[]{:S(2)}, u32[]{:S(2)}) %collective-permute-start.39) | collective-permute-done | bytes 8224 | tf_op jit(solution)/shard_map/ppermute | solution.py:225
  (83 shorter events, 23.2 us)
Async XLA Ops:
  0.6 16.7 %collective-permute-start.5 = (bf16[2048,512]{1,0:T(8,128)(2,1)}, bf16[2048,512]{1,0:T(8,128)(2,1)S(1)}, u32[]{:S(2)}, u32[]{:S(2)}) collective-permute-start(bf16[2048,512]{1,0:T(8,128)(2,1)} %plan.5), channel_id=1, source_target_pairs={{0,1},{1,0},{2,3},{3,2},{4,5},{5,4},{6,7},{7,6},{8,9},{9,8},{10,11... | collective-permute-start | bytes 6291464 | tf_op jit(solution)/shard_map/ppermute | solution.py:222
  1.1 12.2 %collective-permute-start = (bf16[512,256]{1,0:T(8,128)(2,1)}, bf16[512,256]{1,0:T(8,128)(2,1)S(1)}, u32[]{:S(2)}, u32[]{:S(2)}) collective-permute-start(bf16[512,256]{1,0:T(8,128)(2,1)} %near.3), channel_id=1, source_target_pairs={{0,16},{16,0},{1,17},{17,1},{2,18},{18,2},{3,19},{19,3},{4,20},{20... | collective-permute-start | bytes 786440 | tf_op jit(solution)/shard_map/ppermute | solution.py:225
  3.7 9.6 %collective-permute-start.3 = (bf16[32,2048]{1,0:T(8,128)(2,1)}, bf16[32,2048]{1,0:T(8,128)(2,1)S(1)}, u32[]{:S(2)}, u32[]{:S(2)}) collective-permute-start(bf16[32,2048]{1,0:T(8,128)(2,1)} %bitcast.5), channel_id=1, source_target_pairs={{0,9},{1,8},{2,11},{3,10},{4,13},{5,12},{6,15},{7,14},{8,1},{9,0},... | collective-permute-start | bytes 393224 | tf_op jit(solution)/shard_map/ppermute | solution.py:222
  6.1 7.2 %collective-permute-start.2 = (bf16[32,2048]{1,0:T(8,128)(2,1)}, bf16[32,2048]{1,0:T(8,128)(2,1)S(1)}, u32[]{:S(2)}, u32[]{:S(2)}) collective-permute-start(bf16[32,2048]{1,0:T(8,128)(2,1)} %bitcast.6), channel_id=1, source_target_pairs={{0,5},{1,4},{2,7},{3,6},{4,1},{5,0},{6,3},{7,2},{8,13},{9,12},{10,... | collective-permute-start | bytes 393224 | tf_op jit(solution)/shard_map/ppermute | solution.py:222
  7.6 5.8 %collective-permute-start.1 = (bf16[32,2048]{1,0:T(8,128)(2,1)}, bf16[32,2048]{1,0:T(8,128)(2,1)S(1)}, u32[]{:S(2)}, u32[]{:S(2)}) collective-permute-start(bf16[32,2048]{1,0:T(8,128)(2,1)} %bitcast.7), channel_id=1, source_target_pairs={{0,3},{1,2},{2,1},{3,0},{4,7},{5,6},{6,5},{7,4},{8,11},{9,10},{10,... | collective-permute-start | bytes 393224 | tf_op jit(solution)/shard_map/ppermute | solution.py:222
  13.6 3.4 %collective-permute-start.4 = (bf16[512,512]{1,0:T(8,128)(2,1)S(1)}, bf16[512,512]{1,0:T(8,128)(2,1)S(1)}, u32[]{:S(2)}, u32[]{:S(2)}) collective-permute-start(bf16[512,512]{1,0:T(8,128)(2,1)S(1)} %shard_map.69.units.targets), channel_id=1, source_target_pairs={{0,1},{1,0},{2,3},{3,2},{4,5},{5,4},{6,7},{7,6},{8,9},{9,8},{10,11... | collective-permute-start | bytes 1572872 | tf_op jit(solution)/shard_map/ppermute | solution.py:222
  13.9 5.4 %collective-permute-start.7 = (bf16[32,2048]{1,0:T(8,128)(2,1)S(1)}, bf16[32,2048]{1,0:T(8,128)(2,1)S(1)}, u32[]{:S(2)}, u32[]{:S(2)}) collective-permute-start(bf16[32,2048]{1,0:T(8,128)(2,1)S(1)} %collective-permute-done.3.refs_1_.p1), channel_id=1, source_target_pairs={{0,5},{1,4},{2,7},{3,6},{4,1},{5,0},{6,3},{7,2},{8,13},{9,12},{10,... | collective-permute-start | bytes 393224 | tf_op jit(solution)/shard_map/ppermute | solution.py:222
  15.4 3.4 %collective-permute-start.6 = (f32[1,512]{1,0:T(1,128)S(1)}, f32[1,512]{1,0:T(1,128)S(1)}, u32[]{:S(2)}, u32[]{:S(2)}) collective-permute-start(f32[1,512]{1,0:T(1,128)S(1)} %get-tuple-element.39.mass), channel_id=1, source_target_pairs={{0,1},{1,0},{2,3},{3,2},{4,5},{5,4},{6,7},{7,6},{8,9},{9,8},{10,11... | collective-permute-start | bytes 6152 | tf_op jit(solution)/shard_map/ppermute | solution.py:222
  15.5 6.0 %collective-permute-start.8 = (bf16[32,2048]{1,0:T(8,128)(2,1)S(1)}, bf16[32,2048]{1,0:T(8,128)(2,1)S(1)}, u32[]{:S(2)}, u32[]{:S(2)}) collective-permute-start(bf16[32,2048]{1,0:T(8,128)(2,1)S(1)} %collective-permute-done.3.refs_1_.p1), channel_id=1, source_target_pairs={{0,3},{1,2},{2,1},{3,0},{4,7},{5,6},{6,5},{7,4},{8,11},{9,10},{10,... | collective-permute-start | bytes 393224 | tf_op jit(solution)/shard_map/ppermute | solution.py:222
  17.0 7.2 %collective-permute-start.10 = (bf16[32,2048]{1,0:T(8,128)(2,1)S(1)}, bf16[32,2048]{1,0:T(8,128)(2,1)S(1)}, u32[]{:S(2)}, u32[]{:S(2)}) collective-permute-start(bf16[32,2048]{1,0:T(8,128)(2,1)S(1)} %collective-permute-done.1.p4), channel_id=1, source_target_pairs={{0,5},{1,4},{2,7},{3,6},{4,1},{5,0},{6,3},{7,2},{8,13},{9,12},{10,... | collective-permute-start | bytes 393224 | tf_op jit(solution)/shard_map/ppermute | solution.py:222
  19.4 6.5 %collective-permute-start.9 = (bf16[32,2048]{1,0:T(8,128)(2,1)S(1)}, bf16[32,2048]{1,0:T(8,128)(2,1)S(1)}, u32[]{:S(2)}, u32[]{:S(2)}) collective-permute-start(bf16[32,2048]{1,0:T(8,128)(2,1)S(1)} %collective-permute-done.7.refs_3_.p3), channel_id=1, source_target_pairs={{0,3},{1,2},{2,1},{3,0},{4,7},{5,6},{6,5},{7,4},{8,11},{9,10},{10,... | collective-permute-start | bytes 393224 | tf_op jit(solution)/shard_map/ppermute | solution.py:222
  22.7 3.1 %collective-permute-start.12 = (f32[1,2048]{1,0:T(1,128)S(1)}, f32[1,2048]{1,0:T(1,128)S(1)}, u32[]{:S(2)}, u32[]{:S(2)}) collective-permute-start(f32[1,2048]{1,0:T(1,128)S(1)} %add.42.squares), channel_id=1, source_target_pairs={{0,3},{1,2},{2,1},{3,0},{4,7},{5,6},{6,5},{7,4},{8,11},{9,10},{10,... | collective-permute-start | bytes 24584 | tf_op jit(solution)/shard_map/ppermute | solution.py:222
  26.4 4.3 %collective-permute-start.13 = (bf16[128,256]{1,0:T(8,128)(2,1)S(1)}, bf16[128,256]{1,0:T(8,128)(2,1)S(1)}, u32[]{:S(2)}, u32[]{:S(2)}) collective-permute-start(bf16[128,256]{1,0:T(8,128)(2,1)S(1)} %get-tuple-element.50), channel_id=1, source_target_pairs={{0,16},{16,0},{1,17},{17,1},{2,18},{18,2},{3,19},{19,3},{4,20},{20... | collective-permute-start | bytes 196616 | tf_op jit(solution)/shard_map/ppermute | solution.py:225
  27.0 5.7 %collective-permute-start.14 = (bf16[128,256]{1,0:T(8,128)(2,1)S(1)}, bf16[128,256]{1,0:T(8,128)(2,1)S(1)}, u32[]{:S(2)}, u32[]{:S(2)}) collective-permute-start(bf16[128,256]{1,0:T(8,128)(2,1)S(1)} %get-tuple-element.51), channel_id=1, source_target_pairs={{0,3},{1,2},{2,1},{3,0},{4,7},{5,6},{6,5},{7,4},{8,11},{9,10},{10,... | collective-permute-start | bytes 196616 | tf_op jit(solution)/shard_map/ppermute | solution.py:222
  27.2 5.5 %collective-permute-start.15 = (bf16[128,256]{1,0:T(8,128)(2,1)S(1)}, bf16[128,256]{1,0:T(8,128)(2,1)S(1)}, u32[]{:S(2)}, u32[]{:S(2)}) collective-permute-start(bf16[128,256]{1,0:T(8,128)(2,1)S(1)} %get-tuple-element.52), channel_id=1, source_target_pairs={{0,19},{1,18},{2,17},{3,16},{4,23},{5,22},{6,21},{7,20},{8,27},{9,... | collective-permute-start | bytes 196616 | tf_op jit(solution)/shard_map/ppermute | solution.py:229
  32.8 4.2 %collective-permute-start.16 = (bf16[128,256]{1,0:T(8,128)(2,1)S(1)}, bf16[128,256]{1,0:T(8,128)(2,1)S(1)}, u32[]{:S(2)}, u32[]{:S(2)}) collective-permute-start(bf16[128,256]{1,0:T(8,128)(2,1)S(1)} %get-tuple-element.64), channel_id=1, source_target_pairs={{0,5},{1,4},{2,7},{3,6},{4,1},{5,0},{6,3},{7,2},{8,13},{9,12},{10,... | collective-permute-start | bytes 196616 | tf_op jit(solution)/shard_map/ppermute | solution.py:222
  34.2 16.6 %collective-permute-start.25 = (bf16[256,2048]{1,0:T(8,128)(2,1)S(1)}, bf16[256,2048]{1,0:T(8,128)(2,1)S(1)}, u32[]{:S(2)}, u32[]{:S(2)}) collective-permute-start(bf16[256,2048]{1,0:T(8,128)(2,1)S(1)} %get-tuple-element.49.units.near), channel_id=1, source_target_pairs={{0,1},{1,0},{2,3},{3,2},{4,5},{5,4},{6,7},{7,6},{8,9},{9,8},{10,11... | collective-permute-start | bytes 3145736 | tf_op jit(solution)/shard_map/ppermute | solution.py:222
  37.0 5.1 %collective-permute-start.17 = (bf16[128,256]{1,0:T(8,128)(2,1)S(1)}, bf16[128,256]{1,0:T(8,128)(2,1)S(1)}, u32[]{:S(2)}, u32[]{:S(2)}) collective-permute-start(bf16[128,256]{1,0:T(8,128)(2,1)S(1)} %fusion.1), channel_id=1, source_target_pairs={{0,9},{1,8},{2,11},{3,10},{4,13},{5,12},{6,15},{7,14},{8,1},{9,0},... | collective-permute-start | bytes 196616 | tf_op jit(solution)/shard_map/ppermute | solution.py:222
  42.1 4.7 %collective-permute-start.20 = (bf16[128,256]{1,0:T(8,128)(2,1)S(1)}, bf16[128,256]{1,0:T(8,128)(2,1)S(1)}, u32[]{:S(2)}, u32[]{:S(2)}) collective-permute-start(bf16[128,256]{1,0:T(8,128)(2,1)S(1)} %fusion.c0), channel_id=1, source_target_pairs={{0,19},{1,18},{2,17},{3,16},{4,23},{5,22},{6,21},{7,20},{8,27},{9,... | collective-permute-start | bytes 196616 | tf_op jit(solution)/shard_map/ppermute | solution.py:229
  44.3 4.7 %collective-permute-start.19 = (bf16[128,256]{1,0:T(8,128)(2,1)S(1)}, bf16[128,256]{1,0:T(8,128)(2,1)S(1)}, u32[]{:S(2)}, u32[]{:S(2)}) collective-permute-start(bf16[128,256]{1,0:T(8,128)(2,1)S(1)} %fusion.c0), channel_id=1, source_target_pairs={{0,3},{1,2},{2,1},{3,0},{4,7},{5,6},{6,5},{7,4},{8,11},{9,10},{10,... | collective-permute-start | bytes 196616 | tf_op jit(solution)/shard_map/ppermute | solution.py:222
  44.9 4.6 %collective-permute-start.18 = (bf16[128,256]{1,0:T(8,128)(2,1)S(1)}, bf16[128,256]{1,0:T(8,128)(2,1)S(1)}, u32[]{:S(2)}, u32[]{:S(2)}) collective-permute-start(bf16[128,256]{1,0:T(8,128)(2,1)S(1)} %fusion.c0), channel_id=1, source_target_pairs={{0,16},{16,0},{1,17},{17,1},{2,18},{18,2},{3,19},{19,3},{4,20},{20... | collective-permute-start | bytes 196616 | tf_op jit(solution)/shard_map/ppermute | solution.py:225
  45.4 4.7 %collective-permute-start.21 = (bf16[128,256]{1,0:T(8,128)(2,1)S(1)}, bf16[128,256]{1,0:T(8,128)(2,1)S(1)}, u32[]{:S(2)}, u32[]{:S(2)}) collective-permute-start(bf16[128,256]{1,0:T(8,128)(2,1)S(1)} %fusion.c0), channel_id=1, source_target_pairs={{0,1},{1,0},{2,3},{3,2},{4,5},{5,4},{6,7},{7,6},{8,9},{9,8},{10,11... | collective-permute-start | bytes 196616 | tf_op jit(solution)/shard_map/ppermute | solution.py:222
  46.8 3.4 %collective-permute-start.24 = (bf16[128,256]{1,0:T(8,128)(2,1)S(1)}, bf16[128,256]{1,0:T(8,128)(2,1)S(1)}, u32[]{:S(2)}, u32[]{:S(2)}) collective-permute-start(bf16[128,256]{1,0:T(8,128)(2,1)S(1)} %collective-permute-done.20.x1), channel_id=1, source_target_pairs={{0,1},{1,0},{2,3},{3,2},{4,5},{5,4},{6,7},{7,6},{8,9},{9,8},{10,11... | collective-permute-start | bytes 196616 | tf_op jit(solution)/shard_map/ppermute | solution.py:222
  52.3 4.6 %collective-permute-start.28 = (f32[8,128]{1,0:T(8,128)S(1)}, f32[8,128]{1,0:T(8,128)S(1)}, u32[]{:S(2)}, u32[]{:S(2)}) collective-permute-start(f32[8,128]{1,0:T(8,128)S(1)} %get-tuple-element.56), channel_id=1, source_target_pairs={{0,6},{1,7},{2,4},{3,5},{4,2},{5,3},{6,0},{7,1},{8,14},{9,15},{10,... | collective-permute-start | bytes 12296 | tf_op jit(solution)/shard_map/ppermute | solution.py:222
  57.6 3.9 %collective-permute-start.29 = (f32[8,128]{1,0:T(8,128)S(1)}, f32[8,128]{1,0:T(8,128)S(1)}, u32[]{:S(2)}, u32[]{:S(2)}) collective-permute-start(f32[8,128]{1,0:T(8,128)S(1)} %add_add_fusion.1), channel_id=1, source_target_pairs={{0,9},{1,8},{2,11},{3,10},{4,13},{5,12},{6,15},{7,14},{8,1},{9,0},... | collective-permute-start | bytes 12296 | tf_op jit(solution)/shard_map/ppermute | solution.py:222
  61.9 3.7 %collective-permute-start.32 = (f32[1,1024]{1,0:T(1,128)S(1)}, f32[1,1024]{1,0:T(1,128)S(1)}, u32[]{:S(2)}, u32[]{:S(2)}) collective-permute-start(f32[1,1024]{1,0:T(1,128)S(1)} %shard_map.77.own), channel_id=1, source_target_pairs={{0,16},{16,0},{1,17},{17,1},{2,18},{18,2},{3,19},{19,3},{4,20},{20... | collective-permute-start | bytes 12296 | tf_op jit(solution)/shard_map/ppermute | solution.py:225
  66.5 4.6 %collective-permute-start.35 = (f32[8,128]{1,0:T(8,128)S(1)}, f32[8,128]{1,0:T(8,128)S(1)}, u32[]{:S(2)}, u32[]{:S(2)}) collective-permute-start(f32[8,128]{1,0:T(8,128)S(1)} %shard_map.78), channel_id=1, source_target_pairs={{0,6},{1,7},{2,4},{3,5},{4,2},{5,3},{6,0},{7,1},{8,14},{9,15},{10,... | collective-permute-start | bytes 12296 | tf_op jit(solution)/shard_map/ppermute | solution.py:222
  68.7 3.1 %collective-permute-start.34 = (f32[8,128]{1,0:T(8,128)S(1)}, f32[8,128]{1,0:T(8,128)S(1)}, u32[]{:S(2)}, u32[]{:S(2)}) collective-permute-start(f32[8,128]{1,0:T(8,128)S(1)} %shard_map.78), channel_id=1, source_target_pairs={{0,5},{1,4},{2,7},{3,6},{4,1},{5,0},{6,3},{7,2},{8,13},{9,12},{10,... | collective-permute-start | bytes 12296 | tf_op jit(solution)/shard_map/ppermute | solution.py:222
  71.8 4.0 %collective-permute-start.36 = (f32[8,128]{1,0:T(8,128)S(1)}, f32[8,128]{1,0:T(8,128)S(1)}, u32[]{:S(2)}, u32[]{:S(2)}) collective-permute-start(f32[8,128]{1,0:T(8,128)S(1)} %add_add_fusion), channel_id=1, source_target_pairs={{0,9},{1,8},{2,11},{3,10},{4,13},{5,12},{6,15},{7,14},{8,1},{9,0},... | collective-permute-start | bytes 12296 | tf_op jit(solution)/shard_map/ppermute | solution.py:222
  76.2 3.7 %collective-permute-start.39 = (f32[16,128]{1,0:T(8,128)S(1)}, f32[16,128]{1,0:T(8,128)S(1)}, u32[]{:S(2)}, u32[]{:S(2)}) collective-permute-start(f32[16,128]{1,0:T(8,128)S(1)} %get-tuple-element.61), channel_id=1, source_target_pairs={{0,16},{16,0},{1,17},{17,1},{2,18},{18,2},{3,19},{19,3},{4,20},{20... | collective-permute-start | bytes 24584 | tf_op jit(solution)/shard_map/ppermute | solution.py:225
  77.7 3.2 %collective-permute-start.38 = (f32[16,128]{1,0:T(8,128)S(1)}, f32[16,128]{1,0:T(8,128)S(1)}, u32[]{:S(2)}, u32[]{:S(2)}) collective-permute-start(f32[16,128]{1,0:T(8,128)S(1)} %get-tuple-element.61), channel_id=1, source_target_pairs={{0,17},{1,16},{2,19},{3,18},{4,21},{5,20},{6,23},{7,22},{8,25},{9,... | collective-permute-start | bytes 24584 | tf_op jit(solution)/shard_map/ppermute | solution.py:229
  77.8 3.1 %collective-permute-start.37 = (f32[16,128]{1,0:T(8,128)S(1)}, f32[16,128]{1,0:T(8,128)S(1)}, u32[]{:S(2)}, u32[]{:S(2)}) collective-permute-start(f32[16,128]{1,0:T(8,128)S(1)} %get-tuple-element.61), channel_id=1, source_target_pairs={{0,1},{1,0},{2,3},{3,2},{4,5},{5,4},{6,7},{7,6},{8,9},{9,8},{10,11... | collective-permute-start | bytes 24584 | tf_op jit(solution)/shard_map/ppermute | solution.py:222
  (14 other events, 32.7 us)

commit v9 on v8

--- a/solution.py
+++ b/solution.py
@@ -157,10 +157,10 @@
             sums[row : row + 1, :] = total[:, j * LANES : (j + 1) * LANES]
 
 
-def sweep_rows(target_count, block, totals, mass, sums, rows, acc):
+def sweep_rows(target_count, block, totals, more, mass, sums, rows, acc):
     count = rows.shape[0]
     start = pl.multiple_of(half_index() * count, count)
-    rows[...] = mass[pl.ds(start, count), :] / (totals[...] / target_count)
+    rows[...] = mass[pl.ds(start, count), :] / ((totals[...] + more[...]) / target_count)
     for start in range(0, block.shape[0], 64):
         here = slice(start, start + 64)
         total = jnp.zeros((64, LANES), F32)
@@ -170,8 +170,8 @@
     sums[...] = jnp.sum(acc[...].T, axis=0, keepdims=True)
 
 
-def last_rows(target_count, block, totals, mass, sums, rows, packed, acc):
-    sweep_rows(target_count, block, totals, mass, sums, rows, acc)
+def last_rows(target_count, block, totals, more, mass, sums, rows, packed, acc):
+    sweep_rows(target_count, block, totals, more, mass, sums, rows, acc)
     count = rows.shape[0]
     for j in range(sums.shape[1] // LANES):
         packed[j : j + 1, :] = sums[:, j * LANES : (j + 1) * LANES]
@@ -349,7 +349,7 @@
 
     for repeat in range(2):
         sums = sums + swap(sums, 3) + swap(sums, 5) + swap(sums, 6)
-        sums = sums + swap(sums, 9)
+        more = swap(sums, 9)
         scratch = (((chip, LANES), F32),)
         if repeat == 0:
             (totals,) = call(
@@ -357,6 +357,7 @@
                 ((wide, F32),),
                 block,
                 sums,
+                more,
                 mass,
                 scratch=((part, F32),) + scratch,
             )
@@ -378,6 +379,7 @@
                 ((wide, F32), (part, F32), ((chip // LANES + part[0], LANES), F32)),
                 block,
                 sums,
+                more,
                 mass,
                 scratch=scratch,
             )

time: 81.7 us -> 81.7 us (level)
  no operation moved by 1% of the time
where the time goes in v9:
time: 81.7 us; the launch traced here: 81.5 us
  starting transfers between devices  43.8 us (54%)
  waiting for transfers between devices  24.8 us (30%)
  Pallas kernels  8.04 us (10%)
  local copies, waits for them, and re-layouts  3.95 us (5%)
  between operations  0.82 us (1%)
    ppermute x31, starting transfers between devices, swap(): return lax.ppermute(value, 'cols', [(i, i ^ bits) for i in range(n)])  31.9 us
    ppermute x31, waiting for transfers between devices, swap(): return lax.ppermute(value, 'cols', [(i, i ^ bits) for i in range(n)])  19.5 us
    pallas_call x13, Pallas kernels, call(): pl.pallas_call(function, out_shape=outs, in_specs=[ANY if i in loose else...  8.04 us
    ppermute x5, starting transfers between devices, cross(): return lax.ppermute(value, 'rows', [(0, 1), (1, 0)])  6.35 us
    ppermute x4, starting transfers between devices, both(): return lax.ppermute(value, ('rows', 'cols'), pairs)  5.55 us
    unnamed x12, local copies, waits for them, and re-layouts  3.92 us
    ppermute x5, waiting for transfers between devices, cross(): return lax.ppermute(value, 'rows', [(0, 1), (1, 0)])  3.72 us
  transfers between devices with their start and end apart: 40, of which 23 were waited for; matrix products, arithmetic and copies ran while one was open for 0% of the time, Pallas kernels for 5%

profile of v9, /device:TPU:0, one launch (start us, length us, event | category | flops | bytes accessed | tf_op | source)
XLA Modules:
  0.0 81.5 jit_solution(1682690771491509611)
XLA Ops:
  1.1 2.6 %collective-permute-start = (bf16[512,256]{1,0:T(8,128)(2,1)}, bf16[512,256]{1,0:T(8,128)(2,1)S(1)}, u32[]{:S(2)}, u32[]{:S(2)}) collective-permute-start(bf16[512,256]{1,0:T(8,128)(2,1)} %near.3), channel_id=1, source_target_pairs={{0,16},{16,0},{1,17},{17,1},{2,18},{18,2},{3,19},{19,3},{4,20},{20... | collective-permute-start | bytes 786440 | tf_op jit(solution)/shard_map/ppermute | solution.py:225
  3.7 2.4 %collective-permute-start.3 = (bf16[32,2048]{1,0:T(8,128)(2,1)}, bf16[32,2048]{1,0:T(8,128)(2,1)S(1)}, u32[]{:S(2)}, u32[]{:S(2)}) collective-permute-start(bf16[32,2048]{1,0:T(8,128)(2,1)} %bitcast.5), channel_id=1, source_target_pairs={{0,9},{1,8},{2,11},{3,10},{4,13},{5,12},{6,15},{7,14},{8,1},{9,0},... | collective-permute-start | bytes 393224 | tf_op jit(solution)/shard_map/ppermute | solution.py:222
  6.1 1.5 %collective-permute-start.2 = (bf16[32,2048]{1,0:T(8,128)(2,1)}, bf16[32,2048]{1,0:T(8,128)(2,1)S(1)}, u32[]{:S(2)}, u32[]{:S(2)}) collective-permute-start(bf16[32,2048]{1,0:T(8,128)(2,1)} %bitcast.6), channel_id=1, source_target_pairs={{0,5},{1,4},{2,7},{3,6},{4,1},{5,0},{6,3},{7,2},{8,13},{9,12},{10,... | collective-permute-start | bytes 393224 | tf_op jit(solution)/shard_map/ppermute | solution.py:222
  7.6 1.3 %collective-permute-start.1 = (bf16[32,2048]{1,0:T(8,128)(2,1)}, bf16[32,2048]{1,0:T(8,128)(2,1)S(1)}, u32[]{:S(2)}, u32[]{:S(2)}) collective-permute-start(bf16[32,2048]{1,0:T(8,128)(2,1)} %bitcast.7), channel_id=1, source_target_pairs={{0,3},{1,2},{2,1},{3,0},{4,7},{5,6},{6,5},{7,4},{8,11},{9,10},{10,... | collective-permute-start | bytes 393224 | tf_op jit(solution)/shard_map/ppermute | solution.py:222
  8.9 1.6 %copy-done = bf16[2048,512]{1,0:T(8,128)(2,1)S(1)} copy-done((bf16[2048,512]{1,0:T(8,128)(2,1)S(1)}, bf16[2048,512]{1,0:T(8,128)(2,1)}, u32[]{:S(2)}) %copy-start) | copy-done | bytes 2097176
  13.9 1.4 %collective-permute-start.7 = (bf16[32,2048]{1,0:T(8,128)(2,1)S(1)}, bf16[32,2048]{1,0:T(8,128)(2,1)S(1)}, u32[]{:S(2)}, u32[]{:S(2)}) collective-permute-start(bf16[32,2048]{1,0:T(8,128)(2,1)S(1)} %collective-permute-done.3.refs_1_.p1), channel_id=1, source_target_pairs={{0,5},{1,4},{2,7},{3,6},{4,1},{5,0},{6,3},{7,2},{8,13},{9,12},{10,... | collective-permute-start | bytes 393224 | tf_op jit(solution)/shard_map/ppermute | solution.py:222
  15.5 1.5 %collective-permute-start.8 = (bf16[32,2048]{1,0:T(8,128)(2,1)S(1)}, bf16[32,2048]{1,0:T(8,128)(2,1)S(1)}, u32[]{:S(2)}, u32[]{:S(2)}) collective-permute-start(bf16[32,2048]{1,0:T(8,128)(2,1)S(1)} %collective-permute-done.3.refs_1_.p1), channel_id=1, source_target_pairs={{0,3},{1,2},{2,1},{3,0},{4,7},{5,6},{6,5},{7,4},{8,11},{9,10},{10,... | collective-permute-start | bytes 393224 | tf_op jit(solution)/shard_map/ppermute | solution.py:222
  17.3 1.4 %shard_map.70.upper = bf16[1024,512]{1,0:T(8,128)(2,1)S(1)} custom-call(bf16[2048,512]{1,0:T(8,128)(2,1)S(1)} %copy-done.1, bf16[2048,512]{1,0:T(8,128)(2,1)S(1)} %collective-permute-done.5.plan_far, bf16[512,512]{1,0:T(8,128)(2,1)S(1)} %shard_map.69.units.targets, bf16[512,512]{1,0:T(8,128)(2,1)S(1)} %collective-permute-done.4.units_far.targets_far), custom_call_target="tpu_custom_call" | custom-call | flops 1073741824 | bytes 6291456 | tf_op jit(solution)/shard_map/pallas_call | solution.py:234
  19.4 1.9 %collective-permute-start.9 = (bf16[32,2048]{1,0:T(8,128)(2,1)S(1)}, bf16[32,2048]{1,0:T(8,128)(2,1)S(1)}, u32[]{:S(2)}, u32[]{:S(2)}) collective-permute-start(bf16[32,2048]{1,0:T(8,128)(2,1)S(1)} %collective-permute-done.7.refs_3_.p3), channel_id=1, source_target_pairs={{0,3},{1,2},{2,1},{3,0},{4,7},{5,6},{6,5},{7,4},{8,11},{9,10},{10,... | collective-permute-start | bytes 393224 | tf_op jit(solution)/shard_map/ppermute | solution.py:222
  22.8 1.4 %shard_map.72.lower = bf16[1024,512]{1,0:T(8,128)(2,1)S(1)} custom-call(bf16[2048,512]{1,0:T(8,128)(2,1)S(1)} %copy-done.1, bf16[2048,512]{1,0:T(8,128)(2,1)S(1)} %collective-permute-done.5.plan_far, bf16[512,512]{1,0:T(8,128)(2,1)S(1)} %shard_map.69.units.targets, bf16[512,512]{1,0:T(8,128)(2,1)S(1)} %collective-permute-done.4.units_far.targets_far), custom_call_target="tpu_custom_call" | custom-call | flops 1073741824 | bytes 6291456 | tf_op jit(solution)/shard_map/pallas_call | solution.py:234
  24.2 1.6 %collective-permute-done.12.squares_y = f32[1,2048]{1,0:T(1,128)S(1)} collective-permute-done((f32[1,2048]{1,0:T(1,128)S(1)}, f32[1,2048]{1,0:T(1,128)S(1)}, u32[]{:S(2)}, u32[]{:S(2)}) %collective-permute-start.12) | collective-permute-done | bytes 8224 | tf_op jit(solution)/shard_map/ppermute | solution.py:222
  27.2 2.5 %collective-permute-start.15 = (bf16[128,256]{1,0:T(8,128)(2,1)S(1)}, bf16[128,256]{1,0:T(8,128)(2,1)S(1)}, u32[]{:S(2)}, u32[]{:S(2)}) collective-permute-start(bf16[128,256]{1,0:T(8,128)(2,1)S(1)} %get-tuple-element.52), channel_id=1, source_target_pairs={{0,19},{1,18},{2,17},{3,16},{4,23},{5,22},{6,21},{7,20},{8,27},{9,... | collective-permute-start | bytes 196616 | tf_op jit(solution)/shard_map/ppermute | solution.py:229
  30.8 2.0 %collective-permute-done.14 = bf16[128,256]{1,0:T(8,128)(2,1)S(1)} collective-permute-done((bf16[128,256]{1,0:T(8,128)(2,1)S(1)}, bf16[128,256]{1,0:T(8,128)(2,1)S(1)}, u32[]{:S(2)}, u32[]{:S(2)}) %collective-permute-start.14) | collective-permute-done | bytes 65568 | tf_op jit(solution)/shard_map/ppermute | solution.py:222
  32.8 1.4 %collective-permute-start.16 = (bf16[128,256]{1,0:T(8,128)(2,1)S(1)}, bf16[128,256]{1,0:T(8,128)(2,1)S(1)}, u32[]{:S(2)}, u32[]{:S(2)}) collective-permute-start(bf16[128,256]{1,0:T(8,128)(2,1)S(1)} %get-tuple-element.64), channel_id=1, source_target_pairs={{0,5},{1,4},{2,7},{3,6},{4,1},{5,0},{6,3},{7,2},{8,13},{9,12},{10,... | collective-permute-start | bytes 196616 | tf_op jit(solution)/shard_map/ppermute | solution.py:222
  34.6 2.4 %collective-permute-done.16 = bf16[128,256]{1,0:T(8,128)(2,1)S(1)} collective-permute-done((bf16[128,256]{1,0:T(8,128)(2,1)S(1)}, bf16[128,256]{1,0:T(8,128)(2,1)S(1)}, u32[]{:S(2)}, u32[]{:S(2)}) %collective-permute-start.16) | collective-permute-done | bytes 65568 | tf_op jit(solution)/shard_map/ppermute | solution.py:222
  37.0 1.9 %collective-permute-start.17 = (bf16[128,256]{1,0:T(8,128)(2,1)S(1)}, bf16[128,256]{1,0:T(8,128)(2,1)S(1)}, u32[]{:S(2)}, u32[]{:S(2)}) collective-permute-start(bf16[128,256]{1,0:T(8,128)(2,1)S(1)} %fusion.1), channel_id=1, source_target_pairs={{0,9},{1,8},{2,11},{3,10},{4,13},{5,12},{6,15},{7,14},{8,1},{9,0},... | collective-permute-start | bytes 196616 | tf_op jit(solution)/shard_map/ppermute | solution.py:222
  38.9 3.2 %collective-permute-done.17 = bf16[128,256]{1,0:T(8,128)(2,1)S(1)} collective-permute-done((bf16[128,256]{1,0:T(8,128)(2,1)S(1)}, bf16[128,256]{1,0:T(8,128)(2,1)S(1)}, u32[]{:S(2)}, u32[]{:S(2)}) %collective-permute-start.17) | collective-permute-done | bytes 65568 | tf_op jit(solution)/shard_map/ppermute | solution.py:222
  42.1 2.2 %collective-permute-start.20 = (bf16[128,256]{1,0:T(8,128)(2,1)S(1)}, bf16[128,256]{1,0:T(8,128)(2,1)S(1)}, u32[]{:S(2)}, u32[]{:S(2)}) collective-permute-start(bf16[128,256]{1,0:T(8,128)(2,1)S(1)} %fusion.c0), channel_id=1, source_target_pairs={{0,19},{1,18},{2,17},{3,16},{4,23},{5,22},{6,21},{7,20},{8,27},{9,... | collective-permute-start | bytes 196616 | tf_op jit(solution)/shard_map/ppermute | solution.py:229
  45.4 1.2 %collective-permute-start.21 = (bf16[128,256]{1,0:T(8,128)(2,1)S(1)}, bf16[128,256]{1,0:T(8,128)(2,1)S(1)}, u32[]{:S(2)}, u32[]{:S(2)}) collective-permute-start(bf16[128,256]{1,0:T(8,128)(2,1)S(1)} %fusion.c0), channel_id=1, source_target_pairs={{0,1},{1,0},{2,3},{3,2},{4,5},{5,4},{6,7},{7,6},{8,9},{9,8},{10,11... | collective-permute-start | bytes 196616 | tf_op jit(solution)/shard_map/ppermute | solution.py:222
  46.8 1.6 %collective-permute-start.24 = (bf16[128,256]{1,0:T(8,128)(2,1)S(1)}, bf16[128,256]{1,0:T(8,128)(2,1)S(1)}, u32[]{:S(2)}, u32[]{:S(2)}) collective-permute-start(bf16[128,256]{1,0:T(8,128)(2,1)S(1)} %collective-permute-done.20.x1), channel_id=1, source_target_pairs={{0,1},{1,0},{2,3},{3,2},{4,5},{5,4},{6,7},{7,6},{8,9},{9,8},{10,11... | collective-permute-start | bytes 196616 | tf_op jit(solution)/shard_map/ppermute | solution.py:222
  50.7 1.6 %shard_map.76 = (f32[1024,1024]{1,0:T(8,128)S(1)}, f32[8,128]{1,0:T(8,128)S(1)}) custom-call(bf16[1024,256]{1,0:T(8,128)(2,1)S(1)} %get-tuple-element.53.left, f32[8,128]{1,0:T(8,128)S(1)} %get-tuple-element.54.squares, bf16[512,512]{1,0:T(8,128)(2,1)S(1)} %shard_map.69.units.targets, bf16[512,512]{1,0:T(8,128)(2,1)S(1)} %collective-permute-done.4.units_far.targets_far, ...), custom_call_target="tpu_custom_call" | custom-call | flops 1342177280 | bytes 8134656 | tf_op jit(solution)/shard_map/pallas_call | solution.py:234
  52.3 1.6 %collective-permute-start.28 = (f32[8,128]{1,0:T(8,128)S(1)}, f32[8,128]{1,0:T(8,128)S(1)}, u32[]{:S(2)}, u32[]{:S(2)}) collective-permute-start(f32[8,128]{1,0:T(8,128)S(1)} %get-tuple-element.56), channel_id=1, source_target_pairs={{0,6},{1,7},{2,4},{3,5},{4,2},{5,3},{6,0},{7,1},{8,14},{9,15},{10,... | collective-permute-start | bytes 12296 | tf_op jit(solution)/shard_map/ppermute | solution.py:222
  55.6 1.3 %collective-permute-done.28 = f32[8,128]{1,0:T(8,128)S(1)} collective-permute-done((f32[8,128]{1,0:T(8,128)S(1)}, f32[8,128]{1,0:T(8,128)S(1)}, u32[]{:S(2)}, u32[]{:S(2)}) %collective-permute-start.28) | collective-permute-done | bytes 4128 | tf_op jit(solution)/shard_map/ppermute | solution.py:222
  57.6 2.4 %collective-permute-start.29 = (f32[8,128]{1,0:T(8,128)S(1)}, f32[8,128]{1,0:T(8,128)S(1)}, u32[]{:S(2)}, u32[]{:S(2)}) collective-permute-start(f32[8,128]{1,0:T(8,128)S(1)} %add_add_fusion.1.totals), channel_id=1, source_target_pairs={{0,9},{1,8},{2,11},{3,10},{4,13},{5,12},{6,15},{7,14},{8,1},{9,0},... | collective-permute-start | bytes 12296 | tf_op jit(solution)/shard_map/ppermute | solution.py:222
  60.0 1.5 %collective-permute-done.29.more = f32[8,128]{1,0:T(8,128)S(1)} collective-permute-done((f32[8,128]{1,0:T(8,128)S(1)}, f32[8,128]{1,0:T(8,128)S(1)}, u32[]{:S(2)}, u32[]{:S(2)}) %collective-permute-start.29) | collective-permute-done | bytes 4128 | tf_op jit(solution)/shard_map/ppermute | solution.py:222
  64.1 1.5 %collective-permute-done.32.x = f32[1,1024]{1,0:T(1,128)S(1)} collective-permute-done((f32[1,1024]{1,0:T(1,128)S(1)}, f32[1,1024]{1,0:T(1,128)S(1)}, u32[]{:S(2)}, u32[]{:S(2)}) %collective-permute-start.32) | collective-permute-done | bytes 4128 | tf_op jit(solution)/shard_map/ppermute | solution.py:225
  66.4 2.3 %collective-permute-start.35 = (f32[8,128]{1,0:T(8,128)S(1)}, f32[8,128]{1,0:T(8,128)S(1)}, u32[]{:S(2)}, u32[]{:S(2)}) collective-permute-start(f32[8,128]{1,0:T(8,128)S(1)} %shard_map.78), channel_id=1, source_target_pairs={{0,6},{1,7},{2,4},{3,5},{4,2},{5,3},{6,0},{7,1},{8,14},{9,15},{10,... | collective-permute-start | bytes 12296 | tf_op jit(solution)/shard_map/ppermute | solution.py:222
  69.7 1.3 %collective-permute-done.35 = f32[8,128]{1,0:T(8,128)S(1)} collective-permute-done((f32[8,128]{1,0:T(8,128)S(1)}, f32[8,128]{1,0:T(8,128)S(1)}, u32[]{:S(2)}, u32[]{:S(2)}) %collective-permute-start.35) | collective-permute-done | bytes 4128 | tf_op jit(solution)/shard_map/ppermute | solution.py:222
  71.8 2.7 %collective-permute-start.36 = (f32[8,128]{1,0:T(8,128)S(1)}, f32[8,128]{1,0:T(8,128)S(1)}, u32[]{:S(2)}, u32[]{:S(2)}) collective-permute-start(f32[8,128]{1,0:T(8,128)S(1)} %add_add_fusion.totals), channel_id=1, source_target_pairs={{0,9},{1,8},{2,11},{3,10},{4,13},{5,12},{6,15},{7,14},{8,1},{9,0},... | collective-permute-start | bytes 12296 | tf_op jit(solution)/shard_map/ppermute | solution.py:222
  74.4 1.3 %collective-permute-done.36.more = f32[8,128]{1,0:T(8,128)S(1)} collective-permute-done((f32[8,128]{1,0:T(8,128)S(1)}, f32[8,128]{1,0:T(8,128)S(1)}, u32[]{:S(2)}, u32[]{:S(2)}) %collective-permute-start.36) | collective-permute-done | bytes 4128 | tf_op jit(solution)/shard_map/ppermute | solution.py:222
  76.2 1.5 %collective-permute-start.39 = (f32[16,128]{1,0:T(8,128)S(1)}, f32[16,128]{1,0:T(8,128)S(1)}, u32[]{:S(2)}, u32[]{:S(2)}) collective-permute-start(f32[16,128]{1,0:T(8,128)S(1)} %get-tuple-element.61), channel_id=1, source_target_pairs={{0,16},{16,0},{1,17},{17,1},{2,18},{18,2},{3,19},{19,3},{4,20},{20... | collective-permute-start | bytes 24584 | tf_op jit(solution)/shard_map/ppermute | solution.py:225
  78.4 1.5 %collective-permute-done.39.x = f32[16,128]{1,0:T(8,128)S(1)} collective-permute-done((f32[16,128]{1,0:T(8,128)S(1)}, f32[16,128]{1,0:T(8,128)S(1)}, u32[]{:S(2)}, u32[]{:S(2)}) %collective-permute-start.39) | collective-permute-done | bytes 8224 | tf_op jit(solution)/shard_map/ppermute | solution.py:225
  (81 shorter events, 23.2 us)
Async XLA Ops:
  0.6 16.7 %collective-permute-start.5 = (bf16[2048,512]{1,0:T(8,128)(2,1)}, bf16[2048,512]{1,0:T(8,128)(2,1)S(1)}, u32[]{:S(2)}, u32[]{:S(2)}) collective-permute-start(bf16[2048,512]{1,0:T(8,128)(2,1)} %plan.5), channel_id=1, source_target_pairs={{0,1},{1,0},{2,3},{3,2},{4,5},{5,4},{6,7},{7,6},{8,9},{9,8},{10,11... | collective-permute-start | bytes 6291464 | tf_op jit(solution)/shard_map/ppermute | solution.py:222
  1.1 12.2 %collective-permute-start = (bf16[512,256]{1,0:T(8,128)(2,1)}, bf16[512,256]{1,0:T(8,128)(2,1)S(1)}, u32[]{:S(2)}, u32[]{:S(2)}) collective-permute-start(bf16[512,256]{1,0:T(8,128)(2,1)} %near.3), channel_id=1, source_target_pairs={{0,16},{16,0},{1,17},{17,1},{2,18},{18,2},{3,19},{19,3},{4,20},{20... | collective-permute-start | bytes 786440 | tf_op jit(solution)/shard_map/ppermute | solution.py:225
  3.7 9.6 %collective-permute-start.3 = (bf16[32,2048]{1,0:T(8,128)(2,1)}, bf16[32,2048]{1,0:T(8,128)(2,1)S(1)}, u32[]{:S(2)}, u32[]{:S(2)}) collective-permute-start(bf16[32,2048]{1,0:T(8,128)(2,1)} %bitcast.5), channel_id=1, source_target_pairs={{0,9},{1,8},{2,11},{3,10},{4,13},{5,12},{6,15},{7,14},{8,1},{9,0},... | collective-permute-start | bytes 393224 | tf_op jit(solution)/shard_map/ppermute | solution.py:222
  6.1 7.2 %collective-permute-start.2 = (bf16[32,2048]{1,0:T(8,128)(2,1)}, bf16[32,2048]{1,0:T(8,128)(2,1)S(1)}, u32[]{:S(2)}, u32[]{:S(2)}) collective-permute-start(bf16[32,2048]{1,0:T(8,128)(2,1)} %bitcast.6), channel_id=1, source_target_pairs={{0,5},{1,4},{2,7},{3,6},{4,1},{5,0},{6,3},{7,2},{8,13},{9,12},{10,... | collective-permute-start | bytes 393224 | tf_op jit(solution)/shard_map/ppermute | solution.py:222
  7.6 5.8 %collective-permute-start.1 = (bf16[32,2048]{1,0:T(8,128)(2,1)}, bf16[32,2048]{1,0:T(8,128)(2,1)S(1)}, u32[]{:S(2)}, u32[]{:S(2)}) collective-permute-start(bf16[32,2048]{1,0:T(8,128)(2,1)} %bitcast.7), channel_id=1, source_target_pairs={{0,3},{1,2},{2,1},{3,0},{4,7},{5,6},{6,5},{7,4},{8,11},{9,10},{10,... | collective-permute-start | bytes 393224 | tf_op jit(solution)/shard_map/ppermute | solution.py:222
  13.6 3.4 %collective-permute-start.4 = (bf16[512,512]{1,0:T(8,128)(2,1)S(1)}, bf16[512,512]{1,0:T(8,128)(2,1)S(1)}, u32[]{:S(2)}, u32[]{:S(2)}) collective-permute-start(bf16[512,512]{1,0:T(8,128)(2,1)S(1)} %shard_map.69.units.targets), channel_id=1, source_target_pairs={{0,1},{1,0},{2,3},{3,2},{4,5},{5,4},{6,7},{7,6},{8,9},{9,8},{10,11... | collective-permute-start | bytes 1572872 | tf_op jit(solution)/shard_map/ppermute | solution.py:222
  13.9 5.4 %collective-permute-start.7 = (bf16[32,2048]{1,0:T(8,128)(2,1)S(1)}, bf16[32,2048]{1,0:T(8,128)(2,1)S(1)}, u32[]{:S(2)}, u32[]{:S(2)}) collective-permute-start(bf16[32,2048]{1,0:T(8,128)(2,1)S(1)} %collective-permute-done.3.refs_1_.p1), channel_id=1, source_target_pairs={{0,5},{1,4},{2,7},{3,6},{4,1},{5,0},{6,3},{7,2},{8,13},{9,12},{10,... | collective-permute-start | bytes 393224 | tf_op jit(solution)/shard_map/ppermute | solution.py:222
  15.4 3.4 %collective-permute-start.6 = (f32[1,512]{1,0:T(1,128)S(1)}, f32[1,512]{1,0:T(1,128)S(1)}, u32[]{:S(2)}, u32[]{:S(2)}) collective-permute-start(f32[1,512]{1,0:T(1,128)S(1)} %get-tuple-element.39.mass), channel_id=1, source_target_pairs={{0,1},{1,0},{2,3},{3,2},{4,5},{5,4},{6,7},{7,6},{8,9},{9,8},{10,11... | collective-permute-start | bytes 6152 | tf_op jit(solution)/shard_map/ppermute | solution.py:222
  15.5 6.0 %collective-permute-start.8 = (bf16[32,2048]{1,0:T(8,128)(2,1)S(1)}, bf16[32,2048]{1,0:T(8,128)(2,1)S(1)}, u32[]{:S(2)}, u32[]{:S(2)}) collective-permute-start(bf16[32,2048]{1,0:T(8,128)(2,1)S(1)} %collective-permute-done.3.refs_1_.p1), channel_id=1, source_target_pairs={{0,3},{1,2},{2,1},{3,0},{4,7},{5,6},{6,5},{7,4},{8,11},{9,10},{10,... | collective-permute-start | bytes 393224 | tf_op jit(solution)/shard_map/ppermute | solution.py:222
  17.0 7.2 %collective-permute-start.10 = (bf16[32,2048]{1,0:T(8,128)(2,1)S(1)}, bf16[32,2048]{1,0:T(8,128)(2,1)S(1)}, u32[]{:S(2)}, u32[]{:S(2)}) collective-permute-start(bf16[32,2048]{1,0:T(8,128)(2,1)S(1)} %collective-permute-done.1.p4), channel_id=1, source_target_pairs={{0,5},{1,4},{2,7},{3,6},{4,1},{5,0},{6,3},{7,2},{8,13},{9,12},{10,... | collective-permute-start | bytes 393224 | tf_op jit(solution)/shard_map/ppermute | solution.py:222
  19.4 6.5 %collective-permute-start.9 = (bf16[32,2048]{1,0:T(8,128)(2,1)S(1)}, bf16[32,2048]{1,0:T(8,128)(2,1)S(1)}, u32[]{:S(2)}, u32[]{:S(2)}) collective-permute-start(bf16[32,2048]{1,0:T(8,128)(2,1)S(1)} %collective-permute-done.7.refs_3_.p3), channel_id=1, source_target_pairs={{0,3},{1,2},{2,1},{3,0},{4,7},{5,6},{6,5},{7,4},{8,11},{9,10},{10,... | collective-permute-start | bytes 393224 | tf_op jit(solution)/shard_map/ppermute | solution.py:222
  22.7 3.1 %collective-permute-start.12 = (f32[1,2048]{1,0:T(1,128)S(1)}, f32[1,2048]{1,0:T(1,128)S(1)}, u32[]{:S(2)}, u32[]{:S(2)}) collective-permute-start(f32[1,2048]{1,0:T(1,128)S(1)} %add.36.squares), channel_id=1, source_target_pairs={{0,3},{1,2},{2,1},{3,0},{4,7},{5,6},{6,5},{7,4},{8,11},{9,10},{10,... | collective-permute-start | bytes 24584 | tf_op jit(solution)/shard_map/ppermute | solution.py:222
  26.4 4.3 %collective-permute-start.13 = (bf16[128,256]{1,0:T(8,128)(2,1)S(1)}, bf16[128,256]{1,0:T(8,128)(2,1)S(1)}, u32[]{:S(2)}, u32[]{:S(2)}) collective-permute-start(bf16[128,256]{1,0:T(8,128)(2,1)S(1)} %get-tuple-element.50), channel_id=1, source_target_pairs={{0,16},{16,0},{1,17},{17,1},{2,18},{18,2},{3,19},{19,3},{4,20},{20... | collective-permute-start | bytes 196616 | tf_op jit(solution)/shard_map/ppermute | solution.py:225
  27.0 5.7 %collective-permute-start.14 = (bf16[128,256]{1,0:T(8,128)(2,1)S(1)}, bf16[128,256]{1,0:T(8,128)(2,1)S(1)}, u32[]{:S(2)}, u32[]{:S(2)}) collective-permute-start(bf16[128,256]{1,0:T(8,128)(2,1)S(1)} %get-tuple-element.51), channel_id=1, source_target_pairs={{0,3},{1,2},{2,1},{3,0},{4,7},{5,6},{6,5},{7,4},{8,11},{9,10},{10,... | collective-permute-start | bytes 196616 | tf_op jit(solution)/shard_map/ppermute | solution.py:222
  27.2 5.5 %collective-permute-start.15 = (bf16[128,256]{1,0:T(8,128)(2,1)S(1)}, bf16[128,256]{1,0:T(8,128)(2,1)S(1)}, u32[]{:S(2)}, u32[]{:S(2)}) collective-permute-start(bf16[128,256]{1,0:T(8,128)(2,1)S(1)} %get-tuple-element.52), channel_id=1, source_target_pairs={{0,19},{1,18},{2,17},{3,16},{4,23},{5,22},{6,21},{7,20},{8,27},{9,... | collective-permute-start | bytes 196616 | tf_op jit(solution)/shard_map/ppermute | solution.py:229
  32.8 4.2 %collective-permute-start.16 = (bf16[128,256]{1,0:T(8,128)(2,1)S(1)}, bf16[128,256]{1,0:T(8,128)(2,1)S(1)}, u32[]{:S(2)}, u32[]{:S(2)}) collective-permute-start(bf16[128,256]{1,0:T(8,128)(2,1)S(1)} %get-tuple-element.64), channel_id=1, source_target_pairs={{0,5},{1,4},{2,7},{3,6},{4,1},{5,0},{6,3},{7,2},{8,13},{9,12},{10,... | collective-permute-start | bytes 196616 | tf_op jit(solution)/shard_map/ppermute | solution.py:222
  34.2 16.6 %collective-permute-start.25 = (bf16[256,2048]{1,0:T(8,128)(2,1)S(1)}, bf16[256,2048]{1,0:T(8,128)(2,1)S(1)}, u32[]{:S(2)}, u32[]{:S(2)}) collective-permute-start(bf16[256,2048]{1,0:T(8,128)(2,1)S(1)} %get-tuple-element.49.units.near), channel_id=1, source_target_pairs={{0,1},{1,0},{2,3},{3,2},{4,5},{5,4},{6,7},{7,6},{8,9},{9,8},{10,11... | collective-permute-start | bytes 3145736 | tf_op jit(solution)/shard_map/ppermute | solution.py:222
  37.0 5.1 %collective-permute-start.17 = (bf16[128,256]{1,0:T(8,128)(2,1)S(1)}, bf16[128,256]{1,0:T(8,128)(2,1)S(1)}, u32[]{:S(2)}, u32[]{:S(2)}) collective-permute-start(bf16[128,256]{1,0:T(8,128)(2,1)S(1)} %fusion.1), channel_id=1, source_target_pairs={{0,9},{1,8},{2,11},{3,10},{4,13},{5,12},{6,15},{7,14},{8,1},{9,0},... | collective-permute-start | bytes 196616 | tf_op jit(solution)/shard_map/ppermute | solution.py:222
  42.1 4.7 %collective-permute-start.20 = (bf16[128,256]{1,0:T(8,128)(2,1)S(1)}, bf16[128,256]{1,0:T(8,128)(2,1)S(1)}, u32[]{:S(2)}, u32[]{:S(2)}) collective-permute-start(bf16[128,256]{1,0:T(8,128)(2,1)S(1)} %fusion.c0), channel_id=1, source_target_pairs={{0,19},{1,18},{2,17},{3,16},{4,23},{5,22},{6,21},{7,20},{8,27},{9,... | collective-permute-start | bytes 196616 | tf_op jit(solution)/shard_map/ppermute | solution.py:229
  44.3 4.7 %collective-permute-start.19 = (bf16[128,256]{1,0:T(8,128)(2,1)S(1)}, bf16[128,256]{1,0:T(8,128)(2,1)S(1)}, u32[]{:S(2)}, u32[]{:S(2)}) collective-permute-start(bf16[128,256]{1,0:T(8,128)(2,1)S(1)} %fusion.c0), channel_id=1, source_target_pairs={{0,3},{1,2},{2,1},{3,0},{4,7},{5,6},{6,5},{7,4},{8,11},{9,10},{10,... | collective-permute-start | bytes 196616 | tf_op jit(solution)/shard_map/ppermute | solution.py:222
  44.9 4.6 %collective-permute-start.18 = (bf16[128,256]{1,0:T(8,128)(2,1)S(1)}, bf16[128,256]{1,0:T(8,128)(2,1)S(1)}, u32[]{:S(2)}, u32[]{:S(2)}) collective-permute-start(bf16[128,256]{1,0:T(8,128)(2,1)S(1)} %fusion.c0), channel_id=1, source_target_pairs={{0,16},{16,0},{1,17},{17,1},{2,18},{18,2},{3,19},{19,3},{4,20},{20... | collective-permute-start | bytes 196616 | tf_op jit(solution)/shard_map/ppermute | solution.py:225
  45.4 4.7 %collective-permute-start.21 = (bf16[128,256]{1,0:T(8,128)(2,1)S(1)}, bf16[128,256]{1,0:T(8,128)(2,1)S(1)}, u32[]{:S(2)}, u32[]{:S(2)}) collective-permute-start(bf16[128,256]{1,0:T(8,128)(2,1)S(1)} %fusion.c0), channel_id=1, source_target_pairs={{0,1},{1,0},{2,3},{3,2},{4,5},{5,4},{6,7},{7,6},{8,9},{9,8},{10,11... | collective-permute-start | bytes 196616 | tf_op jit(solution)/shard_map/ppermute | solution.py:222
  46.8 3.4 %collective-permute-start.24 = (bf16[128,256]{1,0:T(8,128)(2,1)S(1)}, bf16[128,256]{1,0:T(8,128)(2,1)S(1)}, u32[]{:S(2)}, u32[]{:S(2)}) collective-permute-start(bf16[128,256]{1,0:T(8,128)(2,1)S(1)} %collective-permute-done.20.x1), channel_id=1, source_target_pairs={{0,1},{1,0},{2,3},{3,2},{4,5},{5,4},{6,7},{7,6},{8,9},{9,8},{10,11... | collective-permute-start | bytes 196616 | tf_op jit(solution)/shard_map/ppermute | solution.py:222
  52.3 4.6 %collective-permute-start.28 = (f32[8,128]{1,0:T(8,128)S(1)}, f32[8,128]{1,0:T(8,128)S(1)}, u32[]{:S(2)}, u32[]{:S(2)}) collective-permute-start(f32[8,128]{1,0:T(8,128)S(1)} %get-tuple-element.56), channel_id=1, source_target_pairs={{0,6},{1,7},{2,4},{3,5},{4,2},{5,3},{6,0},{7,1},{8,14},{9,15},{10,... | collective-permute-start | bytes 12296 | tf_op jit(solution)/shard_map/ppermute | solution.py:222
  57.6 3.9 %collective-permute-start.29 = (f32[8,128]{1,0:T(8,128)S(1)}, f32[8,128]{1,0:T(8,128)S(1)}, u32[]{:S(2)}, u32[]{:S(2)}) collective-permute-start(f32[8,128]{1,0:T(8,128)S(1)} %add_add_fusion.1.totals), channel_id=1, source_target_pairs={{0,9},{1,8},{2,11},{3,10},{4,13},{5,12},{6,15},{7,14},{8,1},{9,0},... | collective-permute-start | bytes 12296 | tf_op jit(solution)/shard_map/ppermute | solution.py:222
  61.9 3.7 %collective-permute-start.32 = (f32[1,1024]{1,0:T(1,128)S(1)}, f32[1,1024]{1,0:T(1,128)S(1)}, u32[]{:S(2)}, u32[]{:S(2)}) collective-permute-start(f32[1,1024]{1,0:T(1,128)S(1)} %shard_map.77.own), channel_id=1, source_target_pairs={{0,16},{16,0},{1,17},{17,1},{2,18},{18,2},{3,19},{19,3},{4,20},{20... | collective-permute-start | bytes 12296 | tf_op jit(solution)/shard_map/ppermute | solution.py:225
  66.4 4.6 %collective-permute-start.35 = (f32[8,128]{1,0:T(8,128)S(1)}, f32[8,128]{1,0:T(8,128)S(1)}, u32[]{:S(2)}, u32[]{:S(2)}) collective-permute-start(f32[8,128]{1,0:T(8,128)S(1)} %shard_map.78), channel_id=1, source_target_pairs={{0,6},{1,7},{2,4},{3,5},{4,2},{5,3},{6,0},{7,1},{8,14},{9,15},{10,... | collective-permute-start | bytes 12296 | tf_op jit(solution)/shard_map/ppermute | solution.py:222
  68.7 3.1 %collective-permute-start.34 = (f32[8,128]{1,0:T(8,128)S(1)}, f32[8,128]{1,0:T(8,128)S(1)}, u32[]{:S(2)}, u32[]{:S(2)}) collective-permute-start(f32[8,128]{1,0:T(8,128)S(1)} %shard_map.78), channel_id=1, source_target_pairs={{0,5},{1,4},{2,7},{3,6},{4,1},{5,0},{6,3},{7,2},{8,13},{9,12},{10,... | collective-permute-start | bytes 12296 | tf_op jit(solution)/shard_map/ppermute | solution.py:222
  71.8 4.0 %collective-permute-start.36 = (f32[8,128]{1,0:T(8,128)S(1)}, f32[8,128]{1,0:T(8,128)S(1)}, u32[]{:S(2)}, u32[]{:S(2)}) collective-permute-start(f32[8,128]{1,0:T(8,128)S(1)} %add_add_fusion.totals), channel_id=1, source_target_pairs={{0,9},{1,8},{2,11},{3,10},{4,13},{5,12},{6,15},{7,14},{8,1},{9,0},... | collective-permute-start | bytes 12296 | tf_op jit(solution)/shard_map/ppermute | solution.py:222
  76.2 3.7 %collective-permute-start.39 = (f32[16,128]{1,0:T(8,128)S(1)}, f32[16,128]{1,0:T(8,128)S(1)}, u32[]{:S(2)}, u32[]{:S(2)}) collective-permute-start(f32[16,128]{1,0:T(8,128)S(1)} %get-tuple-element.61), channel_id=1, source_target_pairs={{0,16},{16,0},{1,17},{17,1},{2,18},{18,2},{3,19},{19,3},{4,20},{20... | collective-permute-start | bytes 24584 | tf_op jit(solution)/shard_map/ppermute | solution.py:225
  77.7 3.2 %collective-permute-start.38 = (f32[16,128]{1,0:T(8,128)S(1)}, f32[16,128]{1,0:T(8,128)S(1)}, u32[]{:S(2)}, u32[]{:S(2)}) collective-permute-start(f32[16,128]{1,0:T(8,128)S(1)} %get-tuple-element.61), channel_id=1, source_target_pairs={{0,17},{1,16},{2,19},{3,18},{4,21},{5,20},{6,23},{7,22},{8,25},{9,... | collective-permute-start | bytes 24584 | tf_op jit(solution)/shard_map/ppermute | solution.py:229
  77.8 3.1 %collective-permute-start.37 = (f32[16,128]{1,0:T(8,128)S(1)}, f32[16,128]{1,0:T(8,128)S(1)}, u32[]{:S(2)}, u32[]{:S(2)}) collective-permute-start(f32[16,128]{1,0:T(8,128)S(1)} %get-tuple-element.61), channel_id=1, source_target_pairs={{0,1},{1,0},{2,3},{3,2},{4,5},{5,4},{6,7},{7,6},{8,9},{9,8},{10,11... | collective-permute-start | bytes 24584 | tf_op jit(solution)/shard_map/ppermute | solution.py:222
  (14 other events, 32.7 us)
